TPU v7x, 32 devices: a whole 2x2x4 slice. The times are simulated.
32 devices in a mesh: ax: 4 (over y, core), az: 4 (over z), rad: 2 (over x).
Axes of the slice: x: 2, y: 2, z: 4, core: 2. Of those that a mesh axis runs over, the one named last changes fastest.
Arguments:
- density: float32 [32, 64, 256], P('ax', 'az', 'rad'), may hold values from 0.855 to 1.21
- velocity: float32 [3, 32, 64, 256], P(None, 'ax', 'az', 'rad'), may hold values from -2.9 to 2.9
- pressure: float32 [32, 64, 256], P('ax', 'az', 'rad'), may hold values from 0.51 to 1.84
- panel_cell: int32 [1024], P(('ax', 'az', 'rad')), may hold values from -1 to 16383, as said below
- obs_weight: bfloat16 [8192, 1024], P(('ax', 'az', 'rad')), may hold values from -1 to 1
- bin_offset: int32 [32, 32], P(('ax', 'az', 'rad')), may hold values from 0 to 125
Outputs:
- state: float32 [5, 32, 64, 256], P(None, 'ax', 'az', 'rad')
- signal: float32 [8192, 128], P(('ax', 'az', 'rad'))
Inputs may be any that keep to these rules, and one draw needn't show every extreme that they name: `panel_cell`: live slots of one device come first, then -1; some device has all 32 slots live.
All inputs are finite; a program needn't handle non-finite values.
Results may differ from a plain program's by a relative error of at most 0.0029.
Values may be sent and summed in bfloat16 or wider, within the bound.
No kernel may reach another device: no remote copies, remote signals or barrier semaphores. Data moves between devices by JAX's collectives and lax.ppermute only.
A program may use at most 64 MiB of HBM per device.

v0:
```python
import jax
import jax.numpy as jnp
from jax import lax
from jax.sharding import PartitionSpec as P

NB = 128


GAMMA_M = 0.4
LAMBDA = 0.1
P_REF = 1.0


def with_halo(block, sides, width, periodic):
    for axis, dim in sides:
        count = lax.axis_size(axis)
        forward = [(i, i + 1) for i in range(count - 1)]
        if periodic:
            forward.append((count - 1, 0))
        backward = [(target, source) for source, target in forward]
        low = lax.ppermute(
            lax.slice_in_dim(block, block.shape[dim] - width, None, axis=dim), axis, forward
        )
        high = lax.ppermute(lax.slice_in_dim(block, 0, width, axis=dim), axis, backward)
        block = jnp.concatenate([low, block, high], axis=dim)
    return block


def primitives(state):
    rho = state[0]
    vel = state[1:4] / rho
    pres = GAMMA_M * (state[4] - 0.5 * rho * jnp.sum(vel * vel, axis=0))
    return jnp.concatenate([rho[None], vel, pres[None]], 0)


def flux(prim, direc):
    rho = prim[0]
    vel = prim[1:4]
    pres = prim[4]
    normal = vel[direc]
    energy = pres / GAMMA_M + 0.5 * rho * jnp.sum(vel * vel, axis=0)
    moment = rho[None] * normal[None] * vel
    moment = moment.at[direc].add(pres)
    return jnp.concatenate([(rho * normal)[None], moment, ((energy + pres) * normal)[None]], 0)


def deriv(padded, axis, count):

    def piece(low):
        return lax.slice_in_dim(padded, low, low + count, axis=axis)

    return (piece(0) - 8.0 * piece(1) + 8.0 * piece(3) - piece(4)) / 12.0


def tendency(state):
    prim = primitives(state)
    pad_ax = with_halo(flux(prim, 0), (("ax", 1),), 2, False)
    pad_az = with_halo(flux(prim, 1), (("az", 2),), 2, True)
    pad_rad = with_halo(flux(prim, 2), (("rad", 3),), 2, False)
    total = deriv(pad_ax, 1, state.shape[1])
    total = total + deriv(pad_az, 2, state.shape[2])
    total = total + deriv(pad_rad, 3, state.shape[3])
    return (-LAMBDA * total, prim)


def sample(state, prim, panel_cell):
    value = (prim[4] - P_REF + state[1]).reshape(-1)
    picked = value[jnp.maximum(panel_cell, 0)]
    return jnp.where(panel_cell >= 0, picked, 0.0).astype(jnp.bfloat16)


def local(density, velocity, pressure, panel_cell, obs_weight, bin_offset):
    slots = panel_cell.shape[0]
    offsets = bin_offset[0]
    ndev = offsets.shape[0]
    times = jnp.arange(NB, dtype=jnp.int32)
    owners = jnp.arange(ndev, dtype=jnp.int32)

    def add_panels(carry, piece):
        count = piece.shape[1]
        source = jnp.arange(count, dtype=jnp.int32) // slots
        chosen = jnp.sum(jnp.where(source[:, None] == owners[None, :], offsets[None, :], 0), axis=1)
        spread = jnp.zeros((count, NB), jnp.float32)
        for section in range(piece.shape[0]):
            hit = times[None, :] == chosen[:, None] + section
            spread = spread + jnp.where(hit, piece[section].astype(jnp.float32)[:, None], 0.0)
        return carry + jnp.dot(
            obs_weight, spread.astype(jnp.bfloat16), preferred_element_type=jnp.float32
        )

    momentum = density[None] * velocity
    energy = pressure / GAMMA_M + 0.5 * density * jnp.sum(velocity * velocity, axis=0)
    first = jnp.concatenate([density[None], momentum, energy[None]], 0)
    signal = jnp.zeros((obs_weight.shape[0], NB), jnp.float32)
    change, prim = tendency(first)
    samples = [sample(first, prim, panel_cell)]
    second = first + change
    change, prim = tendency(second)
    samples.append(sample(second, prim, panel_cell))
    third = 0.75 * first + 0.25 * (second + change)
    change, prim = tendency(third)
    samples.append(sample(third, prim, panel_cell))
    final = first / 3.0 + 2.0 / 3.0 * (third + change)
    for section in range(3):

        def add_section(carry, piece, start, section=section):
            shifted = jnp.concatenate([jnp.zeros((section, piece.shape[1]), piece.dtype), piece], 0)
            return add_panels(carry, shifted)

        signal = add_section(
            signal,
            lax.all_gather(samples[section][None], ("ax", "az", "rad"), axis=1, tiled=True),
            jnp.int32(0),
        )
    return (final, signal)


def solution(mesh):
    in_specs = (
        P("ax", "az", "rad"),
        P(None, "ax", "az", "rad"),
        P("ax", "az", "rad"),
        P(("ax", "az", "rad")),
        P(("ax", "az", "rad"), None),
        P(("ax", "az", "rad"), None),
    )
    out_specs = (P(None, "ax", "az", "rad"), P(("ax", "az", "rad"), None))
    return jax.shard_map(local, mesh=mesh, in_specs=in_specs, out_specs=out_specs, check_vma=False)
```

profile of v0, /device:TPU:14, one launch (start us, length us, event | category | flops | bytes accessed | tf_op | source)
XLA Modules:
  0.0 114.9 jit_solution(18014615877915066391)
XLA Ops:
  0.7 1.1 multiply_reduce_fusion.2
  1.8 0.8 copy-done.2
  2.8 0.6 pad_maximum_fusion.30
  3.4 1.6 %collective-permute-start.2 = (f32[5,8,2,128]{3,2,1,0:T(2,128)}, f32[5,8,2,128]{3,2,1,0:T(2,128)S(1)}, u32[]{:S(2)}, u32[]{:S(2)}) collective-permute-start(f32[5,8,2,128]{3,2,1,0:T(2,128)} %get-tuple-element.181), channel_id=1, source_target_pairs={{0,2},{2,4},{4,6},{6,0},{1,3},{3,5},{5,7},{7,1},{8,10},{10,12},{12... | collective-permute-start | bytes 122888 | tf_op jit(solution)/shard_map/ppermute | solution.py:21
  5.0 0.4 collective-permute-start.3
  5.5 1.9 %collective-permute-start = (f32[5,2,16,128]{3,2,1,0:T(8,128)S(1)}, f32[5,2,16,128]{3,2,1,0:T(8,128)S(1)}, u32[]{:S(2)}, u32[]{:S(2)}) collective-permute-start(f32[5,2,16,128]{3,2,1,0:T(8,128)S(1)} %get-tuple-element.177), channel_id=1, source_target_pairs={{0,8},{8,16},{16,24},{1,9},{9,17},{17,25},{2,10},{10,18},{18,26},{... | collective-permute-start | bytes 245768 | tf_op jit(solution)/shard_map/ppermute | solution.py:21
  7.4 0.2 fusion.70
  7.6 1.3 %collective-permute-start.4 = (f32[5,8,16,2]{3,2,1,0:T(8,128)S(1)}, f32[5,8,16,2]{3,2,1,0:T(8,128)S(1)}, u32[]{:S(2)}, u32[]{:S(2)}) collective-permute-start(f32[5,8,16,2]{3,2,1,0:T(8,128)S(1)} %get-tuple-element.185), channel_id=1, source_target_pairs={{0,1},{2,3},{4,5},{6,7},{8,9},{10,11},{12,13},{14,15},{16,17},{18,... | collective-permute-start | bytes 15368 | tf_op jit(solution)/shard_map/ppermute | solution.py:21
  8.9 4.6 %collective-permute-start.5 = (f32[5,8,16,2]{3,2,1,0:T(8,128)S(1)}, f32[5,8,16,2]{3,2,1,0:T(8,128)S(1)}, u32[]{:S(2)}, u32[]{:S(2)}) collective-permute-start(f32[5,8,16,2]{3,2,1,0:T(8,128)S(1)} %get-tuple-element.186), channel_id=1, source_target_pairs={{1,0},{3,2},{5,4},{7,6},{9,8},{11,10},{13,12},{15,14},{17,16},{19,... | collective-permute-start | bytes 15368 | tf_op jit(solution)/shard_map/ppermute | solution.py:24
  13.5 0.6 copy-done.6
  14.3 0.6 broadcast_add_fusion
  14.9 1.2 %gather_fusion = bf16[32]{0:T(256)(128)(2,1)} fusion(bf16[16384]{0:T(1024)(128)(2,1)S(1)} %bitcast.94, s32[1024]{0:T(1024)S(1)} %pad_clamp_fusion), kind=kCustom, calls=%fused_computation | custom fusion | bytes 256 | tf_op jit(solution)/shard_map/gather | solution.py:68
  16.1 1.6 %collective-permute-done.4 = f32[5,8,16,2]{3,2,1,0:T(8,128)S(1)} collective-permute-done((f32[5,8,16,2]{3,2,1,0:T(8,128)S(1)}, f32[5,8,16,2]{3,2,1,0:T(8,128)S(1)}, u32[]{:S(2)}, u32[]{:S(2)}) %collective-permute-start.4) | collective-permute-done | bytes 5152 | tf_op jit(solution)/shard_map/ppermute | solution.py:21
  17.7 3.5 %collective-permute-start.1 = (f32[5,2,16,128]{3,2,1,0:T(8,128)S(1)}, f32[5,2,16,128]{3,2,1,0:T(8,128)S(1)}, u32[]{:S(2)}, u32[]{:S(2)}) collective-permute-start(f32[5,2,16,128]{3,2,1,0:T(8,128)S(1)} %get-tuple-element.178), channel_id=1, source_target_pairs={{8,0},{16,8},{24,16},{9,1},{17,9},{25,17},{10,2},{18,10},{26,18},{... | collective-permute-start | bytes 245768 | tf_op jit(solution)/shard_map/ppermute | solution.py:24
  21.3 0.3 maximum_maximum_fusion
  21.7 1.7 %collective-permute-done.1 = f32[5,2,16,128]{3,2,1,0:T(8,128)S(1)} collective-permute-done((f32[5,2,16,128]{3,2,1,0:T(8,128)S(1)}, f32[5,2,16,128]{3,2,1,0:T(8,128)S(1)}, u32[]{:S(2)}, u32[]{:S(2)}) %collective-permute-start.1) | collective-permute-done | bytes 81952 | tf_op jit(solution)/shard_map/ppermute | solution.py:24
  23.4 0.4 fusion.27
  24.0 0.7 gather_fusion.1
  24.7 1.9 %collective-permute-start.6 = (f32[5,2,16,128]{3,2,1,0:T(8,128)S(1)}, f32[5,2,16,128]{3,2,1,0:T(8,128)S(1)}, u32[]{:S(2)}, u32[]{:S(2)}) collective-permute-start(f32[5,2,16,128]{3,2,1,0:T(8,128)S(1)} %get-tuple-element.165), channel_id=1, source_target_pairs={{0,8},{8,16},{16,24},{1,9},{9,17},{17,25},{2,10},{10,18},{18,26},{... | collective-permute-start | bytes 245768 | tf_op jit(solution)/shard_map/ppermute | solution.py:21
  26.7 3.7 %collective-permute-start.7 = (f32[5,2,16,128]{3,2,1,0:T(8,128)S(1)}, f32[5,2,16,128]{3,2,1,0:T(8,128)S(1)}, u32[]{:S(2)}, u32[]{:S(2)}) collective-permute-start(f32[5,2,16,128]{3,2,1,0:T(8,128)S(1)} %get-tuple-element.166), channel_id=1, source_target_pairs={{8,0},{16,8},{24,16},{9,1},{17,9},{25,17},{10,2},{18,10},{26,18},{... | collective-permute-start | bytes 245768 | tf_op jit(solution)/shard_map/ppermute | solution.py:24
  30.5 0.2 fusion.69
  30.7 1.3 %collective-permute-start.10 = (f32[5,8,16,2]{3,2,1,0:T(8,128)S(1)}, f32[5,8,16,2]{3,2,1,0:T(8,128)S(1)}, u32[]{:S(2)}, u32[]{:S(2)}) collective-permute-start(f32[5,8,16,2]{3,2,1,0:T(8,128)S(1)} %get-tuple-element.173), channel_id=1, source_target_pairs={{0,1},{2,3},{4,5},{6,7},{8,9},{10,11},{12,13},{14,15},{16,17},{18,... | collective-permute-start | bytes 15368 | tf_op jit(solution)/shard_map/ppermute | solution.py:21
  32.0 4.6 %collective-permute-start.11 = (f32[5,8,16,2]{3,2,1,0:T(8,128)S(1)}, f32[5,8,16,2]{3,2,1,0:T(8,128)S(1)}, u32[]{:S(2)}, u32[]{:S(2)}) collective-permute-start(f32[5,8,16,2]{3,2,1,0:T(8,128)S(1)} %get-tuple-element.174), channel_id=1, source_target_pairs={{1,0},{3,2},{5,4},{7,6},{9,8},{11,10},{13,12},{15,14},{17,16},{19,... | collective-permute-start | bytes 15368 | tf_op jit(solution)/shard_map/ppermute | solution.py:24
  36.6 1.6 %collective-permute-start.8 = (f32[5,8,2,128]{3,2,1,0:T(2,128)S(1)}, f32[5,8,2,128]{3,2,1,0:T(2,128)S(1)}, u32[]{:S(2)}, u32[]{:S(2)}) collective-permute-start(f32[5,8,2,128]{3,2,1,0:T(2,128)S(1)} %get-tuple-element.169), channel_id=1, source_target_pairs={{0,2},{2,4},{4,6},{6,0},{1,3},{3,5},{5,7},{7,1},{8,10},{10,12},{12... | collective-permute-start | bytes 122888 | tf_op jit(solution)/shard_map/ppermute | solution.py:21
  38.2 2.7 %collective-permute-done.10 = f32[5,8,16,2]{3,2,1,0:T(8,128)S(1)} collective-permute-done((f32[5,8,16,2]{3,2,1,0:T(8,128)S(1)}, f32[5,8,16,2]{3,2,1,0:T(8,128)S(1)}, u32[]{:S(2)}, u32[]{:S(2)}) %collective-permute-start.10) | collective-permute-done | bytes 5152 | tf_op jit(solution)/shard_map/ppermute | solution.py:21
  40.9 2.2 %collective-permute-start.9 = (f32[5,8,2,128]{3,2,1,0:T(2,128)S(1)}, f32[5,8,2,128]{3,2,1,0:T(2,128)S(1)}, u32[]{:S(2)}, u32[]{:S(2)}) collective-permute-start(f32[5,8,2,128]{3,2,1,0:T(2,128)S(1)} %get-tuple-element.170), channel_id=1, source_target_pairs={{2,0},{4,2},{6,4},{0,6},{3,1},{5,3},{7,5},{1,7},{10,8},{12,10},{14... | collective-permute-start | bytes 122888 | tf_op jit(solution)/shard_map/ppermute | solution.py:24
  43.1 0.2 maximum_maximum_fusion.1
  43.4 1.5 %collective-permute-done.9 = f32[5,8,2,128]{3,2,1,0:T(2,128)S(1)} collective-permute-done((f32[5,8,2,128]{3,2,1,0:T(2,128)S(1)}, f32[5,8,2,128]{3,2,1,0:T(2,128)S(1)}, u32[]{:S(2)}, u32[]{:S(2)}) %collective-permute-start.9) | collective-permute-done | bytes 40992 | tf_op jit(solution)/shard_map/ppermute | solution.py:24
  45.1 0.4 fusion.17
  45.7 0.7 gather_fusion.2
  46.4 0.2 dynamic-update-slice.27
  46.6 0.2 dynamic-update-slice.29
  46.9 0.2 dynamic-update-slice.28
  47.1 43.5 %all-reduce.3 = (bf16[1024]{0:T(1024)(128)(2,1)S(1)}, bf16[1024]{0:T(1024)(128)(2,1)S(1)}, bf16[1024]{0:T(1024)(128)(2,1)S(1)}) all-reduce(bf16[1024]{0:T(1024)(128)(2,1)S(1)} %dynamic-update-slice.27, bf16[1024]{0:T(1024)(128)(2,1)S(1)} %dynamic-update-slice.28, ...), channel_id=2, replica_groups=mesh['ax'=4,'az'=4,'rad'=2] {'ax','az','rad'}, use_global_device_ids=true, to_apply=%add | all-reduce | flops 3072 | bytes 12288
  90.6 0.7 fusion.35
  91.3 0.7 convolution_add_fusion.1
  92.0 0.7 fusion
  92.6 0.8 copy.10
  93.5 1.9 %collective-permute-start.12 = (f32[5,2,16,128]{3,2,1,0:T(8,128)S(1)}, f32[5,2,16,128]{3,2,1,0:T(8,128)S(1)}, u32[]{:S(2)}, u32[]{:S(2)}) collective-permute-start(f32[5,2,16,128]{3,2,1,0:T(8,128)S(1)} %get-tuple-element.153), channel_id=1, source_target_pairs={{0,8},{8,16},{16,24},{1,9},{9,17},{17,25},{2,10},{10,18},{18,26},{... | collective-permute-start | bytes 245768 | tf_op jit(solution)/shard_map/ppermute | solution.py:21
  95.4 3.6 %collective-permute-start.13 = (f32[5,2,16,128]{3,2,1,0:T(8,128)S(1)}, f32[5,2,16,128]{3,2,1,0:T(8,128)S(1)}, u32[]{:S(2)}, u32[]{:S(2)}) collective-permute-start(f32[5,2,16,128]{3,2,1,0:T(8,128)S(1)} %get-tuple-element.154), channel_id=1, source_target_pairs={{8,0},{16,8},{24,16},{9,1},{17,9},{25,17},{10,2},{18,10},{26,18},{... | collective-permute-start | bytes 245768 | tf_op jit(solution)/shard_map/ppermute | solution.py:24
  99.3 1.3 %collective-permute-start.16 = (f32[5,8,16,2]{3,2,1,0:T(8,128)S(1)}, f32[5,8,16,2]{3,2,1,0:T(8,128)S(1)}, u32[]{:S(2)}, u32[]{:S(2)}) collective-permute-start(f32[5,8,16,2]{3,2,1,0:T(8,128)S(1)} %get-tuple-element.161), channel_id=1, source_target_pairs={{0,1},{2,3},{4,5},{6,7},{8,9},{10,11},{12,13},{14,15},{16,17},{18,... | collective-permute-start | bytes 15368 | tf_op jit(solution)/shard_map/ppermute | solution.py:21
  100.6 4.6 %collective-permute-start.17 = (f32[5,8,16,2]{3,2,1,0:T(8,128)S(1)}, f32[5,8,16,2]{3,2,1,0:T(8,128)S(1)}, u32[]{:S(2)}, u32[]{:S(2)}) collective-permute-start(f32[5,8,16,2]{3,2,1,0:T(8,128)S(1)} %get-tuple-element.162), channel_id=1, source_target_pairs={{1,0},{3,2},{5,4},{7,6},{9,8},{11,10},{13,12},{15,14},{17,16},{19,... | collective-permute-start | bytes 15368 | tf_op jit(solution)/shard_map/ppermute | solution.py:24
  105.2 1.4 %collective-permute-start.14 = (f32[5,8,2,128]{3,2,1,0:T(2,128)S(1)}, f32[5,8,2,128]{3,2,1,0:T(2,128)S(1)}, u32[]{:S(2)}, u32[]{:S(2)}) collective-permute-start(f32[5,8,2,128]{3,2,1,0:T(2,128)S(1)} %get-tuple-element.157), channel_id=1, source_target_pairs={{0,2},{2,4},{4,6},{6,0},{1,3},{3,5},{5,7},{7,1},{8,10},{10,12},{12... | collective-permute-start | bytes 122888 | tf_op jit(solution)/shard_map/ppermute | solution.py:21
  106.7 2.9 %collective-permute-done.16 = f32[5,8,16,2]{3,2,1,0:T(8,128)S(1)} collective-permute-done((f32[5,8,16,2]{3,2,1,0:T(8,128)S(1)}, f32[5,8,16,2]{3,2,1,0:T(8,128)S(1)}, u32[]{:S(2)}, u32[]{:S(2)}) %collective-permute-start.16) | collective-permute-done | bytes 5152 | tf_op jit(solution)/shard_map/ppermute | solution.py:21
  109.6 1.2 %collective-permute-done.17 = f32[5,8,16,2]{3,2,1,0:T(8,128)S(1)} collective-permute-done((f32[5,8,16,2]{3,2,1,0:T(8,128)S(1)}, f32[5,8,16,2]{3,2,1,0:T(8,128)S(1)}, u32[]{:S(2)}, u32[]{:S(2)}) %collective-permute-start.17) | collective-permute-done | bytes 5152 | tf_op jit(solution)/shard_map/ppermute | solution.py:24
  110.8 0.2 maximum_maximum_fusion.2
  111.1 2.5 %collective-permute-done.15 = f32[5,8,2,128]{3,2,1,0:T(2,128)S(1)} collective-permute-done((f32[5,8,2,128]{3,2,1,0:T(2,128)S(1)}, f32[5,8,2,128]{3,2,1,0:T(2,128)S(1)}, u32[]{:S(2)}, u32[]{:S(2)}) %collective-permute-start.15) | collective-permute-done | bytes 40992 | tf_op jit(solution)/shard_map/ppermute | solution.py:24
  113.8 1.1 fusion.5
  (76 shorter events, 1.7 us)
Async XLA Ops:
  0.6 89.9 %copy-start = (bf16[256,1024]{1,0:T(8,128)(2,1)S(1)}, bf16[256,1024]{1,0:T(8,128)(2,1)}, u32[]{:S(2)}) copy-start(bf16[256,1024]{1,0:T(8,128)(2,1)} %param.28) | copy-start | bytes 1572868
  0.6 1.1 copy-start.1
  1.7 0.8 copy-start.2
  3.4 18.1 %collective-permute-start.2 = (f32[5,8,2,128]{3,2,1,0:T(2,128)}, f32[5,8,2,128]{3,2,1,0:T(2,128)S(1)}, u32[]{:S(2)}, u32[]{:S(2)}) collective-permute-start(f32[5,8,2,128]{3,2,1,0:T(2,128)} %get-tuple-element.181), channel_id=1, source_target_pairs={{0,2},{2,4},{4,6},{6,0},{1,3},{3,5},{5,7},{7,1},{8,10},{10,12},{12... | collective-permute-start | bytes 122888 | tf_op jit(solution)/shard_map/ppermute | solution.py:21
  5.0 16.6 %collective-permute-start.3 = (f32[5,8,2,128]{3,2,1,0:T(2,128)S(1)}, f32[5,8,2,128]{3,2,1,0:T(2,128)S(1)}, u32[]{:S(2)}, u32[]{:S(2)}) collective-permute-start(f32[5,8,2,128]{3,2,1,0:T(2,128)S(1)} %get-tuple-element.182), channel_id=1, source_target_pairs={{2,0},{4,2},{6,4},{0,6},{3,1},{5,3},{7,5},{1,7},{10,8},{12,10},{14... | collective-permute-start | bytes 122888 | tf_op jit(solution)/shard_map/ppermute | solution.py:24
  5.5 16.2 %collective-permute-start = (f32[5,2,16,128]{3,2,1,0:T(8,128)S(1)}, f32[5,2,16,128]{3,2,1,0:T(8,128)S(1)}, u32[]{:S(2)}, u32[]{:S(2)}) collective-permute-start(f32[5,2,16,128]{3,2,1,0:T(8,128)S(1)} %get-tuple-element.177), channel_id=1, source_target_pairs={{0,8},{8,16},{16,24},{1,9},{9,17},{17,25},{2,10},{10,18},{18,26},{... | collective-permute-start | bytes 245768 | tf_op jit(solution)/shard_map/ppermute | solution.py:21
  7.6 10.2 %collective-permute-start.4 = (f32[5,8,16,2]{3,2,1,0:T(8,128)S(1)}, f32[5,8,16,2]{3,2,1,0:T(8,128)S(1)}, u32[]{:S(2)}, u32[]{:S(2)}) collective-permute-start(f32[5,8,16,2]{3,2,1,0:T(8,128)S(1)} %get-tuple-element.185), channel_id=1, source_target_pairs={{0,1},{2,3},{4,5},{6,7},{8,9},{10,11},{12,13},{14,15},{16,17},{18,... | collective-permute-start | bytes 15368 | tf_op jit(solution)/shard_map/ppermute | solution.py:21
  8.9 4.6 %copy-start.7 = (s32[32]{0:T(128)S(1)}, s32[32]{0:T(128)}, u32[]{:S(2)}) copy-start(s32[32]{0:T(128)} %param.27) | copy-start | bytes 388
  8.9 12.4 %collective-permute-start.5 = (f32[5,8,16,2]{3,2,1,0:T(8,128)S(1)}, f32[5,8,16,2]{3,2,1,0:T(8,128)S(1)}, u32[]{:S(2)}, u32[]{:S(2)}) collective-permute-start(f32[5,8,16,2]{3,2,1,0:T(8,128)S(1)} %get-tuple-element.186), channel_id=1, source_target_pairs={{1,0},{3,2},{5,4},{7,6},{9,8},{11,10},{13,12},{15,14},{17,16},{19,... | collective-permute-start | bytes 15368 | tf_op jit(solution)/shard_map/ppermute | solution.py:24
  13.5 0.7 copy-start.6
  17.7 5.6 %collective-permute-start.1 = (f32[5,2,16,128]{3,2,1,0:T(8,128)S(1)}, f32[5,2,16,128]{3,2,1,0:T(8,128)S(1)}, u32[]{:S(2)}, u32[]{:S(2)}) collective-permute-start(f32[5,2,16,128]{3,2,1,0:T(8,128)S(1)} %get-tuple-element.178), channel_id=1, source_target_pairs={{8,0},{16,8},{24,16},{9,1},{17,9},{25,17},{10,2},{18,10},{26,18},{... | collective-permute-start | bytes 245768 | tf_op jit(solution)/shard_map/ppermute | solution.py:24
  24.7 20.2 %collective-permute-start.6 = (f32[5,2,16,128]{3,2,1,0:T(8,128)S(1)}, f32[5,2,16,128]{3,2,1,0:T(8,128)S(1)}, u32[]{:S(2)}, u32[]{:S(2)}) collective-permute-start(f32[5,2,16,128]{3,2,1,0:T(8,128)S(1)} %get-tuple-element.165), channel_id=1, source_target_pairs={{0,8},{8,16},{16,24},{1,9},{9,17},{17,25},{2,10},{10,18},{18,26},{... | collective-permute-start | bytes 245768 | tf_op jit(solution)/shard_map/ppermute | solution.py:21
  26.7 18.3 %collective-permute-start.7 = (f32[5,2,16,128]{3,2,1,0:T(8,128)S(1)}, f32[5,2,16,128]{3,2,1,0:T(8,128)S(1)}, u32[]{:S(2)}, u32[]{:S(2)}) collective-permute-start(f32[5,2,16,128]{3,2,1,0:T(8,128)S(1)} %get-tuple-element.166), channel_id=1, source_target_pairs={{8,0},{16,8},{24,16},{9,1},{17,9},{25,17},{10,2},{18,10},{26,18},{... | collective-permute-start | bytes 245768 | tf_op jit(solution)/shard_map/ppermute | solution.py:24
  30.7 10.2 %collective-permute-start.10 = (f32[5,8,16,2]{3,2,1,0:T(8,128)S(1)}, f32[5,8,16,2]{3,2,1,0:T(8,128)S(1)}, u32[]{:S(2)}, u32[]{:S(2)}) collective-permute-start(f32[5,8,16,2]{3,2,1,0:T(8,128)S(1)} %get-tuple-element.173), channel_id=1, source_target_pairs={{0,1},{2,3},{4,5},{6,7},{8,9},{10,11},{12,13},{14,15},{16,17},{18,... | collective-permute-start | bytes 15368 | tf_op jit(solution)/shard_map/ppermute | solution.py:21
  32.0 11.2 %collective-permute-start.11 = (f32[5,8,16,2]{3,2,1,0:T(8,128)S(1)}, f32[5,8,16,2]{3,2,1,0:T(8,128)S(1)}, u32[]{:S(2)}, u32[]{:S(2)}) collective-permute-start(f32[5,8,16,2]{3,2,1,0:T(8,128)S(1)} %get-tuple-element.174), channel_id=1, source_target_pairs={{1,0},{3,2},{5,4},{7,6},{9,8},{11,10},{13,12},{15,14},{17,16},{19,... | collective-permute-start | bytes 15368 | tf_op jit(solution)/shard_map/ppermute | solution.py:24
  36.6 6.8 %collective-permute-start.8 = (f32[5,8,2,128]{3,2,1,0:T(2,128)S(1)}, f32[5,8,2,128]{3,2,1,0:T(2,128)S(1)}, u32[]{:S(2)}, u32[]{:S(2)}) collective-permute-start(f32[5,8,2,128]{3,2,1,0:T(2,128)S(1)} %get-tuple-element.169), channel_id=1, source_target_pairs={{0,2},{2,4},{4,6},{6,0},{1,3},{3,5},{5,7},{7,1},{8,10},{10,12},{12... | collective-permute-start | bytes 122888 | tf_op jit(solution)/shard_map/ppermute | solution.py:21
  40.9 4.0 %collective-permute-start.9 = (f32[5,8,2,128]{3,2,1,0:T(2,128)S(1)}, f32[5,8,2,128]{3,2,1,0:T(2,128)S(1)}, u32[]{:S(2)}, u32[]{:S(2)}) collective-permute-start(f32[5,8,2,128]{3,2,1,0:T(2,128)S(1)} %get-tuple-element.170), channel_id=1, source_target_pairs={{2,0},{4,2},{6,4},{0,6},{3,1},{5,3},{7,5},{1,7},{10,8},{12,10},{14... | collective-permute-start | bytes 122888 | tf_op jit(solution)/shard_map/ppermute | solution.py:24
  45.6 0.7 copy-start.5
  45.6 0.7 copy-start.8
  90.6 0.7 copy-start.4
  91.2 0.7 copy-start.3
  93.5 20.2 %collective-permute-start.12 = (f32[5,2,16,128]{3,2,1,0:T(8,128)S(1)}, f32[5,2,16,128]{3,2,1,0:T(8,128)S(1)}, u32[]{:S(2)}, u32[]{:S(2)}) collective-permute-start(f32[5,2,16,128]{3,2,1,0:T(8,128)S(1)} %get-tuple-element.153), channel_id=1, source_target_pairs={{0,8},{8,16},{16,24},{1,9},{9,17},{17,25},{2,10},{10,18},{18,26},{... | collective-permute-start | bytes 245768 | tf_op jit(solution)/shard_map/ppermute | solution.py:21
  95.4 18.3 %collective-permute-start.13 = (f32[5,2,16,128]{3,2,1,0:T(8,128)S(1)}, f32[5,2,16,128]{3,2,1,0:T(8,128)S(1)}, u32[]{:S(2)}, u32[]{:S(2)}) collective-permute-start(f32[5,2,16,128]{3,2,1,0:T(8,128)S(1)} %get-tuple-element.154), channel_id=1, source_target_pairs={{8,0},{16,8},{24,16},{9,1},{17,9},{25,17},{10,2},{18,10},{26,18},{... | collective-permute-start | bytes 245768 | tf_op jit(solution)/shard_map/ppermute | solution.py:24
  99.3 10.3 %collective-permute-start.16 = (f32[5,8,16,2]{3,2,1,0:T(8,128)S(1)}, f32[5,8,16,2]{3,2,1,0:T(8,128)S(1)}, u32[]{:S(2)}, u32[]{:S(2)}) collective-permute-start(f32[5,8,16,2]{3,2,1,0:T(8,128)S(1)} %get-tuple-element.161), channel_id=1, source_target_pairs={{0,1},{2,3},{4,5},{6,7},{8,9},{10,11},{12,13},{14,15},{16,17},{18,... | collective-permute-start | bytes 15368 | tf_op jit(solution)/shard_map/ppermute | solution.py:21
  100.6 10.2 %collective-permute-start.17 = (f32[5,8,16,2]{3,2,1,0:T(8,128)S(1)}, f32[5,8,16,2]{3,2,1,0:T(8,128)S(1)}, u32[]{:S(2)}, u32[]{:S(2)}) collective-permute-start(f32[5,8,16,2]{3,2,1,0:T(8,128)S(1)} %get-tuple-element.162), channel_id=1, source_target_pairs={{1,0},{3,2},{5,4},{7,6},{9,8},{11,10},{13,12},{15,14},{17,16},{19,... | collective-permute-start | bytes 15368 | tf_op jit(solution)/shard_map/ppermute | solution.py:24
  105.2 5.8 %collective-permute-start.14 = (f32[5,8,2,128]{3,2,1,0:T(2,128)S(1)}, f32[5,8,2,128]{3,2,1,0:T(2,128)S(1)}, u32[]{:S(2)}, u32[]{:S(2)}) collective-permute-start(f32[5,8,2,128]{3,2,1,0:T(2,128)S(1)} %get-tuple-element.157), channel_id=1, source_target_pairs={{0,2},{2,4},{4,6},{6,0},{1,3},{3,5},{5,7},{7,1},{8,10},{10,12},{12... | collective-permute-start | bytes 122888 | tf_op jit(solution)/shard_map/ppermute | solution.py:21
  109.6 4.0 %collective-permute-start.15 = (f32[5,8,2,128]{3,2,1,0:T(2,128)S(1)}, f32[5,8,2,128]{3,2,1,0:T(2,128)S(1)}, u32[]{:S(2)}, u32[]{:S(2)}) collective-permute-start(f32[5,8,2,128]{3,2,1,0:T(2,128)S(1)} %get-tuple-element.158), channel_id=1, source_target_pairs={{2,0},{4,2},{6,4},{0,6},{3,1},{5,3},{7,5},{1,7},{10,8},{12,10},{14... | collective-permute-start | bytes 122888 | tf_op jit(solution)/shard_map/ppermute | solution.py:24
where the time goes:
time: 116 us; the launch traced here: 115 us
  blocking collectives  43.5 us (38%)
  starting transfers between devices  41.6 us (36%)
  waiting for transfers between devices  14.1 us (12%)
  other arithmetic  6.36 us (5%)
  local copies, waits for them, and re-layouts  6.06 us (5%)
  matrix products  2.01 us (2%)
  between operations  1.26 us (1%)
    unnamed x1, blocking collectives  43.5 us
    ppermute x9, starting transfers between devices, with_halo(): lax.ppermute(lax.slice_in_dim(block, 0, width, axis=dim), axis, backward)  27.3 us
    ppermute x9, starting transfers between devices, with_halo(): lax.ppermute(lax.slice_in_dim(block, block.shape[dim] - width, None, axis...  14.3 us
    ppermute x9, waiting for transfers between devices, with_halo(): lax.ppermute(lax.slice_in_dim(block, block.shape[dim] - width, None, axis...  7.22 us
    ppermute x9, waiting for transfers between devices, with_halo(): lax.ppermute(lax.slice_in_dim(block, 0, width, axis=dim), axis, backward)  6.89 us
    unnamed x25, local copies, waits for them, and re-layouts  2.9 us
    gather x3, local copies, waits for them, and re-layouts, sample(): picked = value[jnp.maximum(panel_cell, 0)]  2.67 us
  transfers between devices with their start and end apart: 18, of which 7 were waited for; matrix products, arithmetic and copies ran while one was open for 3% of the time, Pallas kernels for 0%

commit v1 on v0

v1 whole, which is shorter than its diff:
```python
import jax
import jax.numpy as jnp
from jax import lax
from jax.sharding import PartitionSpec as P

NB = 128
GAMMA_M = 0.4
LAMBDA = 0.1
P_REF = 1.0


def shift_pairs(count, periodic):
    pairs = [(i, i + 1) for i in range(count - 1)]
    if periodic:
        pairs.append((count - 1, 0))
    return pairs


def with_halo(block, axis, dim, width, periodic):
    count = lax.axis_size(axis)
    forward = shift_pairs(count, periodic)
    backward = [(target, source) for source, target in forward]
    last = lax.slice_in_dim(block, block.shape[dim] - width, None, axis=dim)
    first = lax.slice_in_dim(block, 0, width, axis=dim)
    low = lax.ppermute(last, axis, forward)
    high = lax.ppermute(first, axis, backward)
    return jnp.concatenate([low, block, high], axis=dim)


def with_swap(block, axis, dim, width):
    index = lax.axis_index(axis)
    last = lax.slice_in_dim(block, block.shape[dim] - width, None, axis=dim)
    first = lax.slice_in_dim(block, 0, width, axis=dim)
    edge = jnp.where(index == 0, last, first)
    moved = jnp.moveaxis(edge, dim, 0).reshape(-1, block.shape[1] * block.shape[2])
    got = lax.ppermute(moved, axis, [(0, 1), (1, 0)])
    got = jnp.moveaxis(got.reshape((width,) + edge.shape[:3]), 0, dim)
    zero = jnp.zeros_like(got)
    low = jnp.where(index == 1, got, zero)
    high = jnp.where(index == 0, got, zero)
    return jnp.concatenate([low, block, high], axis=dim)


def primitives(state):
    rho = state[0]
    vel = state[1:4] / rho
    pres = GAMMA_M * (state[4] - 0.5 * rho * jnp.sum(vel * vel, axis=0))
    return jnp.concatenate([rho[None], vel, pres[None]], 0)


def flux(prim, direc):
    rho = prim[0]
    vel = prim[1:4]
    pres = prim[4]
    normal = vel[direc]
    energy = pres / GAMMA_M + 0.5 * rho * jnp.sum(vel * vel, axis=0)
    moment = rho[None] * normal[None] * vel
    moment = moment.at[direc].add(pres)
    return jnp.concatenate([(rho * normal)[None], moment, ((energy + pres) * normal)[None]], 0)


def deriv(padded, axis, count):
    def piece(low):
        return lax.slice_in_dim(padded, low, low + count, axis=axis)

    return (piece(0) - 8.0 * piece(1) + 8.0 * piece(3) - piece(4)) / 12.0


def tendency(state):
    prim = primitives(state)
    pad_ax = with_halo(flux(prim, 0), "ax", 1, 2, False)
    pad_az = with_halo(flux(prim, 1), "az", 2, 2, True)
    if lax.axis_size("rad") == 2:
        pad_rad = with_swap(flux(prim, 2), "rad", 3, 2)
    else:
        pad_rad = with_halo(flux(prim, 2), "rad", 3, 2, False)
    total = deriv(pad_ax, 1, state.shape[1])
    total = total + deriv(pad_az, 2, state.shape[2])
    total = total + deriv(pad_rad, 3, state.shape[3])
    return (-LAMBDA * total, prim)


def sample(state, prim, panel_cell):
    value = (prim[4] - P_REF + state[1]).reshape(-1)
    picked = value[jnp.maximum(panel_cell, 0)]
    return jnp.where(panel_cell >= 0, picked, 0.0)


def local(density, velocity, pressure, panel_cell, obs_weight, bin_offset):
    slots = panel_cell.shape[0]
    offsets = bin_offset[0]
    ndev = offsets.shape[0]
    times = jnp.arange(NB, dtype=jnp.int32)

    momentum = density[None] * velocity
    energy = pressure / GAMMA_M + 0.5 * density * jnp.sum(velocity * velocity, axis=0)
    first = jnp.concatenate([density[None], momentum, energy[None]], 0)
    change, prim = tendency(first)
    samples = [sample(first, prim, panel_cell)]
    second = first + change
    change, prim = tendency(second)
    samples.append(sample(second, prim, panel_cell))
    third = 0.75 * first + 0.25 * (second + change)
    change, prim = tendency(third)
    samples.append(sample(third, prim, panel_cell))

    row = jnp.concatenate(samples + [jnp.zeros((128 - 3 * slots,), jnp.float32)])
    row = jnp.broadcast_to(row[None, None], (ndev, 1, 128))
    rows = lax.all_to_all(row, ("ax", "az", "rad"), 0, 0, tiled=True)
    rows = rows[:, 0, : 3 * slots].reshape(ndev, 3, slots).astype(jnp.bfloat16)

    final = first / 3.0 + 2.0 / 3.0 * (third + change)

    bins = offsets[:, None, None] + jnp.arange(3, dtype=jnp.int32)[None, :, None]
    hit = times[None, None, :] == bins
    spread = jnp.zeros((ndev, slots, NB), jnp.bfloat16)
    for section in range(3):
        spread = spread + jnp.where(hit[:, section][:, None, :], rows[:, section, :, None], 0)
    signal = jnp.dot(
        obs_weight, spread.reshape(ndev * slots, NB), preferred_element_type=jnp.float32
    )
    return (final, signal)


def solution(mesh):
    in_specs = (
        P("ax", "az", "rad"),
        P(None, "ax", "az", "rad"),
        P("ax", "az", "rad"),
        P(("ax", "az", "rad")),
        P(("ax", "az", "rad"), None),
        P(("ax", "az", "rad"), None),
    )
    out_specs = (P(None, "ax", "az", "rad"), P(("ax", "az", "rad"), None))
    return jax.shard_map(local, mesh=mesh, in_specs=in_specs, out_specs=out_specs, check_vma=False)
```

time: 116 us -> 63.5 us (0.55)
  the two profiles are of different devices: /device:TPU:14 before, /device:TPU:0 now
where the time goes in v1:
time: 63.5 us; the launch traced here: 62.7 us
  starting transfers between devices  38.1 us (60%)
  local copies, waits for them, and re-layouts  11.7 us (18%)
  other arithmetic  10.3 us (16%)
  between operations  1.29 us (2%)
  waiting for transfers between devices  1.03 us (2%)
    ppermute x6, starting transfers between devices, with_halo(): low = lax.ppermute(last, axis, forward)  13.3 us
    ppermute x6, starting transfers between devices, with_halo(): high = lax.ppermute(first, axis, backward)  12.1 us
    all_to_all x1, starting transfers between devices, local(): rows = lax.all_to_all(row, ('ax', 'az', 'rad'), 0, 0, tiled=True)  8.62 us
    ppermute x3, starting transfers between devices, with_swap(): got = lax.ppermute(moved, axis, [(0, 1), (1, 0)])  4.09 us
    unnamed x29, local copies, waits for them, and re-layouts  3.56 us
    concatenate x6, other arithmetic, with_halo(): return jnp.concatenate([low, block, high], axis=dim)  2.18 us
    gather x3, local copies, waits for them, and re-layouts, sample(): picked = value[jnp.maximum(panel_cell, 0)]  2.14 us
    select_n x6, local copies, waits for them, and re-layouts, with_swap(): low = jnp.where(index == 1, got, zero)  1.89 us
  transfers between devices with their start and end apart: 16, of which 2 were waited for; matrix products, arithmetic and copies ran while one was open for 20% of the time, Pallas kernels for 0%

profile of v1, /device:TPU:0, one launch (start us, length us, event | category | flops | bytes accessed | tf_op | source)
XLA Modules:
  0.0 62.7 jit_solution(3071826162443916264)
XLA Ops:
  0.7 1.1 %multiply_reduce_fusion.2 = (f32[8,16,128]{2,1,0:T(8,128)S(1)}, f32[3,8,16,128]{3,2,1,0:T(8,128)S(1)}, f32[3,8,16,128]{3,2,1,0:T(8,128)S(1)}, f32[8,16,128]{2,1,0:T(8,128)S(1)}) fusion(f32[3,8,16,128]{3,2,1,0:T(8,128)} %param.25, f32[8,16,128]{2,1,0:T(8,128)} %param.24), kind=kLoop, calls=%fused_computation.102 | loop fusion | flops 262144 | bytes 786432 | tf_op jit(solution)/shard_map/reduce_sum | solution.py:47
  1.8 0.8 %copy-done.8 = f32[8,16,128]{2,1,0:T(8,128)S(1)} copy-done((f32[8,16,128]{2,1,0:T(8,128)S(1)}, f32[8,16,128]{2,1,0:T(8,128)}, u32[]{:S(2)}) %copy-start.8) | copy-done | bytes 65560
  2.8 3.1 %collective-permute-start.2 = (f32[5,8,2,128]{3,2,1,0:T(2,128)S(1)}, f32[5,8,2,128]{3,2,1,0:T(2,128)S(1)}, u32[]{:S(2)}, u32[]{:S(2)}) collective-permute-start(f32[5,8,2,128]{3,2,1,0:T(2,128)S(1)} %get-tuple-element.177), channel_id=1, source_target_pairs={{0,2},{2,4},{4,6},{6,0},{1,3},{3,5},{5,7},{7,1},{8,10},{10,12},{12... | collective-permute-start | bytes 122888 | tf_op jit(solution)/shard_map/ppermute | solution.py:25
  5.9 2.1 %collective-permute-start.3 = (f32[5,8,2,128]{3,2,1,0:T(2,128)S(1)}, f32[5,8,2,128]{3,2,1,0:T(2,128)S(1)}, u32[]{:S(2)}, u32[]{:S(2)}) collective-permute-start(f32[5,8,2,128]{3,2,1,0:T(2,128)S(1)} %get-tuple-element.178), channel_id=1, source_target_pairs={{2,0},{4,2},{6,4},{0,6},{3,1},{5,3},{7,5},{1,7},{10,8},{12,10},{14... | collective-permute-start | bytes 122888 | tf_op jit(solution)/shard_map/ppermute | solution.py:26
  8.0 1.5 %collective-permute-start = (f32[5,2,16,128]{3,2,1,0:T(8,128)S(1)}, f32[5,2,16,128]{3,2,1,0:T(8,128)S(1)}, u32[]{:S(2)}, u32[]{:S(2)}) collective-permute-start(f32[5,2,16,128]{3,2,1,0:T(8,128)S(1)} %get-tuple-element.173), channel_id=1, source_target_pairs={{0,8},{8,16},{16,24},{1,9},{9,17},{17,25},{2,10},{10,18},{18,26},{... | collective-permute-start | bytes 245768 | tf_op jit(solution)/shard_map/ppermute | solution.py:25
  9.5 1.3 %collective-permute-start.1 = (f32[5,2,16,128]{3,2,1,0:T(8,128)S(1)}, f32[5,2,16,128]{3,2,1,0:T(8,128)S(1)}, u32[]{:S(2)}, u32[]{:S(2)}) collective-permute-start(f32[5,2,16,128]{3,2,1,0:T(8,128)S(1)} %get-tuple-element.174), channel_id=1, source_target_pairs={{8,0},{16,8},{24,16},{9,1},{17,9},{25,17},{10,2},{18,10},{26,18},{... | collective-permute-start | bytes 245768 | tf_op jit(solution)/shard_map/ppermute | solution.py:26
  11.0 0.3 copy.19
  11.4 1.5 %collective-permute-start.4 = (f32[10,128]{1,0:T(8,128)S(1)}, f32[10,128]{1,0:T(8,128)S(1)}, u32[]{:S(2)}, u32[]{:S(2)}) collective-permute-start(f32[10,128]{1,0:T(8,128)S(1)} %reshape.382), channel_id=1, source_target_pairs={{0,1},{1,0},{2,3},{3,2},{4,5},{5,4},{6,7},{7,6},{8,9},{9,8},{10,11... | collective-permute-start | bytes 15368 | tf_op jit(solution)/shard_map/ppermute | solution.py:36
  12.9 0.7 %copy-done.12 = s32[1,32]{1,0:T(1,128)S(1)} copy-done((s32[1,32]{1,0:T(1,128)S(1)}, s32[1,32]{1,0:T(1,128)}, u32[]{:S(2)}) %copy-start.12) | copy-done | bytes 152
  13.6 0.6 slice_bitcast_fusion.5
  14.3 0.7 %gather_fusion = bf16[32]{0:T(256)(128)(2,1)S(1)} fusion(bf16[16384]{0:T(1024)(128)(2,1)S(1)} %bitcast.131, s32[1024]{0:T(1024)S(1)} %pad_clamp_fusion), kind=kCustom, calls=%fused_computation | custom fusion | bytes 256 | tf_op jit(solution)/shard_map/gather | solution.py:85
  15.2 0.3 copy.21
  15.5 0.3 copy.20
  15.8 0.3 maximum_maximum_fusion
  16.3 0.4 fusion.28
  16.9 0.7 %gather_fusion.1 = bf16[32]{0:T(256)(128)(2,1)S(1)} fusion(bf16[16384]{0:T(1024)(128)(2,1)S(1)} %add_add_fusion.1, s32[1024]{0:T(1024)S(1)} %pad_clamp_fusion), kind=kCustom, calls=%fused_computation.1 | custom fusion | bytes 256 | tf_op jit(solution)/shard_map/gather | solution.py:85
  17.6 4.4 %collective-permute-start.5 = (f32[5,2,16,128]{3,2,1,0:T(8,128)S(1)}, f32[5,2,16,128]{3,2,1,0:T(8,128)S(1)}, u32[]{:S(2)}, u32[]{:S(2)}) collective-permute-start(f32[5,2,16,128]{3,2,1,0:T(8,128)S(1)} %get-tuple-element.163), channel_id=1, source_target_pairs={{0,8},{8,16},{16,24},{1,9},{9,17},{17,25},{2,10},{10,18},{18,26},{... | collective-permute-start | bytes 245768 | tf_op jit(solution)/shard_map/ppermute | solution.py:25
  22.1 1.3 %collective-permute-start.6 = (f32[5,2,16,128]{3,2,1,0:T(8,128)S(1)}, f32[5,2,16,128]{3,2,1,0:T(8,128)S(1)}, u32[]{:S(2)}, u32[]{:S(2)}) collective-permute-start(f32[5,2,16,128]{3,2,1,0:T(8,128)S(1)} %get-tuple-element.164), channel_id=1, source_target_pairs={{8,0},{16,8},{24,16},{9,1},{17,9},{25,17},{10,2},{18,10},{26,18},{... | collective-permute-start | bytes 245768 | tf_op jit(solution)/shard_map/ppermute | solution.py:26
  23.7 0.3 copy.22
  24.1 0.9 %collective-permute-start.9 = (f32[10,128]{1,0:T(8,128)S(1)}, f32[10,128]{1,0:T(8,128)S(1)}, u32[]{:S(2)}, u32[]{:S(2)}) collective-permute-start(f32[10,128]{1,0:T(8,128)S(1)} %reshape.383), channel_id=1, source_target_pairs={{0,1},{1,0},{2,3},{3,2},{4,5},{5,4},{6,7},{7,6},{8,9},{9,8},{10,11... | collective-permute-start | bytes 15368 | tf_op jit(solution)/shard_map/ppermute | solution.py:36
  25.0 3.8 %collective-permute-start.8 = (f32[5,8,2,128]{3,2,1,0:T(2,128)S(1)}, f32[5,8,2,128]{3,2,1,0:T(2,128)S(1)}, u32[]{:S(2)}, u32[]{:S(2)}) collective-permute-start(f32[5,8,2,128]{3,2,1,0:T(2,128)S(1)} %get-tuple-element.168), channel_id=1, source_target_pairs={{2,0},{4,2},{6,4},{0,6},{3,1},{5,3},{7,5},{1,7},{10,8},{12,10},{14... | collective-permute-start | bytes 122888 | tf_op jit(solution)/shard_map/ppermute | solution.py:26
  29.0 0.3 copy.24
  29.3 0.3 copy.23
  29.6 0.3 maximum_maximum_fusion.1
  29.9 0.9 %collective-permute-done.7 = f32[5,8,2,128]{3,2,1,0:T(2,128)S(1)} collective-permute-done((f32[5,8,2,128]{3,2,1,0:T(2,128)S(1)}, f32[5,8,2,128]{3,2,1,0:T(2,128)S(1)}, u32[]{:S(2)}, u32[]{:S(2)}) %collective-permute-start.7) | collective-permute-done | bytes 40992 | tf_op jit(solution)/shard_map/ppermute | solution.py:25
  31.0 0.4 fusion.17
  31.6 0.7 %gather_fusion.2 = bf16[32]{0:T(256)(128)(2,1)S(1)} fusion(bf16[16384]{0:T(1024)(128)(2,1)S(1)} %add_add_fusion, s32[1024]{0:T(1024)S(1)} %pad_clamp_fusion), kind=kCustom, calls=%fused_computation.2 | custom fusion | bytes 256 | tf_op jit(solution)/shard_map/gather | solution.py:85
  32.4 0.6 broadcast_in_dim.130
  33.0 8.6 %all-to-all-start = ((bf16[32,1,128]{2,1,0:T(2,128)(2,1)}), bf16[32,1,128]{2,1,0:T(2,128)(2,1)S(1)}, u32[]{:S(2)}, u32[]{:S(2)}) async-start(bf16[32,1,128]{2,1,0:T(2,128)(2,1)} %broadcast_in_dim.130), calls=%async_computation | async-start | bytes 32768 | tf_op jit(solution)/shard_map/all_to_all | solution.py:109
  41.7 0.6 copy-done.6
  42.3 0.7 %pad_maximum_fusion.15 = (f32[5,2,16,128]{3,2,1,0:T(8,128)}, f32[5,2,16,128]{3,2,1,0:T(8,128)}) fusion(f32[1,8,16,128]{3,2,1,0:T(8,128)S(1)} %get-tuple-element.139, f32[3,8,16,128]{3,2,1,0:T(8,128)S(1)} %get-tuple-element.121, f32[1,8,16,128]{3,2,1,0:T(8,128)S(1)} %slice_multiply_fusion.23), kind=kLoop, calls=%fused_computation.117 | loop fusion | flops 81920 | bytes 491520 | tf_op jit(solution)/shard_map/slice | solution.py:23
  43.0 2.8 %collective-permute-start.10 = (f32[5,2,16,128]{3,2,1,0:T(8,128)}, f32[5,2,16,128]{3,2,1,0:T(8,128)}, u32[]{:S(2)}, u32[]{:S(2)}) collective-permute-start(f32[5,2,16,128]{3,2,1,0:T(8,128)} %get-tuple-element.153), channel_id=1, source_target_pairs={{0,8},{8,16},{16,24},{1,9},{9,17},{17,25},{2,10},{10,18},{18,26},{... | collective-permute-start | bytes 245768 | tf_op jit(solution)/shard_map/ppermute | solution.py:25
  45.7 1.3 %collective-permute-start.11 = (f32[5,2,16,128]{3,2,1,0:T(8,128)}, f32[5,2,16,128]{3,2,1,0:T(8,128)}, u32[]{:S(2)}, u32[]{:S(2)}) collective-permute-start(f32[5,2,16,128]{3,2,1,0:T(8,128)} %get-tuple-element.154), channel_id=1, source_target_pairs={{8,0},{16,8},{24,16},{9,1},{17,9},{25,17},{10,2},{18,10},{26,18},{... | collective-permute-start | bytes 245768 | tf_op jit(solution)/shard_map/ppermute | solution.py:26
  47.3 0.3 copy.25
  47.7 1.7 %collective-permute-start.14 = (f32[10,128]{1,0:T(8,128)S(1)}, f32[10,128]{1,0:T(8,128)S(1)}, u32[]{:S(2)}, u32[]{:S(2)}) collective-permute-start(f32[10,128]{1,0:T(8,128)S(1)} %reshape.384), channel_id=1, source_target_pairs={{0,1},{1,0},{2,3},{3,2},{4,5},{5,4},{6,7},{7,6},{8,9},{9,8},{10,11... | collective-permute-start | bytes 15368 | tf_op jit(solution)/shard_map/ppermute | solution.py:36
  49.4 0.7 %pad_maximum_fusion.24 = (f32[5,8,2,128]{3,2,1,0:T(2,128)}, f32[5,8,2,128]{3,2,1,0:T(2,128)}) fusion(f32[1,8,16,128]{3,2,1,0:T(8,128)S(1)} %get-tuple-element.181, f32[3,8,16,128]{3,2,1,0:T(8,128)S(1)} %get-tuple-element.203, f32[1,8,16,128]{3,2,1,0:T(8,128)S(1)} %get-tuple-element.137), kind=kLoop, calls=%fused_computation.190 | loop fusion | flops 40960 | bytes 409600 | tf_op jit(solution)/shard_map/slice | solution.py:23
  50.1 1.5 %collective-permute-start.12 = (f32[5,8,2,128]{3,2,1,0:T(2,128)}, f32[5,8,2,128]{3,2,1,0:T(2,128)}, u32[]{:S(2)}, u32[]{:S(2)}) collective-permute-start(f32[5,8,2,128]{3,2,1,0:T(2,128)} %get-tuple-element.157), channel_id=1, source_target_pairs={{0,2},{2,4},{4,6},{6,0},{1,3},{3,5},{5,7},{7,1},{8,10},{10,12},{12... | collective-permute-start | bytes 122888 | tf_op jit(solution)/shard_map/ppermute | solution.py:25
  51.5 2.4 %collective-permute-start.13 = (f32[5,8,2,128]{3,2,1,0:T(2,128)}, f32[5,8,2,128]{3,2,1,0:T(2,128)}, u32[]{:S(2)}, u32[]{:S(2)}) collective-permute-start(f32[5,8,2,128]{3,2,1,0:T(2,128)} %get-tuple-element.158), channel_id=1, source_target_pairs={{2,0},{4,2},{6,4},{0,6},{3,1},{5,3},{7,5},{1,7},{10,8},{12,10},{14... | collective-permute-start | bytes 122888 | tf_op jit(solution)/shard_map/ppermute | solution.py:26
  54.1 0.3 copy.27
  54.4 1.0 %copy.26 = f32[5,8,16,2]{3,2,1,0:T(8,128)} copy(f32[5,8,16,2]{2,1,0,3:T(8,128)S(1)} %bitcast.151) | data formatting | bytes 10240 | tf_op jit(solution)/shard_map/jit(_where)/select_n | solution.py:39
  55.4 1.4 %maximum_maximum_fusion.2 = (f32[5,8,16,130]{3,2,1,0:T(8,128)S(1)}, f32[5,8,16,130]{3,2,1,0:T(8,128)S(1)}) fusion(f32[1,8,16,128]{3,2,1,0:T(8,128)} %copy-done.5, f32[3,8,16,128]{3,2,1,0:T(8,128)S(1)} %get-tuple-element.204, f32[1,8,16,128]{3,2,1,0:T(8,128)} %copy-done.2, f32[5,8,16,2]{3,2,1,0:T(8,128)} %copy.26, f32[5,8,16,2]{3,2,1,0:T(8,128)S(1)} %copy.27), kind=kLoop, calls=%fused_computation.8 | loop fusion | flops 499200 | bytes 1003520 | tf_op jit(solution)/shard_map/concatenate | solution.py:41
  57.4 0.6 copy-done.10
  58.0 0.5 fusion.38
  58.5 0.3 convolution_bitcast_fusion
  58.9 0.8 %copy.28 = f32[256,128]{1,0:T(8,128)} copy(f32[256,128]{0,1:T(8,128)S(1)} %convolution_bitcast_fusion) | data formatting | bytes 262144
  59.7 0.9 %maximum_maximum_fusion.5 = (f32[5,8,18,128]{3,2,1,0:T(8,128)S(1)}, f32[5,8,18,128]{3,2,1,0:T(8,128)S(1)}) fusion(f32[1,8,16,128]{3,2,1,0:T(8,128)S(1)} %copy-done.4, f32[3,8,16,128]{3,2,1,0:T(8,128)S(1)} %get-tuple-element.203, f32[1,8,16,128]{3,2,1,0:T(8,128)S(1)} %get-tuple-element.137, f32[5,8,2,128]{3,2,1,0:T(2,128)} %collective-permute-done.12, ...), kind=kLoop, calls=%fused_computation.17 | loop fusion | flops 552960 | bytes 1146880 | tf_op jit(solution)/shard_map/concatenate | solution.py:27
  60.6 1.0 %maximum_maximum_fusion.8 = (f32[5,10,16,128]{3,2,1,0:T(8,128)S(1)}, f32[5,10,16,128]{3,2,1,0:T(8,128)S(1)}) fusion(f32[1,8,16,128]{3,2,1,0:T(8,128)S(1)} %copy-done.7, f32[3,8,16,128]{3,2,1,0:T(8,128)S(1)} %get-tuple-element.121, f32[1,8,16,128]{3,2,1,0:T(8,128)S(1)} %slice_multiply_fusion.23, f32[5,2,16,128]{3,2,1,0:T(8,128)} %collective-permute-done.10, ...), kind=kLoop, calls=%fused_computation.23 | loop fusion | flops 614400 | bytes 1310720 | tf_op jit(solution)/shard_map/concatenate | solution.py:27
  61.6 1.1 %fusion.4 = f32[5,8,16,128]{3,2,1,0:T(8,128)} fusion(f32[5,8,16,128]{3,2,1,0:T(8,128)S(1)} %fusion.17, f32[5,8,16,130]{3,2,1,0:T(8,128)S(1)} %get-tuple-element.160, f32[5,8,16,130]{3,2,1,0:T(8,128)S(1)} %get-tuple-element.159, f32[5,8,18,128]{3,2,1,0:T(8,128)S(1)} %get-tuple-element.156, f32[5,8,18,128]{3,2,1,0:T(8,128)S(1)} %get-tuple-element.155, ...), kind=kLoop, calls=%fused_computation.30 | loop fusion | flops 1966080 | bytes 4915200 | tf_op jit(solution)/shard_map/add | solution.py:112
  (104 shorter events, 3.5 us)
Async XLA Ops:
  0.6 57.9 %copy-start = (bf16[256,1024]{1,0:T(8,128)(2,1)S(1)}, bf16[256,1024]{1,0:T(8,128)(2,1)}, u32[]{:S(2)}) copy-start(bf16[256,1024]{1,0:T(8,128)(2,1)} %param.28) | copy-start | bytes 1572868
  0.6 1.1 %copy-start.1 = (f32[8,16,128]{2,1,0:T(8,128)S(1)}, f32[8,16,128]{2,1,0:T(8,128)}, u32[]{:S(2)}) copy-start(f32[8,16,128]{2,1,0:T(8,128)} %param.24) | copy-start | bytes 196612
  1.7 0.8 %copy-start.8 = (f32[8,16,128]{2,1,0:T(8,128)S(1)}, f32[8,16,128]{2,1,0:T(8,128)}, u32[]{:S(2)}) copy-start(f32[8,16,128]{2,1,0:T(8,128)} %param.26) | copy-start | bytes 196612
  2.8 13.3 %collective-permute-start.2 = (f32[5,8,2,128]{3,2,1,0:T(2,128)S(1)}, f32[5,8,2,128]{3,2,1,0:T(2,128)S(1)}, u32[]{:S(2)}, u32[]{:S(2)}) collective-permute-start(f32[5,8,2,128]{3,2,1,0:T(2,128)S(1)} %get-tuple-element.177), channel_id=1, source_target_pairs={{0,2},{2,4},{4,6},{6,0},{1,3},{3,5},{5,7},{7,1},{8,10},{10,12},{12... | collective-permute-start | bytes 122888 | tf_op jit(solution)/shard_map/ppermute | solution.py:25
  5.9 10.2 %collective-permute-start.3 = (f32[5,8,2,128]{3,2,1,0:T(2,128)S(1)}, f32[5,8,2,128]{3,2,1,0:T(2,128)S(1)}, u32[]{:S(2)}, u32[]{:S(2)}) collective-permute-start(f32[5,8,2,128]{3,2,1,0:T(2,128)S(1)} %get-tuple-element.178), channel_id=1, source_target_pairs={{2,0},{4,2},{6,4},{0,6},{3,1},{5,3},{7,5},{1,7},{10,8},{12,10},{14... | collective-permute-start | bytes 122888 | tf_op jit(solution)/shard_map/ppermute | solution.py:26
  8.0 8.2 %collective-permute-start = (f32[5,2,16,128]{3,2,1,0:T(8,128)S(1)}, f32[5,2,16,128]{3,2,1,0:T(8,128)S(1)}, u32[]{:S(2)}, u32[]{:S(2)}) collective-permute-start(f32[5,2,16,128]{3,2,1,0:T(8,128)S(1)} %get-tuple-element.173), channel_id=1, source_target_pairs={{0,8},{8,16},{16,24},{1,9},{9,17},{17,25},{2,10},{10,18},{18,26},{... | collective-permute-start | bytes 245768 | tf_op jit(solution)/shard_map/ppermute | solution.py:25
  9.5 6.7 %collective-permute-start.1 = (f32[5,2,16,128]{3,2,1,0:T(8,128)S(1)}, f32[5,2,16,128]{3,2,1,0:T(8,128)S(1)}, u32[]{:S(2)}, u32[]{:S(2)}) collective-permute-start(f32[5,2,16,128]{3,2,1,0:T(8,128)S(1)} %get-tuple-element.174), channel_id=1, source_target_pairs={{8,0},{16,8},{24,16},{9,1},{17,9},{25,17},{10,2},{18,10},{26,18},{... | collective-permute-start | bytes 245768 | tf_op jit(solution)/shard_map/ppermute | solution.py:26
  11.2 1.6 %copy-start.13 = (s32[32]{0:T(128)S(1)}, s32[32]{0:T(128)}, u32[]{:S(2)}) copy-start(s32[32]{0:T(128)} %param.27) | copy-start | bytes 388
  11.4 3.7 %collective-permute-start.4 = (f32[10,128]{1,0:T(8,128)S(1)}, f32[10,128]{1,0:T(8,128)S(1)}, u32[]{:S(2)}, u32[]{:S(2)}) collective-permute-start(f32[10,128]{1,0:T(8,128)S(1)} %reshape.382), channel_id=1, source_target_pairs={{0,1},{1,0},{2,3},{3,2},{4,5},{5,4},{6,7},{7,6},{8,9},{9,8},{10,11... | collective-permute-start | bytes 15368 | tf_op jit(solution)/shard_map/ppermute | solution.py:36
  12.9 0.7 %copy-start.12 = (s32[1,32]{1,0:T(1,128)S(1)}, s32[1,32]{1,0:T(1,128)}, u32[]{:S(2)}) copy-start(s32[1,32]{1,0:T(1,128)} %param.29) | copy-start | bytes 388
  17.6 13.2 %collective-permute-start.5 = (f32[5,2,16,128]{3,2,1,0:T(8,128)S(1)}, f32[5,2,16,128]{3,2,1,0:T(8,128)S(1)}, u32[]{:S(2)}, u32[]{:S(2)}) collective-permute-start(f32[5,2,16,128]{3,2,1,0:T(8,128)S(1)} %get-tuple-element.163), channel_id=1, source_target_pairs={{0,8},{8,16},{16,24},{1,9},{9,17},{17,25},{2,10},{10,18},{18,26},{... | collective-permute-start | bytes 245768 | tf_op jit(solution)/shard_map/ppermute | solution.py:25
  22.1 8.8 %collective-permute-start.6 = (f32[5,2,16,128]{3,2,1,0:T(8,128)S(1)}, f32[5,2,16,128]{3,2,1,0:T(8,128)S(1)}, u32[]{:S(2)}, u32[]{:S(2)}) collective-permute-start(f32[5,2,16,128]{3,2,1,0:T(8,128)S(1)} %get-tuple-element.164), channel_id=1, source_target_pairs={{8,0},{16,8},{24,16},{9,1},{17,9},{25,17},{10,2},{18,10},{26,18},{... | collective-permute-start | bytes 245768 | tf_op jit(solution)/shard_map/ppermute | solution.py:26
  24.1 4.8 %collective-permute-start.9 = (f32[10,128]{1,0:T(8,128)S(1)}, f32[10,128]{1,0:T(8,128)S(1)}, u32[]{:S(2)}, u32[]{:S(2)}) collective-permute-start(f32[10,128]{1,0:T(8,128)S(1)} %reshape.383), channel_id=1, source_target_pairs={{0,1},{1,0},{2,3},{3,2},{4,5},{5,4},{6,7},{7,6},{8,9},{9,8},{10,11... | collective-permute-start | bytes 15368 | tf_op jit(solution)/shard_map/ppermute | solution.py:36
  24.9 5.9 %collective-permute-start.7 = (f32[5,8,2,128]{3,2,1,0:T(2,128)S(1)}, f32[5,8,2,128]{3,2,1,0:T(2,128)S(1)}, u32[]{:S(2)}, u32[]{:S(2)}) collective-permute-start(f32[5,8,2,128]{3,2,1,0:T(2,128)S(1)} %get-tuple-element.167), channel_id=1, source_target_pairs={{0,2},{2,4},{4,6},{6,0},{1,3},{3,5},{5,7},{7,1},{8,10},{10,12},{12... | collective-permute-start | bytes 122888 | tf_op jit(solution)/shard_map/ppermute | solution.py:25
  25.0 5.8 %collective-permute-start.8 = (f32[5,8,2,128]{3,2,1,0:T(2,128)S(1)}, f32[5,8,2,128]{3,2,1,0:T(2,128)S(1)}, u32[]{:S(2)}, u32[]{:S(2)}) collective-permute-start(f32[5,8,2,128]{3,2,1,0:T(2,128)S(1)} %get-tuple-element.168), channel_id=1, source_target_pairs={{2,0},{4,2},{6,4},{0,6},{3,1},{5,3},{7,5},{1,7},{10,8},{12,10},{14... | collective-permute-start | bytes 122888 | tf_op jit(solution)/shard_map/ppermute | solution.py:26
  33.0 23.8 %all-to-all-start = ((bf16[32,1,128]{2,1,0:T(2,128)(2,1)}), bf16[32,1,128]{2,1,0:T(2,128)(2,1)S(1)}, u32[]{:S(2)}, u32[]{:S(2)}) async-start(bf16[32,1,128]{2,1,0:T(2,128)(2,1)} %broadcast_in_dim.130), calls=%async_computation | async-start | bytes 32768 | tf_op jit(solution)/shard_map/all_to_all | solution.py:109
  41.7 0.6 copy-start.6
  41.7 5.4 %copy-start.2 = (f32[1,8,16,128]{3,2,1,0:T(8,128)}, f32[1,8,16,128]{3,2,1,0:T(8,128)S(1)}, u32[]{:S(2)}) copy-start(f32[1,8,16,128]{3,2,1,0:T(8,128)S(1)} %get-tuple-element.138) | copy-start | bytes 196612
  41.7 5.4 %copy-start.5 = (f32[1,8,16,128]{3,2,1,0:T(8,128)}, f32[1,8,16,128]{3,2,1,0:T(8,128)S(1)}, u32[]{:S(2)}) copy-start(f32[1,8,16,128]{3,2,1,0:T(8,128)S(1)} %get-tuple-element.182) | copy-start | bytes 196612
  41.7 7.7 %copy-start.3 = (f32[1,8,16,128]{3,2,1,0:T(8,128)}, f32[1,8,16,128]{3,2,1,0:T(8,128)S(1)}, u32[]{:S(2)}) copy-start(f32[1,8,16,128]{3,2,1,0:T(8,128)S(1)} %get-tuple-element.181) | copy-start | bytes 196612
  43.0 17.6 %collective-permute-start.10 = (f32[5,2,16,128]{3,2,1,0:T(8,128)}, f32[5,2,16,128]{3,2,1,0:T(8,128)}, u32[]{:S(2)}, u32[]{:S(2)}) collective-permute-start(f32[5,2,16,128]{3,2,1,0:T(8,128)} %get-tuple-element.153), channel_id=1, source_target_pairs={{0,8},{8,16},{16,24},{1,9},{9,17},{17,25},{2,10},{10,18},{18,26},{... | collective-permute-start | bytes 245768 | tf_op jit(solution)/shard_map/ppermute | solution.py:25
  45.7 14.9 %collective-permute-start.11 = (f32[5,2,16,128]{3,2,1,0:T(8,128)}, f32[5,2,16,128]{3,2,1,0:T(8,128)}, u32[]{:S(2)}, u32[]{:S(2)}) collective-permute-start(f32[5,2,16,128]{3,2,1,0:T(8,128)} %get-tuple-element.154), channel_id=1, source_target_pairs={{8,0},{16,8},{24,16},{9,1},{17,9},{25,17},{10,2},{18,10},{26,18},{... | collective-permute-start | bytes 245768 | tf_op jit(solution)/shard_map/ppermute | solution.py:26
  47.7 6.2 %collective-permute-start.14 = (f32[10,128]{1,0:T(8,128)S(1)}, f32[10,128]{1,0:T(8,128)S(1)}, u32[]{:S(2)}, u32[]{:S(2)}) collective-permute-start(f32[10,128]{1,0:T(8,128)S(1)} %reshape.384), channel_id=1, source_target_pairs={{0,1},{1,0},{2,3},{3,2},{4,5},{5,4},{6,7},{7,6},{8,9},{9,8},{10,11... | collective-permute-start | bytes 15368 | tf_op jit(solution)/shard_map/ppermute | solution.py:36
  50.1 9.6 %collective-permute-start.12 = (f32[5,8,2,128]{3,2,1,0:T(2,128)}, f32[5,8,2,128]{3,2,1,0:T(2,128)}, u32[]{:S(2)}, u32[]{:S(2)}) collective-permute-start(f32[5,8,2,128]{3,2,1,0:T(2,128)} %get-tuple-element.157), channel_id=1, source_target_pairs={{0,2},{2,4},{4,6},{6,0},{1,3},{3,5},{5,7},{7,1},{8,10},{10,12},{12... | collective-permute-start | bytes 122888 | tf_op jit(solution)/shard_map/ppermute | solution.py:25
  51.5 8.1 %collective-permute-start.13 = (f32[5,8,2,128]{3,2,1,0:T(2,128)}, f32[5,8,2,128]{3,2,1,0:T(2,128)}, u32[]{:S(2)}, u32[]{:S(2)}) collective-permute-start(f32[5,8,2,128]{3,2,1,0:T(2,128)} %get-tuple-element.158), channel_id=1, source_target_pairs={{2,0},{4,2},{6,4},{0,6},{3,1},{5,3},{7,5},{1,7},{10,8},{12,10},{14... | collective-permute-start | bytes 122888 | tf_op jit(solution)/shard_map/ppermute | solution.py:26
  57.3 0.7 %copy-start.10 = (pred[32,128]{1,0:T(8,128)(4,1)S(1)}, pred[32,128]{1,0:T(8,128)(4,1)}, u32[]{:S(2)}) copy-start(pred[32,128]{1,0:T(8,128)(4,1)} %get-tuple-element.211) | copy-start | bytes 12292
  57.3 0.7 %copy-start.11 = (pred[32,128]{1,0:T(8,128)(4,1)S(1)}, pred[32,128]{1,0:T(8,128)(4,1)}, u32[]{:S(2)}) copy-start(pred[32,128]{1,0:T(8,128)(4,1)} %get-tuple-element.212) | copy-start | bytes 12292
  57.4 0.7 %copy-start.9 = (pred[32,128]{1,0:T(8,128)(4,1)S(1)}, pred[32,128]{1,0:T(8,128)(4,1)}, u32[]{:S(2)}) copy-start(pred[32,128]{1,0:T(8,128)(4,1)} %get-tuple-element.210) | copy-start | bytes 12292
  58.9 0.8 %copy-start.4 = (f32[1,8,16,128]{3,2,1,0:T(8,128)S(1)}, f32[1,8,16,128]{3,2,1,0:T(8,128)}, u32[]{:S(2)}) copy-start(f32[1,8,16,128]{3,2,1,0:T(8,128)} %copy-done.3) | copy-start | bytes 196612
  59.6 1.0 %copy-start.7 = (f32[1,8,16,128]{3,2,1,0:T(8,128)S(1)}, f32[1,8,16,128]{3,2,1,0:T(8,128)}, u32[]{:S(2)}) copy-start(f32[1,8,16,128]{3,2,1,0:T(8,128)} %copy-done.6) | copy-start | bytes 196612

commit v2 on v1

v2 whole, which is shorter than its diff:
```python
import functools

import jax
import jax.numpy as jnp
from jax import lax
from jax.experimental import pallas as pl
from jax.experimental.pallas import tpu as pltpu
from jax.sharding import PartitionSpec as P

NB = 128
GAMMA_M = 0.4
LAMBDA = 0.1
P_REF = 1.0
REACH = 6
MID = 4
STRIP = 8
C1 = -LAMBDA * 8.0 / 12.0
C2 = LAMBDA / 12.0
HIGHEST = lax.Precision.HIGHEST
VMEM = pltpu.MemorySpace.VMEM
SMEM = pltpu.MemorySpace.SMEM


def params():
    return pltpu.CompilerParams(vmem_limit_bytes=56 * 1024 * 1024)


def call(kernel, outs, in_spaces, scratch=()):
    return pl.pallas_call(
        kernel,
        out_shape=outs,
        in_specs=[pl.BlockSpec(memory_space=s) for s in in_spaces],
        out_specs=jax.tree.map(lambda _: pl.BlockSpec(memory_space=VMEM), outs),
        scratch_shapes=list(scratch),
        compiler_params=params(),
    )


def f32(*shape):
    return jax.ShapeDtypeStruct(shape, jnp.float32)


def field(f, den, vel, pre):
    return den if f == 0 else (pre if f == 4 else vel.at[f - 1])


def pack_ax(den, vel, pre, low_out, high_out):
    ca = den.shape[0]
    for f in range(5):
        home = field(f, den, vel, pre)
        low_out[f] = home[0:REACH]
        high_out[f] = home[ca - REACH : ca]


def pack_az(den, vel, pre, lo, hi, low_out, high_out):
    ca, cz, _ = den.shape
    for f in range(5):
        home = field(f, den, vel, pre)
        for out, rows in ((low_out, slice(0, STRIP)), (high_out, slice(cz - STRIP, cz))):
            out[f, 0:MID] = lo[f, REACH - MID : REACH, rows]
            out[f, MID : MID + ca] = home[:, rows]
            out[f, MID + ca : ca + 2 * MID] = hi[f, 0:MID, rows]


def one_hot_lanes(start, lanes):
    row = lax.broadcasted_iota(jnp.int32, (8, lanes), 0)
    lane = lax.broadcasted_iota(jnp.int32, (8, lanes), 1)
    return jnp.where((row < REACH) & (lane == row + start), 1.0, 0.0)


def pack_rad(ends, den, vel, pre, lo, hi, azlo, azhi, *outs):
    ca, cz, cr = den.shape
    rad = lax.axis_index("rad")
    planes = ca + 2 * MID
    rows = cz + 2 * STRIP
    for f in range(5):
        home = field(f, den, vel, pre)
        mid = jnp.concatenate([lo[f, REACH - MID : REACH], home[...], hi[f, 0:MID]], axis=0)
        whole = jnp.concatenate([azlo[f], mid, azhi[f]], axis=1).reshape(planes * rows, cr)
        for end, out in zip(ends, outs):
            start = {"low": 0, "high": cr - REACH, "either": jnp.where(rad == 0, cr - REACH, 0)}[end]
            out[f] = lax.dot_general(
                one_hot_lanes(start, cr),
                whole,
                (((1,), (1,)), ((), ())),
                precision=HIGHEST,
                preferred_element_type=jnp.float32,
            )


def fluxes(rho, mom, vel, pres, energy, want):
    total = energy + pres
    out = {}
    for d in want:
        parts = [mom[d]]
        for j in range(3):
            parts.append(mom[d] * vel[j] + pres if j == d else mom[d] * vel[j])
        parts.append(total * vel[d])
        out[d] = parts
    return out


def diff(value, axis):
    n = value.shape[axis]
    near = pltpu.roll(value, n - 1, axis) - pltpu.roll(value, 1, axis)
    far = pltpu.roll(value, n - 2, axis) - pltpu.roll(value, 2, axis)
    return C1 * near + C2 * far


def stages(counts, den, vel, pre, lo, hi, azlo, azhi, rlo, rhi, cells, cell_col, state, q_out, prim, first, second, third, fax, part, value, picked):
    n_ax, n_rad = counts
    ca, cz, cr = den.shape
    slots = cells.shape[0]
    rows = cz + 2 * STRIP
    wide = 2 * cr
    planes = ca + 2 * REACH
    inner = (slice(STRIP, STRIP + cz), slice(0, cr))
    full = (slice(0, rows), slice(0, wide))
    ax = lax.axis_index("ax")
    rad = lax.axis_index("rad")

    lane = lax.broadcasted_iota(jnp.int32, (rows, wide), 1)
    lane_ok = (
        (lane < cr)
        | ((lane < cr + REACH) & (rad < n_rad - 1))
        | ((lane >= wide - REACH) & (rad > 0))
    )
    lane_base = jnp.where(lane_ok, 0.0, 1.0)[:, cr:wide]

    place_high = one_hot_lanes(0, cr)
    place_low = one_hot_lanes(cr - REACH, cr)
    place_high = jnp.where(rad < n_rad - 1, place_high, 0.0)
    place_low = jnp.where(rad > 0, place_low, 0.0)
    inside = slice(REACH - MID, REACH + ca + MID)
    for f in range(5):
        home = field(f, den, vel, pre)
        prim[f, 0:REACH, STRIP : STRIP + cz, 0:cr] = lo[f]
        prim[f, REACH : REACH + ca, STRIP : STRIP + cz, 0:cr] = home[...]
        prim[f, REACH + ca : planes, STRIP : STRIP + cz, 0:cr] = hi[f]
        prim[f, inside, 0:STRIP, 0:cr] = azlo[f]
        prim[f, inside, STRIP + cz : rows, 0:cr] = azhi[f]
        side = 0.0
        for got, place in ((rhi, place_high), (rlo, place_low)):
            side = side + lax.dot_general(
                got[f],
                place,
                (((0,), (0,)), ((), ())),
                precision=HIGHEST,
                preferred_element_type=jnp.float32,
            )
        side = side.reshape(ca + 2 * MID, rows, cr)
        if f == 0:
            side = side + lane_base[None]
        prim[f, inside, :, cr:wide] = side

    def load(ref, j):
        return [ref[f, j] for f in range(5)]

    def work(stage, j, with_sides):
        if stage == 0:
            rho, u, v, w, pres = load(prim, j)
            vels = [u, v, w]
            mom = [rho * x for x in vels]
            energy = pres * (1.0 / GAMMA_M) + 0.5 * (mom[0] * u + mom[1] * v + mom[2] * w)
            if with_sides:
                for f, x in enumerate([rho] + mom + [energy]):
                    first[f, j] = x
        else:
            rho, m0, m1, m2, energy = load(second if stage == 1 else third, j)
            mom = [m0, m1, m2]
            inv = 1.0 / rho
            vels = [m * inv for m in mom]
            pres = GAMMA_M * (energy - 0.5 * (m0 * vels[0] + m1 * vels[1] + m2 * vels[2]))
        got = fluxes(rho, mom, vels, pres, energy, (0, 1, 2) if with_sides else (0,))
        if with_sides:
            value[stage, j] = (pres - P_REF + mom[0])[inner]
            region = inner if stage == 2 else full
            for f in range(5):
                fax[f, j] = got[0][f]
                part[(f, j) + region] = (diff(got[1][f], 0) + diff(got[2][f], 1))[region]
        else:
            for f in range(5):
                fax[(f, j) + inner] = got[0][f][inner]

    def update(stage, j, region):
        beyond = ((j < REACH) & (ax == 0)) | ((j >= REACH + ca) & (ax == n_ax - 1))
        ok = lane_ok[region] & jnp.logical_not(beyond)
        for f in range(5):
            near = fax[(f, j + 1) + region] - fax[(f, j - 1) + region]
            far = fax[(f, j + 2) + region] - fax[(f, j - 2) + region]
            change = C1 * near + C2 * far + part[(f, j) + region]
            base = 1.0 if f == 0 else 0.0
            u0 = first[(f, j) + region]
            if stage == 0:
                second[(f, j) + region] = jnp.where(ok, u0 + change, base)
            elif stage == 1:
                mixed = 0.75 * u0 + 0.25 * (second[(f, j) + region] + change)
                third[(f, j) + region] = jnp.where(ok, mixed, base)
            else:
                mixed = u0 * (1.0 / 3.0) + (2.0 / 3.0) * (third[(f, j) + region] + change)
                state[f, j - REACH] = mixed

    def loop(low, high, body):
        @pl.loop(low, high)
        def _(j):
            body(j)

    start, stop = REACH, REACH + ca
    for stage in range(3):
        reach = 4 - 2 * stage
        for a, b in ((start - reach - 2, start - reach), (stop + reach, stop + reach + 2)):
            loop(a, b, lambda j: work(stage, j, False))
        loop(start - reach, stop + reach, lambda j: work(stage, j, True))
        if reach > 0:
            for a, b in ((start - reach, start - reach + 2), (stop + reach - 2, stop + reach)):
                loop(a, b, lambda j: update(stage, j, inner))
        inset = max(reach - 2, 0)
        region = full if reach > 0 else inner
        loop(start - inset, stop + inset, lambda j: update(stage, j, region))

    picked[...] = jnp.zeros_like(picked)
    col = cell_col[...]
    want = jnp.where(col >= 0, col % cr, -1)
    hit = lax.broadcasted_iota(jnp.int32, (slots, cr), 1) == want
    for p in range(slots):
        cell = jnp.maximum(cells[p], 0)
        plane = cell // (cz * cr) + REACH
        row = (cell // cr) % cz
        for s in range(3):
            picked[s * slots + p, :] = value[s, plane, row, :]
    for s in range(3):
        rowset = pl.ds(s * slots, slots)
        picked[rowset, :] = jnp.where(hit, picked[rowset, :], 0.0)
    ones = jnp.ones((8, cr), jnp.bfloat16)
    q = lax.dot_general(
        ones,
        picked[...].astype(jnp.bfloat16),
        (((1,), (1,)), ((), ())),
        preferred_element_type=jnp.float32,
    )
    q_out[...] = jnp.broadcast_to(q[0:1][None], q_out.shape)


def signals(slots, rows, offsets, weight, out):
    ndev = rows.shape[0]
    group = 32
    cols = group * slots
    lanes = rows.shape[2]
    col = lax.broadcasted_iota(jnp.int32, (1, cols), 1)
    owner = lax.broadcasted_iota(jnp.int32, (group, cols), 0) == col // slots
    lane = lax.broadcasted_iota(jnp.int32, (lanes, cols), 0)
    time = lax.broadcasted_iota(jnp.int32, (NB, cols), 0).astype(jnp.float32)
    total = jnp.zeros(out.shape, jnp.float32)
    for g in range(ndev // group):
        q = rows[g * group : (g + 1) * group, 0, :].astype(jnp.bfloat16)
        off = offsets[0:1, g * group : (g + 1) * group].astype(jnp.float32)
        off = jnp.broadcast_to(off, (8, group)).astype(jnp.bfloat16)
        bins = jnp.dot(off, owner.astype(jnp.bfloat16), preferred_element_type=jnp.float32)[0:1]
        table = jnp.zeros((NB, cols), jnp.float32)
        for s in range(3):
            pick = jnp.where(lane == s * slots + col % slots, 1.0, 0.0).astype(jnp.bfloat16)
            spread = jnp.dot(q, pick, preferred_element_type=jnp.float32)
            line = jnp.sum(jnp.where(owner, spread, 0.0), axis=0, keepdims=True)
            table = jnp.where(time == bins + s, line, table)
        total = total + lax.dot_general(
            weight[:, g * cols : (g + 1) * cols],
            table.astype(jnp.bfloat16),
            (((1,), (1,)), ((), ())),
            preferred_element_type=jnp.float32,
        )
    out[...] = total


def neighbour_pairs(count, periodic):
    pairs = [(i, i + 1) for i in range(count - 1)]
    if periodic:
        pairs.append((count - 1, 0))
    return pairs


def exchange(low_edge, high_edge, axis, periodic):
    forward = neighbour_pairs(lax.axis_size(axis), periodic)
    backward = [(target, source) for source, target in forward]
    return lax.ppermute(high_edge, axis, forward), lax.ppermute(low_edge, axis, backward)


def local(density, velocity, pressure, panel_cell, obs_weight, bin_offset):
    ca, cz, cr = density.shape
    slots = panel_cell.shape[0]
    ndev = bin_offset.shape[1]
    n_ax, n_rad = lax.axis_size("ax"), lax.axis_size("rad")
    home = (density, velocity, pressure)

    edge = f32(5, REACH, cz, cr)
    low, high = call(pack_ax, (edge, edge), [VMEM] * 3)(*home)
    lo, hi = exchange(low, high, "ax", False)

    strip = f32(5, ca + 2 * MID, STRIP, cr)
    low, high = call(pack_az, (strip, strip), [VMEM] * 5)(*home, lo, hi)
    azlo, azhi = exchange(low, high, "az", True)

    lanes = f32(5, 8, (ca + 2 * MID) * (cz + 2 * STRIP))
    ends = ("either",) if n_rad == 2 else ("low", "high")
    sides = call(functools.partial(pack_rad, ends), tuple(lanes for _ in ends), [VMEM] * 7)(
        *home, lo, hi, azlo, azhi
    )
    if n_rad == 2:
        rlo = rhi = lax.ppermute(sides[0], "rad", [(0, 1), (1, 0)])
    else:
        rlo, rhi = exchange(sides[0], sides[1], "rad", False)

    grid = (5, ca + 2 * REACH, cz + 2 * STRIP, 2 * cr)
    scratch = [pltpu.VMEM(grid, jnp.float32) for _ in range(6)]
    scratch += [pltpu.VMEM((3, ca + 2 * REACH, cz, cr), jnp.float32)]
    scratch += [pltpu.VMEM((128, cr), jnp.float32)]
    state, q = call(
        functools.partial(stages, (n_ax, n_rad)),
        (f32(5, ca, cz, cr), f32(ndev, 1, 128)),
        [VMEM] * 9 + [SMEM, VMEM],
        scratch,
    )(*home, lo, hi, azlo, azhi, rlo, rhi, panel_cell, panel_cell[:, None])

    rows = lax.all_to_all(q, ("ax", "az", "rad"), 0, 0, tiled=True)
    signal = call(functools.partial(signals, slots), f32(obs_weight.shape[0], NB), [VMEM] * 3)(
        rows, bin_offset, obs_weight
    )
    return (state, signal)


def solution(mesh):
    in_specs = (
        P("ax", "az", "rad"),
        P(None, "ax", "az", "rad"),
        P("ax", "az", "rad"),
        P(("ax", "az", "rad")),
        P(("ax", "az", "rad"), None),
        P(("ax", "az", "rad"), None),
    )
    out_specs = (P(None, "ax", "az", "rad"), P(("ax", "az", "rad"), None))
    return jax.shard_map(local, mesh=mesh, in_specs=in_specs, out_specs=out_specs, check_vma=False)
```

time: 63.5 us -> 69.6 us (1.096)
  starting transfers between devices: 38.1 us -> 8.97 us
  Pallas kernels: 0 us -> 24.2 us
  waiting for transfers between devices: 1.03 us -> 22.2 us
  blocking collectives: 0 us -> 10.5 us
  other arithmetic: 10.3 us -> 0 us
  local copies, waits for them, and re-layouts: 11.7 us -> 2.74 us
    pallas_call x0 -> x5, Pallas kernels: none -> 24.2 us  [the longest x1 14.8 us: local(): call(functools.partial(stages, (n_ax, n_rad)), (f32(5, ca, cz, cr), f32(n...]
    ppermute x15 -> x5, waiting for transfers between devices: 1.03 us -> 22.2 us  [the longest x2 14.1 us: exchange(): lax.ppermute(low_edge, axis, backward)]
    ppermute x15 -> x5, starting transfers between devices: 29.5 us -> 8.97 us  [the longest x2 3.94 us: exchange(): lax.ppermute(high_edge, axis, forward)]
    all_to_all x0 -> x1, blocking collectives: none -> 10.5 us  [local(): rows = lax.all_to_all(q, ('ax', 'az', 'rad'), 0, 0, tiled=True)]
    all_to_all x1 -> x0, starting transfers between devices: 8.62 us -> none  [local(): rows = lax.all_to_all(row, ('ax', 'az', 'rad'), 0, 0, tiled=True)]
    concatenate x13 -> x0, other arithmetic: 4.2 us -> none  [the longest x6 2.18 us: with_halo(): return jnp.concatenate([low, block, high], axis=dim)]
    select_n x12 -> x0, local copies, waits for them, and re-layouts: 3.04 us -> none  [the longest x6 1.89 us: with_swap(): low = jnp.where(index == 1, got, zero)]
    add x8 -> x0, other arithmetic: 2.47 us -> none  [the longest x1 1.14 us: local(): final = first / 3.0 + 2.0 / 3.0 * (third + change)]
  transfers between devices with their start and end apart: 16 -> 5, of which waited for: 2 -> 4; matrix products, arithmetic and copies ran while one was open for 20% -> 1% of each run, Pallas kernels for 0% -> 0%
where the time goes in v2:
time: 69.6 us; the launch traced here: 69.3 us
  Pallas kernels  24.2 us (35%)
  waiting for transfers between devices  22.2 us (32%)
  blocking collectives  10.5 us (15%)
  starting transfers between devices  8.97 us (13%)
  local copies, waits for them, and re-layouts  2.74 us (4%)
    pallas_call x1, Pallas kernels, local(): call(functools.partial(stages, (n_ax, n_rad)), (f32(5, ca, cz, cr), f32(n...  14.8 us
    ppermute x2, waiting for transfers between devices, exchange(): lax.ppermute(low_edge, axis, backward)  14.1 us
    all_to_all x1, blocking collectives, local(): rows = lax.all_to_all(q, ('ax', 'az', 'rad'), 0, 0, tiled=True)  10.5 us
    ppermute x2, waiting for transfers between devices, exchange(): lax.ppermute(high_edge, axis, forward)  5.43 us
    ppermute x2, starting transfers between devices, exchange(): lax.ppermute(high_edge, axis, forward)  3.94 us
    ppermute x2, starting transfers between devices, exchange(): lax.ppermute(low_edge, axis, backward)  3.54 us
    pallas_call x1, Pallas kernels, local(): call(functools.partial(pack_rad, ends), tuple((lanes for _ in ends)), [VM...  3.2 us
    ppermute x1, waiting for transfers between devices, local(): rlo = rhi = lax.ppermute(sides[0], 'rad', [(0, 1), (1, 0)])  2.64 us
  transfers between devices with their start and end apart: 5, of which 4 were waited for; matrix products, arithmetic and copies ran while one was open for 1% of the time, Pallas kernels for 0%

profile of v2, /device:TPU:0, one launch (start us, length us, event | category | flops | bytes accessed | tf_op | source)
XLA Modules:
  0.0 69.3 jit_solution(14786598969183761475)
XLA Ops:
  0.6 1.8 %shard_map.77 = (f32[5,6,16,128]{3,2,1,0:T(8,128)}, f32[5,6,16,128]{3,2,1,0:T(8,128)}) custom-call(f32[8,16,128]{2,1,0:T(8,128)} %den.7, f32[3,8,16,128]{3,2,1,0:T(8,128)} %vel.7, f32[8,16,128]{2,1,0:T(8,128)} %pre.7), custom_call_target="tpu_custom_call" | custom-call | tf_op jit(solution)/shard_map/pallas_call | solution.py:295
  2.4 2.4 %collective-permute-start = (f32[5,6,16,128]{3,2,1,0:T(8,128)}, f32[5,6,16,128]{3,2,1,0:T(8,128)S(1)}, u32[]{:S(2)}, u32[]{:S(2)}) collective-permute-start(f32[5,6,16,128]{3,2,1,0:T(8,128)} %get-tuple-element.8), channel_id=1, source_target_pairs={{0,8},{8,16},{16,24},{1,9},{9,17},{17,25},{2,10},{10,18},{18,26},{... | collective-permute-start | bytes 737288 | tf_op jit(solution)/shard_map/ppermute | solution.py:284
  4.8 1.3 %collective-permute-start.1 = (f32[5,6,16,128]{3,2,1,0:T(8,128)}, f32[5,6,16,128]{3,2,1,0:T(8,128)S(1)}, u32[]{:S(2)}, u32[]{:S(2)}) collective-permute-start(f32[5,6,16,128]{3,2,1,0:T(8,128)} %get-tuple-element.9), channel_id=1, source_target_pairs={{8,0},{16,8},{24,16},{9,1},{17,9},{25,17},{10,2},{18,10},{26,18},{... | collective-permute-start | bytes 737288 | tf_op jit(solution)/shard_map/ppermute | solution.py:284
  6.1 0.0 collective-permute-done.lo
  6.1 0.0 copy-start
  6.1 4.4 %collective-permute-done.1.hi = f32[5,6,16,128]{3,2,1,0:T(8,128)S(1)} collective-permute-done((f32[5,6,16,128]{3,2,1,0:T(8,128)}, f32[5,6,16,128]{3,2,1,0:T(8,128)S(1)}, u32[]{:S(2)}, u32[]{:S(2)}) %collective-permute-start.1) | collective-permute-done | bytes 245792 | tf_op jit(solution)/shard_map/ppermute | solution.py:284
  10.5 0.0 copy-done
  10.5 0.0 copy-start.1
  10.5 0.7 copy-done.1
  11.2 2.1 %shard_map.78 = (f32[5,16,8,128]{3,2,1,0:T(8,128)}, f32[5,16,8,128]{3,2,1,0:T(8,128)}) custom-call(f32[8,16,128]{2,1,0:T(8,128)} %den.7, f32[3,8,16,128]{3,2,1,0:T(8,128)} %vel.7, f32[8,16,128]{2,1,0:T(8,128)} %pre.7, f32[5,6,16,128]{3,2,1,0:T(8,128)} %copy-done, f32[5,6,16,128]{3,2,1,0:T(8,128)} %copy-done.1), custom_call_target="tpu_custom_call" | custom-call | tf_op jit(solution)/shard_map/pallas_call | solution.py:299
  13.3 1.6 %collective-permute-start.2 = (f32[5,16,8,128]{3,2,1,0:T(8,128)}, f32[5,16,8,128]{3,2,1,0:T(8,128)S(1)}, u32[]{:S(2)}, u32[]{:S(2)}) collective-permute-start(f32[5,16,8,128]{3,2,1,0:T(8,128)} %get-tuple-element.10), channel_id=1, source_target_pairs={{0,2},{2,4},{4,6},{6,0},{1,3},{3,5},{5,7},{7,1},{8,10},{10,12},{12... | collective-permute-start | bytes 983048 | tf_op jit(solution)/shard_map/ppermute | solution.py:284
  14.9 2.2 %collective-permute-start.3 = (f32[5,16,8,128]{3,2,1,0:T(8,128)}, f32[5,16,8,128]{3,2,1,0:T(8,128)S(1)}, u32[]{:S(2)}, u32[]{:S(2)}) collective-permute-start(f32[5,16,8,128]{3,2,1,0:T(8,128)} %get-tuple-element.11), channel_id=1, source_target_pairs={{2,0},{4,2},{6,4},{0,6},{3,1},{5,3},{7,5},{1,7},{10,8},{12,10},{14... | collective-permute-start | bytes 983048 | tf_op jit(solution)/shard_map/ppermute | solution.py:284
  17.1 5.4 %collective-permute-done.2.azlo = f32[5,16,8,128]{3,2,1,0:T(8,128)S(1)} collective-permute-done((f32[5,16,8,128]{3,2,1,0:T(8,128)}, f32[5,16,8,128]{3,2,1,0:T(8,128)S(1)}, u32[]{:S(2)}, u32[]{:S(2)}) %collective-permute-start.2) | collective-permute-done | bytes 327712 | tf_op jit(solution)/shard_map/ppermute | solution.py:284
  22.5 0.0 copy-start.2
  22.5 9.7 %collective-permute-done.3.azhi = f32[5,16,8,128]{3,2,1,0:T(8,128)S(1)} collective-permute-done((f32[5,16,8,128]{3,2,1,0:T(8,128)}, f32[5,16,8,128]{3,2,1,0:T(8,128)S(1)}, u32[]{:S(2)}, u32[]{:S(2)}) %collective-permute-start.3) | collective-permute-done | bytes 327712 | tf_op jit(solution)/shard_map/ppermute | solution.py:284
  32.2 0.0 copy-done.2
  32.2 0.0 copy-start.3
  32.2 0.7 %copy-done.3 = f32[5,16,8,128]{3,2,1,0:T(8,128)} copy-done((f32[5,16,8,128]{3,2,1,0:T(8,128)}, f32[5,16,8,128]{3,2,1,0:T(8,128)S(1)}, u32[]{:S(2)}) %copy-start.3) | copy-done | bytes 327704
  33.0 3.2 %shard_map.79 = f32[5,8,512]{2,1,0:T(8,128)} custom-call(f32[8,16,128]{2,1,0:T(8,128)} %den.7, f32[3,8,16,128]{3,2,1,0:T(8,128)} %vel.7, f32[8,16,128]{2,1,0:T(8,128)} %pre.7, f32[5,6,16,128]{3,2,1,0:T(8,128)} %copy-done, f32[5,6,16,128]{3,2,1,0:T(8,128)} %copy-done.1, f32[5,16,8,128]{3,2,1,0:T(8,128)} %copy-done.2, f32[5,16,8,128]{3,2,1,0:T(8,128)} %copy-done.3), custom_call_target="tpu_custom_call" | custom-call | tf_op jit(solution)/shard_map/pallas_call | solution.py:304
  36.2 0.0 copy-start.5
  36.2 1.5 %collective-permute-start.4 = (f32[5,8,512]{2,1,0:T(8,128)}, f32[5,8,512]{2,1,0:T(8,128)S(1)}, u32[]{:S(2)}, u32[]{:S(2)}) collective-permute-start(f32[5,8,512]{2,1,0:T(8,128)} %shard_map.79), channel_id=1, source_target_pairs={{0,1},{1,0},{2,3},{3,2},{4,5},{5,4},{6,7},{7,6},{8,9},{9,8},{10,11... | collective-permute-start | bytes 245768 | tf_op jit(solution)/shard_map/ppermute | solution.py:308
  37.7 0.0 copy-done.5
  37.7 0.7 copy.8.cell_col
  38.3 2.6 %collective-permute-done.4.rlo.rhi = f32[5,8,512]{2,1,0:T(8,128)S(1)} collective-permute-done((f32[5,8,512]{2,1,0:T(8,128)}, f32[5,8,512]{2,1,0:T(8,128)S(1)}, u32[]{:S(2)}, u32[]{:S(2)}) %collective-permute-start.4) | collective-permute-done | bytes 81952 | tf_op jit(solution)/shard_map/ppermute | solution.py:308
  41.0 0.0 copy-start.4
  41.0 0.6 copy-done.4
  41.6 14.8 %shard_map.80 = (f32[5,8,16,128]{3,2,1,0:T(8,128)}, f32[32,1,128]{2,1,0:T(1,128)}) custom-call(f32[8,16,128]{2,1,0:T(8,128)} %den.7, f32[3,8,16,128]{3,2,1,0:T(8,128)} %vel.7, f32[8,16,128]{2,1,0:T(8,128)} %pre.7, f32[5,6,16,128]{3,2,1,0:T(8,128)} %copy-done, f32[5,6,16,128]{3,2,1,0:T(8,128)} %copy-done.1, f32[5,16,8,128]{3,2,1,0:T(8,128)} %copy-done.2, ...), custom_call_target="tpu_custom_call" | custom-call | tf_op jit(solution)/shard_map/pallas_call | solution.py:316
  56.5 10.5 %all_to_all.5.rows = f32[32,1,128]{2,1,0:T(1,128)} all-to-all(f32[32,1,128]{2,1,0:T(1,128)} %get-tuple-element.13), channel_id=1, replica_groups=mesh['ax'=4,'az'=4,'rad'=2] {'ax','az','rad'}, dimensions={0} | all-to-all | bytes 32768 | tf_op jit(solution)/shard_map/all_to_all | solution.py:323
  67.0 2.3 %shard_map.81 = f32[256,128]{1,0:T(8,128)} custom-call(f32[32,1,128]{2,1,0:T(1,128)} %all_to_all.5.rows, s32[1,32]{1,0:T(1,128)} %offsets.1, bf16[256,1024]{1,0:T(8,128)(2,1)} %weight.1), custom_call_target="tpu_custom_call" | custom-call | tf_op jit(solution)/shard_map/pallas_call | solution.py:324
Async XLA Ops:
  2.4 3.7 %collective-permute-start = (f32[5,6,16,128]{3,2,1,0:T(8,128)}, f32[5,6,16,128]{3,2,1,0:T(8,128)S(1)}, u32[]{:S(2)}, u32[]{:S(2)}) collective-permute-start(f32[5,6,16,128]{3,2,1,0:T(8,128)} %get-tuple-element.8), channel_id=1, source_target_pairs={{0,8},{8,16},{16,24},{1,9},{9,17},{17,25},{2,10},{10,18},{18,26},{... | collective-permute-start | bytes 737288 | tf_op jit(solution)/shard_map/ppermute | solution.py:284
  4.8 5.7 %collective-permute-start.1 = (f32[5,6,16,128]{3,2,1,0:T(8,128)}, f32[5,6,16,128]{3,2,1,0:T(8,128)S(1)}, u32[]{:S(2)}, u32[]{:S(2)}) collective-permute-start(f32[5,6,16,128]{3,2,1,0:T(8,128)} %get-tuple-element.9), channel_id=1, source_target_pairs={{8,0},{16,8},{24,16},{9,1},{17,9},{25,17},{10,2},{18,10},{26,18},{... | collective-permute-start | bytes 737288 | tf_op jit(solution)/shard_map/ppermute | solution.py:284
  6.1 4.4 %copy-start = (f32[5,6,16,128]{3,2,1,0:T(8,128)}, f32[5,6,16,128]{3,2,1,0:T(8,128)S(1)}, u32[]{:S(2)}) copy-start(f32[5,6,16,128]{3,2,1,0:T(8,128)S(1)} %collective-permute-done.lo) | copy-start | bytes 737284
  10.5 0.7 copy-start.1
  13.3 9.2 %collective-permute-start.2 = (f32[5,16,8,128]{3,2,1,0:T(8,128)}, f32[5,16,8,128]{3,2,1,0:T(8,128)S(1)}, u32[]{:S(2)}, u32[]{:S(2)}) collective-permute-start(f32[5,16,8,128]{3,2,1,0:T(8,128)} %get-tuple-element.10), channel_id=1, source_target_pairs={{0,2},{2,4},{4,6},{6,0},{1,3},{3,5},{5,7},{7,1},{8,10},{10,12},{12... | collective-permute-start | bytes 983048 | tf_op jit(solution)/shard_map/ppermute | solution.py:284
  14.9 17.4 %collective-permute-start.3 = (f32[5,16,8,128]{3,2,1,0:T(8,128)}, f32[5,16,8,128]{3,2,1,0:T(8,128)S(1)}, u32[]{:S(2)}, u32[]{:S(2)}) collective-permute-start(f32[5,16,8,128]{3,2,1,0:T(8,128)} %get-tuple-element.11), channel_id=1, source_target_pairs={{2,0},{4,2},{6,4},{0,6},{3,1},{5,3},{7,5},{1,7},{10,8},{12,10},{14... | collective-permute-start | bytes 983048 | tf_op jit(solution)/shard_map/ppermute | solution.py:284
  22.5 9.7 %copy-start.2 = (f32[5,16,8,128]{3,2,1,0:T(8,128)}, f32[5,16,8,128]{3,2,1,0:T(8,128)S(1)}, u32[]{:S(2)}) copy-start(f32[5,16,8,128]{3,2,1,0:T(8,128)S(1)} %collective-permute-done.2.azlo) | copy-start | bytes 983044
  32.2 0.7 %copy-start.3 = (f32[5,16,8,128]{3,2,1,0:T(8,128)}, f32[5,16,8,128]{3,2,1,0:T(8,128)S(1)}, u32[]{:S(2)}) copy-start(f32[5,16,8,128]{3,2,1,0:T(8,128)S(1)} %collective-permute-done.3.azhi) | copy-start | bytes 983044
  36.2 1.5 %copy-start.5 = (s32[32]{0:T(128)S(1)}, s32[32]{0:T(128)}, u32[]{:S(2)}) copy-start(s32[32]{0:T(128)} %cells.1) | copy-start | bytes 388
  36.2 4.8 %collective-permute-start.4 = (f32[5,8,512]{2,1,0:T(8,128)}, f32[5,8,512]{2,1,0:T(8,128)S(1)}, u32[]{:S(2)}, u32[]{:S(2)}) collective-permute-start(f32[5,8,512]{2,1,0:T(8,128)} %shard_map.79), channel_id=1, source_target_pairs={{0,1},{1,0},{2,3},{3,2},{4,5},{5,4},{6,7},{7,6},{8,9},{9,8},{10,11... | collective-permute-start | bytes 245768 | tf_op jit(solution)/shard_map/ppermute | solution.py:308
  41.0 0.6 copy-start.4

commit v3 on v0

v3 whole, which is shorter than its diff:
```python
import functools

import jax
import jax.numpy as jnp
from jax import lax
from jax.experimental import pallas as pl
from jax.experimental.pallas import tpu as pltpu
from jax.sharding import PartitionSpec as P

NB = 128
GAMMA_M = 0.4
LAMBDA = 0.1
P_REF = 1.0
REACH = 6
MID = 4
SCALE = -LAMBDA / 12.0
ROWS = 32
OFF = 8
VMEM = pltpu.MemorySpace.VMEM
SMEM = pltpu.MemorySpace.SMEM
F32 = jnp.float32
BF16 = jnp.bfloat16


def call(kernel, outs, in_spaces, scratch=(), mib=8, cost=None):
    return pl.pallas_call(
        kernel,
        out_shape=outs,
        in_specs=[pl.BlockSpec(memory_space=s) for s in in_spaces],
        out_specs=jax.tree.map(lambda _: pl.BlockSpec(memory_space=VMEM), outs),
        scratch_shapes=list(scratch),
        compiler_params=pltpu.CompilerParams(vmem_limit_bytes=mib * 1024 * 1024),
        cost_estimate=cost,
    )


def struct(shape, dtype=F32):
    return jax.ShapeDtypeStruct(shape, dtype)


def kept(row):
    return 8 * (row % 4) + row // 4


def home_ref(f, den, vel, pre):
    if f == 0:
        return den, 0
    if f == 4:
        return pre, 0
    return vel, (f - 1) * den.shape[0]


def is_even(axis):
    return lax.axis_index(axis) % 2 == 0


def pack_ax(ca, cz, den, vel, pre, first_out, second_out):
    even = is_even("ax")
    size = REACH * cz
    for f in range(5):
        ref, at = home_ref(f, den, vel, pre)
        low = ref[at : at + size, :]
        high = ref[at + ca * cz - size : at + ca * cz, :]
        rows = slice(f * size, (f + 1) * size)
        first_out[rows, :] = jnp.where(even, high, low).astype(BF16)
        second_out[rows, :] = jnp.where(even, low, high).astype(BF16)


def ax_sides(n_ax, got1, got2, rows):
    ax = lax.axis_index("ax")
    a, b = got1[rows, :].astype(F32), got2[rows, :].astype(F32)
    even = is_even("ax")
    lo = jnp.where(ax == 0, 0.0, jnp.where(even, b, a))
    hi = jnp.where(ax == n_ax - 1, 0.0, jnp.where(even, a, b))
    return lo, hi


def pack_az(n_ax, ca, cz, den, vel, pre, got1, got2, first_out, second_out, near):
    even = is_even("az")
    half = MID * cz
    for f in range(5):
        base = f * REACH * cz
        lo, hi = ax_sides(n_ax, got1, got2, slice(base, base + REACH * cz))
        near[f, 0:half, :] = lo[REACH * cz - half :]
        near[f, half : 2 * half, :] = hi[0:half]
    low, high = [], []
    for f in range(5):
        ref, at = home_ref(f, den, vel, pre)
        for d in range(REACH):
            low.append(ref[pl.ds(at + d, ca, stride=cz), :])
            high.append(ref[pl.ds(at + cz - 1 - d, ca, stride=cz), :])
        for d in range(MID):
            low.append(near[f, pl.ds(d, 2 * MID, stride=cz), :])
            high.append(near[f, pl.ds(cz - 1 - d, 2 * MID, stride=cz), :])
    low, high = jnp.concatenate(low, axis=0), jnp.concatenate(high, axis=0)
    first_out[...] = jnp.where(even, high, low).astype(BF16)
    second_out[...] = jnp.where(even, low, high).astype(BF16)


def one_hot_lanes(start, height, lanes, row0=0):
    row = lax.broadcasted_iota(jnp.int32, (height, lanes), 0) - row0
    lane = lax.broadcasted_iota(jnp.int32, (height, lanes), 1)
    return jnp.where((row >= 0) & (row < REACH) & (lane == row + start), 1.0, 0.0).astype(BF16)


def assemble(n_ax, ends, ca, cz, den, vel, pre, ax1, ax2, az1, az2, block, *rest):
    outs, (sides, strips) = rest[: len(ends)], rest[len(ends) :]
    cr = den.shape[1]
    planes = ca + 2 * REACH
    size = REACH * cz
    quarter = cz // 4
    first = OFF // 4

    def put(f, plane, ref, at):
        for l in range(4):
            row = (f * planes + plane) * ROWS + 8 * l + first
            block[pl.ds(row, quarter), :] = ref[pl.ds(at + l, quarter, stride=4), :]

    for f in range(5):
        ref, at = home_ref(f, den, vel, pre)
        for k in range(ca):
            put(f, REACH + k, ref, at + k * cz)
        lo, hi = ax_sides(n_ax, ax1, ax2, slice(f * size, (f + 1) * size))
        sides[f, 0:size, :] = lo
        sides[f, size : 2 * size, :] = hi
    for f in range(5):
        for k in range(REACH):
            put(f, k, sides.at[f], k * cz)
            put(f, REACH + ca + k, sides.at[f], size + k * cz)

    even = is_even("az")
    a, b = az1[...].astype(F32), az2[...].astype(F32)
    strips[0] = jnp.where(even, b, a)
    strips[1] = jnp.where(even, a, b)
    for f in range(5):
        base = f * (REACH * ca + MID * 2 * MID)
        for d in range(REACH):
            for side, row in ((0, OFF - 1 - d), (1, OFF + cz + d)):
                at = kept(row) + f * planes * ROWS
                block[pl.ds(at + REACH * ROWS, ca, stride=ROWS), :] = strips[side, pl.ds(base + d * ca, ca), :]
                if d < MID:
                    start = base + REACH * ca + d * 2 * MID
                    block[pl.ds(at + (REACH - MID) * ROWS, MID, stride=ROWS), :] = strips[side, pl.ds(start, MID), :]
                    block[pl.ds(at + (REACH + ca) * ROWS, MID, stride=ROWS), :] = strips[side, pl.ds(start + MID, MID), :]

    rad = lax.axis_index("rad")
    for end, out in zip(ends, outs):
        start = {"low": 0, "high": cr - REACH, "either": jnp.where(rad == 0, cr - REACH, 0)}[end]
        hot = one_hot_lanes(start, 8, cr)
        packed = []
        for f in range(5):
            row = (f * planes + REACH - MID) * ROWS
            cells = block[pl.ds(row, (ca + 2 * MID) * ROWS), :].astype(BF16)
            packed.append(
                lax.dot_general(hot, cells, (((1,), (1,)), ((), ())), preferred_element_type=F32)
            )
        packed.append(jnp.zeros_like(packed[0]))
        out[...] = jnp.concatenate(packed, axis=0).astype(BF16)


def az_terms(flux):
    out = []
    for group in (0, 4):
        v = [flux[8 * (group + l) : 8 * (group + l + 1)] for l in range(4)]
        v = [pltpu.roll(v[2], 1, 0), pltpu.roll(v[3], 1, 0)] + v + [pltpu.roll(v[0], 7, 0), pltpu.roll(v[1], 7, 0)]
        for l in range(4):
            out.append(8.0 * (v[l + 3] - v[l + 1]) - (v[l + 4] - v[l]))
    return jnp.concatenate(out, axis=0)


def band(wide):
    k = lax.broadcasted_iota(jnp.int32, (wide, wide), 0)
    n = lax.broadcasted_iota(jnp.int32, (wide, wide), 1)
    gap = (k - n + wide) % wide
    out = jnp.where(gap == 1, 8.0, 0.0) + jnp.where(gap == wide - 1, -8.0, 0.0)
    out = out + jnp.where(gap == 2, -1.0, 0.0) + jnp.where(gap == wide - 2, 1.0, 0.0)
    return out.astype(BF16)


def split_state(u):
    rho, m0, m1, m2, energy = u
    inv = 1.0 / rho
    vel = [m0 * inv, m1 * inv, m2 * inv]
    pres = GAMMA_M * (energy - 0.5 * (m0 * vel[0] + m1 * vel[1] + m2 * vel[2]))
    return [m0, m1, m2], vel, pres, energy


def flux(d, mom, vel, pres, energy):
    parts = [mom[d]]
    for j in range(3):
        parts.append(mom[d] * vel[j] + pres if j == d else mom[d] * vel[j])
    parts.append((energy + pres) * vel[d])
    return parts


def ax_only(u, fax, j):
    got = flux(0, *u)
    for f in range(5):
        fax[f, j, 0:ROWS] = got[f]


def both_sides(us, js, fax, part, banded):
    rows = []
    for u, j in zip(us, js):
        got = flux(0, *u)
        for f in range(5):
            fax[f, j] = got[f]
        got = flux(2, *u)
        for f in range(5):
            rows.append(jnp.concatenate([got[f][0:ROWS], got[f][ROWS:]], axis=1))
    rows = jnp.concatenate(rows, axis=0)
    coarse = rows.astype(BF16)
    fine = (rows - coarse.astype(F32)).astype(BF16)
    matrix = banded[...]
    out = jnp.dot(coarse, matrix, preferred_element_type=F32)
    out = out + jnp.dot(fine, matrix, preferred_element_type=F32)
    half = out.shape[1] // 2
    for i, (u, j) in enumerate(zip(us, js)):
        got = flux(1, *u)
        for f in range(5):
            at = (i * 5 + f) * ROWS
            mine = out[at : at + ROWS]
            radial = jnp.concatenate([mine[:, 0:half], mine[:, half:]], axis=0)
            part[f, j] = az_terms(got[f]) + radial


def change(fa, part, f, j, size):
    near = fa(j + 1)[0:size] - fa(j - 1)[0:size]
    far = fa(j + 2)[0:size] - fa(j - 2)[0:size]
    return SCALE * (8.0 * near - far + part[f, j, 0:size])


def window(fax, f):
    held = {}

    def get(j):
        if j not in held:
            held[j] = fax[f, j]
        return held[j]

    return get


def stages(n_ax, n_rad, ca, cz, block, rlo, rhi, cells, q_out, u2_out, u0_out, ghost, first, second, fax, part, banded, value, picked):
    cr = block.shape[-1]
    slots = cells.shape[0]
    low, high = REACH, REACH + ca
    ax = lax.axis_index("ax")
    rad = lax.axis_index("rad")
    banded[...] = band(2 * cr)

    lane = lax.broadcasted_iota(jnp.int32, (ROWS, cr), 1)
    kept_row = lax.broadcasted_iota(jnp.int32, (ROWS, cr), 0)
    row = 4 * (kept_row % 8) + kept_row // 8
    steps_rad = jnp.where(
        (lane < REACH) & (rad < n_rad - 1),
        1 + lane // 2,
        jnp.where((lane >= cr - REACH) & (rad > 0), 1 + (cr - 1 - lane) // 2, 99),
    )
    beyond_row = jnp.maximum(OFF - row, row - (OFF + cz - 1))
    steps = steps_rad + jnp.where(beyond_row > 0, (beyond_row + 1) // 2, 0)
    base0 = jnp.where(steps_rad < 99, 0.0, 1.0)

    count = ca + 2 * MID
    got_hi, got_lo = rhi[...], rlo[...]
    for f in range(5):
        side = 0.0
        for got, start, there in ((got_hi, 0, rad < n_rad - 1), (got_lo, cr - REACH, rad > 0)):
            place = one_hot_lanes(start, got.shape[0], cr, row0=8 * f)
            place = jnp.where(there, place, jnp.zeros_like(place))
            side = side + lax.dot_general(
                got, place, (((0,), (0,)), ((), ())), preferred_element_type=F32
            )
        side = side.reshape(count, ROWS, cr)
        ghost[f] = side + base0[None] if f == 0 else side

    def start_state(j, both):
        u = []
        for f in range(5):
            x = block[f, j]
            u.append(jnp.concatenate([x, ghost[f, j - (REACH - MID)]], axis=0) if both else x)
        rho, vel, pres = u[0], u[1:4], u[4]
        mom = [rho * x for x in vel]
        energy = pres * (1.0 / GAMMA_M) + 0.5 * (mom[0] * vel[0] + mom[1] * vel[1] + mom[2] * vel[2])
        return rho, (mom, vel, pres, energy)

    def note(s, j, u):
        value[s, j] = (u[2] - P_REF + u[0][0])[0:ROWS]

    for j in (low - 6, low - 5, high + 4, high + 5):
        ax_only(start_state(j, False)[1], fax, j)

    @pl.loop(0, (ca + 8) // 2)
    def _(i):
        js = [low - 4 + 2 * i, low - 3 + 2 * i]
        us = []
        for j in js:
            rho, u = start_state(j, True)
            for f, x in enumerate([rho] + u[0] + [u[3]]):
                first[f, j] = x
            note(0, j, u)
            us.append(u)
        both_sides(us, js, fax, part, banded)

    def update(f, j, fa, stage):
        a = max(low - j, j - (high - 1), 0)
        a = (a + 1) // 2
        lim = 2 - stage
        base = jnp.where(f == 0, 1.0, 0.0)
        size = ROWS if a == lim else 2 * ROWS
        new = change(fa, part, f, j, size)
        u0 = first[f, j, 0:size]
        if stage == 0:
            new = u0 + new
        else:
            new = 0.75 * u0 + 0.25 * (second[f, j, 0:size] + new)
        beyond = (ax == 0) if j < low else (ax == n_ax - 1)
        home = new[0:ROWS]
        if a > 0:
            home = jnp.where(beyond, base, home)
        if size == ROWS:
            return home, None
        ok = steps <= lim - a
        if a > 0:
            ok = ok & jnp.logical_not(beyond)
        return home, jnp.where(ok, new[ROWS:], base)

    @pl.loop(0, 5)
    def _(f):
        fa = window(fax, f)
        for j in range(low - 4, high + 4):
            home, side = update(f, j, fa, 0)
            second[f, j, 0:ROWS] = home
            if side is not None:
                second[f, j, ROWS:] = side

    for j in (low - 4, low - 3, high + 2, high + 3):
        ax_only(split_state([second[f, j, 0:ROWS] for f in range(5)]), fax, j)

    @pl.loop(0, (ca + 4) // 2)
    def _(i):
        js = [low - 2 + 2 * i, low - 1 + 2 * i]
        us = []
        for j in js:
            u = split_state([second[f, j] for f in range(5)])
            note(1, j, u)
            us.append(u)
        both_sides(us, js, fax, part, banded)

    @pl.loop(0, 5)
    def _(f):
        fa = window(fax, f)
        for j in range(low - 2, high + 2):
            home, side = update(f, j, fa, 1)
            u2_out[f, j - (low - 2), 0:ROWS] = home
            if side is not None:
                u2_out[f, j - (low - 2), ROWS:] = side
        for j in range(low, high):
            u0_out[f, j - low] = first[f, j, 0:ROWS]

    @pl.loop(0, ca)
    def _(i):
        u = split_state([u2_out[f, i + 2, 0:ROWS] for f in range(5)])
        note(2, low + i, u)

    picked[...] = jnp.zeros_like(picked)
    lanes = lax.broadcasted_iota(jnp.int32, (1, cr), 1)
    for p in range(slots):
        cell = cells[p]
        at = jnp.maximum(cell, 0)
        column = jnp.where(cell >= 0, lax.rem(at, cr), -1)
        at = lax.div(at, cr)
        plane = low + lax.div(at, cz)
        r = lax.rem(at, cz) + OFF
        r = 8 * lax.rem(r, 4) + lax.div(r, 4)
        hit = lanes == column
        for s in range(3):
            picked[pl.ds(s * slots + p, 1), :] = jnp.where(hit, value[s, plane, pl.ds(r, 1), :], 0.0)
    q = lax.dot_general(
        jnp.ones((8, cr), BF16),
        picked[...].astype(BF16),
        (((1,), (1,)), ((), ())),
        preferred_element_type=F32,
    )
    q_out[...] = jnp.broadcast_to(q[0:1][None], q_out.shape)


def last_stage(ca, cz, u2, u0, state, fax, part, banded):
    cr = u2.shape[-1]
    banded[...] = band(2 * cr)
    for j in (0, 1, ca + 2, ca + 3):
        ax_only(split_state([u2[f, j, 0:ROWS] for f in range(5)]), fax, j)

    @pl.loop(0, ca // 2)
    def _(i):
        js = [2 + 2 * i, 3 + 2 * i]
        us = [split_state([u2[f, j] for f in range(5)]) for j in js]
        both_sides(us, js, fax, part, banded)

    first, quarter = OFF // 4, cz // 4

    @pl.loop(0, 5)
    def _(f):
        fa = window(fax, f)
        for k in range(ca):
            j = k + 2
            new = u2[f, j, 0:ROWS] + change(fa, part, f, j, ROWS)
            new = u0[f, k] * (1.0 / 3.0) + (2.0 / 3.0) * new
            for l in range(4):
                state[f, k, pl.ds(l, quarter, stride=4), :] = new[8 * l + first : 8 * l + first + quarter]


def signals(slots, rows, offsets, weight, out):
    ndev = rows.shape[0]
    group = 32
    cols = group * slots
    lanes = rows.shape[2]
    col = lax.broadcasted_iota(jnp.int32, (1, cols), 1)
    owner = lax.broadcasted_iota(jnp.int32, (group, cols), 0) == col // slots
    lane = lax.broadcasted_iota(jnp.int32, (lanes, cols), 0)
    time = lax.broadcasted_iota(jnp.int32, (NB, cols), 0).astype(F32)
    total = jnp.zeros(out.shape, F32)
    for g in range(ndev // group):
        q = rows[g * group : (g + 1) * group, 0, :].astype(BF16)
        off = offsets[0:1, g * group : (g + 1) * group].astype(F32)
        off = jnp.broadcast_to(off, (8, group)).astype(BF16)
        bins = jnp.dot(off, owner.astype(BF16), preferred_element_type=F32)[0:1]
        table = jnp.zeros((NB, cols), F32)
        for s in range(3):
            pick = jnp.where(lane == s * slots + col % slots, 1.0, 0.0).astype(BF16)
            spread = jnp.dot(q, pick, preferred_element_type=F32)
            line = jnp.sum(jnp.where(owner, spread, 0.0), axis=0, keepdims=True)
            table = jnp.where(time == bins + s, line, table)
        total = total + lax.dot_general(
            weight[:, g * cols : (g + 1) * cols],
            table.astype(BF16),
            (((1,), (1,)), ((), ())),
            preferred_element_type=F32,
        )
    out[...] = total


def swap_pairs(count, periodic):
    one = [(i, i ^ 1) for i in range(count)]
    two = []
    for i in range(count):
        j = i - 1 if i % 2 == 0 else i + 1
        two.append((i, j % count if periodic or 0 <= j < count else i))
    return one, two


def swap(first, second, axis, periodic):
    one, two = swap_pairs(lax.axis_size(axis), periodic)
    return lax.ppermute(first, axis, one), lax.ppermute(second, axis, two)


def local(density, velocity, pressure, panel_cell, obs_weight, bin_offset):
    ca, cz, cr = density.shape
    slots = panel_cell.shape[0]
    ndev = bin_offset.shape[1]
    n_ax, n_rad = lax.axis_size("ax"), lax.axis_size("rad")
    home = (density.reshape(ca * cz, cr), velocity.reshape(3 * ca * cz, cr), pressure.reshape(ca * cz, cr))
    planes = ca + 2 * REACH
    part = functools.partial

    edge = struct((5 * REACH * cz, cr), BF16)
    ax1, ax2 = call(part(pack_ax, ca, cz), (edge, edge), [VMEM] * 3)(*home)
    ax1, ax2 = swap(ax1, ax2, "ax", False)

    strip = struct((5 * (REACH * ca + MID * 2 * MID), cr), BF16)
    near = pltpu.VMEM((5, 2 * MID * cz, cr), F32)
    az1, az2 = call(part(pack_az, n_ax, ca, cz), (strip, strip), [VMEM] * 5, [near])(*home, ax1, ax2)
    az1, az2 = swap(az1, az2, "az", True)

    side = struct((48, (ca + 2 * MID) * ROWS), BF16)
    ends = ("either",) if n_rad == 2 else ("low", "high")
    got = call(
        part(assemble, n_ax, ends, ca, cz),
        (struct((5 * planes * ROWS, cr)),) + tuple(side for _ in ends),
        [VMEM] * 7,
        [pltpu.VMEM((5, 2 * REACH * cz, cr), F32), pltpu.VMEM((2,) + strip.shape, F32)],
        mib=12,
    )(*home, ax1, ax2, az1, az2)
    block = got[0].reshape(5, planes, ROWS, cr)
    if n_rad == 2:
        rlo = rhi = lax.ppermute(got[1], "rad", [(0, 1), (1, 0)])
    else:
        up = [(i, i + 1) for i in range(n_rad - 1)]
        rlo = lax.ppermute(got[2], "rad", up)
        rhi = lax.ppermute(got[1], "rad", [(j, i) for i, j in up])

    grid = (5, planes, 2 * ROWS, cr)
    banded = pltpu.VMEM((2 * cr, 2 * cr), BF16)
    q, u2, u0 = call(
        part(stages, n_ax, n_rad, ca, cz),
        (struct((ndev, 1, 128)), struct((5, ca + 4, 2 * ROWS, cr)), struct((5, ca, ROWS, cr))),
        [VMEM] * 3 + [SMEM],
        [pltpu.VMEM((5, ca + 2 * MID, ROWS, cr), F32)]
        + [pltpu.VMEM(grid, F32) for _ in range(4)]
        + [banded, pltpu.VMEM((3, planes, ROWS, cr), F32), pltpu.VMEM((128, cr), F32)],
        mib=28,
    )(block, rlo, rhi, panel_cell)

    rows = lax.all_to_all(q, ("ax", "az", "rad"), 0, 0, tiled=True)

    grid = (5, ca + 4, 2 * ROWS, cr)
    state = call(
        part(last_stage, ca, cz),
        struct((5, ca, cz, cr)),
        [VMEM] * 2,
        [pltpu.VMEM(grid, F32), pltpu.VMEM(grid, F32), banded],
        mib=12,
        cost=pl.CostEstimate(flops=400_000_000, bytes_accessed=8_000_000, transcendentals=0),
    )(u2, u0)
    signal = call(part(signals, slots), struct((obs_weight.shape[0], NB)), [VMEM] * 3, mib=24)(
        rows, bin_offset, obs_weight
    )
    return (state, signal)


def solution(mesh):
    in_specs = (
        P("ax", "az", "rad"),
        P(None, "ax", "az", "rad"),
        P("ax", "az", "rad"),
        P(("ax", "az", "rad")),
        P(("ax", "az", "rad"), None),
        P(("ax", "az", "rad"), None),
    )
    out_specs = (P(None, "ax", "az", "rad"), P(("ax", "az", "rad"), None))
    return jax.shard_map(local, mesh=mesh, in_specs=in_specs, out_specs=out_specs, check_vma=False)
```

time: 116 us -> 48.2 us (0.42)
  the two profiles are of different devices: /device:TPU:14 before, /device:TPU:0 now
where the time goes in v3:
time: 48.2 us; the launch traced here: 47.8 us
  starting transfers between devices  17.9 us (37%)
  Pallas kernels  11.7 us (24%)
  waiting for transfers between devices  11.7 us (24%)
  local copies, waits for them, and re-layouts  5.87 us (12%)
  between operations  0.68 us (1%)
    all_to_all x1, starting transfers between devices, local(): rows = lax.all_to_all(q, ('ax', 'az', 'rad'), 0, 0, tiled=True)  9.71 us
    pallas_call x1, Pallas kernels, local(): call(part(stages, n_ax, n_rad, ca, cz), (struct((ndev, 1, 128)), struct((...  7.42 us
    ppermute x4, starting transfers between devices, swap(): return (lax.ppermute(first, axis, one), lax.ppermute(second, axis, two))  6.65 us
    unnamed x18, local copies, waits for them, and re-layouts  5.87 us
    all_to_all x1, waiting for transfers between devices, local(): rows = lax.all_to_all(q, ('ax', 'az', 'rad'), 0, 0, tiled=True)  4.79 us
    ppermute x4, waiting for transfers between devices, swap(): return (lax.ppermute(first, axis, one), lax.ppermute(second, axis, two))  4.3 us
    ppermute x1, waiting for transfers between devices, local(): rlo = rhi = lax.ppermute(got[1], 'rad', [(0, 1), (1, 0)])  2.6 us
    pallas_call x1, Pallas kernels, local(): call(part(last_stage, ca, cz), struct((5, ca, cz, cr)), [VMEM] * 2, [pltp...  2.25 us
  transfers between devices with their start and end apart: 6, of which 5 were waited for; matrix products, arithmetic and copies ran while one was open for 0% of the time, Pallas kernels for 5%

profile of v3, /device:TPU:0, one launch (start us, length us, event | category | flops | bytes accessed | tf_op | source)
XLA Modules:
  0.0 47.8 jit_solution(417609663670018967)
XLA Ops:
  0.6 0.0 copy-start
  0.6 0.9 %copy-done = f32[3,8,16,128]{3,2,1,0:T(8,128)S(1)} copy-done((f32[3,8,16,128]{3,2,1,0:T(8,128)S(1)}, f32[3,8,16,128]{3,2,1,0:T(8,128)}, u32[]{:S(2)}) %copy-start) | copy-done | bytes 196632
  1.6 0.0 copy-start.2
  1.6 0.8 %copy-done.2 = f32[8,16,128]{2,1,0:T(8,128)S(1)} copy-done((f32[8,16,128]{2,1,0:T(8,128)S(1)}, f32[8,16,128]{2,1,0:T(8,128)}, u32[]{:S(2)}) %copy-start.2) | copy-done | bytes 65560
  2.4 0.0 copy-start.4
  2.4 0.8 %copy-done.4 = f32[8,16,128]{2,1,0:T(8,128)S(1)} copy-done((f32[8,16,128]{2,1,0:T(8,128)S(1)}, f32[8,16,128]{2,1,0:T(8,128)}, u32[]{:S(2)}) %copy-start.4) | copy-done | bytes 65560
  3.3 0.5 %collective-permute-start = (bf16[480,128]{1,0:T(8,128)(2,1)S(1)}, bf16[480,128]{1,0:T(8,128)(2,1)S(1)}, u32[]{:S(2)}, u32[]{:S(2)}) collective-permute-start(bf16[480,128]{1,0:T(8,128)(2,1)S(1)} %get-tuple-element.11), channel_id=1, source_target_pairs={{0,8},{8,0},{16,24},{24,16},{1,9},{9,1},{17,25},{25,17},{2,10},{10... | collective-permute-start | bytes 368648 | tf_op jit(solution)/shard_map/ppermute | solution.py:454
  3.8 0.7 %collective-permute-start.1 = (bf16[480,128]{1,0:T(8,128)(2,1)S(1)}, bf16[480,128]{1,0:T(8,128)(2,1)S(1)}, u32[]{:S(2)}, u32[]{:S(2)}) collective-permute-start(bf16[480,128]{1,0:T(8,128)(2,1)S(1)} %get-tuple-element.12), channel_id=1, source_target_pairs={{0,0},{8,16},{16,8},{24,24},{1,1},{9,17},{17,9},{25,25},{2,2},{10,... | collective-permute-start | bytes 368648 | tf_op jit(solution)/shard_map/ppermute | solution.py:454
  4.5 0.3 collective-permute-done.got1.ax1
  4.8 0.0 collective-permute-done.1.got2.ax2
  4.8 0.2 shard_map.78
  5.0 3.0 %collective-permute-start.2 = (bf16[400,128]{1,0:T(8,128)(2,1)S(1)}, bf16[400,128]{1,0:T(8,128)(2,1)S(1)}, u32[]{:S(2)}, u32[]{:S(2)}) collective-permute-start(bf16[400,128]{1,0:T(8,128)(2,1)S(1)} %get-tuple-element.13), channel_id=1, source_target_pairs={{0,2},{2,0},{4,6},{6,4},{1,3},{3,1},{5,7},{7,5},{8,10},{10,8},{12,... | collective-permute-start | bytes 307208 | tf_op jit(solution)/shard_map/ppermute | solution.py:454
  8.0 2.5 %collective-permute-start.3 = (bf16[400,128]{1,0:T(8,128)(2,1)S(1)}, bf16[400,128]{1,0:T(8,128)(2,1)S(1)}, u32[]{:S(2)}, u32[]{:S(2)}) collective-permute-start(bf16[400,128]{1,0:T(8,128)(2,1)S(1)} %get-tuple-element.14), channel_id=1, source_target_pairs={{0,6},{2,4},{4,2},{6,0},{1,7},{3,5},{5,3},{7,1},{8,14},{10,12},{12... | collective-permute-start | bytes 307208 | tf_op jit(solution)/shard_map/ppermute | solution.py:454
  10.5 0.2 collective-permute-done.2.az1
  10.6 3.8 %collective-permute-done.3.az2 = bf16[400,128]{1,0:T(8,128)(2,1)S(1)} collective-permute-done((bf16[400,128]{1,0:T(8,128)(2,1)S(1)}, bf16[400,128]{1,0:T(8,128)(2,1)S(1)}, u32[]{:S(2)}, u32[]{:S(2)}) %collective-permute-start.3) | collective-permute-done | bytes 102432 | tf_op jit(solution)/shard_map/ppermute | solution.py:454
  14.4 0.0 copy-start.1
  14.4 0.9 %copy-done.1 = f32[3,8,16,128]{3,2,1,0:T(8,128)S(1)} copy-done((f32[3,8,16,128]{3,2,1,0:T(8,128)S(1)}, f32[3,8,16,128]{3,2,1,0:T(8,128)}, u32[]{:S(2)}) %copy-start.1) | copy-done | bytes 196632
  15.4 0.0 copy-start.3
  15.4 0.8 %copy-done.3 = f32[8,16,128]{2,1,0:T(8,128)S(1)} copy-done((f32[8,16,128]{2,1,0:T(8,128)S(1)}, f32[8,16,128]{2,1,0:T(8,128)}, u32[]{:S(2)}) %copy-start.3) | copy-done | bytes 65560
  16.2 0.0 copy-start.5
  16.2 0.8 %copy-done.5 = f32[8,16,128]{2,1,0:T(8,128)S(1)} copy-done((f32[8,16,128]{2,1,0:T(8,128)S(1)}, f32[8,16,128]{2,1,0:T(8,128)}, u32[]{:S(2)}) %copy-start.5) | copy-done | bytes 65560
  17.1 0.6 %shard_map.79 = (f32[3200,128]{1,0:T(8,128)S(1)}, bf16[48,512]{1,0:T(8,128)(2,1)S(1)}) custom-call(f32[128,128]{1,0:T(8,128)S(1)} %bitcast.10, f32[384,128]{1,0:T(8,128)S(1)} %bitcast.6, f32[128,128]{1,0:T(8,128)S(1)} %bitcast.13, bf16[480,128]{1,0:T(8,128)(2,1)S(1)} %collective-permute-done.got1.ax1, bf16[480,128]{1,0:T(8,128)(2,1)S(1)} %collective-permute-done.1.got2.ax2, ...), custom_call_target="tpu_custom_call" | custom-call | tf_op jit(solution)/shard_map/pallas_call | solution.py:477
  17.7 1.5 %collective-permute-start.4 = (bf16[48,512]{1,0:T(8,128)(2,1)S(1)}, bf16[48,512]{1,0:T(8,128)(2,1)S(1)}, u32[]{:S(2)}, u32[]{:S(2)}) collective-permute-start(bf16[48,512]{1,0:T(8,128)(2,1)S(1)} %get-tuple-element.16), channel_id=1, source_target_pairs={{0,1},{1,0},{2,3},{3,2},{4,5},{5,4},{6,7},{7,6},{8,9},{9,8},{10,11... | collective-permute-start | bytes 147464 | tf_op jit(solution)/shard_map/ppermute | solution.py:486
  19.2 2.6 %collective-permute-done.4.rlo.rhi = bf16[48,512]{1,0:T(8,128)(2,1)S(1)} collective-permute-done((bf16[48,512]{1,0:T(8,128)(2,1)S(1)}, bf16[48,512]{1,0:T(8,128)(2,1)S(1)}, u32[]{:S(2)}, u32[]{:S(2)}) %collective-permute-start.4) | collective-permute-done | bytes 49184 | tf_op jit(solution)/shard_map/ppermute | solution.py:486
  21.8 0.0 copy-start.7
  21.8 0.7 %copy-done.7 = s32[32]{0:T(128)S(1)} copy-done((s32[32]{0:T(128)S(1)}, s32[32]{0:T(128)}, u32[]{:S(2)}) %copy-start.7) | copy-done | bytes 152
  22.5 0.0 copy-start.6
  22.5 0.0 copy-start.8
  22.5 7.4 %shard_map.80 = (f32[32,1,128]{2,1,0:T(1,128)}, f32[5,12,64,128]{3,2,1,0:T(8,128)S(1)}, f32[5,8,32,128]{3,2,1,0:T(8,128)S(1)}) custom-call(f32[5,20,32,128]{3,2,1,0:T(8,128)S(1)} %bitcast.7, bf16[48,512]{1,0:T(8,128)(2,1)S(1)} %collective-permute-done.4.rlo.rhi, bf16[48,512]{1,0:T(8,128)(2,1)S(1)} %collective-permute-done.4.rlo.rhi, s32[32]{0:T(128)S(1)} %copy-done.7), custom_call_target="tpu_custom_call" | custom-call | tf_op jit(solution)/shard_map/pallas_call | solution.py:494
  29.9 9.7 %all-to-all-start = ((f32[32,1,128]{2,1,0:T(1,128)}), f32[32,1,128]{2,1,0:T(1,128)S(1)}, u32[]{:S(2)}, u32[]{:S(2)}) async-start(f32[32,1,128]{2,1,0:T(1,128)} %get-tuple-element.19), calls=%async_computation | async-start | bytes 32768 | tf_op jit(solution)/shard_map/all_to_all | solution.py:504
  39.6 2.2 %shard_map.81 = f32[5,8,16,128]{3,2,1,0:T(8,128)} custom-call(f32[5,12,64,128]{3,2,1,0:T(8,128)S(1)} %get-tuple-element.17.u2, f32[5,8,32,128]{3,2,1,0:T(8,128)S(1)} %get-tuple-element.18.u0), custom_call_target="tpu_custom_call" | custom-call | flops 400000000 | bytes 8000000 | tf_op jit(solution)/shard_map/pallas_call | solution.py:507
  41.8 4.8 %all-to-all-done.rows = f32[32,1,128]{2,1,0:T(1,128)S(1)} async-done(((f32[32,1,128]{2,1,0:T(1,128)}), f32[32,1,128]{2,1,0:T(1,128)S(1)}, u32[]{:S(2)}, u32[]{:S(2)}) %all-to-all-start) | async-done | bytes 16416 | tf_op jit(solution)/shard_map/all_to_all | solution.py:504
  46.6 0.0 copy-done.6
  46.6 0.0 copy-done.8
  46.6 1.2 %shard_map.82 = f32[256,128]{1,0:T(8,128)} custom-call(f32[32,1,128]{2,1,0:T(1,128)S(1)} %all-to-all-done.rows, s32[1,32]{1,0:T(1,128)S(1)} %copy-done.8, bf16[256,1024]{1,0:T(8,128)(2,1)S(1)} %copy-done.6), custom_call_target="tpu_custom_call" | custom-call | tf_op jit(solution)/shard_map/pallas_call | solution.py:515
  (1 shorter events, 0.0 us)
Async XLA Ops:
  0.6 0.9 %copy-start = (f32[3,8,16,128]{3,2,1,0:T(8,128)S(1)}, f32[3,8,16,128]{3,2,1,0:T(8,128)}, u32[]{:S(2)}) copy-start(f32[3,8,16,128]{3,2,1,0:T(8,128)} %param.7) | copy-start | bytes 589828
  1.6 0.8 %copy-start.2 = (f32[8,16,128]{2,1,0:T(8,128)S(1)}, f32[8,16,128]{2,1,0:T(8,128)}, u32[]{:S(2)}) copy-start(f32[8,16,128]{2,1,0:T(8,128)} %param.6) | copy-start | bytes 196612
  2.4 0.8 %copy-start.4 = (f32[8,16,128]{2,1,0:T(8,128)S(1)}, f32[8,16,128]{2,1,0:T(8,128)}, u32[]{:S(2)}) copy-start(f32[8,16,128]{2,1,0:T(8,128)} %param.8) | copy-start | bytes 196612
  3.3 1.5 %collective-permute-start = (bf16[480,128]{1,0:T(8,128)(2,1)S(1)}, bf16[480,128]{1,0:T(8,128)(2,1)S(1)}, u32[]{:S(2)}, u32[]{:S(2)}) collective-permute-start(bf16[480,128]{1,0:T(8,128)(2,1)S(1)} %get-tuple-element.11), channel_id=1, source_target_pairs={{0,8},{8,0},{16,24},{24,16},{1,9},{9,1},{17,25},{25,17},{2,10},{10... | collective-permute-start | bytes 368648 | tf_op jit(solution)/shard_map/ppermute | solution.py:454
  3.8 1.0 %collective-permute-start.1 = (bf16[480,128]{1,0:T(8,128)(2,1)S(1)}, bf16[480,128]{1,0:T(8,128)(2,1)S(1)}, u32[]{:S(2)}, u32[]{:S(2)}) collective-permute-start(bf16[480,128]{1,0:T(8,128)(2,1)S(1)} %get-tuple-element.12), channel_id=1, source_target_pairs={{0,0},{8,16},{16,8},{24,24},{1,1},{9,17},{17,9},{25,25},{2,2},{10,... | collective-permute-start | bytes 368648 | tf_op jit(solution)/shard_map/ppermute | solution.py:454
  5.0 5.6 %collective-permute-start.2 = (bf16[400,128]{1,0:T(8,128)(2,1)S(1)}, bf16[400,128]{1,0:T(8,128)(2,1)S(1)}, u32[]{:S(2)}, u32[]{:S(2)}) collective-permute-start(bf16[400,128]{1,0:T(8,128)(2,1)S(1)} %get-tuple-element.13), channel_id=1, source_target_pairs={{0,2},{2,0},{4,6},{6,4},{1,3},{3,1},{5,7},{7,5},{8,10},{10,8},{12,... | collective-permute-start | bytes 307208 | tf_op jit(solution)/shard_map/ppermute | solution.py:454
  8.0 6.5 %collective-permute-start.3 = (bf16[400,128]{1,0:T(8,128)(2,1)S(1)}, bf16[400,128]{1,0:T(8,128)(2,1)S(1)}, u32[]{:S(2)}, u32[]{:S(2)}) collective-permute-start(bf16[400,128]{1,0:T(8,128)(2,1)S(1)} %get-tuple-element.14), channel_id=1, source_target_pairs={{0,6},{2,4},{4,2},{6,0},{1,7},{3,5},{5,3},{7,1},{8,14},{10,12},{12... | collective-permute-start | bytes 307208 | tf_op jit(solution)/shard_map/ppermute | solution.py:454
  14.4 0.9 %copy-start.1 = (f32[3,8,16,128]{3,2,1,0:T(8,128)S(1)}, f32[3,8,16,128]{3,2,1,0:T(8,128)}, u32[]{:S(2)}) copy-start(f32[3,8,16,128]{3,2,1,0:T(8,128)} %param.7) | copy-start | bytes 589828
  15.4 0.8 %copy-start.3 = (f32[8,16,128]{2,1,0:T(8,128)S(1)}, f32[8,16,128]{2,1,0:T(8,128)}, u32[]{:S(2)}) copy-start(f32[8,16,128]{2,1,0:T(8,128)} %param.6) | copy-start | bytes 196612
  16.2 0.8 %copy-start.5 = (f32[8,16,128]{2,1,0:T(8,128)S(1)}, f32[8,16,128]{2,1,0:T(8,128)}, u32[]{:S(2)}) copy-start(f32[8,16,128]{2,1,0:T(8,128)} %param.8) | copy-start | bytes 196612
  17.7 4.1 %collective-permute-start.4 = (bf16[48,512]{1,0:T(8,128)(2,1)S(1)}, bf16[48,512]{1,0:T(8,128)(2,1)S(1)}, u32[]{:S(2)}, u32[]{:S(2)}) collective-permute-start(bf16[48,512]{1,0:T(8,128)(2,1)S(1)} %get-tuple-element.16), channel_id=1, source_target_pairs={{0,1},{1,0},{2,3},{3,2},{4,5},{5,4},{6,7},{7,6},{8,9},{9,8},{10,11... | collective-permute-start | bytes 147464 | tf_op jit(solution)/shard_map/ppermute | solution.py:486
  21.8 0.7 %copy-start.7 = (s32[32]{0:T(128)S(1)}, s32[32]{0:T(128)}, u32[]{:S(2)}) copy-start(s32[32]{0:T(128)} %cells.1) | copy-start | bytes 388
  22.5 24.2 %copy-start.6 = (bf16[256,1024]{1,0:T(8,128)(2,1)S(1)}, bf16[256,1024]{1,0:T(8,128)(2,1)}, u32[]{:S(2)}) copy-start(bf16[256,1024]{1,0:T(8,128)(2,1)} %weight.1) | copy-start | bytes 1572868
  22.5 24.2 %copy-start.8 = (s32[1,32]{1,0:T(1,128)S(1)}, s32[1,32]{1,0:T(1,128)}, u32[]{:S(2)}) copy-start(s32[1,32]{1,0:T(1,128)} %offsets.1) | copy-start | bytes 388
  29.9 16.8 %all-to-all-start = ((f32[32,1,128]{2,1,0:T(1,128)}), f32[32,1,128]{2,1,0:T(1,128)S(1)}, u32[]{:S(2)}, u32[]{:S(2)}) async-start(f32[32,1,128]{2,1,0:T(1,128)} %get-tuple-element.19), calls=%async_computation | async-start | bytes 32768 | tf_op jit(solution)/shard_map/all_to_all | solution.py:504

commit v4 on v3

--- a/solution.py
+++ b/solution.py
@@ -16,13 +16,14 @@
 SCALE = -LAMBDA / 12.0
 ROWS = 32
 OFF = 8
+HBM = pltpu.MemorySpace.HBM
 VMEM = pltpu.MemorySpace.VMEM
 SMEM = pltpu.MemorySpace.SMEM
 F32 = jnp.float32
 BF16 = jnp.bfloat16
 
 
-def call(kernel, outs, in_spaces, scratch=(), mib=8, cost=None):
+def call(kernel, outs, in_spaces, scratch=(), mib=8, cost=None, alias={}):
     return pl.pallas_call(
         kernel,
         out_shape=outs,
@@ -31,6 +32,7 @@
         scratch_shapes=list(scratch),
         compiler_params=pltpu.CompilerParams(vmem_limit_bytes=mib * 1024 * 1024),
         cost_estimate=cost,
+        input_output_aliases=alias,
     )
 
 
@@ -42,28 +44,39 @@
     return 8 * (row % 4) + row // 4
 
 
-def home_ref(f, den, vel, pre):
-    if f == 0:
-        return den, 0
-    if f == 4:
-        return pre, 0
-    return vel, (f - 1) * den.shape[0]
-
-
 def is_even(axis):
     return lax.axis_index(axis) % 2 == 0
 
 
-def pack_ax(ca, cz, den, vel, pre, first_out, second_out):
+def load_and_pack(ca, cz, den, vel, pre, home, ax1, ax2, az1, az2, sems):
+    size = ca * cz
+    copies = [
+        pltpu.make_async_copy(den, home.at[pl.ds(0, size)], sems.at[0]),
+        pltpu.make_async_copy(vel, home.at[pl.ds(size, 3 * size)], sems.at[1]),
+        pltpu.make_async_copy(pre, home.at[pl.ds(4 * size, size)], sems.at[2]),
+    ]
+    for copy in copies:
+        copy.start()
+    for copy in copies:
+        copy.wait()
     even = is_even("ax")
-    size = REACH * cz
-    for f in range(5):
-        ref, at = home_ref(f, den, vel, pre)
-        low = ref[at : at + size, :]
-        high = ref[at + ca * cz - size : at + ca * cz, :]
-        rows = slice(f * size, (f + 1) * size)
-        first_out[rows, :] = jnp.where(even, high, low).astype(BF16)
-        second_out[rows, :] = jnp.where(even, low, high).astype(BF16)
+    edge = REACH * cz
+    for f in range(5):
+        at = f * size
+        low = home[at : at + edge, :]
+        high = home[at + size - edge : at + size, :]
+        rows = slice(f * edge, (f + 1) * edge)
+        ax1[rows, :] = jnp.where(even, high, low).astype(BF16)
+        ax2[rows, :] = jnp.where(even, low, high).astype(BF16)
+    even = is_even("az")
+    low, high = [], []
+    for f in range(5):
+        for d in range(REACH):
+            low.append(home[pl.ds(f * size + d, ca, stride=cz), :])
+            high.append(home[pl.ds(f * size + cz - 1 - d, ca, stride=cz), :])
+    low, high = jnp.concatenate(low, axis=0), jnp.concatenate(high, axis=0)
+    az1[...] = jnp.where(even, high, low).astype(BF16)
+    az2[...] = jnp.where(even, low, high).astype(BF16)
 
 
 def ax_sides(n_ax, got1, got2, rows):
@@ -75,20 +88,16 @@
     return lo, hi
 
 
-def pack_az(n_ax, ca, cz, den, vel, pre, got1, got2, first_out, second_out, near):
+def pack_corners(n_ax, cz, got1, got2, first_out, second_out, near):
     even = is_even("az")
     half = MID * cz
-    for f in range(5):
-        base = f * REACH * cz
-        lo, hi = ax_sides(n_ax, got1, got2, slice(base, base + REACH * cz))
-        near[f, 0:half, :] = lo[REACH * cz - half :]
+    size = REACH * cz
+    for f in range(5):
+        lo, hi = ax_sides(n_ax, got1, got2, slice(f * size, (f + 1) * size))
+        near[f, 0:half, :] = lo[size - half :]
         near[f, half : 2 * half, :] = hi[0:half]
     low, high = [], []
     for f in range(5):
-        ref, at = home_ref(f, den, vel, pre)
-        for d in range(REACH):
-            low.append(ref[pl.ds(at + d, ca, stride=cz), :])
-            high.append(ref[pl.ds(at + cz - 1 - d, ca, stride=cz), :])
         for d in range(MID):
             low.append(near[f, pl.ds(d, 2 * MID, stride=cz), :])
             high.append(near[f, pl.ds(cz - 1 - d, 2 * MID, stride=cz), :])
@@ -97,51 +106,57 @@
     second_out[...] = jnp.where(even, low, high).astype(BF16)
 
 
+def spread_rows(planes, cz, f, plane, ref, at, block):
+    quarter = cz // 4
+    for l in range(4):
+        row = (f * planes + plane) * ROWS + 8 * l + OFF // 4
+        block[pl.ds(row, quarter), :] = ref[pl.ds(at + l, quarter, stride=4), :]
+
+
+def prepare(ca, cz, home, block, banded):
+    for f in range(5):
+        for k in range(ca):
+            spread_rows(ca + 2 * REACH, cz, f, REACH + k, home, (f * ca + k) * cz, block)
+    banded[...] = band(2 * home.shape[1])
+
+
 def one_hot_lanes(start, height, lanes, row0=0):
     row = lax.broadcasted_iota(jnp.int32, (height, lanes), 0) - row0
     lane = lax.broadcasted_iota(jnp.int32, (height, lanes), 1)
     return jnp.where((row >= 0) & (row < REACH) & (lane == row + start), 1.0, 0.0).astype(BF16)
 
 
-def assemble(n_ax, ends, ca, cz, den, vel, pre, ax1, ax2, az1, az2, block, *rest):
-    outs, (sides, strips) = rest[: len(ends)], rest[len(ends) :]
-    cr = den.shape[1]
+def assemble(n_ax, ends, ca, cz, block_in, ax1, ax2, az1, az2, corner1, corner2, block, *rest):
+    outs, (sides, strips, corners) = rest[: len(ends)], rest[len(ends) :]
+    cr = ax1.shape[1]
     planes = ca + 2 * REACH
     size = REACH * cz
-    quarter = cz // 4
-    first = OFF // 4
-
-    def put(f, plane, ref, at):
-        for l in range(4):
-            row = (f * planes + plane) * ROWS + 8 * l + first
-            block[pl.ds(row, quarter), :] = ref[pl.ds(at + l, quarter, stride=4), :]
-
-    for f in range(5):
-        ref, at = home_ref(f, den, vel, pre)
-        for k in range(ca):
-            put(f, REACH + k, ref, at + k * cz)
+    for f in range(5):
         lo, hi = ax_sides(n_ax, ax1, ax2, slice(f * size, (f + 1) * size))
         sides[f, 0:size, :] = lo
         sides[f, size : 2 * size, :] = hi
     for f in range(5):
         for k in range(REACH):
-            put(f, k, sides.at[f], k * cz)
-            put(f, REACH + ca + k, sides.at[f], size + k * cz)
+            spread_rows(planes, cz, f, k, sides.at[f], k * cz, block)
+            spread_rows(planes, cz, f, REACH + ca + k, sides.at[f], size + k * cz, block)
 
     even = is_even("az")
-    a, b = az1[...].astype(F32), az2[...].astype(F32)
-    strips[0] = jnp.where(even, b, a)
-    strips[1] = jnp.where(even, a, b)
-    for f in range(5):
-        base = f * (REACH * ca + MID * 2 * MID)
+    for one, two, into in ((az1, az2, strips), (corner1, corner2, corners)):
+        a, b = one[...].astype(F32), two[...].astype(F32)
+        into[0] = jnp.where(even, b, a)
+        into[1] = jnp.where(even, a, b)
+    for f in range(5):
         for d in range(REACH):
             for side, row in ((0, OFF - 1 - d), (1, OFF + cz + d)):
                 at = kept(row) + f * planes * ROWS
-                block[pl.ds(at + REACH * ROWS, ca, stride=ROWS), :] = strips[side, pl.ds(base + d * ca, ca), :]
+                got = strips[side, pl.ds((f * REACH + d) * ca, ca), :]
+                block[pl.ds(at + REACH * ROWS, ca, stride=ROWS), :] = got
                 if d < MID:
-                    start = base + REACH * ca + d * 2 * MID
-                    block[pl.ds(at + (REACH - MID) * ROWS, MID, stride=ROWS), :] = strips[side, pl.ds(start, MID), :]
-                    block[pl.ds(at + (REACH + ca) * ROWS, MID, stride=ROWS), :] = strips[side, pl.ds(start + MID, MID), :]
+                    start = (f * MID + d) * 2 * MID
+                    got = corners[side, pl.ds(start, MID), :]
+                    block[pl.ds(at + (REACH - MID) * ROWS, MID, stride=ROWS), :] = got
+                    got = corners[side, pl.ds(start + MID, MID), :]
+                    block[pl.ds(at + (REACH + ca) * ROWS, MID, stride=ROWS), :] = got
 
     rad = lax.axis_index("rad")
     for end, out in zip(ends, outs):
@@ -241,13 +256,15 @@
     return get
 
 
-def stages(n_ax, n_rad, ca, cz, block, rlo, rhi, cells, q_out, u2_out, u0_out, ghost, first, second, fax, part, banded, value, picked):
+def stages(n_ax, n_rad, ca, cz, slots, block, banded, cells_far, *refs):
+    sides, refs = refs[: len(refs) - 12], refs[len(refs) - 12 :]
+    q_out, u2_out, u0_out, ghost, first, second, fax, part, value, picked, cells, cells_sem = refs
+    fetch = pltpu.make_async_copy(cells_far, cells, cells_sem)
+    fetch.start()
     cr = block.shape[-1]
-    slots = cells.shape[0]
     low, high = REACH, REACH + ca
     ax = lax.axis_index("ax")
     rad = lax.axis_index("rad")
-    banded[...] = band(2 * cr)
 
     lane = lax.broadcasted_iota(jnp.int32, (ROWS, cr), 1)
     kept_row = lax.broadcasted_iota(jnp.int32, (ROWS, cr), 0)
@@ -262,14 +279,19 @@
     base0 = jnp.where(steps_rad < 99, 0.0, 1.0)
 
     count = ca + 2 * MID
-    got_hi, got_lo = rhi[...], rlo[...]
-    for f in range(5):
+    places = ((0, rad < n_rad - 1), (cr - REACH, rad > 0))
+    messages = [x[...] for x in sides]
+    for f in range(5):
+        hots = []
+        for start, there in places:
+            place = one_hot_lanes(start, messages[0].shape[0], cr, row0=8 * f)
+            hots.append(jnp.where(there, place, jnp.zeros_like(place)))
+        if len(messages) == 1:
+            hots = [hots[0] + hots[1]]
         side = 0.0
-        for got, start, there in ((got_hi, 0, rad < n_rad - 1), (got_lo, cr - REACH, rad > 0)):
-            place = one_hot_lanes(start, got.shape[0], cr, row0=8 * f)
-            place = jnp.where(there, place, jnp.zeros_like(place))
+        for got, hot in zip(messages, hots):
             side = side + lax.dot_general(
-                got, place, (((0,), (0,)), ((), ())), preferred_element_type=F32
+                got, hot, (((0,), (0,)), ((), ())), preferred_element_type=F32
             )
         side = side.reshape(count, ROWS, cr)
         ghost[f] = side + base0[None] if f == 0 else side
@@ -363,6 +385,7 @@
         u = split_state([u2_out[f, i + 2, 0:ROWS] for f in range(5)])
         note(2, low + i, u)
 
+    fetch.wait()
     picked[...] = jnp.zeros_like(picked)
     lanes = lax.broadcasted_iota(jnp.int32, (1, cr), 1)
     for p in range(slots):
@@ -385,9 +408,7 @@
     q_out[...] = jnp.broadcast_to(q[0:1][None], q_out.shape)
 
 
-def last_stage(ca, cz, u2, u0, state, fax, part, banded):
-    cr = u2.shape[-1]
-    banded[...] = band(2 * cr)
+def last_stage(ca, cz, u2, u0, banded, state, fax, part):
     for j in (0, 1, ca + 2, ca + 3):
         ax_only(split_state([u2[f, j, 0:ROWS] for f in range(5)]), fax, j)
 
@@ -410,21 +431,29 @@
                 state[f, k, pl.ds(l, quarter, stride=4), :] = new[8 * l + first : 8 * l + first + quarter]
 
 
-def signals(slots, rows, offsets, weight, out):
+def repeat_rows(rows, out):
+    out[...] = jnp.broadcast_to(rows[...].reshape(1, rows.shape[0], rows.shape[2]), out.shape)
+
+
+def signals(slots, n_az, n_rad, rows, offsets, weight, out):
     ndev = rows.shape[0]
     group = 32
     cols = group * slots
-    lanes = rows.shape[2]
+    lanes = rows.shape[1]
     col = lax.broadcasted_iota(jnp.int32, (1, cols), 1)
-    owner = lax.broadcasted_iota(jnp.int32, (group, cols), 0) == col // slots
+    place = lax.broadcasted_iota(jnp.int32, (group, cols), 0)
+    pair = n_az * n_rad
+    device = place - place % pair + (place % n_az) * n_rad + (place % pair) // n_az
+    owner = device == col // slots
+    holder = place == col // slots
     lane = lax.broadcasted_iota(jnp.int32, (lanes, cols), 0)
     time = lax.broadcasted_iota(jnp.int32, (NB, cols), 0).astype(F32)
     total = jnp.zeros(out.shape, F32)
     for g in range(ndev // group):
-        q = rows[g * group : (g + 1) * group, 0, :].astype(BF16)
+        q = rows[g * group : (g + 1) * group, :].astype(BF16)
         off = offsets[0:1, g * group : (g + 1) * group].astype(F32)
         off = jnp.broadcast_to(off, (8, group)).astype(BF16)
-        bins = jnp.dot(off, owner.astype(BF16), preferred_element_type=F32)[0:1]
+        bins = jnp.dot(off, holder.astype(BF16), preferred_element_type=F32)[0:1]
         table = jnp.zeros((NB, cols), F32)
         for s in range(3):
             pick = jnp.where(lane == s * slots + col % slots, 1.0, 0.0).astype(BF16)
@@ -459,62 +488,80 @@
     slots = panel_cell.shape[0]
     ndev = bin_offset.shape[1]
     n_ax, n_rad = lax.axis_size("ax"), lax.axis_size("rad")
-    home = (density.reshape(ca * cz, cr), velocity.reshape(3 * ca * cz, cr), pressure.reshape(ca * cz, cr))
+    n_az = lax.axis_size("az")
     planes = ca + 2 * REACH
     part = functools.partial
+    given = (density.reshape(ca * cz, cr), velocity.reshape(3 * ca * cz, cr), pressure.reshape(ca * cz, cr))
 
     edge = struct((5 * REACH * cz, cr), BF16)
-    ax1, ax2 = call(part(pack_ax, ca, cz), (edge, edge), [VMEM] * 3)(*home)
+    strip = struct((5 * REACH * ca, cr), BF16)
+    home, ax1, ax2, az1, az2 = call(
+        part(load_and_pack, ca, cz),
+        (struct((5 * ca * cz, cr)), edge, edge, strip, strip),
+        [HBM] * 3,
+        [pltpu.SemaphoreType.DMA((3,))],
+    )(*given)
     ax1, ax2 = swap(ax1, ax2, "ax", False)
-
-    strip = struct((5 * (REACH * ca + MID * 2 * MID), cr), BF16)
+    az1, az2 = swap(az1, az2, "az", True)
+    grid = struct((5 * planes * ROWS, cr))
+    block, banded = call(
+        part(prepare, ca, cz), (grid, struct((2 * cr, 2 * cr), BF16)), [VMEM], mib=8
+    )(home)
+
+    corner = struct((5 * MID * 2 * MID, cr), BF16)
     near = pltpu.VMEM((5, 2 * MID * cz, cr), F32)
-    az1, az2 = call(part(pack_az, n_ax, ca, cz), (strip, strip), [VMEM] * 5, [near])(*home, ax1, ax2)
-    az1, az2 = swap(az1, az2, "az", True)
+    corner1, corner2 = call(part(pack_corners, n_ax, cz), (corner, corner), [VMEM] * 2, [near])(ax1, ax2)
+    corner1, corner2 = swap(corner1, corner2, "az", True)
 
     side = struct((48, (ca + 2 * MID) * ROWS), BF16)
     ends = ("either",) if n_rad == 2 else ("low", "high")
     got = call(
         part(assemble, n_ax, ends, ca, cz),
-        (struct((5 * planes * ROWS, cr)),) + tuple(side for _ in ends),
+        (grid,) + tuple(side for _ in ends),
         [VMEM] * 7,
-        [pltpu.VMEM((5, 2 * REACH * cz, cr), F32), pltpu.VMEM((2,) + strip.shape, F32)],
+        [
+            pltpu.VMEM((5, 2 * REACH * cz, cr), F32),
+            pltpu.VMEM((2,) + strip.shape, F32),
+            pltpu.VMEM((2,) + corner.shape, F32),
+        ],
         mib=12,
-    )(*home, ax1, ax2, az1, az2)
+        alias={0: 0},
+    )(block, ax1, ax2, az1, az2, corner1, corner2)
     block = got[0].reshape(5, planes, ROWS, cr)
     if n_rad == 2:
-        rlo = rhi = lax.ppermute(got[1], "rad", [(0, 1), (1, 0)])
+        sides = (lax.ppermute(got[1], "rad", [(0, 1), (1, 0)]),)
     else:
         up = [(i, i + 1) for i in range(n_rad - 1)]
-        rlo = lax.ppermute(got[2], "rad", up)
-        rhi = lax.ppermute(got[1], "rad", [(j, i) for i, j in up])
+        sides = (lax.ppermute(got[1], "rad", [(j, i) for i, j in up]), lax.ppermute(got[2], "rad", up))
 
     grid = (5, planes, 2 * ROWS, cr)
-    banded = pltpu.VMEM((2 * cr, 2 * cr), BF16)
     q, u2, u0 = call(
-        part(stages, n_ax, n_rad, ca, cz),
-        (struct((ndev, 1, 128)), struct((5, ca + 4, 2 * ROWS, cr)), struct((5, ca, ROWS, cr))),
-        [VMEM] * 3 + [SMEM],
+        part(stages, n_ax, n_rad, ca, cz, slots),
+        (struct((n_az, 1, 128)), struct((5, ca + 4, 2 * ROWS, cr)), struct((5, ca, ROWS, cr))),
+        [VMEM, VMEM, HBM] + [VMEM] * len(sides),
         [pltpu.VMEM((5, ca + 2 * MID, ROWS, cr), F32)]
         + [pltpu.VMEM(grid, F32) for _ in range(4)]
-        + [banded, pltpu.VMEM((3, planes, ROWS, cr), F32), pltpu.VMEM((128, cr), F32)],
+        + [pltpu.VMEM((3, planes, ROWS, cr), F32), pltpu.VMEM((128, cr), F32)]
+        + [pltpu.SMEM((slots,), jnp.int32), pltpu.SemaphoreType.DMA],
         mib=28,
-    )(block, rlo, rhi, panel_cell)
-
-    rows = lax.all_to_all(q, ("ax", "az", "rad"), 0, 0, tiled=True)
+    )(block, banded, panel_cell, *sides)
+
+    rows = lax.all_to_all(q, "az", 0, 0, tiled=True)
+    rows = call(repeat_rows, struct((n_ax * n_rad, n_az, 128)), [VMEM], mib=2)(rows)
+    rows = lax.all_to_all(rows, ("ax", "rad"), 0, 0, tiled=True).reshape(ndev, 128)
 
     grid = (5, ca + 4, 2 * ROWS, cr)
     state = call(
         part(last_stage, ca, cz),
         struct((5, ca, cz, cr)),
-        [VMEM] * 2,
-        [pltpu.VMEM(grid, F32), pltpu.VMEM(grid, F32), banded],
+        [VMEM] * 3,
+        [pltpu.VMEM(grid, F32), pltpu.VMEM(grid, F32)],
         mib=12,
         cost=pl.CostEstimate(flops=400_000_000, bytes_accessed=8_000_000, transcendentals=0),
-    )(u2, u0)
-    signal = call(part(signals, slots), struct((obs_weight.shape[0], NB)), [VMEM] * 3, mib=24)(
-        rows, bin_offset, obs_weight
-    )
+    )(u2, u0, banded)
+    signal = call(
+        part(signals, slots, n_az, n_rad), struct((obs_weight.shape[0], NB)), [VMEM] * 3, mib=24
+    )(rows, bin_offset, obs_weight)
     return (state, signal)
 
 

time: 48.2 us -> 49.5 us (1.027)
  blocking collectives: 0 us -> 8.02 us
  local copies, waits for them, and re-layouts: 5.87 us -> 2.62 us
  waiting for transfers between devices: 11.7 us -> 10.1 us
  starting transfers between devices: 17.9 us -> 16.5 us
  Pallas kernels: 11.7 us -> 11.2 us
    all_to_all x0 -> x1, blocking collectives: none -> 8.02 us  [local(): rows = lax.all_to_all(q, 'az', 0, 0, tiled=True)]
    unnamed x18 -> x12, local copies, waits for them, and re-layouts: 5.87 us -> 2.62 us
    all_to_all x1, starting transfers between devices: 9.71 us -> 7.01 us  [local(): lax.all_to_all(rows, ('ax', 'rad'), 0, 0, tiled=True).reshape(ndev, 128)]
    all_to_all x1, waiting for transfers between devices: 4.79 us -> 2.64 us  [local(): lax.all_to_all(rows, ('ax', 'rad'), 0, 0, tiled=True).reshape(ndev, 128)]
    ppermute x4 -> x6, starting transfers between devices: 6.65 us -> 7.96 us  [swap(): return (lax.ppermute(first, axis, one), lax.ppermute(second, axis, two))]
    pallas_call x6 -> x8, Pallas kernels: 11.7 us -> 11.2 us  [the longest x1 5.85 us: local(): call(part(stages, n_ax, n_rad, ca, cz, slots), (struct((n_az, 1, 128)), s...]
    ppermute x4 -> x6, waiting for transfers between devices: 4.3 us -> 4.64 us  [swap(): return (lax.ppermute(first, axis, one), lax.ppermute(second, axis, two))]
  transfers between devices with their start and end apart: 6 -> 8, of which waited for: 5 -> 5; matrix products, arithmetic and copies ran while one was open for 0% -> 0% of each run, Pallas kernels for 5% -> 5%
where the time goes in v4:
time: 49.5 us; the launch traced here: 49.1 us
  starting transfers between devices  16.5 us (33%)
  Pallas kernels  11.2 us (23%)
  waiting for transfers between devices  10.1 us (20%)
  blocking collectives  8.02 us (16%)
  local copies, waits for them, and re-layouts  2.62 us (5%)
  between operations  0.71 us (1%)
    all_to_all x1, blocking collectives, local(): rows = lax.all_to_all(q, 'az', 0, 0, tiled=True)  8.02 us
    ppermute x6, starting transfers between devices, swap(): return (lax.ppermute(first, axis, one), lax.ppermute(second, axis, two))  7.96 us
    all_to_all x1, starting transfers between devices, local(): lax.all_to_all(rows, ('ax', 'rad'), 0, 0, tiled=True).reshape(ndev, 128)  7.01 us
    pallas_call x1, Pallas kernels, local(): call(part(stages, n_ax, n_rad, ca, cz, slots), (struct((n_az, 1, 128)), s...  5.85 us
    ppermute x6, waiting for transfers between devices, swap(): return (lax.ppermute(first, axis, one), lax.ppermute(second, axis, two))  4.64 us
    ppermute x1, waiting for transfers between devices, local(): sides = (lax.ppermute(got[1], 'rad', [(0, 1), (1, 0)]),)  2.83 us
    all_to_all x1, waiting for transfers between devices, local(): lax.all_to_all(rows, ('ax', 'rad'), 0, 0, tiled=True).reshape(ndev, 128)  2.64 us
    unnamed x12, local copies, waits for them, and re-layouts  2.62 us
  transfers between devices with their start and end apart: 8, of which 5 were waited for; matrix products, arithmetic and copies ran while one was open for 0% of the time, Pallas kernels for 5%

profile of v4, /device:TPU:0, one launch (start us, length us, event | category | flops | bytes accessed | tf_op | source)
XLA Modules:
  0.0 49.1 jit_solution(18051002298590177744)
XLA Ops:
  0.6 0.0 copy-start.5
  0.6 0.0 copy-start.1
  0.7 0.9 %copy-done.1 = f32[3,8,16,128]{3,2,1,0:T(8,128)S(1)} copy-done((f32[3,8,16,128]{3,2,1,0:T(8,128)S(1)}, f32[3,8,16,128]{3,2,1,0:T(8,128)}, u32[]{:S(2)}) %copy-start.1) | copy-done | bytes 196632
  1.6 0.0 copy-start.2
  1.6 0.8 %copy-done.2 = f32[8,16,128]{2,1,0:T(8,128)S(1)} copy-done((f32[8,16,128]{2,1,0:T(8,128)S(1)}, f32[8,16,128]{2,1,0:T(8,128)}, u32[]{:S(2)}) %copy-start.2) | copy-done | bytes 65560
  2.4 0.0 copy-start.3
  2.4 0.8 %copy-done.3 = f32[8,16,128]{2,1,0:T(8,128)S(1)} copy-done((f32[8,16,128]{2,1,0:T(8,128)S(1)}, f32[8,16,128]{2,1,0:T(8,128)}, u32[]{:S(2)}) %copy-start.3) | copy-done | bytes 65560
  3.3 0.5 %shard_map.77 = (f32[640,128]{1,0:T(8,128)S(1)}, bf16[480,128]{1,0:T(8,128)(2,1)S(1)}, bf16[480,128]{1,0:T(8,128)(2,1)S(1)}, bf16[240,128]{1,0:T(8,128)(2,1)S(1)}, bf16[240,128]{1,0:T(8,128)(2,1)S(1)}) custom-call(f32[128,128]{1,0:T(8,128)S(1)} %bitcast.7, f32[384,128]{1,0:T(8,128)S(1)} %bitcast.6, f32[128,128]{1,0:T(8,128)S(1)} %bitcast.8), custom_call_target="tpu_custom_call" | custom-call | tf_op jit(solution)/shard_map/pallas_call | solution.py:498
  3.8 0.5 %collective-permute-start = (bf16[480,128]{1,0:T(8,128)(2,1)S(1)}, bf16[480,128]{1,0:T(8,128)(2,1)S(1)}, u32[]{:S(2)}, u32[]{:S(2)}) collective-permute-start(bf16[480,128]{1,0:T(8,128)(2,1)S(1)} %get-tuple-element.18), channel_id=1, source_target_pairs={{0,8},{8,0},{16,24},{24,16},{1,9},{9,1},{17,25},{25,17},{2,10},{10... | collective-permute-start | bytes 368648 | tf_op jit(solution)/shard_map/ppermute | solution.py:483
  4.3 0.7 %collective-permute-start.1 = (bf16[480,128]{1,0:T(8,128)(2,1)S(1)}, bf16[480,128]{1,0:T(8,128)(2,1)S(1)}, u32[]{:S(2)}, u32[]{:S(2)}) collective-permute-start(bf16[480,128]{1,0:T(8,128)(2,1)S(1)} %get-tuple-element.19), channel_id=1, source_target_pairs={{0,0},{8,16},{16,8},{24,24},{1,1},{9,17},{17,9},{25,25},{2,2},{10,... | collective-permute-start | bytes 368648 | tf_op jit(solution)/shard_map/ppermute | solution.py:483
  5.0 2.7 %collective-permute-start.2 = (bf16[240,128]{1,0:T(8,128)(2,1)S(1)}, bf16[240,128]{1,0:T(8,128)(2,1)S(1)}, u32[]{:S(2)}, u32[]{:S(2)}) collective-permute-start(bf16[240,128]{1,0:T(8,128)(2,1)S(1)} %get-tuple-element.20), channel_id=1, source_target_pairs={{0,2},{2,0},{4,6},{6,4},{1,3},{3,1},{5,7},{7,5},{8,10},{10,8},{12,... | collective-permute-start | bytes 184328 | tf_op jit(solution)/shard_map/ppermute | solution.py:483
  7.6 2.5 %collective-permute-start.3 = (bf16[240,128]{1,0:T(8,128)(2,1)S(1)}, bf16[240,128]{1,0:T(8,128)(2,1)S(1)}, u32[]{:S(2)}, u32[]{:S(2)}) collective-permute-start(bf16[240,128]{1,0:T(8,128)(2,1)S(1)} %get-tuple-element.21), channel_id=1, source_target_pairs={{0,6},{2,4},{4,2},{6,0},{1,7},{3,5},{5,3},{7,1},{8,14},{10,12},{12... | collective-permute-start | bytes 184328 | tf_op jit(solution)/shard_map/ppermute | solution.py:483
  10.1 0.0 collective-permute-done.got1.ax1
  10.1 0.0 collective-permute-done.1.got2.ax2
  10.1 0.1 shard_map.79
  10.2 0.7 %collective-permute-start.4 = (bf16[160,128]{1,0:T(8,128)(2,1)S(1)}, bf16[160,128]{1,0:T(8,128)(2,1)S(1)}, u32[]{:S(2)}, u32[]{:S(2)}) collective-permute-start(bf16[160,128]{1,0:T(8,128)(2,1)S(1)} %get-tuple-element.22), channel_id=1, source_target_pairs={{0,2},{2,0},{4,6},{6,4},{1,3},{3,1},{5,7},{7,5},{8,10},{10,8},{12,... | collective-permute-start | bytes 122888 | tf_op jit(solution)/shard_map/ppermute | solution.py:483
  11.0 0.9 %collective-permute-start.5 = (bf16[160,128]{1,0:T(8,128)(2,1)S(1)}, bf16[160,128]{1,0:T(8,128)(2,1)S(1)}, u32[]{:S(2)}, u32[]{:S(2)}) collective-permute-start(bf16[160,128]{1,0:T(8,128)(2,1)S(1)} %get-tuple-element.23), channel_id=1, source_target_pairs={{0,6},{2,4},{4,2},{6,0},{1,7},{3,5},{5,3},{7,1},{8,14},{10,12},{12... | collective-permute-start | bytes 122888 | tf_op jit(solution)/shard_map/ppermute | solution.py:483
  11.9 0.2 shard_map.78
  12.1 0.0 collective-permute-done.2.az1
  12.1 1.7 %collective-permute-done.3.az2 = bf16[240,128]{1,0:T(8,128)(2,1)S(1)} collective-permute-done((bf16[240,128]{1,0:T(8,128)(2,1)S(1)}, bf16[240,128]{1,0:T(8,128)(2,1)S(1)}, u32[]{:S(2)}, u32[]{:S(2)}) %collective-permute-start.3) | collective-permute-done | bytes 61472 | tf_op jit(solution)/shard_map/ppermute | solution.py:483
  13.8 0.5 collective-permute-done.4.corner1
  14.3 2.5 %collective-permute-done.5.corner2 = bf16[160,128]{1,0:T(8,128)(2,1)S(1)} collective-permute-done((bf16[160,128]{1,0:T(8,128)(2,1)S(1)}, bf16[160,128]{1,0:T(8,128)(2,1)S(1)}, u32[]{:S(2)}, u32[]{:S(2)}) %collective-permute-start.5) | collective-permute-done | bytes 40992 | tf_op jit(solution)/shard_map/ppermute | solution.py:483
  16.8 0.6 %shard_map.80 = (f32[3200,128]{1,0:T(8,128)S(1)}, bf16[48,512]{1,0:T(8,128)(2,1)S(1)}) custom-call(f32[3200,128]{1,0:T(8,128)S(1)} %get-tuple-element.17.block_in, bf16[480,128]{1,0:T(8,128)(2,1)S(1)} %collective-permute-done.got1.ax1, bf16[480,128]{1,0:T(8,128)(2,1)S(1)} %collective-permute-done.1.got2.ax2, ...), custom_call_target="tpu_custom_call", output_to_operand_aliasing={{0}: (0, {})} | custom-call | tf_op jit(solution)/shard_map/pallas_call | solution.py:518
  17.4 1.5 %collective-permute-start.6 = (bf16[48,512]{1,0:T(8,128)(2,1)S(1)}, bf16[48,512]{1,0:T(8,128)(2,1)S(1)}, u32[]{:S(2)}, u32[]{:S(2)}) collective-permute-start(bf16[48,512]{1,0:T(8,128)(2,1)S(1)} %get-tuple-element.26), channel_id=1, source_target_pairs={{0,1},{1,0},{2,3},{3,2},{4,5},{5,4},{6,7},{7,6},{8,9},{9,8},{10,11... | collective-permute-start | bytes 147464 | tf_op jit(solution)/shard_map/ppermute | solution.py:532
  18.9 2.8 %collective-permute-done.6.refs_0_ = bf16[48,512]{1,0:T(8,128)(2,1)S(1)} collective-permute-done((bf16[48,512]{1,0:T(8,128)(2,1)S(1)}, bf16[48,512]{1,0:T(8,128)(2,1)S(1)}, u32[]{:S(2)}, u32[]{:S(2)}) %collective-permute-start.6) | collective-permute-done | bytes 49184 | tf_op jit(solution)/shard_map/ppermute | solution.py:532
  21.7 0.0 copy-done.5
  21.7 5.8 %shard_map.81 = (f32[4,1,128]{2,1,0:T(1,128)S(1)}, f32[5,12,64,128]{3,2,1,0:T(8,128)S(1)}, f32[5,8,32,128]{3,2,1,0:T(8,128)S(1)}) custom-call(f32[5,20,32,128]{3,2,1,0:T(8,128)S(1)} %bitcast.5, bf16[256,256]{1,0:T(8,128)(2,1)S(1)} %get-tuple-element.25.banded, s32[32]{0:T(128)S(1)} %copy-done.5, bf16[48,512]{1,0:T(8,128)(2,1)S(1)} %collective-permute-done.6.refs_0_), custom_call_target="tpu_custom_call" | custom-call | tf_op jit(solution)/shard_map/pallas_call | solution.py:538
  27.5 0.0 copy-start
  27.6 0.0 copy-start.4
  27.6 8.0 %all_to_all.10.rows = f32[4,1,128]{2,1,0:T(1,128)S(1)} all-to-all(f32[4,1,128]{2,1,0:T(1,128)S(1)} %get-tuple-element.29), channel_id=1, replica_groups=mesh['ax'=4,'az'=4,'rad'=2] {'az'}, dimensions={0} | all-to-all | bytes 4096 | tf_op jit(solution)/shard_map/all_to_all | solution.py:549
  35.6 0.6 %shard_map.83 = f32[8,4,128]{2,1,0:T(4,128)} custom-call(f32[4,1,128]{2,1,0:T(1,128)S(1)} %all_to_all.10.rows), custom_call_target="tpu_custom_call" | custom-call | tf_op jit(solution)/shard_map/pallas_call | solution.py:550
  36.2 7.0 %all-to-all-start.1 = ((f32[8,4,128]{2,1,0:T(4,128)}), f32[8,4,128]{2,1,0:T(4,128)S(1)}, u32[]{:S(2)}, u32[]{:S(2)}) async-start(f32[8,4,128]{2,1,0:T(4,128)} %shard_map.83), calls=%async_computation.1 | async-start | bytes 32768 | tf_op jit(solution)/shard_map/all_to_all | solution.py:551
  43.2 2.1 %shard_map.82 = f32[5,8,16,128]{3,2,1,0:T(8,128)} custom-call(f32[5,12,64,128]{3,2,1,0:T(8,128)S(1)} %get-tuple-element.27.u2, f32[5,8,32,128]{3,2,1,0:T(8,128)S(1)} %get-tuple-element.28.u0, bf16[256,256]{1,0:T(8,128)(2,1)S(1)} %get-tuple-element.25.banded), custom_call_target="tpu_custom_call" | custom-call | flops 400000000 | bytes 8000000 | tf_op jit(solution)/shard_map/pallas_call | solution.py:554
  45.3 2.6 %all-to-all-done.1 = f32[8,4,128]{2,1,0:T(4,128)S(1)} async-done(((f32[8,4,128]{2,1,0:T(4,128)}), f32[8,4,128]{2,1,0:T(4,128)S(1)}, u32[]{:S(2)}, u32[]{:S(2)}) %all-to-all-start.1) | async-done | bytes 16416 | tf_op jit(solution)/shard_map/all_to_all | solution.py:551
  47.9 0.0 copy-done
  47.9 0.0 copy-done.4
  47.9 1.2 %shard_map.84 = f32[256,128]{1,0:T(8,128)} custom-call(f32[32,128]{1,0:T(8,128)S(1)} %bitcast.9, s32[1,32]{1,0:T(1,128)S(1)} %copy-done.4, bf16[256,1024]{1,0:T(8,128)(2,1)S(1)} %copy-done), custom_call_target="tpu_custom_call" | custom-call | tf_op jit(solution)/shard_map/pallas_call | solution.py:562
Async XLA Ops:
  0.6 21.1 %copy-start.5 = (s32[32]{0:T(128)S(1)}, s32[32]{0:T(128)}, u32[]{:S(2)}) copy-start(s32[32]{0:T(128)} %cells_far.1) | copy-start | bytes 388
  0.6 0.9 %copy-start.1 = (f32[3,8,16,128]{3,2,1,0:T(8,128)S(1)}, f32[3,8,16,128]{3,2,1,0:T(8,128)}, u32[]{:S(2)}) copy-start(f32[3,8,16,128]{3,2,1,0:T(8,128)} %param.7) | copy-start | bytes 589828
  1.6 0.8 %copy-start.2 = (f32[8,16,128]{2,1,0:T(8,128)S(1)}, f32[8,16,128]{2,1,0:T(8,128)}, u32[]{:S(2)}) copy-start(f32[8,16,128]{2,1,0:T(8,128)} %param.6) | copy-start | bytes 196612
  2.4 0.8 %copy-start.3 = (f32[8,16,128]{2,1,0:T(8,128)S(1)}, f32[8,16,128]{2,1,0:T(8,128)}, u32[]{:S(2)}) copy-start(f32[8,16,128]{2,1,0:T(8,128)} %param.8) | copy-start | bytes 196612
  3.8 6.3 %collective-permute-start = (bf16[480,128]{1,0:T(8,128)(2,1)S(1)}, bf16[480,128]{1,0:T(8,128)(2,1)S(1)}, u32[]{:S(2)}, u32[]{:S(2)}) collective-permute-start(bf16[480,128]{1,0:T(8,128)(2,1)S(1)} %get-tuple-element.18), channel_id=1, source_target_pairs={{0,8},{8,0},{16,24},{24,16},{1,9},{9,1},{17,25},{25,17},{2,10},{10... | collective-permute-start | bytes 368648 | tf_op jit(solution)/shard_map/ppermute | solution.py:483
  4.3 5.8 %collective-permute-start.1 = (bf16[480,128]{1,0:T(8,128)(2,1)S(1)}, bf16[480,128]{1,0:T(8,128)(2,1)S(1)}, u32[]{:S(2)}, u32[]{:S(2)}) collective-permute-start(bf16[480,128]{1,0:T(8,128)(2,1)S(1)} %get-tuple-element.19), channel_id=1, source_target_pairs={{0,0},{8,16},{16,8},{24,24},{1,1},{9,17},{17,9},{25,25},{2,2},{10,... | collective-permute-start | bytes 368648 | tf_op jit(solution)/shard_map/ppermute | solution.py:483
  5.0 7.2 %collective-permute-start.2 = (bf16[240,128]{1,0:T(8,128)(2,1)S(1)}, bf16[240,128]{1,0:T(8,128)(2,1)S(1)}, u32[]{:S(2)}, u32[]{:S(2)}) collective-permute-start(bf16[240,128]{1,0:T(8,128)(2,1)S(1)} %get-tuple-element.20), channel_id=1, source_target_pairs={{0,2},{2,0},{4,6},{6,4},{1,3},{3,1},{5,7},{7,5},{8,10},{10,8},{12,... | collective-permute-start | bytes 184328 | tf_op jit(solution)/shard_map/ppermute | solution.py:483
  7.6 6.2 %collective-permute-start.3 = (bf16[240,128]{1,0:T(8,128)(2,1)S(1)}, bf16[240,128]{1,0:T(8,128)(2,1)S(1)}, u32[]{:S(2)}, u32[]{:S(2)}) collective-permute-start(bf16[240,128]{1,0:T(8,128)(2,1)S(1)} %get-tuple-element.21), channel_id=1, source_target_pairs={{0,6},{2,4},{4,2},{6,0},{1,7},{3,5},{5,3},{7,1},{8,14},{10,12},{12... | collective-permute-start | bytes 184328 | tf_op jit(solution)/shard_map/ppermute | solution.py:483
  10.2 4.1 %collective-permute-start.4 = (bf16[160,128]{1,0:T(8,128)(2,1)S(1)}, bf16[160,128]{1,0:T(8,128)(2,1)S(1)}, u32[]{:S(2)}, u32[]{:S(2)}) collective-permute-start(bf16[160,128]{1,0:T(8,128)(2,1)S(1)} %get-tuple-element.22), channel_id=1, source_target_pairs={{0,2},{2,0},{4,6},{6,4},{1,3},{3,1},{5,7},{7,5},{8,10},{10,8},{12,... | collective-permute-start | bytes 122888 | tf_op jit(solution)/shard_map/ppermute | solution.py:483
  11.0 5.8 %collective-permute-start.5 = (bf16[160,128]{1,0:T(8,128)(2,1)S(1)}, bf16[160,128]{1,0:T(8,128)(2,1)S(1)}, u32[]{:S(2)}, u32[]{:S(2)}) collective-permute-start(bf16[160,128]{1,0:T(8,128)(2,1)S(1)} %get-tuple-element.23), channel_id=1, source_target_pairs={{0,6},{2,4},{4,2},{6,0},{1,7},{3,5},{5,3},{7,1},{8,14},{10,12},{12... | collective-permute-start | bytes 122888 | tf_op jit(solution)/shard_map/ppermute | solution.py:483
  17.4 4.3 %collective-permute-start.6 = (bf16[48,512]{1,0:T(8,128)(2,1)S(1)}, bf16[48,512]{1,0:T(8,128)(2,1)S(1)}, u32[]{:S(2)}, u32[]{:S(2)}) collective-permute-start(bf16[48,512]{1,0:T(8,128)(2,1)S(1)} %get-tuple-element.26), channel_id=1, source_target_pairs={{0,1},{1,0},{2,3},{3,2},{4,5},{5,4},{6,7},{7,6},{8,9},{9,8},{10,11... | collective-permute-start | bytes 147464 | tf_op jit(solution)/shard_map/ppermute | solution.py:532
  27.5 20.4 %copy-start = (bf16[256,1024]{1,0:T(8,128)(2,1)S(1)}, bf16[256,1024]{1,0:T(8,128)(2,1)}, u32[]{:S(2)}) copy-start(bf16[256,1024]{1,0:T(8,128)(2,1)} %weight.1) | copy-start | bytes 1572868
  27.6 20.4 %copy-start.4 = (s32[1,32]{1,0:T(1,128)S(1)}, s32[1,32]{1,0:T(1,128)}, u32[]{:S(2)}) copy-start(s32[1,32]{1,0:T(1,128)} %offsets.1) | copy-start | bytes 388
  36.2 11.7 %all-to-all-start.1 = ((f32[8,4,128]{2,1,0:T(4,128)}), f32[8,4,128]{2,1,0:T(4,128)S(1)}, u32[]{:S(2)}, u32[]{:S(2)}) async-start(f32[8,4,128]{2,1,0:T(4,128)} %shard_map.83), calls=%async_computation.1 | async-start | bytes 32768 | tf_op jit(solution)/shard_map/all_to_all | solution.py:551

commit v5 on v4

--- a/solution.py
+++ b/solution.py
@@ -34,6 +34,10 @@
         cost_estimate=cost,
         input_output_aliases=alias,
     )
+
+
+def far(x):
+    return pltpu.with_memory_space_constraint(x, HBM)
 
 
 def struct(shape, dtype=F32):
@@ -431,21 +435,13 @@
                 state[f, k, pl.ds(l, quarter, stride=4), :] = new[8 * l + first : 8 * l + first + quarter]
 
 
-def repeat_rows(rows, out):
-    out[...] = jnp.broadcast_to(rows[...].reshape(1, rows.shape[0], rows.shape[2]), out.shape)
-
-
-def signals(slots, n_az, n_rad, rows, offsets, weight, out):
+def signals(slots, rows, offsets, weight, out):
     ndev = rows.shape[0]
     group = 32
     cols = group * slots
     lanes = rows.shape[1]
     col = lax.broadcasted_iota(jnp.int32, (1, cols), 1)
-    place = lax.broadcasted_iota(jnp.int32, (group, cols), 0)
-    pair = n_az * n_rad
-    device = place - place % pair + (place % n_az) * n_rad + (place % pair) // n_az
-    owner = device == col // slots
-    holder = place == col // slots
+    owner = lax.broadcasted_iota(jnp.int32, (group, cols), 0) == col // slots
     lane = lax.broadcasted_iota(jnp.int32, (lanes, cols), 0)
     time = lax.broadcasted_iota(jnp.int32, (NB, cols), 0).astype(F32)
     total = jnp.zeros(out.shape, F32)
@@ -453,7 +449,7 @@
         q = rows[g * group : (g + 1) * group, :].astype(BF16)
         off = offsets[0:1, g * group : (g + 1) * group].astype(F32)
         off = jnp.broadcast_to(off, (8, group)).astype(BF16)
-        bins = jnp.dot(off, holder.astype(BF16), preferred_element_type=F32)[0:1]
+        bins = jnp.dot(off, owner.astype(BF16), preferred_element_type=F32)[0:1]
         table = jnp.zeros((NB, cols), F32)
         for s in range(3):
             pick = jnp.where(lane == s * slots + col % slots, 1.0, 0.0).astype(BF16)
@@ -488,7 +484,6 @@
     slots = panel_cell.shape[0]
     ndev = bin_offset.shape[1]
     n_ax, n_rad = lax.axis_size("ax"), lax.axis_size("rad")
-    n_az = lax.axis_size("az")
     planes = ca + 2 * REACH
     part = functools.partial
     given = (density.reshape(ca * cz, cr), velocity.reshape(3 * ca * cz, cr), pressure.reshape(ca * cz, cr))
@@ -500,7 +495,7 @@
         (struct((5 * ca * cz, cr)), edge, edge, strip, strip),
         [HBM] * 3,
         [pltpu.SemaphoreType.DMA((3,))],
-    )(*given)
+    )(*[far(x) for x in given])
     ax1, ax2 = swap(ax1, ax2, "ax", False)
     az1, az2 = swap(az1, az2, "az", True)
     grid = struct((5 * planes * ROWS, cr))
@@ -537,18 +532,16 @@
     grid = (5, planes, 2 * ROWS, cr)
     q, u2, u0 = call(
         part(stages, n_ax, n_rad, ca, cz, slots),
-        (struct((n_az, 1, 128)), struct((5, ca + 4, 2 * ROWS, cr)), struct((5, ca, ROWS, cr))),
+        (struct((1, 1, 128)), struct((5, ca + 4, 2 * ROWS, cr)), struct((5, ca, ROWS, cr))),
         [VMEM, VMEM, HBM] + [VMEM] * len(sides),
         [pltpu.VMEM((5, ca + 2 * MID, ROWS, cr), F32)]
         + [pltpu.VMEM(grid, F32) for _ in range(4)]
         + [pltpu.VMEM((3, planes, ROWS, cr), F32), pltpu.VMEM((128, cr), F32)]
         + [pltpu.SMEM((slots,), jnp.int32), pltpu.SemaphoreType.DMA],
         mib=28,
-    )(block, banded, panel_cell, *sides)
-
-    rows = lax.all_to_all(q, "az", 0, 0, tiled=True)
-    rows = call(repeat_rows, struct((n_ax * n_rad, n_az, 128)), [VMEM], mib=2)(rows)
-    rows = lax.all_to_all(rows, ("ax", "rad"), 0, 0, tiled=True).reshape(ndev, 128)
+    )(block, banded, far(panel_cell), *sides)
+
+    rows = lax.all_gather(q, ("ax", "az", "rad"), axis=0, tiled=True).reshape(ndev, 128)
 
     grid = (5, ca + 4, 2 * ROWS, cr)
     state = call(
@@ -560,7 +553,7 @@
         cost=pl.CostEstimate(flops=400_000_000, bytes_accessed=8_000_000, transcendentals=0),
     )(u2, u0, banded)
     signal = call(
-        part(signals, slots, n_az, n_rad), struct((obs_weight.shape[0], NB)), [VMEM] * 3, mib=24
+        part(signals, slots), struct((obs_weight.shape[0], NB)), [VMEM] * 3, mib=24
     )(rows, bin_offset, obs_weight)
     return (state, signal)
 

time: 49.5 us -> 94.1 us (1.90)
  blocking collectives: 8.02 us -> 64.5 us
  starting transfers between devices: 16.5 us -> 9.47 us
  waiting for transfers between devices: 10.1 us -> 7.47 us
  local copies, waits for them, and re-layouts: 2.62 us -> 0.01 us
    all_gather x0 -> x1, blocking collectives: none -> 64.5 us  [local(): lax.all_gather(q, ('ax', 'az', 'rad'), axis=0, tiled=True)]
    all_to_all x1 -> x0, blocking collectives: 8.02 us -> none  [local(): rows = lax.all_to_all(q, 'az', 0, 0, tiled=True)]
    all_to_all x1 -> x0, starting transfers between devices: 7.01 us -> none  [local(): lax.all_to_all(rows, ('ax', 'rad'), 0, 0, tiled=True).reshape(ndev, 128)]
    all_to_all x1 -> x0, waiting for transfers between devices: 2.64 us -> none  [local(): lax.all_to_all(rows, ('ax', 'rad'), 0, 0, tiled=True).reshape(ndev, 128)]
    unnamed x12 -> x4, local copies, waits for them, and re-layouts: 2.62 us -> 0.01 us
    pallas_call x3 -> x2, Pallas kernels: 7.66 us -> 7.02 us  [the longest x1 5.84 us: local(): call(part(stages, n_ax, n_rad, ca, cz, slots), (struct((1, 1, 128)), stru...]
  transfers between devices with their start and end apart: 8 -> 7, of which waited for: 5 -> 4; matrix products, arithmetic and copies ran while one was open for 0% -> 0% of each run, Pallas kernels for 5% -> 0%
where the time goes in v5:
time: 94.1 us; the launch traced here: 93.4 us
  blocking collectives  64.5 us (69%)
  Pallas kernels  11.2 us (12%)
  starting transfers between devices  9.47 us (10%)
  waiting for transfers between devices  7.47 us (8%)
    all_gather x1, blocking collectives, local(): lax.all_gather(q, ('ax', 'az', 'rad'), axis=0, tiled=True)  64.5 us
    ppermute x6, starting transfers between devices, swap(): return (lax.ppermute(first, axis, one), lax.ppermute(second, axis, two))  7.96 us
    pallas_call x1, Pallas kernels, local(): call(part(stages, n_ax, n_rad, ca, cz, slots), (struct((1, 1, 128)), stru...  5.84 us
    ppermute x6, waiting for transfers between devices, swap(): return (lax.ppermute(first, axis, one), lax.ppermute(second, axis, two))  4.64 us
    ppermute x1, waiting for transfers between devices, local(): sides = (lax.ppermute(got[1], 'rad', [(0, 1), (1, 0)]),)  2.83 us
    pallas_call x1, Pallas kernels, local(): call(part(last_stage, ca, cz), struct((5, ca, cz, cr)), [VMEM] * 3, [pltp...  2.14 us
  transfers between devices with their start and end apart: 7, of which 4 were waited for; matrix products, arithmetic and copies ran while one was open for 0% of the time, Pallas kernels for 0%

profile of v5, /device:TPU:0, one launch (start us, length us, event | category | flops | bytes accessed | tf_op | source)
XLA Modules:
  0.0 93.4 jit_solution(9686750038515208520)
XLA Ops:
  0.6 1.1 %shard_map.77 = (f32[640,128]{1,0:T(8,128)S(1)}, bf16[480,128]{1,0:T(8,128)(2,1)S(1)}, bf16[480,128]{1,0:T(8,128)(2,1)S(1)}, bf16[240,128]{1,0:T(8,128)(2,1)S(1)}, bf16[240,128]{1,0:T(8,128)(2,1)S(1)}) custom-call(f32[128,128]{1,0:T(8,128)} %bitcast.8, f32[384,128]{1,0:T(8,128)} %bitcast.7, f32[128,128]{1,0:T(8,128)} %bitcast.9), custom_call_target="tpu_custom_call" | custom-call | tf_op jit(solution)/shard_map/pallas_call | solution.py:493
  1.7 0.5 collective-permute-start
  2.2 0.7 collective-permute-start.1
  2.9 2.7 %collective-permute-start.2 = (bf16[240,128]{1,0:T(8,128)(2,1)S(1)}, bf16[240,128]{1,0:T(8,128)(2,1)S(1)}, u32[]{:S(2)}, u32[]{:S(2)}) collective-permute-start(bf16[240,128]{1,0:T(8,128)(2,1)S(1)} %get-tuple-element.20), channel_id=1, source_target_pairs={{0,2},{2,0},{4,6},{6,4},{1,3},{3,1},{5,7},{7,5},{8,10},{10,8},{12,... | collective-permute-start | bytes 184328 | tf_op jit(solution)/shard_map/ppermute | solution.py:479
  5.6 2.5 %collective-permute-start.3 = (bf16[240,128]{1,0:T(8,128)(2,1)S(1)}, bf16[240,128]{1,0:T(8,128)(2,1)S(1)}, u32[]{:S(2)}, u32[]{:S(2)}) collective-permute-start(bf16[240,128]{1,0:T(8,128)(2,1)S(1)} %get-tuple-element.21), channel_id=1, source_target_pairs={{0,6},{2,4},{4,2},{6,0},{1,7},{3,5},{5,3},{7,1},{8,14},{10,12},{12... | collective-permute-start | bytes 184328 | tf_op jit(solution)/shard_map/ppermute | solution.py:479
  8.1 0.0 collective-permute-done.got1.ax1
  8.1 0.0 collective-permute-done.1.got2.ax2
  8.1 0.1 shard_map.79
  8.2 0.7 collective-permute-start.4
  8.9 0.9 collective-permute-start.5
  9.8 0.2 shard_map.78
  10.1 0.0 collective-permute-done.2.az1
  10.1 1.7 %collective-permute-done.3.az2 = bf16[240,128]{1,0:T(8,128)(2,1)S(1)} collective-permute-done((bf16[240,128]{1,0:T(8,128)(2,1)S(1)}, bf16[240,128]{1,0:T(8,128)(2,1)S(1)}, u32[]{:S(2)}, u32[]{:S(2)}) %collective-permute-start.3) | collective-permute-done | bytes 61472 | tf_op jit(solution)/shard_map/ppermute | solution.py:479
  11.8 0.5 collective-permute-done.4.corner1
  12.2 2.5 %collective-permute-done.5.corner2 = bf16[160,128]{1,0:T(8,128)(2,1)S(1)} collective-permute-done((bf16[160,128]{1,0:T(8,128)(2,1)S(1)}, bf16[160,128]{1,0:T(8,128)(2,1)S(1)}, u32[]{:S(2)}, u32[]{:S(2)}) %collective-permute-start.5) | collective-permute-done | bytes 40992 | tf_op jit(solution)/shard_map/ppermute | solution.py:479
  14.7 0.6 shard_map.80
  15.3 1.5 %collective-permute-start.6 = (bf16[48,512]{1,0:T(8,128)(2,1)S(1)}, bf16[48,512]{1,0:T(8,128)(2,1)S(1)}, u32[]{:S(2)}, u32[]{:S(2)}) collective-permute-start(bf16[48,512]{1,0:T(8,128)(2,1)S(1)} %get-tuple-element.26), channel_id=1, source_target_pairs={{0,1},{1,0},{2,3},{3,2},{4,5},{5,4},{6,7},{7,6},{8,9},{9,8},{10,11... | collective-permute-start | bytes 147464 | tf_op jit(solution)/shard_map/ppermute | solution.py:527
  16.8 2.8 %collective-permute-done.6.refs_0_ = bf16[48,512]{1,0:T(8,128)(2,1)S(1)} collective-permute-done((bf16[48,512]{1,0:T(8,128)(2,1)S(1)}, bf16[48,512]{1,0:T(8,128)(2,1)S(1)}, u32[]{:S(2)}, u32[]{:S(2)}) %collective-permute-start.6) | collective-permute-done | bytes 49184 | tf_op jit(solution)/shard_map/ppermute | solution.py:527
  19.6 5.8 %shard_map.81 = (f32[1,1,128]{2,1,0:T(1,128)S(1)}, f32[5,12,64,128]{3,2,1,0:T(8,128)S(1)}, f32[5,8,32,128]{3,2,1,0:T(8,128)S(1)}) custom-call(f32[5,20,32,128]{3,2,1,0:T(8,128)S(1)} %bitcast.5, bf16[256,256]{1,0:T(8,128)(2,1)S(1)} %get-tuple-element.25.banded, s32[32]{0:T(128)} %cells_far.1, bf16[48,512]{1,0:T(8,128)(2,1)S(1)} %collective-permute-done.6.refs_0_), custom_call_target="tpu_custom_call" | custom-call | tf_op jit(solution)/shard_map/pallas_call | solution.py:533
  25.5 0.0 copy-start
  25.5 0.0 copy-start.1
  25.5 64.5 %all_gather.3 = f32[32,1,128]{2,1,0:T(1,128)S(1)} all-gather(f32[1,1,128]{2,1,0:T(1,128)S(1)} %get-tuple-element.29), channel_id=1, replica_groups=mesh['ax'=4,'az'=4,'rad'=2] {'ax','az','rad'}, dimensions={0}, use_global_device_ids=true | all-gather | bytes 16896 | tf_op jit(solution)/shard_map/all_gather | solution.py:544
  90.0 2.1 %shard_map.82 = f32[5,8,16,128]{3,2,1,0:T(8,128)} custom-call(f32[5,12,64,128]{3,2,1,0:T(8,128)S(1)} %get-tuple-element.27.u2, f32[5,8,32,128]{3,2,1,0:T(8,128)S(1)} %get-tuple-element.28.u0, bf16[256,256]{1,0:T(8,128)(2,1)S(1)} %get-tuple-element.25.banded), custom_call_target="tpu_custom_call" | custom-call | flops 400000000 | bytes 8000000 | tf_op jit(solution)/shard_map/pallas_call | solution.py:547
  92.2 0.0 copy-done
  92.2 0.0 copy-done.1
  92.2 1.2 %shard_map.83 = f32[256,128]{1,0:T(8,128)} custom-call(f32[32,128]{1,0:T(8,128)S(1)} %bitcast.6, s32[1,32]{1,0:T(1,128)S(1)} %copy-done.1, bf16[256,1024]{1,0:T(8,128)(2,1)S(1)} %copy-done), custom_call_target="tpu_custom_call" | custom-call | tf_op jit(solution)/shard_map/pallas_call | solution.py:555
Async XLA Ops:
  1.7 6.3 %collective-permute-start = (bf16[480,128]{1,0:T(8,128)(2,1)S(1)}, bf16[480,128]{1,0:T(8,128)(2,1)S(1)}, u32[]{:S(2)}, u32[]{:S(2)}) collective-permute-start(bf16[480,128]{1,0:T(8,128)(2,1)S(1)} %get-tuple-element.18), channel_id=1, source_target_pairs={{0,8},{8,0},{16,24},{24,16},{1,9},{9,1},{17,25},{25,17},{2,10},{10... | collective-permute-start | bytes 368648 | tf_op jit(solution)/shard_map/ppermute | solution.py:479
  2.2 5.8 %collective-permute-start.1 = (bf16[480,128]{1,0:T(8,128)(2,1)S(1)}, bf16[480,128]{1,0:T(8,128)(2,1)S(1)}, u32[]{:S(2)}, u32[]{:S(2)}) collective-permute-start(bf16[480,128]{1,0:T(8,128)(2,1)S(1)} %get-tuple-element.19), channel_id=1, source_target_pairs={{0,0},{8,16},{16,8},{24,24},{1,1},{9,17},{17,9},{25,25},{2,2},{10,... | collective-permute-start | bytes 368648 | tf_op jit(solution)/shard_map/ppermute | solution.py:479
  2.9 7.2 %collective-permute-start.2 = (bf16[240,128]{1,0:T(8,128)(2,1)S(1)}, bf16[240,128]{1,0:T(8,128)(2,1)S(1)}, u32[]{:S(2)}, u32[]{:S(2)}) collective-permute-start(bf16[240,128]{1,0:T(8,128)(2,1)S(1)} %get-tuple-element.20), channel_id=1, source_target_pairs={{0,2},{2,0},{4,6},{6,4},{1,3},{3,1},{5,7},{7,5},{8,10},{10,8},{12,... | collective-permute-start | bytes 184328 | tf_op jit(solution)/shard_map/ppermute | solution.py:479
  5.6 6.2 %collective-permute-start.3 = (bf16[240,128]{1,0:T(8,128)(2,1)S(1)}, bf16[240,128]{1,0:T(8,128)(2,1)S(1)}, u32[]{:S(2)}, u32[]{:S(2)}) collective-permute-start(bf16[240,128]{1,0:T(8,128)(2,1)S(1)} %get-tuple-element.21), channel_id=1, source_target_pairs={{0,6},{2,4},{4,2},{6,0},{1,7},{3,5},{5,3},{7,1},{8,14},{10,12},{12... | collective-permute-start | bytes 184328 | tf_op jit(solution)/shard_map/ppermute | solution.py:479
  8.2 4.1 %collective-permute-start.4 = (bf16[160,128]{1,0:T(8,128)(2,1)S(1)}, bf16[160,128]{1,0:T(8,128)(2,1)S(1)}, u32[]{:S(2)}, u32[]{:S(2)}) collective-permute-start(bf16[160,128]{1,0:T(8,128)(2,1)S(1)} %get-tuple-element.22), channel_id=1, source_target_pairs={{0,2},{2,0},{4,6},{6,4},{1,3},{3,1},{5,7},{7,5},{8,10},{10,8},{12,... | collective-permute-start | bytes 122888 | tf_op jit(solution)/shard_map/ppermute | solution.py:479
  8.9 5.8 %collective-permute-start.5 = (bf16[160,128]{1,0:T(8,128)(2,1)S(1)}, bf16[160,128]{1,0:T(8,128)(2,1)S(1)}, u32[]{:S(2)}, u32[]{:S(2)}) collective-permute-start(bf16[160,128]{1,0:T(8,128)(2,1)S(1)} %get-tuple-element.23), channel_id=1, source_target_pairs={{0,6},{2,4},{4,2},{6,0},{1,7},{3,5},{5,3},{7,1},{8,14},{10,12},{12... | collective-permute-start | bytes 122888 | tf_op jit(solution)/shard_map/ppermute | solution.py:479
  15.3 4.3 %collective-permute-start.6 = (bf16[48,512]{1,0:T(8,128)(2,1)S(1)}, bf16[48,512]{1,0:T(8,128)(2,1)S(1)}, u32[]{:S(2)}, u32[]{:S(2)}) collective-permute-start(bf16[48,512]{1,0:T(8,128)(2,1)S(1)} %get-tuple-element.26), channel_id=1, source_target_pairs={{0,1},{1,0},{2,3},{3,2},{4,5},{5,4},{6,7},{7,6},{8,9},{9,8},{10,11... | collective-permute-start | bytes 147464 | tf_op jit(solution)/shard_map/ppermute | solution.py:527
  25.5 66.7 %copy-start = (bf16[256,1024]{1,0:T(8,128)(2,1)S(1)}, bf16[256,1024]{1,0:T(8,128)(2,1)}, u32[]{:S(2)}) copy-start(bf16[256,1024]{1,0:T(8,128)(2,1)} %weight.1) | copy-start | bytes 1572868
  25.5 66.7 %copy-start.1 = (s32[1,32]{1,0:T(1,128)S(1)}, s32[1,32]{1,0:T(1,128)}, u32[]{:S(2)}) copy-start(s32[1,32]{1,0:T(1,128)} %offsets.1) | copy-start | bytes 388

commit v6 on v5

--- a/solution.py
+++ b/solution.py
@@ -532,7 +532,7 @@
     grid = (5, planes, 2 * ROWS, cr)
     q, u2, u0 = call(
         part(stages, n_ax, n_rad, ca, cz, slots),
-        (struct((1, 1, 128)), struct((5, ca + 4, 2 * ROWS, cr)), struct((5, ca, ROWS, cr))),
+        (struct((ndev, 1, 128)), struct((5, ca + 4, 2 * ROWS, cr)), struct((5, ca, ROWS, cr))),
         [VMEM, VMEM, HBM] + [VMEM] * len(sides),
         [pltpu.VMEM((5, ca + 2 * MID, ROWS, cr), F32)]
         + [pltpu.VMEM(grid, F32) for _ in range(4)]
@@ -541,7 +541,7 @@
         mib=28,
     )(block, banded, far(panel_cell), *sides)
 
-    rows = lax.all_gather(q, ("ax", "az", "rad"), axis=0, tiled=True).reshape(ndev, 128)
+    rows = lax.all_to_all(q, ("ax", "az", "rad"), 0, 0, tiled=True).reshape(ndev, 128)
 
     grid = (5, ca + 4, 2 * ROWS, cr)
     state = call(

time: 94.1 us -> 41.3 us (0.44)
  blocking collectives: 64.5 us -> 0 us
  starting transfers between devices: 9.47 us -> 16.3 us
  waiting for transfers between devices: 7.47 us -> 12.4 us
    all_gather x1 -> x0, blocking collectives: 64.5 us -> none  [local(): lax.all_gather(q, ('ax', 'az', 'rad'), axis=0, tiled=True)]
    all_to_all x0 -> x1, starting transfers between devices: none -> 6.79 us  [local(): lax.all_to_all(q, ('ax', 'az', 'rad'), 0, 0, tiled=True).reshape(ndev, 128)]
    all_to_all x0 -> x1, waiting for transfers between devices: none -> 4.96 us  [local(): lax.all_to_all(q, ('ax', 'az', 'rad'), 0, 0, tiled=True).reshape(ndev, 128)]
  transfers between devices with their start and end apart: 7 -> 8, of which waited for: 4 -> 5; matrix products, arithmetic and copies ran while one was open for 0% -> 0% of each run, Pallas kernels for 0% -> 6%
where the time goes in v6:
time: 41.3 us; the launch traced here: 41.2 us
  starting transfers between devices  16.3 us (39%)
  waiting for transfers between devices  12.4 us (30%)
  Pallas kernels  11.7 us (28%)
  between operations  0.7 us (2%)
    ppermute x6, starting transfers between devices, swap(): return (lax.ppermute(first, axis, one), lax.ppermute(second, axis, two))  7.96 us
    all_to_all x1, starting transfers between devices, local(): lax.all_to_all(q, ('ax', 'az', 'rad'), 0, 0, tiled=True).reshape(ndev, 128)  6.79 us
    pallas_call x1, Pallas kernels, local(): call(part(stages, n_ax, n_rad, ca, cz, slots), (struct((ndev, 1, 128)), s...  6.49 us
    all_to_all x1, waiting for transfers between devices, local(): lax.all_to_all(q, ('ax', 'az', 'rad'), 0, 0, tiled=True).reshape(ndev, 128)  4.96 us
    ppermute x6, waiting for transfers between devices, swap(): return (lax.ppermute(first, axis, one), lax.ppermute(second, axis, two))  4.64 us
    ppermute x1, waiting for transfers between devices, local(): sides = (lax.ppermute(got[1], 'rad', [(0, 1), (1, 0)]),)  2.83 us
    pallas_call x1, Pallas kernels, local(): call(part(last_stage, ca, cz), struct((5, ca, cz, cr)), [VMEM] * 3, [pltp...  2.08 us
    ppermute x1, starting transfers between devices, local(): sides = (lax.ppermute(got[1], 'rad', [(0, 1), (1, 0)]),)  1.51 us
  transfers between devices with their start and end apart: 8, of which 5 were waited for; matrix products, arithmetic and copies ran while one was open for 0% of the time, Pallas kernels for 6%

profile of v6, /device:TPU:0, one launch (start us, length us, event | category | flops | bytes accessed | tf_op | source)
XLA Modules:
  0.0 41.2 jit_solution(12481056398348157317)
XLA Ops:
  0.6 1.1 %shard_map.77 = (f32[640,128]{1,0:T(8,128)S(1)}, bf16[480,128]{1,0:T(8,128)(2,1)S(1)}, bf16[480,128]{1,0:T(8,128)(2,1)S(1)}, bf16[240,128]{1,0:T(8,128)(2,1)S(1)}, bf16[240,128]{1,0:T(8,128)(2,1)S(1)}) custom-call(f32[128,128]{1,0:T(8,128)} %bitcast.8, f32[384,128]{1,0:T(8,128)} %bitcast.7, f32[128,128]{1,0:T(8,128)} %bitcast.9), custom_call_target="tpu_custom_call" | custom-call | tf_op jit(solution)/shard_map/pallas_call | solution.py:493
  1.7 0.5 %collective-permute-start = (bf16[480,128]{1,0:T(8,128)(2,1)S(1)}, bf16[480,128]{1,0:T(8,128)(2,1)S(1)}, u32[]{:S(2)}, u32[]{:S(2)}) collective-permute-start(bf16[480,128]{1,0:T(8,128)(2,1)S(1)} %get-tuple-element.18), channel_id=1, source_target_pairs={{0,8},{8,0},{16,24},{24,16},{1,9},{9,1},{17,25},{25,17},{2,10},{10... | collective-permute-start | bytes 368648 | tf_op jit(solution)/shard_map/ppermute | solution.py:479
  2.2 0.7 %collective-permute-start.1 = (bf16[480,128]{1,0:T(8,128)(2,1)S(1)}, bf16[480,128]{1,0:T(8,128)(2,1)S(1)}, u32[]{:S(2)}, u32[]{:S(2)}) collective-permute-start(bf16[480,128]{1,0:T(8,128)(2,1)S(1)} %get-tuple-element.19), channel_id=1, source_target_pairs={{0,0},{8,16},{16,8},{24,24},{1,1},{9,17},{17,9},{25,25},{2,2},{10,... | collective-permute-start | bytes 368648 | tf_op jit(solution)/shard_map/ppermute | solution.py:479
  2.9 2.7 %collective-permute-start.2 = (bf16[240,128]{1,0:T(8,128)(2,1)S(1)}, bf16[240,128]{1,0:T(8,128)(2,1)S(1)}, u32[]{:S(2)}, u32[]{:S(2)}) collective-permute-start(bf16[240,128]{1,0:T(8,128)(2,1)S(1)} %get-tuple-element.20), channel_id=1, source_target_pairs={{0,2},{2,0},{4,6},{6,4},{1,3},{3,1},{5,7},{7,5},{8,10},{10,8},{12,... | collective-permute-start | bytes 184328 | tf_op jit(solution)/shard_map/ppermute | solution.py:479
  5.6 2.5 %collective-permute-start.3 = (bf16[240,128]{1,0:T(8,128)(2,1)S(1)}, bf16[240,128]{1,0:T(8,128)(2,1)S(1)}, u32[]{:S(2)}, u32[]{:S(2)}) collective-permute-start(bf16[240,128]{1,0:T(8,128)(2,1)S(1)} %get-tuple-element.21), channel_id=1, source_target_pairs={{0,6},{2,4},{4,2},{6,0},{1,7},{3,5},{5,3},{7,1},{8,14},{10,12},{12... | collective-permute-start | bytes 184328 | tf_op jit(solution)/shard_map/ppermute | solution.py:479
  8.1 0.0 collective-permute-done.got1.ax1
  8.1 0.0 collective-permute-done.1.got2.ax2
  8.1 0.1 shard_map.79
  8.2 0.7 %collective-permute-start.4 = (bf16[160,128]{1,0:T(8,128)(2,1)S(1)}, bf16[160,128]{1,0:T(8,128)(2,1)S(1)}, u32[]{:S(2)}, u32[]{:S(2)}) collective-permute-start(bf16[160,128]{1,0:T(8,128)(2,1)S(1)} %get-tuple-element.22), channel_id=1, source_target_pairs={{0,2},{2,0},{4,6},{6,4},{1,3},{3,1},{5,7},{7,5},{8,10},{10,8},{12,... | collective-permute-start | bytes 122888 | tf_op jit(solution)/shard_map/ppermute | solution.py:479
  8.9 0.9 %collective-permute-start.5 = (bf16[160,128]{1,0:T(8,128)(2,1)S(1)}, bf16[160,128]{1,0:T(8,128)(2,1)S(1)}, u32[]{:S(2)}, u32[]{:S(2)}) collective-permute-start(bf16[160,128]{1,0:T(8,128)(2,1)S(1)} %get-tuple-element.23), channel_id=1, source_target_pairs={{0,6},{2,4},{4,2},{6,0},{1,7},{3,5},{5,3},{7,1},{8,14},{10,12},{12... | collective-permute-start | bytes 122888 | tf_op jit(solution)/shard_map/ppermute | solution.py:479
  9.8 0.2 shard_map.78
  10.1 0.0 collective-permute-done.2.az1
  10.1 1.7 %collective-permute-done.3.az2 = bf16[240,128]{1,0:T(8,128)(2,1)S(1)} collective-permute-done((bf16[240,128]{1,0:T(8,128)(2,1)S(1)}, bf16[240,128]{1,0:T(8,128)(2,1)S(1)}, u32[]{:S(2)}, u32[]{:S(2)}) %collective-permute-start.3) | collective-permute-done | bytes 61472 | tf_op jit(solution)/shard_map/ppermute | solution.py:479
  11.8 0.5 %collective-permute-done.4.corner1 = bf16[160,128]{1,0:T(8,128)(2,1)S(1)} collective-permute-done((bf16[160,128]{1,0:T(8,128)(2,1)S(1)}, bf16[160,128]{1,0:T(8,128)(2,1)S(1)}, u32[]{:S(2)}, u32[]{:S(2)}) %collective-permute-start.4) | collective-permute-done | bytes 40992 | tf_op jit(solution)/shard_map/ppermute | solution.py:479
  12.2 2.5 %collective-permute-done.5.corner2 = bf16[160,128]{1,0:T(8,128)(2,1)S(1)} collective-permute-done((bf16[160,128]{1,0:T(8,128)(2,1)S(1)}, bf16[160,128]{1,0:T(8,128)(2,1)S(1)}, u32[]{:S(2)}, u32[]{:S(2)}) %collective-permute-start.5) | collective-permute-done | bytes 40992 | tf_op jit(solution)/shard_map/ppermute | solution.py:479
  14.7 0.6 %shard_map.80 = (f32[3200,128]{1,0:T(8,128)S(1)}, bf16[48,512]{1,0:T(8,128)(2,1)S(1)}) custom-call(f32[3200,128]{1,0:T(8,128)S(1)} %get-tuple-element.17.block_in, bf16[480,128]{1,0:T(8,128)(2,1)S(1)} %collective-permute-done.got1.ax1, bf16[480,128]{1,0:T(8,128)(2,1)S(1)} %collective-permute-done.1.got2.ax2, ...), custom_call_target="tpu_custom_call", output_to_operand_aliasing={{0}: (0, {})} | custom-call | tf_op jit(solution)/shard_map/pallas_call | solution.py:513
  15.3 1.5 %collective-permute-start.6 = (bf16[48,512]{1,0:T(8,128)(2,1)S(1)}, bf16[48,512]{1,0:T(8,128)(2,1)S(1)}, u32[]{:S(2)}, u32[]{:S(2)}) collective-permute-start(bf16[48,512]{1,0:T(8,128)(2,1)S(1)} %get-tuple-element.26), channel_id=1, source_target_pairs={{0,1},{1,0},{2,3},{3,2},{4,5},{5,4},{6,7},{7,6},{8,9},{9,8},{10,11... | collective-permute-start | bytes 147464 | tf_op jit(solution)/shard_map/ppermute | solution.py:527
  16.8 2.8 %collective-permute-done.6.refs_0_ = bf16[48,512]{1,0:T(8,128)(2,1)S(1)} collective-permute-done((bf16[48,512]{1,0:T(8,128)(2,1)S(1)}, bf16[48,512]{1,0:T(8,128)(2,1)S(1)}, u32[]{:S(2)}, u32[]{:S(2)}) %collective-permute-start.6) | collective-permute-done | bytes 49184 | tf_op jit(solution)/shard_map/ppermute | solution.py:527
  19.6 6.5 %shard_map.81 = (f32[32,1,128]{2,1,0:T(1,128)}, f32[5,12,64,128]{3,2,1,0:T(8,128)S(1)}, f32[5,8,32,128]{3,2,1,0:T(8,128)S(1)}) custom-call(f32[5,20,32,128]{3,2,1,0:T(8,128)S(1)} %bitcast.5, bf16[256,256]{1,0:T(8,128)(2,1)S(1)} %get-tuple-element.25.banded, s32[32]{0:T(128)} %cells_far.1, bf16[48,512]{1,0:T(8,128)(2,1)S(1)} %collective-permute-done.6.refs_0_), custom_call_target="tpu_custom_call" | custom-call | tf_op jit(solution)/shard_map/pallas_call | solution.py:533
  26.1 0.0 copy-start
  26.1 0.0 copy-start.1
  26.1 6.8 %all-to-all-start = ((f32[32,1,128]{2,1,0:T(1,128)}), f32[32,1,128]{2,1,0:T(1,128)S(1)}, u32[]{:S(2)}, u32[]{:S(2)}) async-start(f32[32,1,128]{2,1,0:T(1,128)} %get-tuple-element.29), calls=%async_computation | async-start | bytes 32768 | tf_op jit(solution)/shard_map/all_to_all | solution.py:544
  32.9 2.1 %shard_map.82 = f32[5,8,16,128]{3,2,1,0:T(8,128)} custom-call(f32[5,12,64,128]{3,2,1,0:T(8,128)S(1)} %get-tuple-element.27.u2, f32[5,8,32,128]{3,2,1,0:T(8,128)S(1)} %get-tuple-element.28.u0, bf16[256,256]{1,0:T(8,128)(2,1)S(1)} %get-tuple-element.25.banded), custom_call_target="tpu_custom_call" | custom-call | flops 400000000 | bytes 8000000 | tf_op jit(solution)/shard_map/pallas_call | solution.py:547
  35.0 5.0 %all-to-all-done = f32[32,1,128]{2,1,0:T(1,128)S(1)} async-done(((f32[32,1,128]{2,1,0:T(1,128)}), f32[32,1,128]{2,1,0:T(1,128)S(1)}, u32[]{:S(2)}, u32[]{:S(2)}) %all-to-all-start) | async-done | bytes 16416 | tf_op jit(solution)/shard_map/all_to_all | solution.py:544
  40.0 0.0 copy-done
  40.0 0.0 copy-done.1
  40.0 1.2 %shard_map.83 = f32[256,128]{1,0:T(8,128)} custom-call(f32[32,128]{1,0:T(8,128)S(1)} %bitcast.6, s32[1,32]{1,0:T(1,128)S(1)} %copy-done.1, bf16[256,1024]{1,0:T(8,128)(2,1)S(1)} %copy-done), custom_call_target="tpu_custom_call" | custom-call | tf_op jit(solution)/shard_map/pallas_call | solution.py:555
Async XLA Ops:
  1.7 6.3 %collective-permute-start = (bf16[480,128]{1,0:T(8,128)(2,1)S(1)}, bf16[480,128]{1,0:T(8,128)(2,1)S(1)}, u32[]{:S(2)}, u32[]{:S(2)}) collective-permute-start(bf16[480,128]{1,0:T(8,128)(2,1)S(1)} %get-tuple-element.18), channel_id=1, source_target_pairs={{0,8},{8,0},{16,24},{24,16},{1,9},{9,1},{17,25},{25,17},{2,10},{10... | collective-permute-start | bytes 368648 | tf_op jit(solution)/shard_map/ppermute | solution.py:479
  2.2 5.8 %collective-permute-start.1 = (bf16[480,128]{1,0:T(8,128)(2,1)S(1)}, bf16[480,128]{1,0:T(8,128)(2,1)S(1)}, u32[]{:S(2)}, u32[]{:S(2)}) collective-permute-start(bf16[480,128]{1,0:T(8,128)(2,1)S(1)} %get-tuple-element.19), channel_id=1, source_target_pairs={{0,0},{8,16},{16,8},{24,24},{1,1},{9,17},{17,9},{25,25},{2,2},{10,... | collective-permute-start | bytes 368648 | tf_op jit(solution)/shard_map/ppermute | solution.py:479
  2.9 7.2 %collective-permute-start.2 = (bf16[240,128]{1,0:T(8,128)(2,1)S(1)}, bf16[240,128]{1,0:T(8,128)(2,1)S(1)}, u32[]{:S(2)}, u32[]{:S(2)}) collective-permute-start(bf16[240,128]{1,0:T(8,128)(2,1)S(1)} %get-tuple-element.20), channel_id=1, source_target_pairs={{0,2},{2,0},{4,6},{6,4},{1,3},{3,1},{5,7},{7,5},{8,10},{10,8},{12,... | collective-permute-start | bytes 184328 | tf_op jit(solution)/shard_map/ppermute | solution.py:479
  5.6 6.2 %collective-permute-start.3 = (bf16[240,128]{1,0:T(8,128)(2,1)S(1)}, bf16[240,128]{1,0:T(8,128)(2,1)S(1)}, u32[]{:S(2)}, u32[]{:S(2)}) collective-permute-start(bf16[240,128]{1,0:T(8,128)(2,1)S(1)} %get-tuple-element.21), channel_id=1, source_target_pairs={{0,6},{2,4},{4,2},{6,0},{1,7},{3,5},{5,3},{7,1},{8,14},{10,12},{12... | collective-permute-start | bytes 184328 | tf_op jit(solution)/shard_map/ppermute | solution.py:479
  8.2 4.1 %collective-permute-start.4 = (bf16[160,128]{1,0:T(8,128)(2,1)S(1)}, bf16[160,128]{1,0:T(8,128)(2,1)S(1)}, u32[]{:S(2)}, u32[]{:S(2)}) collective-permute-start(bf16[160,128]{1,0:T(8,128)(2,1)S(1)} %get-tuple-element.22), channel_id=1, source_target_pairs={{0,2},{2,0},{4,6},{6,4},{1,3},{3,1},{5,7},{7,5},{8,10},{10,8},{12,... | collective-permute-start | bytes 122888 | tf_op jit(solution)/shard_map/ppermute | solution.py:479
  8.9 5.8 %collective-permute-start.5 = (bf16[160,128]{1,0:T(8,128)(2,1)S(1)}, bf16[160,128]{1,0:T(8,128)(2,1)S(1)}, u32[]{:S(2)}, u32[]{:S(2)}) collective-permute-start(bf16[160,128]{1,0:T(8,128)(2,1)S(1)} %get-tuple-element.23), channel_id=1, source_target_pairs={{0,6},{2,4},{4,2},{6,0},{1,7},{3,5},{5,3},{7,1},{8,14},{10,12},{12... | collective-permute-start | bytes 122888 | tf_op jit(solution)/shard_map/ppermute | solution.py:479
  15.3 4.3 %collective-permute-start.6 = (bf16[48,512]{1,0:T(8,128)(2,1)S(1)}, bf16[48,512]{1,0:T(8,128)(2,1)S(1)}, u32[]{:S(2)}, u32[]{:S(2)}) collective-permute-start(bf16[48,512]{1,0:T(8,128)(2,1)S(1)} %get-tuple-element.26), channel_id=1, source_target_pairs={{0,1},{1,0},{2,3},{3,2},{4,5},{5,4},{6,7},{7,6},{8,9},{9,8},{10,11... | collective-permute-start | bytes 147464 | tf_op jit(solution)/shard_map/ppermute | solution.py:527
  26.1 13.9 %copy-start = (bf16[256,1024]{1,0:T(8,128)(2,1)S(1)}, bf16[256,1024]{1,0:T(8,128)(2,1)}, u32[]{:S(2)}) copy-start(bf16[256,1024]{1,0:T(8,128)(2,1)} %weight.1) | copy-start | bytes 1572868
  26.1 13.9 %copy-start.1 = (s32[1,32]{1,0:T(1,128)S(1)}, s32[1,32]{1,0:T(1,128)}, u32[]{:S(2)}) copy-start(s32[1,32]{1,0:T(1,128)} %offsets.1) | copy-start | bytes 388
  26.1 13.8 %all-to-all-start = ((f32[32,1,128]{2,1,0:T(1,128)}), f32[32,1,128]{2,1,0:T(1,128)S(1)}, u32[]{:S(2)}, u32[]{:S(2)}) async-start(f32[32,1,128]{2,1,0:T(1,128)} %get-tuple-element.29), calls=%async_computation | async-start | bytes 32768 | tf_op jit(solution)/shard_map/all_to_all | solution.py:544

commit v7 on v6

--- a/solution.py
+++ b/solution.py
@@ -16,6 +16,9 @@
 SCALE = -LAMBDA / 12.0
 ROWS = 32
 OFF = 8
+SPAN = 32
+TALL = ROWS + 8
+SLOT = 8
 HBM = pltpu.MemorySpace.HBM
 VMEM = pltpu.MemorySpace.VMEM
 SMEM = pltpu.MemorySpace.SMEM
@@ -117,21 +120,40 @@
         block[pl.ds(row, quarter), :] = ref[pl.ds(at + l, quarter, stride=4), :]
 
 
-def prepare(ca, cz, home, block, banded):
+def prepare(ends, ca, cz, n_rad, home, block, banded, *tables):
+    cr = home.shape[1]
+    rad = lax.axis_index("rad")
     for f in range(5):
         for k in range(ca):
             spread_rows(ca + 2 * REACH, cz, f, REACH + k, home, (f * ca + k) * cz, block)
-    banded[...] = band(2 * home.shape[1])
-
-
-def one_hot_lanes(start, height, lanes, row0=0):
-    row = lax.broadcasted_iota(jnp.int32, (height, lanes), 0) - row0
-    lane = lax.broadcasted_iota(jnp.int32, (height, lanes), 1)
-    return jnp.where((row >= 0) & (row < REACH) & (lane == row + start), 1.0, 0.0).astype(BF16)
-
-
-def assemble(n_ax, ends, ca, cz, block_in, ax1, ax2, az1, az2, corner1, corner2, block, *rest):
-    outs, (sides, strips, corners) = rest[: len(ends)], rest[len(ends) :]
+    banded[...] = band(cr)
+    edges, places = tables[: len(ends)], tables[len(ends) :]
+    tiles = cr // SLOT
+    there = {"high": jnp.where(rad < n_rad - 1, 1.0, 0.0), "low": jnp.where(rad > 0, 1.0, 0.0)}
+    high = place_matrix(0, tiles, cr) * there["high"]
+    low = place_matrix(SPAN - REACH, tiles, cr) * there["low"]
+    for end, edge, place in zip(ends, edges, places):
+        start = {"low": 0, "high": cr - REACH, "either": jnp.where(rad == 0, cr - REACH, 0)}[end]
+        edge[...] = edge_matrix(start, tiles, cr)
+        place[...] = {"low": high, "high": low, "either": high + low}[end].astype(BF16)
+
+
+def edge_matrix(start, tiles, cr):
+    k = lax.broadcasted_iota(jnp.int32, (tiles * cr, tiles * SLOT), 0)
+    n = lax.broadcasted_iota(jnp.int32, (tiles * cr, tiles * SLOT), 1)
+    hit = (k // cr == n // SLOT) & (n % SLOT < REACH) & (k % cr == n % SLOT + start)
+    return jnp.where(hit, 1.0, 0.0).astype(BF16)
+
+
+def place_matrix(start, tiles, cr):
+    k = lax.broadcasted_iota(jnp.int32, (tiles * SLOT, tiles * cr // 4), 0)
+    n = lax.broadcasted_iota(jnp.int32, (tiles * SLOT, tiles * cr // 4), 1)
+    hit = (k // SLOT == n // SPAN) & (k % SLOT < REACH) & (n % SPAN == k % SLOT + start)
+    return jnp.where(hit, 1.0, 0.0)
+
+
+def assemble(n_ax, count, ca, cz, block_in, ax1, ax2, az1, az2, corner1, corner2, *rest):
+    edges, block, outs, (sides, strips, corners) = rest[:count], rest[count], rest[count + 1 : -3], rest[-3:]
     cr = ax1.shape[1]
     planes = ca + 2 * REACH
     size = REACH * cz
@@ -162,38 +184,48 @@
                     got = corners[side, pl.ds(start + MID, MID), :]
                     block[pl.ds(at + (REACH + ca) * ROWS, MID, stride=ROWS), :] = got
 
-    rad = lax.axis_index("rad")
-    for end, out in zip(ends, outs):
-        start = {"low": 0, "high": cr - REACH, "either": jnp.where(rad == 0, cr - REACH, 0)}[end]
-        hot = one_hot_lanes(start, 8, cr)
-        packed = []
-        for f in range(5):
-            row = (f * planes + REACH - MID) * ROWS
-            cells = block[pl.ds(row, (ca + 2 * MID) * ROWS), :].astype(BF16)
-            packed.append(
-                lax.dot_general(hot, cells, (((1,), (1,)), ((), ())), preferred_element_type=F32)
-            )
-        packed.append(jnp.zeros_like(packed[0]))
-        out[...] = jnp.concatenate(packed, axis=0).astype(BF16)
+    tiles = cr // SLOT
+    step = tiles * 8
+    rows = []
+    for f in range(5):
+        for k in range((ca + 2 * MID) * ROWS // step):
+            at = (f * planes + REACH - MID) * ROWS + k * step
+            rows.append(jnp.concatenate([block[at + 8 * t : at + 8 * t + 8, :] for t in range(tiles)], axis=1))
+    rows = jnp.concatenate(rows, axis=0).astype(BF16)
+    for edge, out in zip(edges, outs):
+        out[...] = jnp.dot(rows, edge[...], preferred_element_type=F32).astype(BF16)
 
 
 def az_terms(flux):
-    out = []
-    for group in (0, 4):
-        v = [flux[8 * (group + l) : 8 * (group + l + 1)] for l in range(4)]
-        v = [pltpu.roll(v[2], 1, 0), pltpu.roll(v[3], 1, 0)] + v + [pltpu.roll(v[0], 7, 0), pltpu.roll(v[1], 7, 0)]
-        for l in range(4):
-            out.append(8.0 * (v[l + 3] - v[l + 1]) - (v[l + 4] - v[l]))
+    v = [flux[8 * l : 8 * l + 8] for l in range(4)]
+    v = [pltpu.roll(v[2], 1, 0), pltpu.roll(v[3], 1, 0)] + v + [pltpu.roll(v[0], 7, 0), pltpu.roll(v[1], 7, 0)]
+    out = [8.0 * (v[l + 3] - v[l + 1]) - (v[l + 4] - v[l]) for l in range(4)]
+    side = flux[ROWS:]
+    lanes = side.shape[1]
+    span = lax.broadcasted_iota(jnp.int32, side.shape, 1) // SPAN
+    up, down = pltpu.roll(side, 7, 0), pltpu.roll(side, 1, 0)
+    up1 = pltpu.roll(jnp.where(span == 0, up, side), lanes - SPAN, 1)
+    up2 = pltpu.roll(jnp.where(span < 2, up, side), lanes - 2 * SPAN, 1)
+    down1 = pltpu.roll(jnp.where(span == 3, down, side), SPAN, 1)
+    down2 = pltpu.roll(jnp.where(span >= 2, down, side), 2 * SPAN, 1)
+    out.append(8.0 * (up1 - down1) - (up2 - down2))
     return jnp.concatenate(out, axis=0)
 
 
-def band(wide):
-    k = lax.broadcasted_iota(jnp.int32, (wide, wide), 0)
-    n = lax.broadcasted_iota(jnp.int32, (wide, wide), 1)
-    gap = (k - n + wide) % wide
-    out = jnp.where(gap == 1, 8.0, 0.0) + jnp.where(gap == wide - 1, -8.0, 0.0)
-    out = out + jnp.where(gap == 2, -1.0, 0.0) + jnp.where(gap == wide - 2, 1.0, 0.0)
-    return out.astype(BF16)
+def band(cr):
+    def place(axis, none):
+        i = lax.broadcasted_iota(jnp.int32, (2 * cr, 2 * cr), axis)
+        j = i % SPAN
+        beyond = jnp.where(j < REACH, cr + j, jnp.where(j >= SPAN - REACH, j - SPAN, none))
+        return jnp.where(i < cr, i, beyond), jnp.where(i < cr, -1, i // SPAN)
+
+    k, k_span = place(0, 4 * cr)
+    n, n_span = place(1, -4 * cr)
+    gap = k - n
+    out = jnp.where(gap == 1, 8.0, 0.0) + jnp.where(gap == -1, -8.0, 0.0)
+    out = out + jnp.where(gap == 2, -1.0, 0.0) + jnp.where(gap == -2, 1.0, 0.0)
+    apart = (k_span >= 0) & (n_span >= 0) & (k_span != n_span)
+    return jnp.where(apart, 0.0, out).astype(BF16)
 
 
 def split_state(u):
@@ -220,13 +252,17 @@
 
 def both_sides(us, js, fax, part, banded):
     rows = []
+    shape = (ROWS, banded.shape[0] // 2)
+    span = lax.broadcasted_iota(jnp.int32, shape, 1) // SPAN
+    mine = span == lax.broadcasted_iota(jnp.int32, shape, 0) // 8
     for u, j in zip(us, js):
         got = flux(0, *u)
         for f in range(5):
             fax[f, j] = got[f]
         got = flux(2, *u)
         for f in range(5):
-            rows.append(jnp.concatenate([got[f][0:ROWS], got[f][ROWS:]], axis=1))
+            side = jnp.where(mine, jnp.concatenate([got[f][ROWS:]] * 4, axis=0), 0.0)
+            rows.append(jnp.concatenate([got[f][0:ROWS], side], axis=1))
     rows = jnp.concatenate(rows, axis=0)
     coarse = rows.astype(BF16)
     fine = (rows - coarse.astype(F32)).astype(BF16)
@@ -238,8 +274,10 @@
         got = flux(1, *u)
         for f in range(5):
             at = (i * 5 + f) * ROWS
-            mine = out[at : at + ROWS]
-            radial = jnp.concatenate([mine[:, 0:half], mine[:, half:]], axis=0)
+            side = out[at : at + 8, half:]
+            for l in range(1, 4):
+                side = jnp.where(span[0:8] == l, out[at + 8 * l : at + 8 * l + 8, half:], side)
+            radial = jnp.concatenate([out[at : at + ROWS, 0:half], side], axis=0)
             part[f, j] = az_terms(got[f]) + radial
 
 
@@ -262,6 +300,7 @@
 
 def stages(n_ax, n_rad, ca, cz, slots, block, banded, cells_far, *refs):
     sides, refs = refs[: len(refs) - 12], refs[len(refs) - 12 :]
+    sides, places = sides[: len(sides) // 2], sides[len(sides) // 2 :]
     q_out, u2_out, u0_out, ghost, first, second, fax, part, value, picked, cells, cells_sem = refs
     fetch = pltpu.make_async_copy(cells_far, cells, cells_sem)
     fetch.start()
@@ -270,35 +309,29 @@
     ax = lax.axis_index("ax")
     rad = lax.axis_index("rad")
 
-    lane = lax.broadcasted_iota(jnp.int32, (ROWS, cr), 1)
-    kept_row = lax.broadcasted_iota(jnp.int32, (ROWS, cr), 0)
-    row = 4 * (kept_row % 8) + kept_row // 8
+    lane = lax.broadcasted_iota(jnp.int32, (8, cr), 1)
+    row = 4 * lax.broadcasted_iota(jnp.int32, (8, cr), 0) + lane // SPAN
+    j = lane % SPAN
     steps_rad = jnp.where(
-        (lane < REACH) & (rad < n_rad - 1),
-        1 + lane // 2,
-        jnp.where((lane >= cr - REACH) & (rad > 0), 1 + (cr - 1 - lane) // 2, 99),
+        (j < REACH) & (rad < n_rad - 1),
+        1 + j // 2,
+        jnp.where((j >= SPAN - REACH) & (rad > 0), 1 + (SPAN - 1 - j) // 2, 99),
     )
     beyond_row = jnp.maximum(OFF - row, row - (OFF + cz - 1))
     steps = steps_rad + jnp.where(beyond_row > 0, (beyond_row + 1) // 2, 0)
     base0 = jnp.where(steps_rad < 99, 0.0, 1.0)
 
-    count = ca + 2 * MID
-    places = ((0, rad < n_rad - 1), (cr - REACH, rad > 0))
-    messages = [x[...] for x in sides]
-    for f in range(5):
-        hots = []
-        for start, there in places:
-            place = one_hot_lanes(start, messages[0].shape[0], cr, row0=8 * f)
-            hots.append(jnp.where(there, place, jnp.zeros_like(place)))
-        if len(messages) == 1:
-            hots = [hots[0] + hots[1]]
-        side = 0.0
-        for got, hot in zip(messages, hots):
-            side = side + lax.dot_general(
-                got, hot, (((0,), (0,)), ((), ())), preferred_element_type=F32
-            )
-        side = side.reshape(count, ROWS, cr)
-        ghost[f] = side + base0[None] if f == 0 else side
+    side = 0.0
+    for got, place in zip(sides, places):
+        side = side + jnp.dot(got[...], place[...], preferred_element_type=F32)
+    group = side.shape[1] // cr
+    count = (ca + 2 * MID) // group
+    for f in range(5):
+        for k in range(count):
+            for i in range(group):
+                at = (f * count + k) * 8
+                tile = side[at : at + 8, i * cr : (i + 1) * cr]
+                ghost[f, k * group + i] = tile + base0 if f == 0 else tile
 
     def start_state(j, both):
         u = []
@@ -333,7 +366,7 @@
         a = (a + 1) // 2
         lim = 2 - stage
         base = jnp.where(f == 0, 1.0, 0.0)
-        size = ROWS if a == lim else 2 * ROWS
+        size = ROWS if a == lim else TALL
         new = change(fa, part, f, j, size)
         u0 = first[f, j, 0:size]
         if stage == 0:
@@ -499,21 +532,26 @@
     ax1, ax2 = swap(ax1, ax2, "ax", False)
     az1, az2 = swap(az1, az2, "az", True)
     grid = struct((5 * planes * ROWS, cr))
-    block, banded = call(
-        part(prepare, ca, cz), (grid, struct((2 * cr, 2 * cr), BF16)), [VMEM], mib=8
+    ends = ("either",) if n_rad == 2 else ("low", "high")
+    tiles = cr // SLOT
+    table = [struct((tiles * cr, cr), BF16)] * len(ends) + [struct((cr, tiles * cr // 4), BF16)] * len(ends)
+    block, banded, *tables = call(
+        part(prepare, ends, ca, cz, n_rad),
+        (grid, struct((2 * cr, 2 * cr), BF16), *table),
+        [VMEM],
     )(home)
+    edges, places = tables[: len(ends)], tables[len(ends) :]
 
     corner = struct((5 * MID * 2 * MID, cr), BF16)
     near = pltpu.VMEM((5, 2 * MID * cz, cr), F32)
     corner1, corner2 = call(part(pack_corners, n_ax, cz), (corner, corner), [VMEM] * 2, [near])(ax1, ax2)
     corner1, corner2 = swap(corner1, corner2, "az", True)
 
-    side = struct((48, (ca + 2 * MID) * ROWS), BF16)
-    ends = ("either",) if n_rad == 2 else ("low", "high")
+    side = struct((5 * (ca + 2 * MID) * ROWS // tiles, cr), BF16)
     got = call(
-        part(assemble, n_ax, ends, ca, cz),
+        part(assemble, n_ax, len(ends), ca, cz),
         (grid,) + tuple(side for _ in ends),
-        [VMEM] * 7,
+        [VMEM] * (7 + len(ends)),
         [
             pltpu.VMEM((5, 2 * REACH * cz, cr), F32),
             pltpu.VMEM((2,) + strip.shape, F32),
@@ -521,7 +559,7 @@
         ],
         mib=12,
         alias={0: 0},
-    )(block, ax1, ax2, az1, az2, corner1, corner2)
+    )(block, ax1, ax2, az1, az2, corner1, corner2, *edges)
     block = got[0].reshape(5, planes, ROWS, cr)
     if n_rad == 2:
         sides = (lax.ppermute(got[1], "rad", [(0, 1), (1, 0)]),)
@@ -529,21 +567,21 @@
         up = [(i, i + 1) for i in range(n_rad - 1)]
         sides = (lax.ppermute(got[1], "rad", [(j, i) for i, j in up]), lax.ppermute(got[2], "rad", up))
 
-    grid = (5, planes, 2 * ROWS, cr)
+    grid = (5, planes, TALL, cr)
     q, u2, u0 = call(
         part(stages, n_ax, n_rad, ca, cz, slots),
-        (struct((ndev, 1, 128)), struct((5, ca + 4, 2 * ROWS, cr)), struct((5, ca, ROWS, cr))),
-        [VMEM, VMEM, HBM] + [VMEM] * len(sides),
-        [pltpu.VMEM((5, ca + 2 * MID, ROWS, cr), F32)]
+        (struct((ndev, 1, 128)), struct((5, ca + 4, TALL, cr)), struct((5, ca, ROWS, cr))),
+        [VMEM, VMEM, HBM] + [VMEM] * (2 * len(sides)),
+        [pltpu.VMEM((5, ca + 2 * MID, 8, cr), F32)]
         + [pltpu.VMEM(grid, F32) for _ in range(4)]
         + [pltpu.VMEM((3, planes, ROWS, cr), F32), pltpu.VMEM((128, cr), F32)]
         + [pltpu.SMEM((slots,), jnp.int32), pltpu.SemaphoreType.DMA],
         mib=28,
-    )(block, banded, far(panel_cell), *sides)
+    )(block, banded, far(panel_cell), *sides, *places)
 
     rows = lax.all_to_all(q, ("ax", "az", "rad"), 0, 0, tiled=True).reshape(ndev, 128)
 
-    grid = (5, ca + 4, 2 * ROWS, cr)
+    grid = (5, ca + 4, TALL, cr)
     state = call(
         part(last_stage, ca, cz),
         struct((5, ca, cz, cr)),

time: 41.3 us -> 40.8 us (0.988)
    pallas_call x1, Pallas kernels: 6.49 us -> 5.9 us  [local(): call(part(stages, n_ax, n_rad, ca, cz, slots), (struct((ndev, 1, 128)), s...]
  transfers between devices with their start and end apart: 8 -> 8, of which waited for: 5 -> 5; matrix products, arithmetic and copies ran while one was open for 0% -> 0% of each run, Pallas kernels for 6% -> 7%
where the time goes in v7:
time: 40.8 us; the launch traced here: 40.6 us
  starting transfers between devices  16.4 us (40%)
  waiting for transfers between devices  12 us (29%)
  Pallas kernels  11.5 us (28%)
  between operations  0.71 us (2%)
    ppermute x6, starting transfers between devices, swap(): return (lax.ppermute(first, axis, one), lax.ppermute(second, axis, two))  7.96 us
    all_to_all x1, starting transfers between devices, local(): lax.all_to_all(q, ('ax', 'az', 'rad'), 0, 0, tiled=True).reshape(ndev, 128)  6.88 us
    pallas_call x1, Pallas kernels, local(): call(part(stages, n_ax, n_rad, ca, cz, slots), (struct((ndev, 1, 128)), s...  5.9 us
    all_to_all x1, waiting for transfers between devices, local(): lax.all_to_all(q, ('ax', 'az', 'rad'), 0, 0, tiled=True).reshape(ndev, 128)  4.96 us
    ppermute x6, waiting for transfers between devices, swap(): return (lax.ppermute(first, axis, one), lax.ppermute(second, axis, two))  4.4 us
    ppermute x1, waiting for transfers between devices, local(): sides = (lax.ppermute(got[1], 'rad', [(0, 1), (1, 0)]),)  2.65 us
    pallas_call x1, Pallas kernels, local(): call(part(last_stage, ca, cz), struct((5, ca, cz, cr)), [VMEM] * 3, [pltp...  2.08 us
    ppermute x1, starting transfers between devices, local(): sides = (lax.ppermute(got[1], 'rad', [(0, 1), (1, 0)]),)  1.56 us
  transfers between devices with their start and end apart: 8, of which 5 were waited for; matrix products, arithmetic and copies ran while one was open for 0% of the time, Pallas kernels for 7%

profile of v7, /device:TPU:0, one launch (start us, length us, event | category | flops | bytes accessed | tf_op | source)
XLA Modules:
  0.0 40.6 jit_solution(9205552502986355525)
XLA Ops:
  0.6 1.1 %shard_map.77 = (f32[640,128]{1,0:T(8,128)S(1)}, bf16[480,128]{1,0:T(8,128)(2,1)S(1)}, bf16[480,128]{1,0:T(8,128)(2,1)S(1)}, bf16[240,128]{1,0:T(8,128)(2,1)S(1)}, bf16[240,128]{1,0:T(8,128)(2,1)S(1)}) custom-call(f32[128,128]{1,0:T(8,128)} %bitcast.8, f32[384,128]{1,0:T(8,128)} %bitcast.7, f32[128,128]{1,0:T(8,128)} %bitcast.9), custom_call_target="tpu_custom_call" | custom-call | tf_op jit(solution)/shard_map/pallas_call | solution.py:526
  1.7 0.5 %collective-permute-start = (bf16[480,128]{1,0:T(8,128)(2,1)S(1)}, bf16[480,128]{1,0:T(8,128)(2,1)S(1)}, u32[]{:S(2)}, u32[]{:S(2)}) collective-permute-start(bf16[480,128]{1,0:T(8,128)(2,1)S(1)} %get-tuple-element.20), channel_id=1, source_target_pairs={{0,8},{8,0},{16,24},{24,16},{1,9},{9,1},{17,25},{25,17},{2,10},{10... | collective-permute-start | bytes 368648 | tf_op jit(solution)/shard_map/ppermute | solution.py:512
  2.2 0.7 %collective-permute-start.1 = (bf16[480,128]{1,0:T(8,128)(2,1)S(1)}, bf16[480,128]{1,0:T(8,128)(2,1)S(1)}, u32[]{:S(2)}, u32[]{:S(2)}) collective-permute-start(bf16[480,128]{1,0:T(8,128)(2,1)S(1)} %get-tuple-element.21), channel_id=1, source_target_pairs={{0,0},{8,16},{16,8},{24,24},{1,1},{9,17},{17,9},{25,25},{2,2},{10,... | collective-permute-start | bytes 368648 | tf_op jit(solution)/shard_map/ppermute | solution.py:512
  2.9 2.7 %collective-permute-start.2 = (bf16[240,128]{1,0:T(8,128)(2,1)S(1)}, bf16[240,128]{1,0:T(8,128)(2,1)S(1)}, u32[]{:S(2)}, u32[]{:S(2)}) collective-permute-start(bf16[240,128]{1,0:T(8,128)(2,1)S(1)} %get-tuple-element.22), channel_id=1, source_target_pairs={{0,2},{2,0},{4,6},{6,4},{1,3},{3,1},{5,7},{7,5},{8,10},{10,8},{12,... | collective-permute-start | bytes 184328 | tf_op jit(solution)/shard_map/ppermute | solution.py:512
  5.6 2.5 %collective-permute-start.3 = (bf16[240,128]{1,0:T(8,128)(2,1)S(1)}, bf16[240,128]{1,0:T(8,128)(2,1)S(1)}, u32[]{:S(2)}, u32[]{:S(2)}) collective-permute-start(bf16[240,128]{1,0:T(8,128)(2,1)S(1)} %get-tuple-element.23), channel_id=1, source_target_pairs={{0,6},{2,4},{4,2},{6,0},{1,7},{3,5},{5,3},{7,1},{8,14},{10,12},{12... | collective-permute-start | bytes 184328 | tf_op jit(solution)/shard_map/ppermute | solution.py:512
  8.1 0.0 collective-permute-done.got1.ax1
  8.1 0.0 collective-permute-done.1.got2.ax2
  8.1 0.1 shard_map.79
  8.2 0.7 %collective-permute-start.4 = (bf16[160,128]{1,0:T(8,128)(2,1)S(1)}, bf16[160,128]{1,0:T(8,128)(2,1)S(1)}, u32[]{:S(2)}, u32[]{:S(2)}) collective-permute-start(bf16[160,128]{1,0:T(8,128)(2,1)S(1)} %get-tuple-element.24), channel_id=1, source_target_pairs={{0,2},{2,0},{4,6},{6,4},{1,3},{3,1},{5,7},{7,5},{8,10},{10,8},{12,... | collective-permute-start | bytes 122888 | tf_op jit(solution)/shard_map/ppermute | solution.py:512
  8.9 0.9 %collective-permute-start.5 = (bf16[160,128]{1,0:T(8,128)(2,1)S(1)}, bf16[160,128]{1,0:T(8,128)(2,1)S(1)}, u32[]{:S(2)}, u32[]{:S(2)}) collective-permute-start(bf16[160,128]{1,0:T(8,128)(2,1)S(1)} %get-tuple-element.25), channel_id=1, source_target_pairs={{0,6},{2,4},{4,2},{6,0},{1,7},{3,5},{5,3},{7,1},{8,14},{10,12},{12... | collective-permute-start | bytes 122888 | tf_op jit(solution)/shard_map/ppermute | solution.py:512
  9.8 0.5 %shard_map.78 = (f32[3200,128]{1,0:T(8,128)S(1)}, bf16[256,256]{1,0:T(8,128)(2,1)S(1)}, bf16[2048,128]{1,0:T(8,128)(2,1)S(1)}, bf16[128,512]{1,0:T(8,128)(2,1)S(1)}) custom-call(f32[640,128]{1,0:T(8,128)S(1)} %get-tuple-element.18.home), custom_call_target="tpu_custom_call" | custom-call | tf_op jit(solution)/shard_map/pallas_call | solution.py:538
  10.3 0.0 collective-permute-done.2.az1
  10.3 1.5 %collective-permute-done.3.az2 = bf16[240,128]{1,0:T(8,128)(2,1)S(1)} collective-permute-done((bf16[240,128]{1,0:T(8,128)(2,1)S(1)}, bf16[240,128]{1,0:T(8,128)(2,1)S(1)}, u32[]{:S(2)}, u32[]{:S(2)}) %collective-permute-start.3) | collective-permute-done | bytes 61472 | tf_op jit(solution)/shard_map/ppermute | solution.py:512
  11.8 0.5 %collective-permute-done.4.corner1 = bf16[160,128]{1,0:T(8,128)(2,1)S(1)} collective-permute-done((bf16[160,128]{1,0:T(8,128)(2,1)S(1)}, bf16[160,128]{1,0:T(8,128)(2,1)S(1)}, u32[]{:S(2)}, u32[]{:S(2)}) %collective-permute-start.4) | collective-permute-done | bytes 40992 | tf_op jit(solution)/shard_map/ppermute | solution.py:512
  12.2 2.5 %collective-permute-done.5.corner2 = bf16[160,128]{1,0:T(8,128)(2,1)S(1)} collective-permute-done((bf16[160,128]{1,0:T(8,128)(2,1)S(1)}, bf16[160,128]{1,0:T(8,128)(2,1)S(1)}, u32[]{:S(2)}, u32[]{:S(2)}) %collective-permute-start.5) | collective-permute-done | bytes 40992 | tf_op jit(solution)/shard_map/ppermute | solution.py:512
  14.7 0.7 %shard_map.80 = (f32[3200,128]{1,0:T(8,128)S(1)}, bf16[160,128]{1,0:T(8,128)(2,1)S(1)}) custom-call(f32[3200,128]{1,0:T(8,128)S(1)} %get-tuple-element.19.block_in, bf16[480,128]{1,0:T(8,128)(2,1)S(1)} %collective-permute-done.got1.ax1, bf16[480,128]{1,0:T(8,128)(2,1)S(1)} %collective-permute-done.1.got2.ax2, ...), custom_call_target="tpu_custom_call", output_to_operand_aliasing={{0}: (0, {})} | custom-call | tf_op jit(solution)/shard_map/pallas_call | solution.py:551
  15.4 1.6 %collective-permute-start.6 = (bf16[160,128]{1,0:T(8,128)(2,1)S(1)}, bf16[160,128]{1,0:T(8,128)(2,1)S(1)}, u32[]{:S(2)}, u32[]{:S(2)}) collective-permute-start(bf16[160,128]{1,0:T(8,128)(2,1)S(1)} %get-tuple-element.29), channel_id=1, source_target_pairs={{0,1},{1,0},{2,3},{3,2},{4,5},{5,4},{6,7},{7,6},{8,9},{9,8},{10,11... | collective-permute-start | bytes 122888 | tf_op jit(solution)/shard_map/ppermute | solution.py:565
  16.9 2.7 %collective-permute-done.6.refs_0_ = bf16[160,128]{1,0:T(8,128)(2,1)S(1)} collective-permute-done((bf16[160,128]{1,0:T(8,128)(2,1)S(1)}, bf16[160,128]{1,0:T(8,128)(2,1)S(1)}, u32[]{:S(2)}, u32[]{:S(2)}) %collective-permute-start.6) | collective-permute-done | bytes 40992 | tf_op jit(solution)/shard_map/ppermute | solution.py:565
  19.6 5.9 %shard_map.81 = (f32[32,1,128]{2,1,0:T(1,128)}, f32[5,12,40,128]{3,2,1,0:T(8,128)S(1)}, f32[5,8,32,128]{3,2,1,0:T(8,128)S(1)}) custom-call(f32[5,20,32,128]{3,2,1,0:T(8,128)S(1)} %bitcast.5, bf16[256,256]{1,0:T(8,128)(2,1)S(1)} %get-tuple-element.28.banded, s32[32]{0:T(128)} %cells_far.1, bf16[160,128]{1,0:T(8,128)(2,1)S(1)} %collective-permute-done.6.refs_0_, ...), custom_call_target="tpu_custom_call" | custom-call | tf_op jit(solution)/shard_map/pallas_call | solution.py:571
  25.5 0.0 copy-start
  25.5 0.0 copy-start.1
  25.5 6.9 %all-to-all-start = ((f32[32,1,128]{2,1,0:T(1,128)}), f32[32,1,128]{2,1,0:T(1,128)S(1)}, u32[]{:S(2)}, u32[]{:S(2)}) async-start(f32[32,1,128]{2,1,0:T(1,128)} %get-tuple-element.33), calls=%async_computation | async-start | bytes 32768 | tf_op jit(solution)/shard_map/all_to_all | solution.py:582
  32.4 2.1 %shard_map.82 = f32[5,8,16,128]{3,2,1,0:T(8,128)} custom-call(f32[5,12,40,128]{3,2,1,0:T(8,128)S(1)} %get-tuple-element.31.u2, f32[5,8,32,128]{3,2,1,0:T(8,128)S(1)} %get-tuple-element.32.u0, bf16[256,256]{1,0:T(8,128)(2,1)S(1)} %get-tuple-element.28.banded), custom_call_target="tpu_custom_call" | custom-call | flops 400000000 | bytes 8000000 | tf_op jit(solution)/shard_map/pallas_call | solution.py:585
  34.5 5.0 %all-to-all-done = f32[32,1,128]{2,1,0:T(1,128)S(1)} async-done(((f32[32,1,128]{2,1,0:T(1,128)}), f32[32,1,128]{2,1,0:T(1,128)S(1)}, u32[]{:S(2)}, u32[]{:S(2)}) %all-to-all-start) | async-done | bytes 16416 | tf_op jit(solution)/shard_map/all_to_all | solution.py:582
  39.5 0.0 copy-done
  39.5 0.0 copy-done.1
  39.5 1.2 %shard_map.83 = f32[256,128]{1,0:T(8,128)} custom-call(f32[32,128]{1,0:T(8,128)S(1)} %bitcast.6, s32[1,32]{1,0:T(1,128)S(1)} %copy-done.1, bf16[256,1024]{1,0:T(8,128)(2,1)S(1)} %copy-done), custom_call_target="tpu_custom_call" | custom-call | tf_op jit(solution)/shard_map/pallas_call | solution.py:593
Async XLA Ops:
  1.7 6.3 %collective-permute-start = (bf16[480,128]{1,0:T(8,128)(2,1)S(1)}, bf16[480,128]{1,0:T(8,128)(2,1)S(1)}, u32[]{:S(2)}, u32[]{:S(2)}) collective-permute-start(bf16[480,128]{1,0:T(8,128)(2,1)S(1)} %get-tuple-element.20), channel_id=1, source_target_pairs={{0,8},{8,0},{16,24},{24,16},{1,9},{9,1},{17,25},{25,17},{2,10},{10... | collective-permute-start | bytes 368648 | tf_op jit(solution)/shard_map/ppermute | solution.py:512
  2.2 5.8 %collective-permute-start.1 = (bf16[480,128]{1,0:T(8,128)(2,1)S(1)}, bf16[480,128]{1,0:T(8,128)(2,1)S(1)}, u32[]{:S(2)}, u32[]{:S(2)}) collective-permute-start(bf16[480,128]{1,0:T(8,128)(2,1)S(1)} %get-tuple-element.21), channel_id=1, source_target_pairs={{0,0},{8,16},{16,8},{24,24},{1,1},{9,17},{17,9},{25,25},{2,2},{10,... | collective-permute-start | bytes 368648 | tf_op jit(solution)/shard_map/ppermute | solution.py:512
  2.9 7.4 %collective-permute-start.2 = (bf16[240,128]{1,0:T(8,128)(2,1)S(1)}, bf16[240,128]{1,0:T(8,128)(2,1)S(1)}, u32[]{:S(2)}, u32[]{:S(2)}) collective-permute-start(bf16[240,128]{1,0:T(8,128)(2,1)S(1)} %get-tuple-element.22), channel_id=1, source_target_pairs={{0,2},{2,0},{4,6},{6,4},{1,3},{3,1},{5,7},{7,5},{8,10},{10,8},{12,... | collective-permute-start | bytes 184328 | tf_op jit(solution)/shard_map/ppermute | solution.py:512
  5.6 6.2 %collective-permute-start.3 = (bf16[240,128]{1,0:T(8,128)(2,1)S(1)}, bf16[240,128]{1,0:T(8,128)(2,1)S(1)}, u32[]{:S(2)}, u32[]{:S(2)}) collective-permute-start(bf16[240,128]{1,0:T(8,128)(2,1)S(1)} %get-tuple-element.23), channel_id=1, source_target_pairs={{0,6},{2,4},{4,2},{6,0},{1,7},{3,5},{5,3},{7,1},{8,14},{10,12},{12... | collective-permute-start | bytes 184328 | tf_op jit(solution)/shard_map/ppermute | solution.py:512
  8.2 4.1 %collective-permute-start.4 = (bf16[160,128]{1,0:T(8,128)(2,1)S(1)}, bf16[160,128]{1,0:T(8,128)(2,1)S(1)}, u32[]{:S(2)}, u32[]{:S(2)}) collective-permute-start(bf16[160,128]{1,0:T(8,128)(2,1)S(1)} %get-tuple-element.24), channel_id=1, source_target_pairs={{0,2},{2,0},{4,6},{6,4},{1,3},{3,1},{5,7},{7,5},{8,10},{10,8},{12,... | collective-permute-start | bytes 122888 | tf_op jit(solution)/shard_map/ppermute | solution.py:512
  8.9 5.8 %collective-permute-start.5 = (bf16[160,128]{1,0:T(8,128)(2,1)S(1)}, bf16[160,128]{1,0:T(8,128)(2,1)S(1)}, u32[]{:S(2)}, u32[]{:S(2)}) collective-permute-start(bf16[160,128]{1,0:T(8,128)(2,1)S(1)} %get-tuple-element.25), channel_id=1, source_target_pairs={{0,6},{2,4},{4,2},{6,0},{1,7},{3,5},{5,3},{7,1},{8,14},{10,12},{12... | collective-permute-start | bytes 122888 | tf_op jit(solution)/shard_map/ppermute | solution.py:512
  15.4 4.2 %collective-permute-start.6 = (bf16[160,128]{1,0:T(8,128)(2,1)S(1)}, bf16[160,128]{1,0:T(8,128)(2,1)S(1)}, u32[]{:S(2)}, u32[]{:S(2)}) collective-permute-start(bf16[160,128]{1,0:T(8,128)(2,1)S(1)} %get-tuple-element.29), channel_id=1, source_target_pairs={{0,1},{1,0},{2,3},{3,2},{4,5},{5,4},{6,7},{7,6},{8,9},{9,8},{10,11... | collective-permute-start | bytes 122888 | tf_op jit(solution)/shard_map/ppermute | solution.py:565
  25.5 14.0 %copy-start = (bf16[256,1024]{1,0:T(8,128)(2,1)S(1)}, bf16[256,1024]{1,0:T(8,128)(2,1)}, u32[]{:S(2)}) copy-start(bf16[256,1024]{1,0:T(8,128)(2,1)} %weight.1) | copy-start | bytes 1572868
  25.5 13.9 %copy-start.1 = (s32[1,32]{1,0:T(1,128)S(1)}, s32[1,32]{1,0:T(1,128)}, u32[]{:S(2)}) copy-start(s32[1,32]{1,0:T(1,128)} %offsets.1) | copy-start | bytes 388
  25.5 13.9 %all-to-all-start = ((f32[32,1,128]{2,1,0:T(1,128)}), f32[32,1,128]{2,1,0:T(1,128)S(1)}, u32[]{:S(2)}, u32[]{:S(2)}) async-start(f32[32,1,128]{2,1,0:T(1,128)} %get-tuple-element.33), calls=%async_computation | async-start | bytes 32768 | tf_op jit(solution)/shard_map/all_to_all | solution.py:582

commit v8 on v7

--- a/solution.py
+++ b/solution.py
@@ -5,7 +5,7 @@
 from jax import lax
 from jax.experimental import pallas as pl
 from jax.experimental.pallas import tpu as pltpu
-from jax.sharding import PartitionSpec as P
+from jax.sharding import Mesh, PartitionSpec as P
 
 NB = 128
 GAMMA_M = 0.4
@@ -18,6 +18,7 @@
 OFF = 8
 SPAN = 32
 TALL = ROWS + 8
+STEP = 4
 SLOT = 8
 HBM = pltpu.MemorySpace.HBM
 VMEM = pltpu.MemorySpace.VMEM
@@ -51,8 +52,12 @@
     return 8 * (row % 4) + row // 4
 
 
+def ax_index():
+    return lax.axis_index("y") * lax.axis_size("core") + lax.axis_index("core")
+
+
 def is_even(axis):
-    return lax.axis_index(axis) % 2 == 0
+    return lax.axis_index("core" if axis == "ax" else axis) % 2 == 0
 
 
 def load_and_pack(ca, cz, den, vel, pre, home, ax1, ax2, az1, az2, sems):
@@ -87,7 +92,7 @@
 
 
 def ax_sides(n_ax, got1, got2, rows):
-    ax = lax.axis_index("ax")
+    ax = ax_index()
     a, b = got1[rows, :].astype(F32), got2[rows, :].astype(F32)
     even = is_even("ax")
     lo = jnp.where(ax == 0, 0.0, jnp.where(even, b, a))
@@ -306,7 +311,7 @@
     fetch.start()
     cr = block.shape[-1]
     low, high = REACH, REACH + ca
-    ax = lax.axis_index("ax")
+    ax = ax_index()
     rad = lax.axis_index("rad")
 
     lane = lax.broadcasted_iota(jnp.int32, (8, cr), 1)
@@ -349,9 +354,9 @@
     for j in (low - 6, low - 5, high + 4, high + 5):
         ax_only(start_state(j, False)[1], fax, j)
 
-    @pl.loop(0, (ca + 8) // 2)
+    @pl.loop(0, (ca + 8) // STEP)
     def _(i):
-        js = [low - 4 + 2 * i, low - 3 + 2 * i]
+        js = [low - 4 + STEP * i + k for k in range(STEP)]
         us = []
         for j in js:
             rho, u = start_state(j, True)
@@ -396,9 +401,9 @@
     for j in (low - 4, low - 3, high + 2, high + 3):
         ax_only(split_state([second[f, j, 0:ROWS] for f in range(5)]), fax, j)
 
-    @pl.loop(0, (ca + 4) // 2)
+    @pl.loop(0, (ca + 4) // STEP)
     def _(i):
-        js = [low - 2 + 2 * i, low - 1 + 2 * i]
+        js = [low - 2 + STEP * i + k for k in range(STEP)]
         us = []
         for j in js:
             u = split_state([second[f, j] for f in range(5)])
@@ -445,13 +450,14 @@
     q_out[...] = jnp.broadcast_to(q[0:1][None], q_out.shape)
 
 
-def last_stage(ca, cz, u2, u0, banded, state, fax, part):
+def last_stage(ca, cz, u2, u0, banded, after, state, fax, part):
+    del after
     for j in (0, 1, ca + 2, ca + 3):
         ax_only(split_state([u2[f, j, 0:ROWS] for f in range(5)]), fax, j)
 
-    @pl.loop(0, ca // 2)
+    @pl.loop(0, ca // STEP)
     def _(i):
-        js = [2 + 2 * i, 3 + 2 * i]
+        js = [2 + STEP * i + k for k in range(STEP)]
         us = [split_state([u2[f, j] for f in range(5)]) for j in js]
         both_sides(us, js, fax, part, banded)
 
@@ -468,13 +474,24 @@
                 state[f, k, pl.ds(l, quarter, stride=4), :] = new[8 * l + first : 8 * l + first + quarter]
 
 
-def signals(slots, rows, offsets, weight, out):
+def pair_rows(mine, other, out):
+    first = is_even("ax")
+    a, b = mine[0], other[0]
+    rows = jnp.concatenate([jnp.where(first, a, b), jnp.where(first, b, a)], axis=0)
+    out[...] = jnp.broadcast_to(rows[None], out.shape)
+
+
+def signals(slots, cores, pair, rows, offsets, weight, out):
     ndev = rows.shape[0]
-    group = 32
+    group = max(32, cores * pair)
     cols = group * slots
     lanes = rows.shape[1]
     col = lax.broadcasted_iota(jnp.int32, (1, cols), 1)
-    owner = lax.broadcasted_iota(jnp.int32, (group, cols), 0) == col // slots
+    place = lax.broadcasted_iota(jnp.int32, (group, cols), 0)
+    inner = place % (cores * pair)
+    device = place - inner + (inner % cores) * pair + inner // cores
+    owner = device == col // slots
+    holder = place == col // slots
     lane = lax.broadcasted_iota(jnp.int32, (lanes, cols), 0)
     time = lax.broadcasted_iota(jnp.int32, (NB, cols), 0).astype(F32)
     total = jnp.zeros(out.shape, F32)
@@ -482,7 +499,7 @@
         q = rows[g * group : (g + 1) * group, :].astype(BF16)
         off = offsets[0:1, g * group : (g + 1) * group].astype(F32)
         off = jnp.broadcast_to(off, (8, group)).astype(BF16)
-        bins = jnp.dot(off, owner.astype(BF16), preferred_element_type=F32)[0:1]
+        bins = jnp.dot(off, holder.astype(BF16), preferred_element_type=F32)[0:1]
         table = jnp.zeros((NB, cols), F32)
         for s in range(3):
             pick = jnp.where(lane == s * slots + col % slots, 1.0, 0.0).astype(BF16)
@@ -508,7 +525,10 @@
 
 
 def swap(first, second, axis, periodic):
-    one, two = swap_pairs(lax.axis_size(axis), periodic)
+    count = 1
+    for name in (axis,) if isinstance(axis, str) else axis:
+        count = count * lax.axis_size(name)
+    one, two = swap_pairs(count, periodic)
     return lax.ppermute(first, axis, one), lax.ppermute(second, axis, two)
 
 
@@ -516,7 +536,7 @@
     ca, cz, cr = density.shape
     slots = panel_cell.shape[0]
     ndev = bin_offset.shape[1]
-    n_ax, n_rad = lax.axis_size("ax"), lax.axis_size("rad")
+    n_ax, n_rad = lax.axis_size("y") * lax.axis_size("core"), lax.axis_size("rad")
     planes = ca + 2 * REACH
     part = functools.partial
     given = (density.reshape(ca * cz, cr), velocity.reshape(3 * ca * cz, cr), pressure.reshape(ca * cz, cr))
@@ -529,7 +549,7 @@
         [HBM] * 3,
         [pltpu.SemaphoreType.DMA((3,))],
     )(*[far(x) for x in given])
-    ax1, ax2 = swap(ax1, ax2, "ax", False)
+    ax1, ax2 = swap(ax1, ax2, ("y", "core"), False)
     az1, az2 = swap(az1, az2, "az", True)
     grid = struct((5 * planes * ROWS, cr))
     ends = ("either",) if n_rad == 2 else ("low", "high")
@@ -570,7 +590,7 @@
     grid = (5, planes, TALL, cr)
     q, u2, u0 = call(
         part(stages, n_ax, n_rad, ca, cz, slots),
-        (struct((ndev, 1, 128)), struct((5, ca + 4, TALL, cr)), struct((5, ca, ROWS, cr))),
+        (struct((1, 1, 128)), struct((5, ca + 4, TALL, cr)), struct((5, ca, ROWS, cr))),
         [VMEM, VMEM, HBM] + [VMEM] * (2 * len(sides)),
         [pltpu.VMEM((5, ca + 2 * MID, 8, cr), F32)]
         + [pltpu.VMEM(grid, F32) for _ in range(4)]
@@ -579,31 +599,39 @@
         mib=28,
     )(block, banded, far(panel_cell), *sides, *places)
 
-    rows = lax.all_to_all(q, ("ax", "az", "rad"), 0, 0, tiled=True).reshape(ndev, 128)
+    cores, n_az = lax.axis_size("core"), lax.axis_size("az")
+    other = lax.ppermute(q, "core", [(0, 1), (1, 0)])
+    rows = call(pair_rows, struct((ndev // cores, cores, 128)), [VMEM] * 2, mib=2)(q, other)
+    sent = rows
+    rows = lax.all_to_all(rows, ("y", "az", "rad"), 0, 0, tiled=True).reshape(ndev, 128)
 
     grid = (5, ca + 4, TALL, cr)
     state = call(
         part(last_stage, ca, cz),
         struct((5, ca, cz, cr)),
-        [VMEM] * 3,
+        [VMEM] * 3 + [pl.ANY],
         [pltpu.VMEM(grid, F32), pltpu.VMEM(grid, F32)],
         mib=12,
         cost=pl.CostEstimate(flops=400_000_000, bytes_accessed=8_000_000, transcendentals=0),
-    )(u2, u0, banded)
+    )(u2, u0, banded, sent)
     signal = call(
-        part(signals, slots), struct((obs_weight.shape[0], NB)), [VMEM] * 3, mib=24
+        part(signals, slots, cores, n_az * n_rad), struct((obs_weight.shape[0], NB)), [VMEM] * 3, mib=24
     )(rows, bin_offset, obs_weight)
     return (state, signal)
 
 
 def solution(mesh):
+    n_ax, n_az, n_rad = (mesh.shape[name] for name in ("ax", "az", "rad"))
+    split = Mesh(mesh.devices.reshape(n_ax // 2, 2, n_az, n_rad), ("y", "core", "az", "rad"))
+    ax = ("y", "core")
+    every = ax + ("az", "rad")
     in_specs = (
-        P("ax", "az", "rad"),
-        P(None, "ax", "az", "rad"),
-        P("ax", "az", "rad"),
-        P(("ax", "az", "rad")),
-        P(("ax", "az", "rad"), None),
-        P(("ax", "az", "rad"), None),
+        P(ax, "az", "rad"),
+        P(None, ax, "az", "rad"),
+        P(ax, "az", "rad"),
+        P(every),
+        P(every, None),
+        P(every, None),
     )
-    out_specs = (P(None, "ax", "az", "rad"), P(("ax", "az", "rad"), None))
-    return jax.shard_map(local, mesh=mesh, in_specs=in_specs, out_specs=out_specs, check_vma=False)
+    out_specs = (P(None, ax, "az", "rad"), P(every, None))
+    return jax.shard_map(local, mesh=split, in_specs=in_specs, out_specs=out_specs, check_vma=False)

time: 40.8 us -> 42.3 us (1.037)
  waiting for transfers between devices: 12 us -> 13.6 us
  Pallas kernels: 11.5 us -> 10.2 us
  starting transfers between devices: 16.4 us -> 17.6 us
    pallas_call x3 -> x4, Pallas kernels: 9.16 us -> 7.85 us  [the longest x1 4.27 us: local(): call(part(stages, n_ax, n_rad, ca, cz, slots), (struct((1, 1, 128)), stru...]
    ppermute x0 -> x1, waiting for transfers between devices: none -> 1.01 us  [local(): other = lax.ppermute(q, 'core', [(0, 1), (1, 0)])]
    all_to_all x1, starting transfers between devices: 6.88 us -> 7.88 us  [local(): lax.all_to_all(rows, ('y', 'az', 'rad'), 0, 0, tiled=True)]
    all_to_all x1, waiting for transfers between devices: 4.96 us -> 5.56 us  [local(): lax.all_to_all(rows, ('y', 'az', 'rad'), 0, 0, tiled=True)]
  transfers between devices with their start and end apart: 8 -> 9, of which waited for: 5 -> 6; matrix products, arithmetic and copies ran while one was open for 0% -> 0% of each run, Pallas kernels for 7% -> 6%
where the time goes in v8:
time: 42.3 us; the launch traced here: 42.1 us
  starting transfers between devices  17.6 us (42%)
  waiting for transfers between devices  13.6 us (32%)
  Pallas kernels  10.2 us (24%)
  between operations  0.71 us (2%)
    ppermute x6, starting transfers between devices, swap(): return (lax.ppermute(first, axis, one), lax.ppermute(second, axis, two))  7.96 us
    all_to_all x1, starting transfers between devices, local(): lax.all_to_all(rows, ('y', 'az', 'rad'), 0, 0, tiled=True)  7.88 us
    all_to_all x1, waiting for transfers between devices, local(): lax.all_to_all(rows, ('y', 'az', 'rad'), 0, 0, tiled=True)  5.56 us
    ppermute x6, waiting for transfers between devices, swap(): return (lax.ppermute(first, axis, one), lax.ppermute(second, axis, two))  4.4 us
    pallas_call x1, Pallas kernels, local(): call(part(stages, n_ax, n_rad, ca, cz, slots), (struct((1, 1, 128)), stru...  4.27 us
    ppermute x1, waiting for transfers between devices, local(): sides = (lax.ppermute(got[1], 'rad', [(0, 1), (1, 0)]),)  2.65 us
    pallas_call x1, Pallas kernels, local(): call(part(last_stage, ca, cz), struct((5, ca, cz, cr)), [VMEM] * 3 + [pl....  1.77 us
    ppermute x1, starting transfers between devices, local(): sides = (lax.ppermute(got[1], 'rad', [(0, 1), (1, 0)]),)  1.56 us
  transfers between devices with their start and end apart: 9, of which 6 were waited for; matrix products, arithmetic and copies ran while one was open for 0% of the time, Pallas kernels for 6%

profile of v8, /device:TPU:0, one launch (start us, length us, event | category | flops | bytes accessed | tf_op | source)
XLA Modules:
  0.0 42.1 jit_solution(6580958251112114281)
XLA Ops:
  0.6 1.1 %shard_map.77 = (f32[640,128]{1,0:T(8,128)S(1)}, bf16[480,128]{1,0:T(8,128)(2,1)S(1)}, bf16[480,128]{1,0:T(8,128)(2,1)S(1)}, bf16[240,128]{1,0:T(8,128)(2,1)S(1)}, bf16[240,128]{1,0:T(8,128)(2,1)S(1)}) custom-call(f32[128,128]{1,0:T(8,128)} %bitcast.8, f32[384,128]{1,0:T(8,128)} %bitcast.7, f32[128,128]{1,0:T(8,128)} %bitcast.9), custom_call_target="tpu_custom_call" | custom-call | tf_op jit(solution)/shard_map/pallas_call | solution.py:546
  1.7 0.5 %collective-permute-start = (bf16[480,128]{1,0:T(8,128)(2,1)S(1)}, bf16[480,128]{1,0:T(8,128)(2,1)S(1)}, u32[]{:S(2)}, u32[]{:S(2)}) collective-permute-start(bf16[480,128]{1,0:T(8,128)(2,1)S(1)} %get-tuple-element.20), channel_id=1, source_target_pairs={{0,8},{8,0},{16,24},{24,16},{1,9},{9,1},{17,25},{25,17},{2,10},{10... | collective-permute-start | bytes 368648 | tf_op jit(solution)/shard_map/ppermute | solution.py:532
  2.2 0.7 %collective-permute-start.1 = (bf16[480,128]{1,0:T(8,128)(2,1)S(1)}, bf16[480,128]{1,0:T(8,128)(2,1)S(1)}, u32[]{:S(2)}, u32[]{:S(2)}) collective-permute-start(bf16[480,128]{1,0:T(8,128)(2,1)S(1)} %get-tuple-element.21), channel_id=1, source_target_pairs={{0,0},{8,16},{16,8},{24,24},{1,1},{9,17},{17,9},{25,25},{2,2},{10,... | collective-permute-start | bytes 368648 | tf_op jit(solution)/shard_map/ppermute | solution.py:532
  2.9 2.7 %collective-permute-start.2 = (bf16[240,128]{1,0:T(8,128)(2,1)S(1)}, bf16[240,128]{1,0:T(8,128)(2,1)S(1)}, u32[]{:S(2)}, u32[]{:S(2)}) collective-permute-start(bf16[240,128]{1,0:T(8,128)(2,1)S(1)} %get-tuple-element.22), channel_id=1, source_target_pairs={{0,2},{2,0},{4,6},{6,4},{1,3},{3,1},{5,7},{7,5},{8,10},{10,8},{12,... | collective-permute-start | bytes 184328 | tf_op jit(solution)/shard_map/ppermute | solution.py:532
  5.6 2.5 %collective-permute-start.3 = (bf16[240,128]{1,0:T(8,128)(2,1)S(1)}, bf16[240,128]{1,0:T(8,128)(2,1)S(1)}, u32[]{:S(2)}, u32[]{:S(2)}) collective-permute-start(bf16[240,128]{1,0:T(8,128)(2,1)S(1)} %get-tuple-element.23), channel_id=1, source_target_pairs={{0,6},{2,4},{4,2},{6,0},{1,7},{3,5},{5,3},{7,1},{8,14},{10,12},{12... | collective-permute-start | bytes 184328 | tf_op jit(solution)/shard_map/ppermute | solution.py:532
  8.1 0.0 collective-permute-done.got1.ax1
  8.1 0.0 collective-permute-done.1.got2.ax2
  8.1 0.1 shard_map.79
  8.2 0.7 %collective-permute-start.4 = (bf16[160,128]{1,0:T(8,128)(2,1)S(1)}, bf16[160,128]{1,0:T(8,128)(2,1)S(1)}, u32[]{:S(2)}, u32[]{:S(2)}) collective-permute-start(bf16[160,128]{1,0:T(8,128)(2,1)S(1)} %get-tuple-element.24), channel_id=1, source_target_pairs={{0,2},{2,0},{4,6},{6,4},{1,3},{3,1},{5,7},{7,5},{8,10},{10,8},{12,... | collective-permute-start | bytes 122888 | tf_op jit(solution)/shard_map/ppermute | solution.py:532
  8.9 0.9 %collective-permute-start.5 = (bf16[160,128]{1,0:T(8,128)(2,1)S(1)}, bf16[160,128]{1,0:T(8,128)(2,1)S(1)}, u32[]{:S(2)}, u32[]{:S(2)}) collective-permute-start(bf16[160,128]{1,0:T(8,128)(2,1)S(1)} %get-tuple-element.25), channel_id=1, source_target_pairs={{0,6},{2,4},{4,2},{6,0},{1,7},{3,5},{5,3},{7,1},{8,14},{10,12},{12... | collective-permute-start | bytes 122888 | tf_op jit(solution)/shard_map/ppermute | solution.py:532
  9.8 0.5 %shard_map.78 = (f32[3200,128]{1,0:T(8,128)S(1)}, bf16[256,256]{1,0:T(8,128)(2,1)S(1)}, bf16[2048,128]{1,0:T(8,128)(2,1)S(1)}, bf16[128,512]{1,0:T(8,128)(2,1)S(1)}) custom-call(f32[640,128]{1,0:T(8,128)S(1)} %get-tuple-element.18.home), custom_call_target="tpu_custom_call" | custom-call | tf_op jit(solution)/shard_map/pallas_call | solution.py:558
  10.3 0.0 collective-permute-done.2.az1
  10.3 1.4 %collective-permute-done.3.az2 = bf16[240,128]{1,0:T(8,128)(2,1)S(1)} collective-permute-done((bf16[240,128]{1,0:T(8,128)(2,1)S(1)}, bf16[240,128]{1,0:T(8,128)(2,1)S(1)}, u32[]{:S(2)}, u32[]{:S(2)}) %collective-permute-start.3) | collective-permute-done | bytes 61472 | tf_op jit(solution)/shard_map/ppermute | solution.py:532
  11.8 0.5 %collective-permute-done.4.corner1 = bf16[160,128]{1,0:T(8,128)(2,1)S(1)} collective-permute-done((bf16[160,128]{1,0:T(8,128)(2,1)S(1)}, bf16[160,128]{1,0:T(8,128)(2,1)S(1)}, u32[]{:S(2)}, u32[]{:S(2)}) %collective-permute-start.4) | collective-permute-done | bytes 40992 | tf_op jit(solution)/shard_map/ppermute | solution.py:532
  12.2 2.5 %collective-permute-done.5.corner2 = bf16[160,128]{1,0:T(8,128)(2,1)S(1)} collective-permute-done((bf16[160,128]{1,0:T(8,128)(2,1)S(1)}, bf16[160,128]{1,0:T(8,128)(2,1)S(1)}, u32[]{:S(2)}, u32[]{:S(2)}) %collective-permute-start.5) | collective-permute-done | bytes 40992 | tf_op jit(solution)/shard_map/ppermute | solution.py:532
  14.7 0.7 %shard_map.80 = (f32[3200,128]{1,0:T(8,128)S(1)}, bf16[160,128]{1,0:T(8,128)(2,1)S(1)}) custom-call(f32[3200,128]{1,0:T(8,128)S(1)} %get-tuple-element.19.block_in, bf16[480,128]{1,0:T(8,128)(2,1)S(1)} %collective-permute-done.got1.ax1, bf16[480,128]{1,0:T(8,128)(2,1)S(1)} %collective-permute-done.1.got2.ax2, ...), custom_call_target="tpu_custom_call", output_to_operand_aliasing={{0}: (0, {})} | custom-call | tf_op jit(solution)/shard_map/pallas_call | solution.py:571
  15.4 1.6 %collective-permute-start.6 = (bf16[160,128]{1,0:T(8,128)(2,1)S(1)}, bf16[160,128]{1,0:T(8,128)(2,1)S(1)}, u32[]{:S(2)}, u32[]{:S(2)}) collective-permute-start(bf16[160,128]{1,0:T(8,128)(2,1)S(1)} %get-tuple-element.29), channel_id=1, source_target_pairs={{0,1},{1,0},{2,3},{3,2},{4,5},{5,4},{6,7},{7,6},{8,9},{9,8},{10,11... | collective-permute-start | bytes 122888 | tf_op jit(solution)/shard_map/ppermute | solution.py:585
  17.0 2.7 %collective-permute-done.6.refs_0_ = bf16[160,128]{1,0:T(8,128)(2,1)S(1)} collective-permute-done((bf16[160,128]{1,0:T(8,128)(2,1)S(1)}, bf16[160,128]{1,0:T(8,128)(2,1)S(1)}, u32[]{:S(2)}, u32[]{:S(2)}) %collective-permute-start.6) | collective-permute-done | bytes 40992 | tf_op jit(solution)/shard_map/ppermute | solution.py:585
  19.6 4.3 %shard_map.81 = (f32[1,1,128]{2,1,0:T(1,128)S(1)}, f32[5,12,40,128]{3,2,1,0:T(8,128)S(1)}, f32[5,8,32,128]{3,2,1,0:T(8,128)S(1)}) custom-call(f32[5,20,32,128]{3,2,1,0:T(8,128)S(1)} %bitcast.5, bf16[256,256]{1,0:T(8,128)(2,1)S(1)} %get-tuple-element.28.banded, s32[32]{0:T(128)} %cells_far.1, bf16[160,128]{1,0:T(8,128)(2,1)S(1)} %collective-permute-done.6.refs_0_, ...), custom_call_target="tpu_custom_call" | custom-call | tf_op jit(solution)/shard_map/pallas_call | solution.py:591
  23.9 0.0 copy-start
  23.9 0.0 copy-start.1
  23.9 0.2 collective-permute-start.7
  24.1 1.0 %collective-permute-done.7.other = f32[1,1,128]{2,1,0:T(1,128)S(1)} collective-permute-done((f32[1,1,128]{2,1,0:T(1,128)S(1)}, f32[1,1,128]{2,1,0:T(1,128)S(1)}, u32[]{:S(2)}, u32[]{:S(2)}) %collective-permute-start.7) | collective-permute-done | bytes 544 | tf_op jit(solution)/shard_map/ppermute | solution.py:603
  25.1 0.6 %shard_map.82.after = f32[16,2,128]{2,1,0:T(2,128)} custom-call(f32[1,1,128]{2,1,0:T(1,128)S(1)} %get-tuple-element.33.mine, f32[1,1,128]{2,1,0:T(1,128)S(1)} %collective-permute-done.7.other), custom_call_target="tpu_custom_call" | custom-call | tf_op jit(solution)/shard_map/pallas_call | solution.py:604
  25.7 7.9 %all-to-all-start = ((f32[16,2,128]{2,1,0:T(2,128)}), f32[16,2,128]{2,1,0:T(2,128)S(1)}, u32[]{:S(2)}, u32[]{:S(2)}) async-start(f32[16,2,128]{2,1,0:T(2,128)} %shard_map.82.after), calls=%async_computation | async-start | bytes 32768 | tf_op jit(solution)/shard_map/all_to_all | solution.py:606
  33.6 1.8 %shard_map.83 = f32[5,8,16,128]{3,2,1,0:T(8,128)} custom-call(f32[5,12,40,128]{3,2,1,0:T(8,128)S(1)} %get-tuple-element.31.u2, f32[5,8,32,128]{3,2,1,0:T(8,128)S(1)} %get-tuple-element.32.u0, bf16[256,256]{1,0:T(8,128)(2,1)S(1)} %get-tuple-element.28.banded, f32[16,2,128]{2,1,0:T(2,128)} %shard_map.82.after), custom_call_target="tpu_custom_call" | custom-call | flops 400000000 | bytes 8000000 | tf_op jit(solution)/shard_map/pallas_call | solution.py:609
  35.4 5.6 %all-to-all-done = f32[16,2,128]{2,1,0:T(2,128)S(1)} async-done(((f32[16,2,128]{2,1,0:T(2,128)}), f32[16,2,128]{2,1,0:T(2,128)S(1)}, u32[]{:S(2)}, u32[]{:S(2)}) %all-to-all-start) | async-done | bytes 16416 | tf_op jit(solution)/shard_map/all_to_all | solution.py:606
  40.9 0.0 copy-done
  40.9 0.0 copy-done.1
  40.9 1.2 %shard_map.84 = f32[256,128]{1,0:T(8,128)} custom-call(f32[32,128]{1,0:T(8,128)S(1)} %bitcast.6, s32[1,32]{1,0:T(1,128)S(1)} %copy-done.1, bf16[256,1024]{1,0:T(8,128)(2,1)S(1)} %copy-done), custom_call_target="tpu_custom_call" | custom-call | tf_op jit(solution)/shard_map/pallas_call | solution.py:617
Async XLA Ops:
  1.7 6.3 %collective-permute-start = (bf16[480,128]{1,0:T(8,128)(2,1)S(1)}, bf16[480,128]{1,0:T(8,128)(2,1)S(1)}, u32[]{:S(2)}, u32[]{:S(2)}) collective-permute-start(bf16[480,128]{1,0:T(8,128)(2,1)S(1)} %get-tuple-element.20), channel_id=1, source_target_pairs={{0,8},{8,0},{16,24},{24,16},{1,9},{9,1},{17,25},{25,17},{2,10},{10... | collective-permute-start | bytes 368648 | tf_op jit(solution)/shard_map/ppermute | solution.py:532
  2.2 5.8 %collective-permute-start.1 = (bf16[480,128]{1,0:T(8,128)(2,1)S(1)}, bf16[480,128]{1,0:T(8,128)(2,1)S(1)}, u32[]{:S(2)}, u32[]{:S(2)}) collective-permute-start(bf16[480,128]{1,0:T(8,128)(2,1)S(1)} %get-tuple-element.21), channel_id=1, source_target_pairs={{0,0},{8,16},{16,8},{24,24},{1,1},{9,17},{17,9},{25,25},{2,2},{10,... | collective-permute-start | bytes 368648 | tf_op jit(solution)/shard_map/ppermute | solution.py:532
  2.9 7.4 %collective-permute-start.2 = (bf16[240,128]{1,0:T(8,128)(2,1)S(1)}, bf16[240,128]{1,0:T(8,128)(2,1)S(1)}, u32[]{:S(2)}, u32[]{:S(2)}) collective-permute-start(bf16[240,128]{1,0:T(8,128)(2,1)S(1)} %get-tuple-element.22), channel_id=1, source_target_pairs={{0,2},{2,0},{4,6},{6,4},{1,3},{3,1},{5,7},{7,5},{8,10},{10,8},{12,... | collective-permute-start | bytes 184328 | tf_op jit(solution)/shard_map/ppermute | solution.py:532
  5.6 6.2 %collective-permute-start.3 = (bf16[240,128]{1,0:T(8,128)(2,1)S(1)}, bf16[240,128]{1,0:T(8,128)(2,1)S(1)}, u32[]{:S(2)}, u32[]{:S(2)}) collective-permute-start(bf16[240,128]{1,0:T(8,128)(2,1)S(1)} %get-tuple-element.23), channel_id=1, source_target_pairs={{0,6},{2,4},{4,2},{6,0},{1,7},{3,5},{5,3},{7,1},{8,14},{10,12},{12... | collective-permute-start | bytes 184328 | tf_op jit(solution)/shard_map/ppermute | solution.py:532
  8.2 4.1 %collective-permute-start.4 = (bf16[160,128]{1,0:T(8,128)(2,1)S(1)}, bf16[160,128]{1,0:T(8,128)(2,1)S(1)}, u32[]{:S(2)}, u32[]{:S(2)}) collective-permute-start(bf16[160,128]{1,0:T(8,128)(2,1)S(1)} %get-tuple-element.24), channel_id=1, source_target_pairs={{0,2},{2,0},{4,6},{6,4},{1,3},{3,1},{5,7},{7,5},{8,10},{10,8},{12,... | collective-permute-start | bytes 122888 | tf_op jit(solution)/shard_map/ppermute | solution.py:532
  8.9 5.8 %collective-permute-start.5 = (bf16[160,128]{1,0:T(8,128)(2,1)S(1)}, bf16[160,128]{1,0:T(8,128)(2,1)S(1)}, u32[]{:S(2)}, u32[]{:S(2)}) collective-permute-start(bf16[160,128]{1,0:T(8,128)(2,1)S(1)} %get-tuple-element.25), channel_id=1, source_target_pairs={{0,6},{2,4},{4,2},{6,0},{1,7},{3,5},{5,3},{7,1},{8,14},{10,12},{12... | collective-permute-start | bytes 122888 | tf_op jit(solution)/shard_map/ppermute | solution.py:532
  15.4 4.2 %collective-permute-start.6 = (bf16[160,128]{1,0:T(8,128)(2,1)S(1)}, bf16[160,128]{1,0:T(8,128)(2,1)S(1)}, u32[]{:S(2)}, u32[]{:S(2)}) collective-permute-start(bf16[160,128]{1,0:T(8,128)(2,1)S(1)} %get-tuple-element.29), channel_id=1, source_target_pairs={{0,1},{1,0},{2,3},{3,2},{4,5},{5,4},{6,7},{7,6},{8,9},{9,8},{10,11... | collective-permute-start | bytes 122888 | tf_op jit(solution)/shard_map/ppermute | solution.py:585
  23.9 17.1 %copy-start = (bf16[256,1024]{1,0:T(8,128)(2,1)S(1)}, bf16[256,1024]{1,0:T(8,128)(2,1)}, u32[]{:S(2)}) copy-start(bf16[256,1024]{1,0:T(8,128)(2,1)} %weight.1) | copy-start | bytes 1572868
  23.9 17.0 %copy-start.1 = (s32[1,32]{1,0:T(1,128)S(1)}, s32[1,32]{1,0:T(1,128)}, u32[]{:S(2)}) copy-start(s32[1,32]{1,0:T(1,128)} %offsets.1) | copy-start | bytes 388
  23.9 1.2 %collective-permute-start.7 = (f32[1,1,128]{2,1,0:T(1,128)S(1)}, f32[1,1,128]{2,1,0:T(1,128)S(1)}, u32[]{:S(2)}, u32[]{:S(2)}) collective-permute-start(f32[1,1,128]{2,1,0:T(1,128)S(1)} %get-tuple-element.33.mine), channel_id=1, source_target_pairs={{0,8},{8,0},{1,9},{9,1},{2,10},{10,2},{3,11},{11,3},{4,12},{12,4},... | collective-permute-start | bytes 1544 | tf_op jit(solution)/shard_map/ppermute | solution.py:603
  25.7 15.2 %all-to-all-start = ((f32[16,2,128]{2,1,0:T(2,128)}), f32[16,2,128]{2,1,0:T(2,128)S(1)}, u32[]{:S(2)}, u32[]{:S(2)}) async-start(f32[16,2,128]{2,1,0:T(2,128)} %shard_map.82.after), calls=%async_computation | async-start | bytes 32768 | tf_op jit(solution)/shard_map/all_to_all | solution.py:606

commit v9 on v8

--- a/solution.py
+++ b/solution.py
@@ -56,8 +56,8 @@
     return lax.axis_index("y") * lax.axis_size("core") + lax.axis_index("core")
 
 
-def is_even(axis):
-    return lax.axis_index("core" if axis == "ax" else axis) % 2 == 0
+def first_is_up(axis):
+    return lax.axis_index("core" if axis == "ax" else axis) % 2 == 1
 
 
 def load_and_pack(ca, cz, den, vel, pre, home, ax1, ax2, az1, az2, sems):
@@ -71,37 +71,37 @@
         copy.start()
     for copy in copies:
         copy.wait()
-    even = is_even("ax")
+    up = first_is_up("ax")
     edge = REACH * cz
     for f in range(5):
         at = f * size
         low = home[at : at + edge, :]
         high = home[at + size - edge : at + size, :]
         rows = slice(f * edge, (f + 1) * edge)
-        ax1[rows, :] = jnp.where(even, high, low).astype(BF16)
-        ax2[rows, :] = jnp.where(even, low, high).astype(BF16)
-    even = is_even("az")
+        ax1[rows, :] = jnp.where(up, high, low).astype(BF16)
+        ax2[rows, :] = jnp.where(up, low, high).astype(BF16)
+    up = first_is_up("az")
     low, high = [], []
     for f in range(5):
         for d in range(REACH):
             low.append(home[pl.ds(f * size + d, ca, stride=cz), :])
             high.append(home[pl.ds(f * size + cz - 1 - d, ca, stride=cz), :])
     low, high = jnp.concatenate(low, axis=0), jnp.concatenate(high, axis=0)
-    az1[...] = jnp.where(even, high, low).astype(BF16)
-    az2[...] = jnp.where(even, low, high).astype(BF16)
+    az1[...] = jnp.where(up, high, low).astype(BF16)
+    az2[...] = jnp.where(up, low, high).astype(BF16)
 
 
 def ax_sides(n_ax, got1, got2, rows):
     ax = ax_index()
     a, b = got1[rows, :].astype(F32), got2[rows, :].astype(F32)
-    even = is_even("ax")
-    lo = jnp.where(ax == 0, 0.0, jnp.where(even, b, a))
-    hi = jnp.where(ax == n_ax - 1, 0.0, jnp.where(even, a, b))
+    up = first_is_up("ax")
+    lo = jnp.where(ax == 0, 0.0, jnp.where(up, b, a))
+    hi = jnp.where(ax == n_ax - 1, 0.0, jnp.where(up, a, b))
     return lo, hi
 
 
 def pack_corners(n_ax, cz, got1, got2, first_out, second_out, near):
-    even = is_even("az")
+    up = first_is_up("az")
     half = MID * cz
     size = REACH * cz
     for f in range(5):
@@ -114,8 +114,8 @@
             low.append(near[f, pl.ds(d, 2 * MID, stride=cz), :])
             high.append(near[f, pl.ds(cz - 1 - d, 2 * MID, stride=cz), :])
     low, high = jnp.concatenate(low, axis=0), jnp.concatenate(high, axis=0)
-    first_out[...] = jnp.where(even, high, low).astype(BF16)
-    second_out[...] = jnp.where(even, low, high).astype(BF16)
+    first_out[...] = jnp.where(up, high, low).astype(BF16)
+    second_out[...] = jnp.where(up, low, high).astype(BF16)
 
 
 def spread_rows(planes, cz, f, plane, ref, at, block):
@@ -171,11 +171,11 @@
             spread_rows(planes, cz, f, k, sides.at[f], k * cz, block)
             spread_rows(planes, cz, f, REACH + ca + k, sides.at[f], size + k * cz, block)
 
-    even = is_even("az")
+    up = first_is_up("az")
     for one, two, into in ((az1, az2, strips), (corner1, corner2, corners)):
         a, b = one[...].astype(F32), two[...].astype(F32)
-        into[0] = jnp.where(even, b, a)
-        into[1] = jnp.where(even, a, b)
+        into[0] = jnp.where(up, b, a)
+        into[1] = jnp.where(up, a, b)
     for f in range(5):
         for d in range(REACH):
             for side, row in ((0, OFF - 1 - d), (1, OFF + cz + d)):
@@ -450,8 +450,7 @@
     q_out[...] = jnp.broadcast_to(q[0:1][None], q_out.shape)
 
 
-def last_stage(ca, cz, u2, u0, banded, after, state, fax, part):
-    del after
+def last_stage(ca, cz, u2, u0, banded, state, fax, part):
     for j in (0, 1, ca + 2, ca + 3):
         ax_only(split_state([u2[f, j, 0:ROWS] for f in range(5)]), fax, j)
 
@@ -474,24 +473,13 @@
                 state[f, k, pl.ds(l, quarter, stride=4), :] = new[8 * l + first : 8 * l + first + quarter]
 
 
-def pair_rows(mine, other, out):
-    first = is_even("ax")
-    a, b = mine[0], other[0]
-    rows = jnp.concatenate([jnp.where(first, a, b), jnp.where(first, b, a)], axis=0)
-    out[...] = jnp.broadcast_to(rows[None], out.shape)
-
-
-def signals(slots, cores, pair, rows, offsets, weight, out):
+def signals(slots, rows, offsets, weight, out):
     ndev = rows.shape[0]
-    group = max(32, cores * pair)
+    group = 32
     cols = group * slots
     lanes = rows.shape[1]
     col = lax.broadcasted_iota(jnp.int32, (1, cols), 1)
-    place = lax.broadcasted_iota(jnp.int32, (group, cols), 0)
-    inner = place % (cores * pair)
-    device = place - inner + (inner % cores) * pair + inner // cores
-    owner = device == col // slots
-    holder = place == col // slots
+    owner = lax.broadcasted_iota(jnp.int32, (group, cols), 0) == col // slots
     lane = lax.broadcasted_iota(jnp.int32, (lanes, cols), 0)
     time = lax.broadcasted_iota(jnp.int32, (NB, cols), 0).astype(F32)
     total = jnp.zeros(out.shape, F32)
@@ -499,7 +487,7 @@
         q = rows[g * group : (g + 1) * group, :].astype(BF16)
         off = offsets[0:1, g * group : (g + 1) * group].astype(F32)
         off = jnp.broadcast_to(off, (8, group)).astype(BF16)
-        bins = jnp.dot(off, holder.astype(BF16), preferred_element_type=F32)[0:1]
+        bins = jnp.dot(off, owner.astype(BF16), preferred_element_type=F32)[0:1]
         table = jnp.zeros((NB, cols), F32)
         for s in range(3):
             pick = jnp.where(lane == s * slots + col % slots, 1.0, 0.0).astype(BF16)
@@ -516,12 +504,11 @@
 
 
 def swap_pairs(count, periodic):
-    one = [(i, i ^ 1) for i in range(count)]
-    two = []
+    one = []
     for i in range(count):
         j = i - 1 if i % 2 == 0 else i + 1
-        two.append((i, j % count if periodic or 0 <= j < count else i))
-    return one, two
+        one.append((i, j % count if periodic or 0 <= j < count else i))
+    return one, [(i, i ^ 1) for i in range(count)]
 
 
 def swap(first, second, axis, periodic):
@@ -590,7 +577,7 @@
     grid = (5, planes, TALL, cr)
     q, u2, u0 = call(
         part(stages, n_ax, n_rad, ca, cz, slots),
-        (struct((1, 1, 128)), struct((5, ca + 4, TALL, cr)), struct((5, ca, ROWS, cr))),
+        (struct((ndev, 1, 128)), struct((5, ca + 4, TALL, cr)), struct((5, ca, ROWS, cr))),
         [VMEM, VMEM, HBM] + [VMEM] * (2 * len(sides)),
         [pltpu.VMEM((5, ca + 2 * MID, 8, cr), F32)]
         + [pltpu.VMEM(grid, F32) for _ in range(4)]
@@ -599,23 +586,19 @@
         mib=28,
     )(block, banded, far(panel_cell), *sides, *places)
 
-    cores, n_az = lax.axis_size("core"), lax.axis_size("az")
-    other = lax.ppermute(q, "core", [(0, 1), (1, 0)])
-    rows = call(pair_rows, struct((ndev // cores, cores, 128)), [VMEM] * 2, mib=2)(q, other)
-    sent = rows
-    rows = lax.all_to_all(rows, ("y", "az", "rad"), 0, 0, tiled=True).reshape(ndev, 128)
+    rows = lax.all_to_all(q, ("y", "core", "az", "rad"), 0, 0, tiled=True).reshape(ndev, 128)
 
     grid = (5, ca + 4, TALL, cr)
     state = call(
         part(last_stage, ca, cz),
         struct((5, ca, cz, cr)),
-        [VMEM] * 3 + [pl.ANY],
+        [VMEM] * 3,
         [pltpu.VMEM(grid, F32), pltpu.VMEM(grid, F32)],
         mib=12,
         cost=pl.CostEstimate(flops=400_000_000, bytes_accessed=8_000_000, transcendentals=0),
-    )(u2, u0, banded, sent)
+    )(u2, u0, banded)
     signal = call(
-        part(signals, slots, cores, n_az * n_rad), struct((obs_weight.shape[0], NB)), [VMEM] * 3, mib=24
+        part(signals, slots), struct((obs_weight.shape[0], NB)), [VMEM] * 3, mib=24
     )(rows, bin_offset, obs_weight)
     return (state, signal)
 

time: 42.3 us -> 39.3 us (0.929)
  waiting for transfers between devices: 13.6 us -> 11.2 us
  starting transfers between devices: 17.6 us -> 17.1 us
    all_to_all x1, starting transfers between devices: 7.88 us -> 4.68 us  [local(): lax.all_to_all(q, ('y', 'core', 'az', 'rad'), 0, 0, tiled=True)]
    ppermute x6, starting transfers between devices: 7.96 us -> 10.8 us  [swap(): return (lax.ppermute(first, axis, one), lax.ppermute(second, axis, two))]
    ppermute x6, waiting for transfers between devices: 4.4 us -> 3.37 us  [swap(): return (lax.ppermute(first, axis, one), lax.ppermute(second, axis, two))]
    ppermute x1 -> x0, waiting for transfers between devices: 1.01 us -> none  [local(): other = lax.ppermute(q, 'core', [(0, 1), (1, 0)])]
    pallas_call x4 -> x3, Pallas kernels: 7.85 us -> 7.83 us  [the longest x1 4.87 us: local(): call(part(stages, n_ax, n_rad, ca, cz, slots), (struct((ndev, 1, 128)), s...]
  transfers between devices with their start and end apart: 9 -> 8, of which waited for: 6 -> 5; matrix products, arithmetic and copies ran while one was open for 0% -> 0% of each run, Pallas kernels for 6% -> 6%
where the time goes in v9:
time: 39.3 us; the launch traced here: 39.1 us
  starting transfers between devices  17.1 us (44%)
  waiting for transfers between devices  11.2 us (28%)
  Pallas kernels  10.2 us (26%)
  between operations  0.7 us (2%)
    ppermute x6, starting transfers between devices, swap(): return (lax.ppermute(first, axis, one), lax.ppermute(second, axis, two))  10.8 us
    all_to_all x1, waiting for transfers between devices, local(): lax.all_to_all(q, ('y', 'core', 'az', 'rad'), 0, 0, tiled=True)  5.27 us
    pallas_call x1, Pallas kernels, local(): call(part(stages, n_ax, n_rad, ca, cz, slots), (struct((ndev, 1, 128)), s...  4.87 us
    all_to_all x1, starting transfers between devices, local(): lax.all_to_all(q, ('y', 'core', 'az', 'rad'), 0, 0, tiled=True)  4.68 us
    ppermute x6, waiting for transfers between devices, swap(): return (lax.ppermute(first, axis, one), lax.ppermute(second, axis, two))  3.37 us
    ppermute x1, waiting for transfers between devices, local(): sides = (lax.ppermute(got[1], 'rad', [(0, 1), (1, 0)]),)  2.51 us
    pallas_call x1, Pallas kernels, local(): call(part(last_stage, ca, cz), struct((5, ca, cz, cr)), [VMEM] * 3, [pltp...  1.77 us
    ppermute x1, starting transfers between devices, local(): sides = (lax.ppermute(got[1], 'rad', [(0, 1), (1, 0)]),)  1.56 us
  transfers between devices with their start and end apart: 8, of which 5 were waited for; matrix products, arithmetic and copies ran while one was open for 0% of the time, Pallas kernels for 6%

profile of v9, /device:TPU:0, one launch (start us, length us, event | category | flops | bytes accessed | tf_op | source)
XLA Modules:
  0.0 39.1 jit_solution(2017364121075056625)
XLA Ops:
  0.6 1.1 %shard_map.77 = (f32[640,128]{1,0:T(8,128)S(1)}, bf16[480,128]{1,0:T(8,128)(2,1)S(1)}, bf16[480,128]{1,0:T(8,128)(2,1)S(1)}, bf16[240,128]{1,0:T(8,128)(2,1)S(1)}, bf16[240,128]{1,0:T(8,128)(2,1)S(1)}) custom-call(f32[128,128]{1,0:T(8,128)} %bitcast.8, f32[384,128]{1,0:T(8,128)} %bitcast.7, f32[128,128]{1,0:T(8,128)} %bitcast.9), custom_call_target="tpu_custom_call" | custom-call | tf_op jit(solution)/shard_map/pallas_call | solution.py:533
  1.7 0.7 %collective-permute-start = (bf16[480,128]{1,0:T(8,128)(2,1)S(1)}, bf16[480,128]{1,0:T(8,128)(2,1)S(1)}, u32[]{:S(2)}, u32[]{:S(2)}) collective-permute-start(bf16[480,128]{1,0:T(8,128)(2,1)S(1)} %get-tuple-element.20), channel_id=1, source_target_pairs={{0,0},{8,16},{16,8},{24,24},{1,1},{9,17},{17,9},{25,25},{2,2},{10,... | collective-permute-start | bytes 368648 | tf_op jit(solution)/shard_map/ppermute | solution.py:519
  2.4 4.4 %collective-permute-start.1 = (bf16[480,128]{1,0:T(8,128)(2,1)S(1)}, bf16[480,128]{1,0:T(8,128)(2,1)S(1)}, u32[]{:S(2)}, u32[]{:S(2)}) collective-permute-start(bf16[480,128]{1,0:T(8,128)(2,1)S(1)} %get-tuple-element.21), channel_id=1, source_target_pairs={{0,8},{8,0},{16,24},{24,16},{1,9},{9,1},{17,25},{25,17},{2,10},{10... | collective-permute-start | bytes 368648 | tf_op jit(solution)/shard_map/ppermute | solution.py:519
  6.8 3.6 %collective-permute-start.2 = (bf16[240,128]{1,0:T(8,128)(2,1)S(1)}, bf16[240,128]{1,0:T(8,128)(2,1)S(1)}, u32[]{:S(2)}, u32[]{:S(2)}) collective-permute-start(bf16[240,128]{1,0:T(8,128)(2,1)S(1)} %get-tuple-element.22), channel_id=1, source_target_pairs={{0,6},{2,4},{4,2},{6,0},{1,7},{3,5},{5,3},{7,1},{8,14},{10,12},{12... | collective-permute-start | bytes 184328 | tf_op jit(solution)/shard_map/ppermute | solution.py:519
  10.4 0.0 collective-permute-start.3
  10.4 0.0 collective-permute-done.got1.ax1
  10.4 0.0 collective-permute-done.1.got2.ax2
  10.4 0.1 shard_map.79
  10.5 1.0 %collective-permute-start.4 = (bf16[160,128]{1,0:T(8,128)(2,1)S(1)}, bf16[160,128]{1,0:T(8,128)(2,1)S(1)}, u32[]{:S(2)}, u32[]{:S(2)}) collective-permute-start(bf16[160,128]{1,0:T(8,128)(2,1)S(1)} %get-tuple-element.24), channel_id=1, source_target_pairs={{0,6},{2,4},{4,2},{6,0},{1,7},{3,5},{5,3},{7,1},{8,14},{10,12},{12... | collective-permute-start | bytes 122888 | tf_op jit(solution)/shard_map/ppermute | solution.py:519
  11.5 1.1 %collective-permute-start.5 = (bf16[160,128]{1,0:T(8,128)(2,1)S(1)}, bf16[160,128]{1,0:T(8,128)(2,1)S(1)}, u32[]{:S(2)}, u32[]{:S(2)}) collective-permute-start(bf16[160,128]{1,0:T(8,128)(2,1)S(1)} %get-tuple-element.25), channel_id=1, source_target_pairs={{0,2},{2,0},{4,6},{6,4},{1,3},{3,1},{5,7},{7,5},{8,10},{10,8},{12,... | collective-permute-start | bytes 122888 | tf_op jit(solution)/shard_map/ppermute | solution.py:519
  12.7 0.5 %shard_map.78 = (f32[3200,128]{1,0:T(8,128)S(1)}, bf16[256,256]{1,0:T(8,128)(2,1)S(1)}, bf16[2048,128]{1,0:T(8,128)(2,1)S(1)}, bf16[128,512]{1,0:T(8,128)(2,1)S(1)}) custom-call(f32[640,128]{1,0:T(8,128)S(1)} %get-tuple-element.18.home), custom_call_target="tpu_custom_call" | custom-call | tf_op jit(solution)/shard_map/pallas_call | solution.py:545
  13.2 0.2 collective-permute-done.2.az1
  13.4 1.2 %collective-permute-done.3.az2 = bf16[240,128]{1,0:T(8,128)(2,1)S(1)} collective-permute-done((bf16[240,128]{1,0:T(8,128)(2,1)S(1)}, bf16[240,128]{1,0:T(8,128)(2,1)S(1)}, u32[]{:S(2)}, u32[]{:S(2)}) %collective-permute-start.3) | collective-permute-done | bytes 61472 | tf_op jit(solution)/shard_map/ppermute | solution.py:519
  14.6 1.9 %collective-permute-done.4.corner1 = bf16[160,128]{1,0:T(8,128)(2,1)S(1)} collective-permute-done((bf16[160,128]{1,0:T(8,128)(2,1)S(1)}, bf16[160,128]{1,0:T(8,128)(2,1)S(1)}, u32[]{:S(2)}, u32[]{:S(2)}) %collective-permute-start.4) | collective-permute-done | bytes 40992 | tf_op jit(solution)/shard_map/ppermute | solution.py:519
  16.5 0.0 collective-permute-done.5.corner2
  16.5 0.7 %shard_map.80 = (f32[3200,128]{1,0:T(8,128)S(1)}, bf16[160,128]{1,0:T(8,128)(2,1)S(1)}) custom-call(f32[3200,128]{1,0:T(8,128)S(1)} %get-tuple-element.19.block_in, bf16[480,128]{1,0:T(8,128)(2,1)S(1)} %collective-permute-done.got1.ax1, bf16[480,128]{1,0:T(8,128)(2,1)S(1)} %collective-permute-done.1.got2.ax2, ...), custom_call_target="tpu_custom_call", output_to_operand_aliasing={{0}: (0, {})} | custom-call | tf_op jit(solution)/shard_map/pallas_call | solution.py:558
  17.2 1.6 %collective-permute-start.6 = (bf16[160,128]{1,0:T(8,128)(2,1)S(1)}, bf16[160,128]{1,0:T(8,128)(2,1)S(1)}, u32[]{:S(2)}, u32[]{:S(2)}) collective-permute-start(bf16[160,128]{1,0:T(8,128)(2,1)S(1)} %get-tuple-element.29), channel_id=1, source_target_pairs={{0,1},{1,0},{2,3},{3,2},{4,5},{5,4},{6,7},{7,6},{8,9},{9,8},{10,11... | collective-permute-start | bytes 122888 | tf_op jit(solution)/shard_map/ppermute | solution.py:572
  18.8 2.5 %collective-permute-done.6.refs_0_ = bf16[160,128]{1,0:T(8,128)(2,1)S(1)} collective-permute-done((bf16[160,128]{1,0:T(8,128)(2,1)S(1)}, bf16[160,128]{1,0:T(8,128)(2,1)S(1)}, u32[]{:S(2)}, u32[]{:S(2)}) %collective-permute-start.6) | collective-permute-done | bytes 40992 | tf_op jit(solution)/shard_map/ppermute | solution.py:572
  21.3 4.9 %shard_map.81 = (f32[32,1,128]{2,1,0:T(1,128)}, f32[5,12,40,128]{3,2,1,0:T(8,128)S(1)}, f32[5,8,32,128]{3,2,1,0:T(8,128)S(1)}) custom-call(f32[5,20,32,128]{3,2,1,0:T(8,128)S(1)} %bitcast.5, bf16[256,256]{1,0:T(8,128)(2,1)S(1)} %get-tuple-element.28.banded, s32[32]{0:T(128)} %cells_far.1, bf16[160,128]{1,0:T(8,128)(2,1)S(1)} %collective-permute-done.6.refs_0_, ...), custom_call_target="tpu_custom_call" | custom-call | tf_op jit(solution)/shard_map/pallas_call | solution.py:578
  26.2 0.0 copy-start
  26.2 0.0 copy-start.1
  26.2 4.7 %all-to-all-start = ((f32[32,1,128]{2,1,0:T(1,128)}), f32[32,1,128]{2,1,0:T(1,128)S(1)}, u32[]{:S(2)}, u32[]{:S(2)}) async-start(f32[32,1,128]{2,1,0:T(1,128)} %get-tuple-element.33), calls=%async_computation | async-start | bytes 32768 | tf_op jit(solution)/shard_map/all_to_all | solution.py:589
  30.9 1.8 %shard_map.82 = f32[5,8,16,128]{3,2,1,0:T(8,128)} custom-call(f32[5,12,40,128]{3,2,1,0:T(8,128)S(1)} %get-tuple-element.31.u2, f32[5,8,32,128]{3,2,1,0:T(8,128)S(1)} %get-tuple-element.32.u0, bf16[256,256]{1,0:T(8,128)(2,1)S(1)} %get-tuple-element.28.banded), custom_call_target="tpu_custom_call" | custom-call | flops 400000000 | bytes 8000000 | tf_op jit(solution)/shard_map/pallas_call | solution.py:592
  32.6 5.3 %all-to-all-done = f32[32,1,128]{2,1,0:T(1,128)S(1)} async-done(((f32[32,1,128]{2,1,0:T(1,128)}), f32[32,1,128]{2,1,0:T(1,128)S(1)}, u32[]{:S(2)}, u32[]{:S(2)}) %all-to-all-start) | async-done | bytes 16416 | tf_op jit(solution)/shard_map/all_to_all | solution.py:589
  37.9 0.0 copy-done
  37.9 0.0 copy-done.1
  37.9 1.2 %shard_map.83 = f32[256,128]{1,0:T(8,128)} custom-call(f32[32,128]{1,0:T(8,128)S(1)} %bitcast.6, s32[1,32]{1,0:T(1,128)S(1)} %copy-done.1, bf16[256,1024]{1,0:T(8,128)(2,1)S(1)} %copy-done), custom_call_target="tpu_custom_call" | custom-call | tf_op jit(solution)/shard_map/pallas_call | solution.py:600
Async XLA Ops:
  1.7 8.7 %collective-permute-start = (bf16[480,128]{1,0:T(8,128)(2,1)S(1)}, bf16[480,128]{1,0:T(8,128)(2,1)S(1)}, u32[]{:S(2)}, u32[]{:S(2)}) collective-permute-start(bf16[480,128]{1,0:T(8,128)(2,1)S(1)} %get-tuple-element.20), channel_id=1, source_target_pairs={{0,0},{8,16},{16,8},{24,24},{1,1},{9,17},{17,9},{25,25},{2,2},{10,... | collective-permute-start | bytes 368648 | tf_op jit(solution)/shard_map/ppermute | solution.py:519
  2.4 8.0 %collective-permute-start.1 = (bf16[480,128]{1,0:T(8,128)(2,1)S(1)}, bf16[480,128]{1,0:T(8,128)(2,1)S(1)}, u32[]{:S(2)}, u32[]{:S(2)}) collective-permute-start(bf16[480,128]{1,0:T(8,128)(2,1)S(1)} %get-tuple-element.21), channel_id=1, source_target_pairs={{0,8},{8,0},{16,24},{24,16},{1,9},{9,1},{17,25},{25,17},{2,10},{10... | collective-permute-start | bytes 368648 | tf_op jit(solution)/shard_map/ppermute | solution.py:519
  6.8 6.6 %collective-permute-start.2 = (bf16[240,128]{1,0:T(8,128)(2,1)S(1)}, bf16[240,128]{1,0:T(8,128)(2,1)S(1)}, u32[]{:S(2)}, u32[]{:S(2)}) collective-permute-start(bf16[240,128]{1,0:T(8,128)(2,1)S(1)} %get-tuple-element.22), channel_id=1, source_target_pairs={{0,6},{2,4},{4,2},{6,0},{1,7},{3,5},{5,3},{7,1},{8,14},{10,12},{12... | collective-permute-start | bytes 184328 | tf_op jit(solution)/shard_map/ppermute | solution.py:519
  10.4 4.2 %collective-permute-start.3 = (bf16[240,128]{1,0:T(8,128)(2,1)S(1)}, bf16[240,128]{1,0:T(8,128)(2,1)S(1)}, u32[]{:S(2)}, u32[]{:S(2)}) collective-permute-start(bf16[240,128]{1,0:T(8,128)(2,1)S(1)} %get-tuple-element.23), channel_id=1, source_target_pairs={{0,2},{2,0},{4,6},{6,4},{1,3},{3,1},{5,7},{7,5},{8,10},{10,8},{12,... | collective-permute-start | bytes 184328 | tf_op jit(solution)/shard_map/ppermute | solution.py:519
  10.5 6.0 %collective-permute-start.4 = (bf16[160,128]{1,0:T(8,128)(2,1)S(1)}, bf16[160,128]{1,0:T(8,128)(2,1)S(1)}, u32[]{:S(2)}, u32[]{:S(2)}) collective-permute-start(bf16[160,128]{1,0:T(8,128)(2,1)S(1)} %get-tuple-element.24), channel_id=1, source_target_pairs={{0,6},{2,4},{4,2},{6,0},{1,7},{3,5},{5,3},{7,1},{8,14},{10,12},{12... | collective-permute-start | bytes 122888 | tf_op jit(solution)/shard_map/ppermute | solution.py:519
  11.5 5.0 %collective-permute-start.5 = (bf16[160,128]{1,0:T(8,128)(2,1)S(1)}, bf16[160,128]{1,0:T(8,128)(2,1)S(1)}, u32[]{:S(2)}, u32[]{:S(2)}) collective-permute-start(bf16[160,128]{1,0:T(8,128)(2,1)S(1)} %get-tuple-element.25), channel_id=1, source_target_pairs={{0,2},{2,0},{4,6},{6,4},{1,3},{3,1},{5,7},{7,5},{8,10},{10,8},{12,... | collective-permute-start | bytes 122888 | tf_op jit(solution)/shard_map/ppermute | solution.py:519
  17.2 4.1 %collective-permute-start.6 = (bf16[160,128]{1,0:T(8,128)(2,1)S(1)}, bf16[160,128]{1,0:T(8,128)(2,1)S(1)}, u32[]{:S(2)}, u32[]{:S(2)}) collective-permute-start(bf16[160,128]{1,0:T(8,128)(2,1)S(1)} %get-tuple-element.29), channel_id=1, source_target_pairs={{0,1},{1,0},{2,3},{3,2},{4,5},{5,4},{6,7},{7,6},{8,9},{9,8},{10,11... | collective-permute-start | bytes 122888 | tf_op jit(solution)/shard_map/ppermute | solution.py:572
  26.2 11.8 %copy-start = (bf16[256,1024]{1,0:T(8,128)(2,1)S(1)}, bf16[256,1024]{1,0:T(8,128)(2,1)}, u32[]{:S(2)}) copy-start(bf16[256,1024]{1,0:T(8,128)(2,1)} %weight.1) | copy-start | bytes 1572868
  26.2 11.7 %copy-start.1 = (s32[1,32]{1,0:T(1,128)S(1)}, s32[1,32]{1,0:T(1,128)}, u32[]{:S(2)}) copy-start(s32[1,32]{1,0:T(1,128)} %offsets.1) | copy-start | bytes 388
  26.2 11.7 %all-to-all-start = ((f32[32,1,128]{2,1,0:T(1,128)}), f32[32,1,128]{2,1,0:T(1,128)S(1)}, u32[]{:S(2)}, u32[]{:S(2)}) async-start(f32[32,1,128]{2,1,0:T(1,128)} %get-tuple-element.33), calls=%async_computation | async-start | bytes 32768 | tf_op jit(solution)/shard_map/all_to_all | solution.py:589

commit v10 on v9

--- a/solution.py
+++ b/solution.py
@@ -11,8 +11,8 @@
 GAMMA_M = 0.4
 LAMBDA = 0.1
 P_REF = 1.0
-REACH = 6
-MID = 4
+REACH = 4
+MID = 2
 SCALE = -LAMBDA / 12.0
 ROWS = 32
 OFF = 8
@@ -57,7 +57,7 @@
 
 
 def first_is_up(axis):
-    return lax.axis_index("core" if axis == "ax" else axis) % 2 == 1
+    return lax.axis_index("core" if axis == "ax" else axis) % 2 == 0
 
 
 def load_and_pack(ca, cz, den, vel, pre, home, ax1, ax2, az1, az2, sems):
@@ -100,7 +100,7 @@
     return lo, hi
 
 
-def pack_corners(n_ax, cz, got1, got2, first_out, second_out, near):
+def pack_corners(n_ax, cz, got1, got2, first_out, second_out, near, strips):
     up = first_is_up("az")
     half = MID * cz
     size = REACH * cz
@@ -108,12 +108,13 @@
         lo, hi = ax_sides(n_ax, got1, got2, slice(f * size, (f + 1) * size))
         near[f, 0:half, :] = lo[size - half :]
         near[f, half : 2 * half, :] = hi[0:half]
-    low, high = [], []
+    strips[...] = jnp.zeros_like(strips)
     for f in range(5):
         for d in range(MID):
-            low.append(near[f, pl.ds(d, 2 * MID, stride=cz), :])
-            high.append(near[f, pl.ds(cz - 1 - d, 2 * MID, stride=cz), :])
-    low, high = jnp.concatenate(low, axis=0), jnp.concatenate(high, axis=0)
+            at = (f * MID + d) * 2 * MID
+            strips[0, at : at + 2 * MID, :] = near[f, pl.ds(d, 2 * MID, stride=cz), :]
+            strips[1, at : at + 2 * MID, :] = near[f, pl.ds(cz - 1 - d, 2 * MID, stride=cz), :]
+    low, high = strips[0], strips[1]
     first_out[...] = jnp.where(up, high, low).astype(BF16)
     second_out[...] = jnp.where(up, low, high).astype(BF16)
 
@@ -128,6 +129,7 @@
 def prepare(ends, ca, cz, n_rad, home, block, banded, *tables):
     cr = home.shape[1]
     rad = lax.axis_index("rad")
+    block[...] = jnp.zeros_like(block)
     for f in range(5):
         for k in range(ca):
             spread_rows(ca + 2 * REACH, cz, f, REACH + k, home, (f * ca + k) * cz, block)
@@ -189,13 +191,18 @@
                     got = corners[side, pl.ds(start + MID, MID), :]
                     block[pl.ds(at + (REACH + ca) * ROWS, MID, stride=ROWS), :] = got
 
-    tiles = cr // SLOT
+    starts = [(f * planes + REACH - MID) * ROWS for f in range(5)]
+    send_edges(block, starts, (ca + 2 * MID) * ROWS, edges, outs)
+
+
+def send_edges(ref, starts, count, edges, outs):
+    tiles = ref.shape[1] // SLOT
     step = tiles * 8
     rows = []
-    for f in range(5):
-        for k in range((ca + 2 * MID) * ROWS // step):
-            at = (f * planes + REACH - MID) * ROWS + k * step
-            rows.append(jnp.concatenate([block[at + 8 * t : at + 8 * t + 8, :] for t in range(tiles)], axis=1))
+    for start in starts:
+        for at in range(start, start + count, step):
+            rows.append(jnp.concatenate([ref[at + 8 * t : at + 8 * t + 8, :] for t in range(tiles)], axis=1))
+    rows += [jnp.zeros_like(rows[0])] * (outs[0].shape[0] // 8 - len(rows))
     rows = jnp.concatenate(rows, axis=0).astype(BF16)
     for edge, out in zip(edges, outs):
         out[...] = jnp.dot(rows, edge[...], preferred_element_type=F32).astype(BF16)
@@ -205,6 +212,8 @@
     v = [flux[8 * l : 8 * l + 8] for l in range(4)]
     v = [pltpu.roll(v[2], 1, 0), pltpu.roll(v[3], 1, 0)] + v + [pltpu.roll(v[0], 7, 0), pltpu.roll(v[1], 7, 0)]
     out = [8.0 * (v[l + 3] - v[l + 1]) - (v[l + 4] - v[l]) for l in range(4)]
+    if flux.shape[0] == ROWS:
+        return jnp.concatenate(out, axis=0)
     side = flux[ROWS:]
     lanes = side.shape[1]
     span = lax.broadcasted_iota(jnp.int32, side.shape, 1) // SPAN
@@ -255,35 +264,47 @@
         fax[f, j, 0:ROWS] = got[f]
 
 
-def both_sides(us, js, fax, part, banded):
-    rows = []
-    shape = (ROWS, banded.shape[0] // 2)
+def radial_terms(homes, sides, banded):
+    shape = homes[0].shape
     span = lax.broadcasted_iota(jnp.int32, shape, 1) // SPAN
     mine = span == lax.broadcasted_iota(jnp.int32, shape, 0) // 8
-    for u, j in zip(us, js):
-        got = flux(0, *u)
-        for f in range(5):
-            fax[f, j] = got[f]
-        got = flux(2, *u)
-        for f in range(5):
-            side = jnp.where(mine, jnp.concatenate([got[f][ROWS:]] * 4, axis=0), 0.0)
-            rows.append(jnp.concatenate([got[f][0:ROWS], side], axis=1))
+    rows = []
+    for home, side in zip(homes, sides):
+        side = jnp.where(mine, jnp.concatenate([side] * 4, axis=0), 0.0)
+        rows.append(jnp.concatenate([home, side], axis=1))
     rows = jnp.concatenate(rows, axis=0)
     coarse = rows.astype(BF16)
     fine = (rows - coarse.astype(F32)).astype(BF16)
     matrix = banded[...]
     out = jnp.dot(coarse, matrix, preferred_element_type=F32)
     out = out + jnp.dot(fine, matrix, preferred_element_type=F32)
-    half = out.shape[1] // 2
+    got = []
+    for i in range(len(homes)):
+        at, half = i * ROWS, shape[1]
+        side = out[at : at + 8, half:]
+        for l in range(1, 4):
+            side = jnp.where(span[0:8] == l, out[at + 8 * l : at + 8 * l + 8, half:], side)
+        got.append((out[at : at + ROWS, 0:half], side))
+    return got
+
+
+def both_sides(us, js, fax, part, banded, height=TALL):
+    homes, sides = [], []
+    for u, j in zip(us, js):
+        got = flux(0, *u)
+        for f in range(5):
+            fax[f, j, 0:height] = got[f][0:height]
+        for x in flux(2, *u):
+            homes.append(x[0:ROWS])
+            sides.append(x[ROWS:])
+    radial = radial_terms(homes, sides, banded)
     for i, (u, j) in enumerate(zip(us, js)):
         got = flux(1, *u)
         for f in range(5):
-            at = (i * 5 + f) * ROWS
-            side = out[at : at + 8, half:]
-            for l in range(1, 4):
-                side = jnp.where(span[0:8] == l, out[at + 8 * l : at + 8 * l + 8, half:], side)
-            radial = jnp.concatenate([out[at : at + ROWS, 0:half], side], axis=0)
-            part[f, j] = az_terms(got[f]) + radial
+            home, side = radial[i * 5 + f]
+            if height > ROWS:
+                home = jnp.concatenate([home, side], axis=0)
+            part[f, j, 0:height] = az_terms(got[f][0:height]) + home
 
 
 def change(fa, part, f, j, size):
@@ -351,12 +372,12 @@
     def note(s, j, u):
         value[s, j] = (u[2] - P_REF + u[0][0])[0:ROWS]
 
-    for j in (low - 6, low - 5, high + 4, high + 5):
+    for j in (low - 4, low - 3, high + 2, high + 3):
         ax_only(start_state(j, False)[1], fax, j)
 
-    @pl.loop(0, (ca + 8) // STEP)
+    @pl.loop(0, (ca + 4) // STEP)
     def _(i):
-        js = [low - 4 + STEP * i + k for k in range(STEP)]
+        js = [low - 2 + STEP * i + k for k in range(STEP)]
         us = []
         for j in js:
             rho, u = start_state(j, True)
@@ -369,7 +390,7 @@
     def update(f, j, fa, stage):
         a = max(low - j, j - (high - 1), 0)
         a = (a + 1) // 2
-        lim = 2 - stage
+        lim = 1 - stage
         base = jnp.where(f == 0, 1.0, 0.0)
         size = ROWS if a == lim else TALL
         new = change(fa, part, f, j, size)
@@ -392,40 +413,35 @@
     @pl.loop(0, 5)
     def _(f):
         fa = window(fax, f)
-        for j in range(low - 4, high + 4):
+        for j in range(low - 2, high + 2):
             home, side = update(f, j, fa, 0)
             second[f, j, 0:ROWS] = home
             if side is not None:
                 second[f, j, ROWS:] = side
 
-    for j in (low - 4, low - 3, high + 2, high + 3):
+    for j in (low - 2, low - 1, high, high + 1):
         ax_only(split_state([second[f, j, 0:ROWS] for f in range(5)]), fax, j)
 
-    @pl.loop(0, (ca + 4) // STEP)
+    @pl.loop(0, ca // STEP)
     def _(i):
-        js = [low - 2 + STEP * i + k for k in range(STEP)]
+        js = [low + STEP * i + k for k in range(STEP)]
         us = []
         for j in js:
             u = split_state([second[f, j] for f in range(5)])
             note(1, j, u)
             us.append(u)
-        both_sides(us, js, fax, part, banded)
+        both_sides(us, js, fax, part, banded, ROWS)
 
     @pl.loop(0, 5)
     def _(f):
         fa = window(fax, f)
-        for j in range(low - 2, high + 2):
-            home, side = update(f, j, fa, 1)
-            u2_out[f, j - (low - 2), 0:ROWS] = home
-            if side is not None:
-                u2_out[f, j - (low - 2), ROWS:] = side
         for j in range(low, high):
+            u2_out[f, j - low] = update(f, j, fa, 1)[0]
             u0_out[f, j - low] = first[f, j, 0:ROWS]
 
     @pl.loop(0, ca)
     def _(i):
-        u = split_state([u2_out[f, i + 2, 0:ROWS] for f in range(5)])
-        note(2, low + i, u)
+        note(2, low + i, split_state([u2_out[f, i] for f in range(5)]))
 
     fetch.wait()
     picked[...] = jnp.zeros_like(picked)
@@ -450,24 +466,103 @@
     q_out[...] = jnp.broadcast_to(q[0:1][None], q_out.shape)
 
 
-def last_stage(ca, cz, u2, u0, banded, state, fax, part):
-    for j in (0, 1, ca + 2, ca + 3):
-        ax_only(split_state([u2[f, j, 0:ROWS] for f in range(5)]), fax, j)
+def edge_fluxes(count, ca, cz, u2, *refs):
+    edges, (ax1, ax2, az1, az2), rads = refs[:count], refs[count : count + 4], refs[count + 4 : 2 * count + 4]
+    fax, faz, frad, strips = refs[2 * count + 4 :]
+    cr = u2.shape[-1]
+    first, quarter = OFF // 4, cz // 4
+
+    @pl.loop(0, ca)
+    def _(k):
+        u = split_state([u2[f, k] for f in range(5)])
+        for d, ref in ((0, fax), (1, faz), (2, frad)):
+            for f, x in enumerate(flux(d, *u)):
+                ref[pl.ds(pl.multiple_of((f * ca + k) * ROWS, ROWS), ROWS), :] = x
+
+    for f in range(5):
+        for d in range(MID):
+            for side, k in ((0, d), (1, ca - MID + d)):
+                for l in range(4):
+                    row = (f * ca + k) * ROWS + 8 * l + first
+                    at = ((f * MID + d) * 4 + l) * quarter
+                    strips[side, at : at + quarter, :] = fax[row : row + quarter, :]
+    up = first_is_up("ax")
+    ax1[...] = jnp.where(up, strips[1], strips[0]).astype(BF16)
+    ax2[...] = jnp.where(up, strips[0], strips[1]).astype(BF16)
+    low, high = [], []
+    for f in range(5):
+        for d in range(MID):
+            low.append(faz[pl.ds(f * ca * ROWS + kept(OFF + d), ca, stride=ROWS), :])
+            high.append(faz[pl.ds(f * ca * ROWS + kept(OFF + cz - 1 - d), ca, stride=ROWS), :])
+    low, high = jnp.concatenate(low, axis=0), jnp.concatenate(high, axis=0)
+    up = first_is_up("az")
+    az1[...] = jnp.where(up, high, low).astype(BF16)
+    az2[...] = jnp.where(up, low, high).astype(BF16)
+    send_edges(frad, [f * ca * ROWS for f in range(5)], ca * ROWS, edges, rads)
+
+
+def last_stage(n_ax, count, ca, cz, faz_in, u2, u0, fax, frad, banded, ax1, ax2, az1, az2, *refs):
+    rads, places = refs[:count], refs[count : 2 * count]
+    faz, state, part, beyond, strips, sides = refs[2 * count :]
+    cr = u2.shape[-1]
+    first, quarter = OFF // 4, cz // 4
+
+    lo, hi = ax_sides(n_ax, ax1, ax2, slice(0, ax1.shape[0]))
+    strips[0, 0 : lo.shape[0], :] = lo
+    strips[1, 0 : hi.shape[0], :] = hi
+    for f in range(5):
+        for d in range(MID):
+            for side in range(2):
+                for l in range(4):
+                    at = ((f * MID + d) * 4 + l) * quarter
+                    row = 8 * l + first
+                    beyond[f, side * MID + d, row : row + quarter] = strips[side, at : at + quarter, :]
+    up = first_is_up("az")
+    a, b = az1[...].astype(F32), az2[...].astype(F32)
+    strips[0, 0 : a.shape[0], :] = jnp.where(up, b, a)
+    strips[1, 0 : a.shape[0], :] = jnp.where(up, a, b)
+    for f in range(5):
+        for d in range(MID):
+            for side, row in ((0, OFF - 1 - d), (1, OFF + cz + d)):
+                got = strips[side, pl.ds((f * MID + d) * ca, ca), :]
+                faz[pl.ds(f * ca * ROWS + kept(row), ca, stride=ROWS), :] = got
+    packed = 0.0
+    for got, place in zip(rads, places):
+        packed = packed + jnp.dot(got[...], place[...], preferred_element_type=F32)
+    group = packed.shape[1] // cr
+    for f in range(5):
+        for k in range(ca):
+            at = (f * (ca // group) + k // group) * 8
+            sides[f, k] = packed[at : at + 8, k % group * cr : (k % group + 1) * cr]
 
     @pl.loop(0, ca // STEP)
     def _(i):
-        js = [2 + STEP * i + k for k in range(STEP)]
-        us = [split_state([u2[f, j] for f in range(5)]) for j in js]
-        both_sides(us, js, fax, part, banded)
-
-    first, quarter = OFF // 4, cz // 4
+        ks = [STEP * i + k for k in range(STEP)]
+
+        def plane(ref, f, k):
+            return ref[pl.ds(pl.multiple_of((f * ca + k) * ROWS, ROWS), ROWS), :]
+
+        radial = radial_terms(
+            [plane(frad, f, k) for k in ks for f in range(5)],
+            [sides[f, k] for k in ks for f in range(5)],
+            banded,
+        )
+        for n, k in enumerate(ks):
+            for f in range(5):
+                part[f, k] = az_terms(plane(faz, f, k)) + radial[n * 5 + f][0]
 
     @pl.loop(0, 5)
     def _(f):
-        fa = window(fax, f)
+        def plane(k):
+            if k < 0:
+                return beyond[f, MID + k]
+            if k >= ca:
+                return beyond[f, MID + k - ca]
+            return fax[pl.ds(pl.multiple_of((f * ca + k) * ROWS, ROWS), ROWS), :]
+
+        held = {k: plane(k) for k in range(-MID, ca + MID)}
         for k in range(ca):
-            j = k + 2
-            new = u2[f, j, 0:ROWS] + change(fa, part, f, j, ROWS)
+            new = u2[f, k] + change(held.get, part, f, k, ROWS)
             new = u0[f, k] * (1.0 / 3.0) + (2.0 / 3.0) * new
             for l in range(4):
                 state[f, k, pl.ds(l, quarter, stride=4), :] = new[8 * l + first : 8 * l + first + quarter]
@@ -504,11 +599,12 @@
 
 
 def swap_pairs(count, periodic):
-    one = []
+    one = [(i, i ^ 1) for i in range(count)]
+    two = []
     for i in range(count):
         j = i - 1 if i % 2 == 0 else i + 1
-        one.append((i, j % count if periodic or 0 <= j < count else i))
-    return one, [(i, i ^ 1) for i in range(count)]
+        two.append((i, j % count if periodic or 0 <= j < count else i))
+    return one, two
 
 
 def swap(first, second, axis, periodic):
@@ -517,6 +613,15 @@
         count = count * lax.axis_size(name)
     one, two = swap_pairs(count, periodic)
     return lax.ppermute(first, axis, one), lax.ppermute(second, axis, two)
+
+
+def radial_exchange(messages):
+    n_rad = lax.axis_size("rad")
+    if n_rad == 2:
+        return (lax.ppermute(messages[0], "rad", [(0, 1), (1, 0)]),)
+    up = [(i, i + 1) for i in range(n_rad - 1)]
+    down = [(j, i) for i, j in up]
+    return (lax.ppermute(messages[0], "rad", down), lax.ppermute(messages[1], "rad", up))
 
 
 def local(density, velocity, pressure, panel_cell, obs_weight, bin_offset):
@@ -549,12 +654,17 @@
     )(home)
     edges, places = tables[: len(ends)], tables[len(ends) :]
 
-    corner = struct((5 * MID * 2 * MID, cr), BF16)
+    corner = struct((-(-5 * MID * 2 * MID // 16) * 16, cr), BF16)
     near = pltpu.VMEM((5, 2 * MID * cz, cr), F32)
-    corner1, corner2 = call(part(pack_corners, n_ax, cz), (corner, corner), [VMEM] * 2, [near])(ax1, ax2)
+    corner1, corner2 = call(
+        part(pack_corners, n_ax, cz),
+        (corner, corner),
+        [VMEM] * 2,
+        [near, pltpu.VMEM((2,) + corner.shape, F32)],
+    )(ax1, ax2)
     corner1, corner2 = swap(corner1, corner2, "az", True)
 
-    side = struct((5 * (ca + 2 * MID) * ROWS // tiles, cr), BF16)
+    side = struct((-(-5 * (ca + 2 * MID) * ROWS // tiles // 16) * 16, cr), BF16)
     got = call(
         part(assemble, n_ax, len(ends), ca, cz),
         (grid,) + tuple(side for _ in ends),
@@ -568,16 +678,12 @@
         alias={0: 0},
     )(block, ax1, ax2, az1, az2, corner1, corner2, *edges)
     block = got[0].reshape(5, planes, ROWS, cr)
-    if n_rad == 2:
-        sides = (lax.ppermute(got[1], "rad", [(0, 1), (1, 0)]),)
-    else:
-        up = [(i, i + 1) for i in range(n_rad - 1)]
-        sides = (lax.ppermute(got[1], "rad", [(j, i) for i, j in up]), lax.ppermute(got[2], "rad", up))
+    sides = radial_exchange(got[1:])
 
     grid = (5, planes, TALL, cr)
     q, u2, u0 = call(
         part(stages, n_ax, n_rad, ca, cz, slots),
-        (struct((ndev, 1, 128)), struct((5, ca + 4, TALL, cr)), struct((5, ca, ROWS, cr))),
+        (struct((ndev, 1, 128)), struct((5, ca, ROWS, cr)), struct((5, ca, ROWS, cr))),
         [VMEM, VMEM, HBM] + [VMEM] * (2 * len(sides)),
         [pltpu.VMEM((5, ca + 2 * MID, 8, cr), F32)]
         + [pltpu.VMEM(grid, F32) for _ in range(4)]
@@ -588,15 +694,34 @@
 
     rows = lax.all_to_all(q, ("y", "core", "az", "rad"), 0, 0, tiled=True).reshape(ndev, 128)
 
-    grid = (5, ca + 4, TALL, cr)
-    state = call(
-        part(last_stage, ca, cz),
-        struct((5, ca, cz, cr)),
-        [VMEM] * 3,
-        [pltpu.VMEM(grid, F32), pltpu.VMEM(grid, F32)],
+    edge = struct((5 * MID * cz, cr), BF16)
+    strip = struct((5 * MID * ca, cr), BF16)
+    side = struct((5 * ca * ROWS // tiles, cr), BF16)
+    grid = struct((5 * ca * ROWS, cr))
+    strips = pltpu.VMEM((2,) + edge.shape, F32)
+    ax1, ax2, az1, az2, *rads, fax, faz, frad = call(
+        part(edge_fluxes, len(ends), ca, cz),
+        (edge, edge, strip, strip) + tuple(side for _ in ends) + (grid,) * 3,
+        [VMEM] * (1 + len(ends)),
+        [strips],
+        cost=pl.CostEstimate(flops=400_000_000, bytes_accessed=8_000_000, transcendentals=0),
+    )(u2, *edges)
+    ax1, ax2 = swap(ax1, ax2, ("y", "core"), False)
+    az1, az2 = swap(az1, az2, "az", True)
+    rads = radial_exchange(rads)
+    _, state = call(
+        part(last_stage, n_ax, len(ends), ca, cz),
+        (grid, struct((5, ca, cz, cr))),
+        [VMEM] * (10 + 2 * len(ends)),
+        [
+            pltpu.VMEM((5, ca, ROWS, cr), F32),
+            pltpu.VMEM((5, 2 * MID, ROWS, cr), F32),
+            strips,
+            pltpu.VMEM((5, ca, 8, cr), F32),
+        ],
         mib=12,
-        cost=pl.CostEstimate(flops=400_000_000, bytes_accessed=8_000_000, transcendentals=0),
-    )(u2, u0, banded)
+        alias={0: 0},
+    )(faz, u2, u0, fax, frad, banded, ax1, ax2, az1, az2, *rads, *places)
     signal = call(
         part(signals, slots), struct((obs_weight.shape[0], NB)), [VMEM] * 3, mib=24
     )(rows, bin_offset, obs_weight)

time: 39.3 us -> 46.7 us (1.19)
  starting transfers between devices: 17.1 us -> 23.2 us
  local copies, waits for them, and re-layouts: 0.01 us -> 3.49 us
  waiting for transfers between devices: 11.2 us -> 8.76 us
    unnamed x4 -> x12, local copies, waits for them, and re-layouts: 0.01 us -> 3.49 us
    all_to_all x1, waiting for transfers between devices: 5.27 us -> 2 us  [local(): lax.all_to_all(q, ('y', 'core', 'az', 'rad'), 0, 0, tiled=True)]
    ppermute x6 -> x10, starting transfers between devices: 10.8 us -> 13.7 us  [swap(): return (lax.ppermute(first, axis, one), lax.ppermute(second, axis, two))]
    pallas_call x2 -> x3, Pallas kernels: 1.88 us -> 3.82 us  [the longest x1 2.69 us: local(): call(part(last_stage, n_ax, len(ends), ca, cz), (grid, struct((5, ca, cz,...]
    all_to_all x1, starting transfers between devices: 4.68 us -> 6.38 us  [local(): lax.all_to_all(q, ('y', 'core', 'az', 'rad'), 0, 0, tiled=True)]
    pallas_call x1, Pallas kernels: 4.87 us -> 3.18 us  [local(): call(part(stages, n_ax, n_rad, ca, cz, slots), (struct((ndev, 1, 128)), s...]
    ppermute x1 -> x2, starting transfers between devices: 1.56 us -> 3.04 us  [radial_exchange(): return (lax.ppermute(messages[0], 'rad', [(0, 1), (1, 0)]),)]
    ppermute x6 -> x10, waiting for transfers between devices: 3.37 us -> 4.04 us  [swap(): return (lax.ppermute(first, axis, one), lax.ppermute(second, axis, two))]
  transfers between devices with their start and end apart: 8 -> 13, of which waited for: 5 -> 5; matrix products, arithmetic and copies ran while one was open for 0% -> 0% of each run, Pallas kernels for 6% -> 4%
where the time goes in v10:
time: 46.7 us; the launch traced here: 46.4 us
  starting transfers between devices  23.2 us (50%)
  Pallas kernels  10.3 us (22%)
  waiting for transfers between devices  8.76 us (19%)
  local copies, waits for them, and re-layouts  3.49 us (7%)
  between operations  0.73 us (2%)
    ppermute x10, starting transfers between devices, swap(): return (lax.ppermute(first, axis, one), lax.ppermute(second, axis, two))  13.7 us
    all_to_all x1, starting transfers between devices, local(): lax.all_to_all(q, ('y', 'core', 'az', 'rad'), 0, 0, tiled=True)  6.38 us
    ppermute x10, waiting for transfers between devices, swap(): return (lax.ppermute(first, axis, one), lax.ppermute(second, axis, two))  4.04 us
    unnamed x12, local copies, waits for them, and re-layouts  3.49 us
    pallas_call x1, Pallas kernels, local(): call(part(stages, n_ax, n_rad, ca, cz, slots), (struct((ndev, 1, 128)), s...  3.18 us
    ppermute x2, starting transfers between devices, radial_exchange(): return (lax.ppermute(messages[0], 'rad', [(0, 1), (1, 0)]),)  3.04 us
    ppermute x2, waiting for transfers between devices, radial_exchange(): return (lax.ppermute(messages[0], 'rad', [(0, 1), (1, 0)]),)  2.72 us
    pallas_call x1, Pallas kernels, local(): call(part(last_stage, n_ax, len(ends), ca, cz), (grid, struct((5, ca, cz,...  2.69 us
  transfers between devices with their start and end apart: 13, of which 5 were waited for; matrix products, arithmetic and copies ran while one was open for 0% of the time, Pallas kernels for 4%

profile of v10, /device:TPU:0, one launch (start us, length us, event | category | flops | bytes accessed | tf_op | source)
XLA Modules:
  0.0 46.4 jit_solution(2890661759163060592)
XLA Ops:
  0.6 1.1 %shard_map.77 = (f32[640,128]{1,0:T(8,128)S(1)}, bf16[320,128]{1,0:T(8,128)(2,1)S(1)}, bf16[320,128]{1,0:T(8,128)(2,1)S(1)}, bf16[160,128]{1,0:T(8,128)(2,1)S(1)}, bf16[160,128]{1,0:T(8,128)(2,1)S(1)}) custom-call(f32[128,128]{1,0:T(8,128)} %bitcast.8, f32[384,128]{1,0:T(8,128)} %bitcast.7, f32[128,128]{1,0:T(8,128)} %bitcast.9), custom_call_target="tpu_custom_call" | custom-call | tf_op jit(solution)/shard_map/pallas_call | solution.py:638
  1.7 0.5 %collective-permute-start = (bf16[320,128]{1,0:T(8,128)(2,1)S(1)}, bf16[320,128]{1,0:T(8,128)(2,1)S(1)}, u32[]{:S(2)}, u32[]{:S(2)}) collective-permute-start(bf16[320,128]{1,0:T(8,128)(2,1)S(1)} %get-tuple-element.29), channel_id=1, source_target_pairs={{0,8},{8,0},{16,24},{24,16},{1,9},{9,1},{17,25},{25,17},{2,10},{10... | collective-permute-start | bytes 245768 | tf_op jit(solution)/shard_map/ppermute | solution.py:615
  2.2 0.7 %collective-permute-start.1 = (bf16[320,128]{1,0:T(8,128)(2,1)S(1)}, bf16[320,128]{1,0:T(8,128)(2,1)S(1)}, u32[]{:S(2)}, u32[]{:S(2)}) collective-permute-start(bf16[320,128]{1,0:T(8,128)(2,1)S(1)} %get-tuple-element.30), channel_id=1, source_target_pairs={{0,0},{8,16},{16,8},{24,24},{1,1},{9,17},{17,9},{25,25},{2,2},{10,... | collective-permute-start | bytes 245768 | tf_op jit(solution)/shard_map/ppermute | solution.py:615
  2.9 2.7 %collective-permute-start.2 = (bf16[160,128]{1,0:T(8,128)(2,1)S(1)}, bf16[160,128]{1,0:T(8,128)(2,1)S(1)}, u32[]{:S(2)}, u32[]{:S(2)}) collective-permute-start(bf16[160,128]{1,0:T(8,128)(2,1)S(1)} %get-tuple-element.31), channel_id=1, source_target_pairs={{0,2},{2,0},{4,6},{6,4},{1,3},{3,1},{5,7},{7,5},{8,10},{10,8},{12,... | collective-permute-start | bytes 122888 | tf_op jit(solution)/shard_map/ppermute | solution.py:615
  5.5 2.5 %collective-permute-start.3 = (bf16[160,128]{1,0:T(8,128)(2,1)S(1)}, bf16[160,128]{1,0:T(8,128)(2,1)S(1)}, u32[]{:S(2)}, u32[]{:S(2)}) collective-permute-start(bf16[160,128]{1,0:T(8,128)(2,1)S(1)} %get-tuple-element.32), channel_id=1, source_target_pairs={{0,6},{2,4},{4,2},{6,0},{1,7},{3,5},{5,3},{7,1},{8,14},{10,12},{12... | collective-permute-start | bytes 122888 | tf_op jit(solution)/shard_map/ppermute | solution.py:615
  8.0 0.0 collective-permute-done.got1.ax1
  8.0 0.0 collective-permute-done.1.got2.ax2
  8.0 0.1 shard_map.79
  8.1 0.7 %collective-permute-start.4 = (bf16[48,128]{1,0:T(8,128)(2,1)S(1)}, bf16[48,128]{1,0:T(8,128)(2,1)S(1)}, u32[]{:S(2)}, u32[]{:S(2)}) collective-permute-start(bf16[48,128]{1,0:T(8,128)(2,1)S(1)} %get-tuple-element.33), channel_id=1, source_target_pairs={{0,2},{2,0},{4,6},{6,4},{1,3},{3,1},{5,7},{7,5},{8,10},{10,8},{12,... | collective-permute-start | bytes 36872 | tf_op jit(solution)/shard_map/ppermute | solution.py:615
  8.8 0.9 %collective-permute-start.5 = (bf16[48,128]{1,0:T(8,128)(2,1)S(1)}, bf16[48,128]{1,0:T(8,128)(2,1)S(1)}, u32[]{:S(2)}, u32[]{:S(2)}) collective-permute-start(bf16[48,128]{1,0:T(8,128)(2,1)S(1)} %get-tuple-element.34), channel_id=1, source_target_pairs={{0,6},{2,4},{4,2},{6,0},{1,7},{3,5},{5,3},{7,1},{8,14},{10,12},{12... | collective-permute-start | bytes 36872 | tf_op jit(solution)/shard_map/ppermute | solution.py:615
  9.7 0.5 %shard_map.78 = (f32[2560,128]{1,0:T(8,128)S(1)}, bf16[256,256]{1,0:T(8,128)(2,1)S(1)}, bf16[2048,128]{1,0:T(8,128)(2,1)S(1)}, bf16[128,512]{1,0:T(8,128)(2,1)S(1)}) custom-call(f32[640,128]{1,0:T(8,128)S(1)} %get-tuple-element.27.home), custom_call_target="tpu_custom_call" | custom-call | tf_op jit(solution)/shard_map/pallas_call | solution.py:650
  10.3 0.0 collective-permute-done.2.az1
  10.3 1.0 %collective-permute-done.3.az2 = bf16[160,128]{1,0:T(8,128)(2,1)S(1)} collective-permute-done((bf16[160,128]{1,0:T(8,128)(2,1)S(1)}, bf16[160,128]{1,0:T(8,128)(2,1)S(1)}, u32[]{:S(2)}, u32[]{:S(2)}) %collective-permute-start.3) | collective-permute-done | bytes 40992 | tf_op jit(solution)/shard_map/ppermute | solution.py:615
  11.3 0.5 %collective-permute-done.4.corner1 = bf16[48,128]{1,0:T(8,128)(2,1)S(1)} collective-permute-done((bf16[48,128]{1,0:T(8,128)(2,1)S(1)}, bf16[48,128]{1,0:T(8,128)(2,1)S(1)}, u32[]{:S(2)}, u32[]{:S(2)}) %collective-permute-start.4) | collective-permute-done | bytes 12320 | tf_op jit(solution)/shard_map/ppermute | solution.py:615
  11.8 2.5 %collective-permute-done.5.corner2 = bf16[48,128]{1,0:T(8,128)(2,1)S(1)} collective-permute-done((bf16[48,128]{1,0:T(8,128)(2,1)S(1)}, bf16[48,128]{1,0:T(8,128)(2,1)S(1)}, u32[]{:S(2)}, u32[]{:S(2)}) %collective-permute-start.5) | collective-permute-done | bytes 12320 | tf_op jit(solution)/shard_map/ppermute | solution.py:615
  14.3 0.5 shard_map.80
  14.8 1.6 %collective-permute-start.6 = (bf16[128,128]{1,0:T(8,128)(2,1)S(1)}, bf16[128,128]{1,0:T(8,128)(2,1)S(1)}, u32[]{:S(2)}, u32[]{:S(2)}) collective-permute-start(bf16[128,128]{1,0:T(8,128)(2,1)S(1)} %get-tuple-element.38), channel_id=1, source_target_pairs={{0,1},{1,0},{2,3},{3,2},{4,5},{5,4},{6,7},{7,6},{8,9},{9,8},{10,11... | collective-permute-start | bytes 98312 | tf_op jit(solution)/shard_map/ppermute | solution.py:621
  16.4 2.7 %collective-permute-done.6.refs_0_ = bf16[128,128]{1,0:T(8,128)(2,1)S(1)} collective-permute-done((bf16[128,128]{1,0:T(8,128)(2,1)S(1)}, bf16[128,128]{1,0:T(8,128)(2,1)S(1)}, u32[]{:S(2)}, u32[]{:S(2)}) %collective-permute-start.6) | collective-permute-done | bytes 32800 | tf_op jit(solution)/shard_map/ppermute | solution.py:621
  19.1 3.2 %shard_map.81 = (f32[32,1,128]{2,1,0:T(1,128)S(1)}, f32[5,8,32,128]{3,2,1,0:T(8,128)S(1)}, f32[5,8,32,128]{3,2,1,0:T(8,128)S(1)}) custom-call(f32[5,16,32,128]{3,2,1,0:T(8,128)S(1)} %bitcast.5, bf16[256,256]{1,0:T(8,128)(2,1)S(1)} %get-tuple-element.37.banded, s32[32]{0:T(128)} %cells_far.1, bf16[128,128]{1,0:T(8,128)(2,1)S(1)} %collective-permute-done.6.refs_0_, ...), custom_call_target="tpu_custom_call" | custom-call | tf_op jit(solution)/shard_map/pallas_call | solution.py:684
  22.3 0.0 copy-start.1
  22.3 1.1 %shard_map.82 = (bf16[160,128]{1,0:T(8,128)(2,1)}, bf16[160,128]{1,0:T(8,128)(2,1)}, bf16[80,128]{1,0:T(8,128)(2,1)S(1)}, bf16[80,128]{1,0:T(8,128)(2,1)S(1)}, b...) custom-call(f32[5,8,32,128]{3,2,1,0:T(8,128)S(1)} %get-tuple-element.40, ...), custom_call_target="tpu_custom_call" | custom-call | flops 400000000 | bytes 8000000 | tf_op jit(solution)/shard_map/pallas_call | solution.py:702
  23.3 0.0 copy-start.3
  23.3 0.6 %copy-done.3 = bf16[80,128]{1,0:T(8,128)(2,1)} copy-done((bf16[80,128]{1,0:T(8,128)(2,1)}, bf16[80,128]{1,0:T(8,128)(2,1)S(1)}, u32[]{:S(2)}) %copy-start.3) | copy-done | bytes 20504
  23.9 0.0 copy-start.4
  23.9 0.6 %copy-done.4 = bf16[80,128]{1,0:T(8,128)(2,1)} copy-done((bf16[80,128]{1,0:T(8,128)(2,1)}, bf16[80,128]{1,0:T(8,128)(2,1)S(1)}, u32[]{:S(2)}) %copy-start.4) | copy-done | bytes 20504
  24.5 0.0 copy-start.5
  24.5 0.6 %copy-done.5 = bf16[80,128]{1,0:T(8,128)(2,1)} copy-done((bf16[80,128]{1,0:T(8,128)(2,1)}, bf16[80,128]{1,0:T(8,128)(2,1)S(1)}, u32[]{:S(2)}) %copy-start.5) | copy-done | bytes 20504
  25.1 0.1 collective-permute-start.7
  25.2 2.0 %collective-permute-start.8 = (bf16[160,128]{1,0:T(8,128)(2,1)}, bf16[160,128]{1,0:T(8,128)(2,1)}, u32[]{:S(2)}, u32[]{:S(2)}) collective-permute-start(bf16[160,128]{1,0:T(8,128)(2,1)} %get-tuple-element.46), channel_id=1, source_target_pairs={{0,0},{8,16},{16,8},{24,24},{1,1},{9,17},{17,9},{25,25},{2,2},{10,... | collective-permute-start | bytes 122888 | tf_op jit(solution)/shard_map/ppermute | solution.py:615
  27.2 0.0 copy-done.1
  27.2 6.4 %all-to-all-start = ((f32[32,1,128]{2,1,0:T(1,128)}), f32[32,1,128]{2,1,0:T(1,128)S(1)}, u32[]{:S(2)}, u32[]{:S(2)}) async-start(f32[32,1,128]{2,1,0:T(1,128)} %copy-done.1), calls=%async_computation | async-start | bytes 32768 | tf_op jit(solution)/shard_map/all_to_all | solution.py:695
  33.6 3.7 %collective-permute-start.10 = (bf16[80,128]{1,0:T(8,128)(2,1)}, bf16[80,128]{1,0:T(8,128)(2,1)}, u32[]{:S(2)}, u32[]{:S(2)}) collective-permute-start(bf16[80,128]{1,0:T(8,128)(2,1)} %copy-done.5), channel_id=1, source_target_pairs={{0,6},{2,4},{4,2},{6,0},{1,7},{3,5},{5,3},{7,1},{8,14},{10,12},{12... | collective-permute-start | bytes 61448 | tf_op jit(solution)/shard_map/ppermute | solution.py:615
  37.3 1.5 %collective-permute-start.11 = (bf16[80,128]{1,0:T(8,128)(2,1)}, bf16[80,128]{1,0:T(8,128)(2,1)}, u32[]{:S(2)}, u32[]{:S(2)}) collective-permute-start(bf16[80,128]{1,0:T(8,128)(2,1)} %copy-done.4), channel_id=1, source_target_pairs={{0,1},{1,0},{2,3},{3,2},{4,5},{5,4},{6,7},{7,6},{8,9},{9,8},{10,11... | collective-permute-start | bytes 61448 | tf_op jit(solution)/shard_map/ppermute | solution.py:621
  38.8 0.0 collective-permute-start.9
  38.8 2.0 %all-to-all-done = f32[32,1,128]{2,1,0:T(1,128)S(1)} async-done(((f32[32,1,128]{2,1,0:T(1,128)}), f32[32,1,128]{2,1,0:T(1,128)S(1)}, u32[]{:S(2)}, u32[]{:S(2)}) %all-to-all-start) | async-done | bytes 16416 | tf_op jit(solution)/shard_map/all_to_all | solution.py:695
  40.8 0.0 copy-start
  40.8 1.0 %copy-done = bf16[256,1024]{1,0:T(8,128)(2,1)S(1)} copy-done((bf16[256,1024]{1,0:T(8,128)(2,1)S(1)}, bf16[256,1024]{1,0:T(8,128)(2,1)}, u32[]{:S(2)}) %copy-start) | copy-done | bytes 524312
  41.8 0.0 copy-start.2
  41.8 0.7 %copy-done.2 = s32[1,32]{1,0:T(1,128)S(1)} copy-done((s32[1,32]{1,0:T(1,128)S(1)}, s32[1,32]{1,0:T(1,128)}, u32[]{:S(2)}) %copy-start.2) | copy-done | bytes 152
  42.5 1.2 %shard_map.84 = f32[256,128]{1,0:T(8,128)} custom-call(f32[32,128]{1,0:T(8,128)S(1)} %bitcast.6, s32[1,32]{1,0:T(1,128)S(1)} %copy-done.2, bf16[256,1024]{1,0:T(8,128)(2,1)S(1)} %copy-done), custom_call_target="tpu_custom_call" | custom-call | tf_op jit(solution)/shard_map/pallas_call | solution.py:725
  43.7 0.0 collective-permute-done.10.az2
  43.7 0.0 collective-permute-done.11.refs_0_
  43.7 0.0 collective-permute-done.9.az1
  43.7 0.0 collective-permute-done.7.ax1
  43.7 0.0 collective-permute-done.8.ax2
  43.7 2.7 %shard_map.83 = (f32[1280,128]{1,0:T(8,128)S(1)}, f32[5,8,16,128]{3,2,1,0:T(8,128)}) custom-call(f32[1280,128]{1,0:T(8,128)S(1)} %get-tuple-element.41.faz_in, f32[5,8,32,128]{3,2,1,0:T(8,128)S(1)} %get-tuple-element.40.u2, f32[5,8,32,128]{3,2,1,0:T(8,128)S(1)} %get-tuple-element.42.u0, ...), custom_call_target="tpu_custom_call", output_to_operand_aliasing={{0}: (0, {})} | custom-call | tf_op jit(solution)/shard_map/pallas_call | solution.py:712
Async XLA Ops:
  1.7 6.3 %collective-permute-start = (bf16[320,128]{1,0:T(8,128)(2,1)S(1)}, bf16[320,128]{1,0:T(8,128)(2,1)S(1)}, u32[]{:S(2)}, u32[]{:S(2)}) collective-permute-start(bf16[320,128]{1,0:T(8,128)(2,1)S(1)} %get-tuple-element.29), channel_id=1, source_target_pairs={{0,8},{8,0},{16,24},{24,16},{1,9},{9,1},{17,25},{25,17},{2,10},{10... | collective-permute-start | bytes 245768 | tf_op jit(solution)/shard_map/ppermute | solution.py:615
  2.2 5.8 %collective-permute-start.1 = (bf16[320,128]{1,0:T(8,128)(2,1)S(1)}, bf16[320,128]{1,0:T(8,128)(2,1)S(1)}, u32[]{:S(2)}, u32[]{:S(2)}) collective-permute-start(bf16[320,128]{1,0:T(8,128)(2,1)S(1)} %get-tuple-element.30), channel_id=1, source_target_pairs={{0,0},{8,16},{16,8},{24,24},{1,1},{9,17},{17,9},{25,25},{2,2},{10,... | collective-permute-start | bytes 245768 | tf_op jit(solution)/shard_map/ppermute | solution.py:615
  2.9 7.4 %collective-permute-start.2 = (bf16[160,128]{1,0:T(8,128)(2,1)S(1)}, bf16[160,128]{1,0:T(8,128)(2,1)S(1)}, u32[]{:S(2)}, u32[]{:S(2)}) collective-permute-start(bf16[160,128]{1,0:T(8,128)(2,1)S(1)} %get-tuple-element.31), channel_id=1, source_target_pairs={{0,2},{2,0},{4,6},{6,4},{1,3},{3,1},{5,7},{7,5},{8,10},{10,8},{12,... | collective-permute-start | bytes 122888 | tf_op jit(solution)/shard_map/ppermute | solution.py:615
  5.5 5.8 %collective-permute-start.3 = (bf16[160,128]{1,0:T(8,128)(2,1)S(1)}, bf16[160,128]{1,0:T(8,128)(2,1)S(1)}, u32[]{:S(2)}, u32[]{:S(2)}) collective-permute-start(bf16[160,128]{1,0:T(8,128)(2,1)S(1)} %get-tuple-element.32), channel_id=1, source_target_pairs={{0,6},{2,4},{4,2},{6,0},{1,7},{3,5},{5,3},{7,1},{8,14},{10,12},{12... | collective-permute-start | bytes 122888 | tf_op jit(solution)/shard_map/ppermute | solution.py:615
  8.1 3.8 %collective-permute-start.4 = (bf16[48,128]{1,0:T(8,128)(2,1)S(1)}, bf16[48,128]{1,0:T(8,128)(2,1)S(1)}, u32[]{:S(2)}, u32[]{:S(2)}) collective-permute-start(bf16[48,128]{1,0:T(8,128)(2,1)S(1)} %get-tuple-element.33), channel_id=1, source_target_pairs={{0,2},{2,0},{4,6},{6,4},{1,3},{3,1},{5,7},{7,5},{8,10},{10,8},{12,... | collective-permute-start | bytes 36872 | tf_op jit(solution)/shard_map/ppermute | solution.py:615
  8.8 5.5 %collective-permute-start.5 = (bf16[48,128]{1,0:T(8,128)(2,1)S(1)}, bf16[48,128]{1,0:T(8,128)(2,1)S(1)}, u32[]{:S(2)}, u32[]{:S(2)}) collective-permute-start(bf16[48,128]{1,0:T(8,128)(2,1)S(1)} %get-tuple-element.34), channel_id=1, source_target_pairs={{0,6},{2,4},{4,2},{6,0},{1,7},{3,5},{5,3},{7,1},{8,14},{10,12},{12... | collective-permute-start | bytes 36872 | tf_op jit(solution)/shard_map/ppermute | solution.py:615
  14.8 4.3 %collective-permute-start.6 = (bf16[128,128]{1,0:T(8,128)(2,1)S(1)}, bf16[128,128]{1,0:T(8,128)(2,1)S(1)}, u32[]{:S(2)}, u32[]{:S(2)}) collective-permute-start(bf16[128,128]{1,0:T(8,128)(2,1)S(1)} %get-tuple-element.38), channel_id=1, source_target_pairs={{0,1},{1,0},{2,3},{3,2},{4,5},{5,4},{6,7},{7,6},{8,9},{9,8},{10,11... | collective-permute-start | bytes 98312 | tf_op jit(solution)/shard_map/ppermute | solution.py:621
  22.3 5.0 %copy-start.1 = (f32[32,1,128]{2,1,0:T(1,128)}, f32[32,1,128]{2,1,0:T(1,128)S(1)}, u32[]{:S(2)}) copy-start(f32[32,1,128]{2,1,0:T(1,128)S(1)} %get-tuple-element.51) | copy-start | bytes 49156
  23.3 0.6 %copy-start.3 = (bf16[80,128]{1,0:T(8,128)(2,1)}, bf16[80,128]{1,0:T(8,128)(2,1)S(1)}, u32[]{:S(2)}) copy-start(bf16[80,128]{1,0:T(8,128)(2,1)S(1)} %get-tuple-element.47) | copy-start | bytes 61444
  23.9 0.6 %copy-start.4 = (bf16[80,128]{1,0:T(8,128)(2,1)}, bf16[80,128]{1,0:T(8,128)(2,1)S(1)}, u32[]{:S(2)}) copy-start(bf16[80,128]{1,0:T(8,128)(2,1)S(1)} %get-tuple-element.49) | copy-start | bytes 61444
  24.5 0.6 %copy-start.5 = (bf16[80,128]{1,0:T(8,128)(2,1)}, bf16[80,128]{1,0:T(8,128)(2,1)S(1)}, u32[]{:S(2)}) copy-start(bf16[80,128]{1,0:T(8,128)(2,1)S(1)} %get-tuple-element.48) | copy-start | bytes 61444
  25.1 18.5 %collective-permute-start.7 = (bf16[160,128]{1,0:T(8,128)(2,1)}, bf16[160,128]{1,0:T(8,128)(2,1)}, u32[]{:S(2)}, u32[]{:S(2)}) collective-permute-start(bf16[160,128]{1,0:T(8,128)(2,1)} %get-tuple-element.45), channel_id=1, source_target_pairs={{0,8},{8,0},{16,24},{24,16},{1,9},{9,1},{17,25},{25,17},{2,10},{10... | collective-permute-start | bytes 122888 | tf_op jit(solution)/shard_map/ppermute | solution.py:615
  25.2 18.5 %collective-permute-start.8 = (bf16[160,128]{1,0:T(8,128)(2,1)}, bf16[160,128]{1,0:T(8,128)(2,1)}, u32[]{:S(2)}, u32[]{:S(2)}) collective-permute-start(bf16[160,128]{1,0:T(8,128)(2,1)} %get-tuple-element.46), channel_id=1, source_target_pairs={{0,0},{8,16},{16,8},{24,24},{1,1},{9,17},{17,9},{25,25},{2,2},{10,... | collective-permute-start | bytes 122888 | tf_op jit(solution)/shard_map/ppermute | solution.py:615
  27.2 13.6 %all-to-all-start = ((f32[32,1,128]{2,1,0:T(1,128)}), f32[32,1,128]{2,1,0:T(1,128)S(1)}, u32[]{:S(2)}, u32[]{:S(2)}) async-start(f32[32,1,128]{2,1,0:T(1,128)} %copy-done.1), calls=%async_computation | async-start | bytes 32768 | tf_op jit(solution)/shard_map/all_to_all | solution.py:695
  33.6 10.0 %collective-permute-start.10 = (bf16[80,128]{1,0:T(8,128)(2,1)}, bf16[80,128]{1,0:T(8,128)(2,1)}, u32[]{:S(2)}, u32[]{:S(2)}) collective-permute-start(bf16[80,128]{1,0:T(8,128)(2,1)} %copy-done.5), channel_id=1, source_target_pairs={{0,6},{2,4},{4,2},{6,0},{1,7},{3,5},{5,3},{7,1},{8,14},{10,12},{12... | collective-permute-start | bytes 61448 | tf_op jit(solution)/shard_map/ppermute | solution.py:615
  37.3 6.4 %collective-permute-start.11 = (bf16[80,128]{1,0:T(8,128)(2,1)}, bf16[80,128]{1,0:T(8,128)(2,1)}, u32[]{:S(2)}, u32[]{:S(2)}) collective-permute-start(bf16[80,128]{1,0:T(8,128)(2,1)} %copy-done.4), channel_id=1, source_target_pairs={{0,1},{1,0},{2,3},{3,2},{4,5},{5,4},{6,7},{7,6},{8,9},{9,8},{10,11... | collective-permute-start | bytes 61448 | tf_op jit(solution)/shard_map/ppermute | solution.py:621
  38.8 4.9 %collective-permute-start.9 = (bf16[80,128]{1,0:T(8,128)(2,1)}, bf16[80,128]{1,0:T(8,128)(2,1)}, u32[]{:S(2)}, u32[]{:S(2)}) collective-permute-start(bf16[80,128]{1,0:T(8,128)(2,1)} %copy-done.3), channel_id=1, source_target_pairs={{0,2},{2,0},{4,6},{6,4},{1,3},{3,1},{5,7},{7,5},{8,10},{10,8},{12,... | collective-permute-start | bytes 61448 | tf_op jit(solution)/shard_map/ppermute | solution.py:615
  40.8 1.0 %copy-start = (bf16[256,1024]{1,0:T(8,128)(2,1)S(1)}, bf16[256,1024]{1,0:T(8,128)(2,1)}, u32[]{:S(2)}) copy-start(bf16[256,1024]{1,0:T(8,128)(2,1)} %weight.1) | copy-start | bytes 1572868
  41.8 0.7 %copy-start.2 = (s32[1,32]{1,0:T(1,128)S(1)}, s32[1,32]{1,0:T(1,128)}, u32[]{:S(2)}) copy-start(s32[1,32]{1,0:T(1,128)} %offsets.1) | copy-start | bytes 388

commit v11 on v9

--- a/solution.py
+++ b/solution.py
@@ -57,7 +57,7 @@
 
 
 def first_is_up(axis):
-    return lax.axis_index("core" if axis == "ax" else axis) % 2 == 1
+    return lax.axis_index("core" if axis == "ax" else axis) % 2 == 0
 
 
 def load_and_pack(ca, cz, den, vel, pre, home, ax1, ax2, az1, az2, sems):
@@ -157,9 +157,7 @@
     return jnp.where(hit, 1.0, 0.0)
 
 
-def assemble(n_ax, count, ca, cz, block_in, ax1, ax2, az1, az2, corner1, corner2, *rest):
-    edges, block, outs, (sides, strips, corners) = rest[:count], rest[count], rest[count + 1 : -3], rest[-3:]
-    cr = ax1.shape[1]
+def add_sides(n_ax, ca, cz, block_in, ax1, ax2, az1, az2, block, sides, strips):
     planes = ca + 2 * REACH
     size = REACH * cz
     for f in range(5):
@@ -170,24 +168,34 @@
         for k in range(REACH):
             spread_rows(planes, cz, f, k, sides.at[f], k * cz, block)
             spread_rows(planes, cz, f, REACH + ca + k, sides.at[f], size + k * cz, block)
-
     up = first_is_up("az")
-    for one, two, into in ((az1, az2, strips), (corner1, corner2, corners)):
-        a, b = one[...].astype(F32), two[...].astype(F32)
-        into[0] = jnp.where(up, b, a)
-        into[1] = jnp.where(up, a, b)
+    a, b = az1[...].astype(F32), az2[...].astype(F32)
+    strips[0] = jnp.where(up, b, a)
+    strips[1] = jnp.where(up, a, b)
     for f in range(5):
         for d in range(REACH):
             for side, row in ((0, OFF - 1 - d), (1, OFF + cz + d)):
+                at = kept(row) + (f * planes + REACH) * ROWS
+                block[pl.ds(at, ca, stride=ROWS), :] = strips[side, pl.ds((f * REACH + d) * ca, ca), :]
+
+
+def add_corners(count, ca, cz, block_in, corner1, corner2, *rest):
+    edges, block, outs, corners = rest[:count], rest[count], rest[count + 1 : -1], rest[-1]
+    cr = corner1.shape[1]
+    planes = ca + 2 * REACH
+    up = first_is_up("az")
+    a, b = corner1[...].astype(F32), corner2[...].astype(F32)
+    corners[0] = jnp.where(up, b, a)
+    corners[1] = jnp.where(up, a, b)
+    for f in range(5):
+        for d in range(MID):
+            for side, row in ((0, OFF - 1 - d), (1, OFF + cz + d)):
                 at = kept(row) + f * planes * ROWS
-                got = strips[side, pl.ds((f * REACH + d) * ca, ca), :]
-                block[pl.ds(at + REACH * ROWS, ca, stride=ROWS), :] = got
-                if d < MID:
-                    start = (f * MID + d) * 2 * MID
-                    got = corners[side, pl.ds(start, MID), :]
-                    block[pl.ds(at + (REACH - MID) * ROWS, MID, stride=ROWS), :] = got
-                    got = corners[side, pl.ds(start + MID, MID), :]
-                    block[pl.ds(at + (REACH + ca) * ROWS, MID, stride=ROWS), :] = got
+                start = (f * MID + d) * 2 * MID
+                got = corners[side, pl.ds(start, MID), :]
+                block[pl.ds(at + (REACH - MID) * ROWS, MID, stride=ROWS), :] = got
+                got = corners[side, pl.ds(start + MID, MID), :]
+                block[pl.ds(at + (REACH + ca) * ROWS, MID, stride=ROWS), :] = got
 
     tiles = cr // SLOT
     step = tiles * 8
@@ -473,27 +481,38 @@
                 state[f, k, pl.ds(l, quarter, stride=4), :] = new[8 * l + first : 8 * l + first + quarter]
 
 
-def signals(slots, rows, offsets, weight, out):
-    ndev = rows.shape[0]
+def signal_tables(slots, offsets, pick, wait):
     group = 32
     cols = group * slots
-    lanes = rows.shape[1]
     col = lax.broadcasted_iota(jnp.int32, (1, cols), 1)
     owner = lax.broadcasted_iota(jnp.int32, (group, cols), 0) == col // slots
-    lane = lax.broadcasted_iota(jnp.int32, (lanes, cols), 0)
+    lane = lax.broadcasted_iota(jnp.int32, (pick.shape[0], cols), 0)
+    for s in range(3):
+        hot = jnp.where(lane == s * slots + col % slots, 1.0, 0.0)
+        pick[:, s * cols : (s + 1) * cols] = hot.astype(BF16)
     time = lax.broadcasted_iota(jnp.int32, (NB, cols), 0).astype(F32)
-    total = jnp.zeros(out.shape, F32)
-    for g in range(ndev // group):
-        q = rows[g * group : (g + 1) * group, :].astype(BF16)
+    for g in range(offsets.shape[1] // group):
         off = offsets[0:1, g * group : (g + 1) * group].astype(F32)
         off = jnp.broadcast_to(off, (8, group)).astype(BF16)
         bins = jnp.dot(off, owner.astype(BF16), preferred_element_type=F32)[0:1]
+        wait[:, g * cols : (g + 1) * cols] = time - bins
+
+
+def signals(slots, rows, pick, wait, weight, out):
+    group = 32
+    cols = group * slots
+    col = lax.broadcasted_iota(jnp.int32, (1, cols), 1)
+    owner = lax.broadcasted_iota(jnp.int32, (group, cols), 0) == col // slots
+    total = jnp.zeros(out.shape, F32)
+    for g in range(rows.shape[0] // group):
+        q = rows[g * group : (g + 1) * group, :].astype(BF16)
+        spread = jnp.dot(q, pick[...], preferred_element_type=F32)
+        bins = wait[:, g * cols : (g + 1) * cols]
         table = jnp.zeros((NB, cols), F32)
         for s in range(3):
-            pick = jnp.where(lane == s * slots + col % slots, 1.0, 0.0).astype(BF16)
-            spread = jnp.dot(q, pick, preferred_element_type=F32)
-            line = jnp.sum(jnp.where(owner, spread, 0.0), axis=0, keepdims=True)
-            table = jnp.where(time == bins + s, line, table)
+            line = jnp.where(owner, spread[:, s * cols : (s + 1) * cols], 0.0)
+            line = jnp.sum(line, axis=0, keepdims=True)
+            table = jnp.where(bins == s, line, table)
         total = total + lax.dot_general(
             weight[:, g * cols : (g + 1) * cols],
             table.astype(BF16),
@@ -504,11 +523,12 @@
 
 
 def swap_pairs(count, periodic):
-    one = []
+    one = [(i, i ^ 1) for i in range(count)]
+    two = []
     for i in range(count):
         j = i - 1 if i % 2 == 0 else i + 1
-        one.append((i, j % count if periodic or 0 <= j < count else i))
-    return one, [(i, i ^ 1) for i in range(count)]
+        two.append((i, j % count if periodic or 0 <= j < count else i))
+    return one, two
 
 
 def swap(first, second, axis, periodic):
@@ -549,24 +569,36 @@
     )(home)
     edges, places = tables[: len(ends)], tables[len(ends) :]
 
+    pick, wait = call(
+        part(signal_tables, slots),
+        (struct((128, 3 * 32 * slots), BF16), struct((NB, ndev * slots))),
+        [VMEM],
+        cost=pl.CostEstimate(flops=100_000_000, bytes_accessed=4_000_000, transcendentals=0),
+    )(bin_offset)
+
     corner = struct((5 * MID * 2 * MID, cr), BF16)
     near = pltpu.VMEM((5, 2 * MID * cz, cr), F32)
     corner1, corner2 = call(part(pack_corners, n_ax, cz), (corner, corner), [VMEM] * 2, [near])(ax1, ax2)
     corner1, corner2 = swap(corner1, corner2, "az", True)
 
     side = struct((5 * (ca + 2 * MID) * ROWS // tiles, cr), BF16)
+    block = call(
+        part(add_sides, n_ax, ca, cz),
+        grid,
+        [VMEM] * 5,
+        [pltpu.VMEM((5, 2 * REACH * cz, cr), F32), pltpu.VMEM((2,) + strip.shape, F32)],
+        mib=8,
+        alias={0: 0},
+        cost=pl.CostEstimate(flops=100_000_000, bytes_accessed=4_000_000, transcendentals=0),
+    )(block, ax1, ax2, az1, az2)
     got = call(
-        part(assemble, n_ax, len(ends), ca, cz),
+        part(add_corners, len(ends), ca, cz),
         (grid,) + tuple(side for _ in ends),
-        [VMEM] * (7 + len(ends)),
-        [
-            pltpu.VMEM((5, 2 * REACH * cz, cr), F32),
-            pltpu.VMEM((2,) + strip.shape, F32),
-            pltpu.VMEM((2,) + corner.shape, F32),
-        ],
-        mib=12,
+        [VMEM] * (3 + len(ends)),
+        [pltpu.VMEM((2,) + corner.shape, F32)],
+        mib=8,
         alias={0: 0},
-    )(block, ax1, ax2, az1, az2, corner1, corner2, *edges)
+    )(block, corner1, corner2, *edges)
     block = got[0].reshape(5, planes, ROWS, cr)
     if n_rad == 2:
         sides = (lax.ppermute(got[1], "rad", [(0, 1), (1, 0)]),)
@@ -597,9 +629,9 @@
         mib=12,
         cost=pl.CostEstimate(flops=400_000_000, bytes_accessed=8_000_000, transcendentals=0),
     )(u2, u0, banded)
-    signal = call(
-        part(signals, slots), struct((obs_weight.shape[0], NB)), [VMEM] * 3, mib=24
-    )(rows, bin_offset, obs_weight)
+    signal = call(part(signals, slots), struct((obs_weight.shape[0], NB)), [VMEM] * 4, mib=24)(
+        rows, pick, wait, obs_weight
+    )
     return (state, signal)
 
 

time: 39.3 us -> 40.7 us (1.036)
  local copies, waits for them, and re-layouts: 0.01 us -> 1.86 us
  starting transfers between devices: 17.1 us -> 16.4 us
    ppermute x6, starting transfers between devices: 10.8 us -> 7.96 us  [swap(): return (lax.ppermute(first, axis, one), lax.ppermute(second, axis, two))]
    all_to_all x1, starting transfers between devices: 4.68 us -> 6.88 us  [local(): lax.all_to_all(q, ('y', 'core', 'az', 'rad'), 0, 0, tiled=True)]
    unnamed x4 -> x8, local copies, waits for them, and re-layouts: 0.01 us -> 1.86 us
    ppermute x1, waiting for transfers between devices: 2.51 us -> 1.62 us  [local(): sides = (lax.ppermute(got[1], 'rad', [(0, 1), (1, 0)]),)]
    ppermute x6, waiting for transfers between devices: 3.37 us -> 4.05 us  [swap(): return (lax.ppermute(first, axis, one), lax.ppermute(second, axis, two))]
    pallas_call x2 -> x4, Pallas kernels: 1.85 us -> 2.23 us  [the longest x1 1.23 us: local(): call(part(signals, slots), struct((obs_weight.shape[0], NB)), [VMEM] * 4,...]
  transfers between devices with their start and end apart: 8 -> 8, of which waited for: 5 -> 5; matrix products, arithmetic and copies ran while one was open for 0% -> 0% of each run, Pallas kernels for 6% -> 7%
where the time goes in v11:
time: 40.7 us; the launch traced here: 40.5 us
  starting transfers between devices  16.4 us (40%)
  waiting for transfers between devices  10.9 us (27%)
  Pallas kernels  10.5 us (26%)
  local copies, waits for them, and re-layouts  1.86 us (5%)
  between operations  0.73 us (2%)
    ppermute x6, starting transfers between devices, swap(): return (lax.ppermute(first, axis, one), lax.ppermute(second, axis, two))  7.96 us
    all_to_all x1, starting transfers between devices, local(): lax.all_to_all(q, ('y', 'core', 'az', 'rad'), 0, 0, tiled=True)  6.88 us
    all_to_all x1, waiting for transfers between devices, local(): lax.all_to_all(q, ('y', 'core', 'az', 'rad'), 0, 0, tiled=True)  5.27 us
    pallas_call x1, Pallas kernels, local(): call(part(stages, n_ax, n_rad, ca, cz, slots), (struct((ndev, 1, 128)), s...  4.87 us
    ppermute x6, waiting for transfers between devices, swap(): return (lax.ppermute(first, axis, one), lax.ppermute(second, axis, two))  4.05 us
    unnamed x8, local copies, waits for them, and re-layouts  1.86 us
    pallas_call x1, Pallas kernels, local(): call(part(last_stage, ca, cz), struct((5, ca, cz, cr)), [VMEM] * 3, [pltp...  1.77 us
    ppermute x1, waiting for transfers between devices, local(): sides = (lax.ppermute(got[1], 'rad', [(0, 1), (1, 0)]),)  1.62 us
  transfers between devices with their start and end apart: 8, of which 5 were waited for; matrix products, arithmetic and copies ran while one was open for 0% of the time, Pallas kernels for 7%

profile of v11, /device:TPU:0, one launch (start us, length us, event | category | flops | bytes accessed | tf_op | source)
XLA Modules:
  0.0 40.5 jit_solution(16526860572291219628)
XLA Ops:
  0.6 1.1 %shard_map.77 = (f32[640,128]{1,0:T(8,128)S(1)}, bf16[480,128]{1,0:T(8,128)(2,1)S(1)}, bf16[480,128]{1,0:T(8,128)(2,1)S(1)}, bf16[240,128]{1,0:T(8,128)(2,1)S(1)}, bf16[240,128]{1,0:T(8,128)(2,1)S(1)}) custom-call(f32[128,128]{1,0:T(8,128)} %bitcast.8, f32[384,128]{1,0:T(8,128)} %bitcast.7, f32[128,128]{1,0:T(8,128)} %bitcast.9), custom_call_target="tpu_custom_call" | custom-call | tf_op jit(solution)/shard_map/pallas_call | solution.py:553
  1.7 0.5 %collective-permute-start = (bf16[480,128]{1,0:T(8,128)(2,1)S(1)}, bf16[480,128]{1,0:T(8,128)(2,1)S(1)}, u32[]{:S(2)}, u32[]{:S(2)}) collective-permute-start(bf16[480,128]{1,0:T(8,128)(2,1)S(1)} %get-tuple-element.22), channel_id=1, source_target_pairs={{0,8},{8,0},{16,24},{24,16},{1,9},{9,1},{17,25},{25,17},{2,10},{10... | collective-permute-start | bytes 368648 | tf_op jit(solution)/shard_map/ppermute | solution.py:539
  2.2 0.7 %collective-permute-start.1 = (bf16[480,128]{1,0:T(8,128)(2,1)S(1)}, bf16[480,128]{1,0:T(8,128)(2,1)S(1)}, u32[]{:S(2)}, u32[]{:S(2)}) collective-permute-start(bf16[480,128]{1,0:T(8,128)(2,1)S(1)} %get-tuple-element.23), channel_id=1, source_target_pairs={{0,0},{8,16},{16,8},{24,24},{1,1},{9,17},{17,9},{25,25},{2,2},{10,... | collective-permute-start | bytes 368648 | tf_op jit(solution)/shard_map/ppermute | solution.py:539
  2.9 2.7 %collective-permute-start.2 = (bf16[240,128]{1,0:T(8,128)(2,1)S(1)}, bf16[240,128]{1,0:T(8,128)(2,1)S(1)}, u32[]{:S(2)}, u32[]{:S(2)}) collective-permute-start(bf16[240,128]{1,0:T(8,128)(2,1)S(1)} %get-tuple-element.24), channel_id=1, source_target_pairs={{0,2},{2,0},{4,6},{6,4},{1,3},{3,1},{5,7},{7,5},{8,10},{10,8},{12,... | collective-permute-start | bytes 184328 | tf_op jit(solution)/shard_map/ppermute | solution.py:539
  5.6 2.5 %collective-permute-start.3 = (bf16[240,128]{1,0:T(8,128)(2,1)S(1)}, bf16[240,128]{1,0:T(8,128)(2,1)S(1)}, u32[]{:S(2)}, u32[]{:S(2)}) collective-permute-start(bf16[240,128]{1,0:T(8,128)(2,1)S(1)} %get-tuple-element.25), channel_id=1, source_target_pairs={{0,6},{2,4},{4,2},{6,0},{1,7},{3,5},{5,3},{7,1},{8,14},{10,12},{12... | collective-permute-start | bytes 184328 | tf_op jit(solution)/shard_map/ppermute | solution.py:539
  8.1 0.0 collective-permute-done.ax1.got1
  8.1 0.0 collective-permute-done.1.ax2.got2
  8.1 0.1 shard_map.80
  8.2 0.7 %collective-permute-start.4 = (bf16[160,128]{1,0:T(8,128)(2,1)S(1)}, bf16[160,128]{1,0:T(8,128)(2,1)S(1)}, u32[]{:S(2)}, u32[]{:S(2)}) collective-permute-start(bf16[160,128]{1,0:T(8,128)(2,1)S(1)} %get-tuple-element.26), channel_id=1, source_target_pairs={{0,2},{2,0},{4,6},{6,4},{1,3},{3,1},{5,7},{7,5},{8,10},{10,8},{12,... | collective-permute-start | bytes 122888 | tf_op jit(solution)/shard_map/ppermute | solution.py:539
  8.9 0.9 %collective-permute-start.5 = (bf16[160,128]{1,0:T(8,128)(2,1)S(1)}, bf16[160,128]{1,0:T(8,128)(2,1)S(1)}, u32[]{:S(2)}, u32[]{:S(2)}) collective-permute-start(bf16[160,128]{1,0:T(8,128)(2,1)S(1)} %get-tuple-element.27), channel_id=1, source_target_pairs={{0,6},{2,4},{4,2},{6,0},{1,7},{3,5},{5,3},{7,1},{8,14},{10,12},{12... | collective-permute-start | bytes 122888 | tf_op jit(solution)/shard_map/ppermute | solution.py:539
  9.8 0.5 %shard_map.78 = (f32[3200,128]{1,0:T(8,128)S(1)}, bf16[256,256]{1,0:T(8,128)(2,1)S(1)}, bf16[2048,128]{1,0:T(8,128)(2,1)S(1)}, bf16[128,512]{1,0:T(8,128)(2,1)S(1)}) custom-call(f32[640,128]{1,0:T(8,128)S(1)} %get-tuple-element.20.home), custom_call_target="tpu_custom_call" | custom-call | tf_op jit(solution)/shard_map/pallas_call | solution.py:565
  10.3 0.0 collective-permute-done.2.az1
  10.3 1.4 %collective-permute-done.3.az2 = bf16[240,128]{1,0:T(8,128)(2,1)S(1)} collective-permute-done((bf16[240,128]{1,0:T(8,128)(2,1)S(1)}, bf16[240,128]{1,0:T(8,128)(2,1)S(1)}, u32[]{:S(2)}, u32[]{:S(2)}) %collective-permute-start.3) | collective-permute-done | bytes 61472 | tf_op jit(solution)/shard_map/ppermute | solution.py:539
  11.8 0.3 shard_map.79.block_in
  12.1 0.0 copy-start.3
  12.1 0.1 collective-permute-done.4.corner1
  12.2 2.5 %collective-permute-done.5.corner2 = bf16[160,128]{1,0:T(8,128)(2,1)S(1)} collective-permute-done((bf16[160,128]{1,0:T(8,128)(2,1)S(1)}, bf16[160,128]{1,0:T(8,128)(2,1)S(1)}, u32[]{:S(2)}, u32[]{:S(2)}) %collective-permute-start.5) | collective-permute-done | bytes 40992 | tf_op jit(solution)/shard_map/ppermute | solution.py:539
  14.7 0.5 %shard_map.81 = (f32[3200,128]{1,0:T(8,128)S(1)}, bf16[160,128]{1,0:T(8,128)(2,1)S(1)}) custom-call(f32[3200,128]{1,0:T(8,128)S(1)} %shard_map.79.block_in, bf16[160,128]{1,0:T(8,128)(2,1)S(1)} %collective-permute-done.4.corner1, bf16[160,128]{1,0:T(8,128)(2,1)S(1)} %collective-permute-done.5.corner2, ...), custom_call_target="tpu_custom_call", output_to_operand_aliasing={{0}: (0, {})} | custom-call | tf_op jit(solution)/shard_map/pallas_call | solution.py:594
  15.2 1.6 %collective-permute-start.6 = (bf16[160,128]{1,0:T(8,128)(2,1)S(1)}, bf16[160,128]{1,0:T(8,128)(2,1)S(1)}, u32[]{:S(2)}, u32[]{:S(2)}) collective-permute-start(bf16[160,128]{1,0:T(8,128)(2,1)S(1)} %get-tuple-element.31), channel_id=1, source_target_pairs={{0,1},{1,0},{2,3},{3,2},{4,5},{5,4},{6,7},{7,6},{8,9},{9,8},{10,11... | collective-permute-start | bytes 122888 | tf_op jit(solution)/shard_map/ppermute | solution.py:604
  16.7 0.0 copy-done.3
  16.7 0.2 shard_map.84
  17.0 0.0 copy-start.1
  17.0 0.8 %copy-done.1 = f32[128,1024]{1,0:T(8,128)} copy-done((f32[128,1024]{1,0:T(8,128)}, f32[128,1024]{1,0:T(8,128)S(1)}, u32[]{:S(2)}) %copy-start.1) | copy-done | bytes 524312
  17.8 1.6 %collective-permute-done.6.refs_0_ = bf16[160,128]{1,0:T(8,128)(2,1)S(1)} collective-permute-done((bf16[160,128]{1,0:T(8,128)(2,1)S(1)}, bf16[160,128]{1,0:T(8,128)(2,1)S(1)}, u32[]{:S(2)}, u32[]{:S(2)}) %collective-permute-start.6) | collective-permute-done | bytes 40992 | tf_op jit(solution)/shard_map/ppermute | solution.py:604
  19.4 4.9 %shard_map.82 = (f32[32,1,128]{2,1,0:T(1,128)}, f32[5,12,40,128]{3,2,1,0:T(8,128)S(1)}, f32[5,8,32,128]{3,2,1,0:T(8,128)S(1)}) custom-call(f32[5,20,32,128]{3,2,1,0:T(8,128)S(1)} %bitcast.5, bf16[256,256]{1,0:T(8,128)(2,1)S(1)} %get-tuple-element.30.banded, s32[32]{0:T(128)} %cells_far.1, bf16[160,128]{1,0:T(8,128)(2,1)S(1)} %collective-permute-done.6.refs_0_, ...), custom_call_target="tpu_custom_call" | custom-call | tf_op jit(solution)/shard_map/pallas_call | solution.py:610
  24.3 0.0 copy-start
  24.3 6.9 %all-to-all-start = ((f32[32,1,128]{2,1,0:T(1,128)}), f32[32,1,128]{2,1,0:T(1,128)S(1)}, u32[]{:S(2)}, u32[]{:S(2)}) async-start(f32[32,1,128]{2,1,0:T(1,128)} %get-tuple-element.35), calls=%async_computation | async-start | bytes 32768 | tf_op jit(solution)/shard_map/all_to_all | solution.py:621
  31.2 1.8 %shard_map.83 = f32[5,8,16,128]{3,2,1,0:T(8,128)} custom-call(f32[5,12,40,128]{3,2,1,0:T(8,128)S(1)} %get-tuple-element.33.u2, f32[5,8,32,128]{3,2,1,0:T(8,128)S(1)} %get-tuple-element.34.u0, bf16[256,256]{1,0:T(8,128)(2,1)S(1)} %get-tuple-element.30.banded), custom_call_target="tpu_custom_call" | custom-call | flops 400000000 | bytes 8000000 | tf_op jit(solution)/shard_map/pallas_call | solution.py:624
  32.9 5.3 %all-to-all-done = f32[32,1,128]{2,1,0:T(1,128)S(1)} async-done(((f32[32,1,128]{2,1,0:T(1,128)}), f32[32,1,128]{2,1,0:T(1,128)S(1)}, u32[]{:S(2)}, u32[]{:S(2)}) %all-to-all-start) | async-done | bytes 16416 | tf_op jit(solution)/shard_map/all_to_all | solution.py:621
  38.2 0.0 copy-done
  38.2 0.0 copy-start.2
  38.2 1.0 %copy-done.2 = f32[128,1024]{1,0:T(8,128)S(1)} copy-done((f32[128,1024]{1,0:T(8,128)S(1)}, f32[128,1024]{1,0:T(8,128)}, u32[]{:S(2)}) %copy-start.2) | copy-done | bytes 524312
  39.3 1.2 %shard_map.85 = f32[256,128]{1,0:T(8,128)} custom-call(f32[32,128]{1,0:T(8,128)S(1)} %bitcast.6, bf16[128,3072]{1,0:T(8,128)(2,1)S(1)} %get-tuple-element.36.pick, f32[128,1024]{1,0:T(8,128)S(1)} %copy-done.2, bf16[256,1024]{1,0:T(8,128)(2,1)S(1)} %copy-done), custom_call_target="tpu_custom_call" | custom-call | tf_op jit(solution)/shard_map/pallas_call | solution.py:632
Async XLA Ops:
  1.7 6.3 %collective-permute-start = (bf16[480,128]{1,0:T(8,128)(2,1)S(1)}, bf16[480,128]{1,0:T(8,128)(2,1)S(1)}, u32[]{:S(2)}, u32[]{:S(2)}) collective-permute-start(bf16[480,128]{1,0:T(8,128)(2,1)S(1)} %get-tuple-element.22), channel_id=1, source_target_pairs={{0,8},{8,0},{16,24},{24,16},{1,9},{9,1},{17,25},{25,17},{2,10},{10... | collective-permute-start | bytes 368648 | tf_op jit(solution)/shard_map/ppermute | solution.py:539
  2.2 5.8 %collective-permute-start.1 = (bf16[480,128]{1,0:T(8,128)(2,1)S(1)}, bf16[480,128]{1,0:T(8,128)(2,1)S(1)}, u32[]{:S(2)}, u32[]{:S(2)}) collective-permute-start(bf16[480,128]{1,0:T(8,128)(2,1)S(1)} %get-tuple-element.23), channel_id=1, source_target_pairs={{0,0},{8,16},{16,8},{24,24},{1,1},{9,17},{17,9},{25,25},{2,2},{10,... | collective-permute-start | bytes 368648 | tf_op jit(solution)/shard_map/ppermute | solution.py:539
  2.9 7.4 %collective-permute-start.2 = (bf16[240,128]{1,0:T(8,128)(2,1)S(1)}, bf16[240,128]{1,0:T(8,128)(2,1)S(1)}, u32[]{:S(2)}, u32[]{:S(2)}) collective-permute-start(bf16[240,128]{1,0:T(8,128)(2,1)S(1)} %get-tuple-element.24), channel_id=1, source_target_pairs={{0,2},{2,0},{4,6},{6,4},{1,3},{3,1},{5,7},{7,5},{8,10},{10,8},{12,... | collective-permute-start | bytes 184328 | tf_op jit(solution)/shard_map/ppermute | solution.py:539
  5.6 6.2 %collective-permute-start.3 = (bf16[240,128]{1,0:T(8,128)(2,1)S(1)}, bf16[240,128]{1,0:T(8,128)(2,1)S(1)}, u32[]{:S(2)}, u32[]{:S(2)}) collective-permute-start(bf16[240,128]{1,0:T(8,128)(2,1)S(1)} %get-tuple-element.25), channel_id=1, source_target_pairs={{0,6},{2,4},{4,2},{6,0},{1,7},{3,5},{5,3},{7,1},{8,14},{10,12},{12... | collective-permute-start | bytes 184328 | tf_op jit(solution)/shard_map/ppermute | solution.py:539
  8.2 4.1 %collective-permute-start.4 = (bf16[160,128]{1,0:T(8,128)(2,1)S(1)}, bf16[160,128]{1,0:T(8,128)(2,1)S(1)}, u32[]{:S(2)}, u32[]{:S(2)}) collective-permute-start(bf16[160,128]{1,0:T(8,128)(2,1)S(1)} %get-tuple-element.26), channel_id=1, source_target_pairs={{0,2},{2,0},{4,6},{6,4},{1,3},{3,1},{5,7},{7,5},{8,10},{10,8},{12,... | collective-permute-start | bytes 122888 | tf_op jit(solution)/shard_map/ppermute | solution.py:539
  8.9 5.8 %collective-permute-start.5 = (bf16[160,128]{1,0:T(8,128)(2,1)S(1)}, bf16[160,128]{1,0:T(8,128)(2,1)S(1)}, u32[]{:S(2)}, u32[]{:S(2)}) collective-permute-start(bf16[160,128]{1,0:T(8,128)(2,1)S(1)} %get-tuple-element.27), channel_id=1, source_target_pairs={{0,6},{2,4},{4,2},{6,0},{1,7},{3,5},{5,3},{7,1},{8,14},{10,12},{12... | collective-permute-start | bytes 122888 | tf_op jit(solution)/shard_map/ppermute | solution.py:539
  12.1 4.6 %copy-start.3 = (s32[1,32]{1,0:T(1,128)S(1)}, s32[1,32]{1,0:T(1,128)}, u32[]{:S(2)}) copy-start(s32[1,32]{1,0:T(1,128)} %offsets.1) | copy-start | bytes 388
  15.2 4.2 %collective-permute-start.6 = (bf16[160,128]{1,0:T(8,128)(2,1)S(1)}, bf16[160,128]{1,0:T(8,128)(2,1)S(1)}, u32[]{:S(2)}, u32[]{:S(2)}) collective-permute-start(bf16[160,128]{1,0:T(8,128)(2,1)S(1)} %get-tuple-element.31), channel_id=1, source_target_pairs={{0,1},{1,0},{2,3},{3,2},{4,5},{5,4},{6,7},{7,6},{8,9},{9,8},{10,11... | collective-permute-start | bytes 122888 | tf_op jit(solution)/shard_map/ppermute | solution.py:604
  17.0 0.8 %copy-start.1 = (f32[128,1024]{1,0:T(8,128)}, f32[128,1024]{1,0:T(8,128)S(1)}, u32[]{:S(2)}) copy-start(f32[128,1024]{1,0:T(8,128)S(1)} %get-tuple-element.37.wait) | copy-start | bytes 1572868
  24.3 13.9 %copy-start = (bf16[256,1024]{1,0:T(8,128)(2,1)S(1)}, bf16[256,1024]{1,0:T(8,128)(2,1)}, u32[]{:S(2)}) copy-start(bf16[256,1024]{1,0:T(8,128)(2,1)} %weight.1) | copy-start | bytes 1572868
  24.3 13.9 %all-to-all-start = ((f32[32,1,128]{2,1,0:T(1,128)}), f32[32,1,128]{2,1,0:T(1,128)S(1)}, u32[]{:S(2)}, u32[]{:S(2)}) async-start(f32[32,1,128]{2,1,0:T(1,128)} %get-tuple-element.35), calls=%async_computation | async-start | bytes 32768 | tf_op jit(solution)/shard_map/all_to_all | solution.py:621
  38.2 1.0 %copy-start.2 = (f32[128,1024]{1,0:T(8,128)S(1)}, f32[128,1024]{1,0:T(8,128)}, u32[]{:S(2)}) copy-start(f32[128,1024]{1,0:T(8,128)} %copy-done.1) | copy-start | bytes 1572868

commit v12 on v11

--- a/solution.py
+++ b/solution.py
@@ -276,12 +276,8 @@
         for f in range(5):
             side = jnp.where(mine, jnp.concatenate([got[f][ROWS:]] * 4, axis=0), 0.0)
             rows.append(jnp.concatenate([got[f][0:ROWS], side], axis=1))
-    rows = jnp.concatenate(rows, axis=0)
-    coarse = rows.astype(BF16)
-    fine = (rows - coarse.astype(F32)).astype(BF16)
-    matrix = banded[...]
-    out = jnp.dot(coarse, matrix, preferred_element_type=F32)
-    out = out + jnp.dot(fine, matrix, preferred_element_type=F32)
+    rows = jnp.concatenate(rows, axis=0).astype(BF16)
+    out = jnp.dot(rows, banded[...], preferred_element_type=F32)
     half = out.shape[1] // 2
     for i, (u, j) in enumerate(zip(us, js)):
         got = flux(1, *u)
@@ -481,38 +477,27 @@
                 state[f, k, pl.ds(l, quarter, stride=4), :] = new[8 * l + first : 8 * l + first + quarter]
 
 
-def signal_tables(slots, offsets, pick, wait):
+def signals(slots, rows, offsets, weight, out):
+    ndev = rows.shape[0]
     group = 32
     cols = group * slots
+    lanes = rows.shape[1]
     col = lax.broadcasted_iota(jnp.int32, (1, cols), 1)
     owner = lax.broadcasted_iota(jnp.int32, (group, cols), 0) == col // slots
-    lane = lax.broadcasted_iota(jnp.int32, (pick.shape[0], cols), 0)
-    for s in range(3):
-        hot = jnp.where(lane == s * slots + col % slots, 1.0, 0.0)
-        pick[:, s * cols : (s + 1) * cols] = hot.astype(BF16)
+    lane = lax.broadcasted_iota(jnp.int32, (lanes, cols), 0)
     time = lax.broadcasted_iota(jnp.int32, (NB, cols), 0).astype(F32)
-    for g in range(offsets.shape[1] // group):
+    total = jnp.zeros(out.shape, F32)
+    for g in range(ndev // group):
+        q = rows[g * group : (g + 1) * group, :].astype(BF16)
         off = offsets[0:1, g * group : (g + 1) * group].astype(F32)
         off = jnp.broadcast_to(off, (8, group)).astype(BF16)
         bins = jnp.dot(off, owner.astype(BF16), preferred_element_type=F32)[0:1]
-        wait[:, g * cols : (g + 1) * cols] = time - bins
-
-
-def signals(slots, rows, pick, wait, weight, out):
-    group = 32
-    cols = group * slots
-    col = lax.broadcasted_iota(jnp.int32, (1, cols), 1)
-    owner = lax.broadcasted_iota(jnp.int32, (group, cols), 0) == col // slots
-    total = jnp.zeros(out.shape, F32)
-    for g in range(rows.shape[0] // group):
-        q = rows[g * group : (g + 1) * group, :].astype(BF16)
-        spread = jnp.dot(q, pick[...], preferred_element_type=F32)
-        bins = wait[:, g * cols : (g + 1) * cols]
         table = jnp.zeros((NB, cols), F32)
         for s in range(3):
-            line = jnp.where(owner, spread[:, s * cols : (s + 1) * cols], 0.0)
-            line = jnp.sum(line, axis=0, keepdims=True)
-            table = jnp.where(bins == s, line, table)
+            pick = jnp.where(lane == s * slots + col % slots, 1.0, 0.0).astype(BF16)
+            spread = jnp.dot(q, pick, preferred_element_type=F32)
+            line = jnp.sum(jnp.where(owner, spread, 0.0), axis=0, keepdims=True)
+            table = jnp.where(time == bins + s, line, table)
         total = total + lax.dot_general(
             weight[:, g * cols : (g + 1) * cols],
             table.astype(BF16),
@@ -568,13 +553,6 @@
         [VMEM],
     )(home)
     edges, places = tables[: len(ends)], tables[len(ends) :]
-
-    pick, wait = call(
-        part(signal_tables, slots),
-        (struct((128, 3 * 32 * slots), BF16), struct((NB, ndev * slots))),
-        [VMEM],
-        cost=pl.CostEstimate(flops=100_000_000, bytes_accessed=4_000_000, transcendentals=0),
-    )(bin_offset)
 
     corner = struct((5 * MID * 2 * MID, cr), BF16)
     near = pltpu.VMEM((5, 2 * MID * cz, cr), F32)
@@ -629,9 +607,9 @@
         mib=12,
         cost=pl.CostEstimate(flops=400_000_000, bytes_accessed=8_000_000, transcendentals=0),
     )(u2, u0, banded)
-    signal = call(part(signals, slots), struct((obs_weight.shape[0], NB)), [VMEM] * 4, mib=24)(
-        rows, pick, wait, obs_weight
-    )
+    signal = call(
+        part(signals, slots), struct((obs_weight.shape[0], NB)), [VMEM] * 3, mib=24
+    )(rows, bin_offset, obs_weight)
     return (state, signal)
 
 

time: 40.7 us -> 38.9 us (0.956)
  local copies, waits for them, and re-layouts: 1.86 us -> 0.01 us
  waiting for transfers between devices: 10.9 us -> 12.2 us
  Pallas kernels: 10.5 us -> 9.41 us
    unnamed x8 -> x4, local copies, waits for them, and re-layouts: 1.86 us -> 0.01 us
    ppermute x1, waiting for transfers between devices: 1.62 us -> 2.65 us  [local(): sides = (lax.ppermute(got[1], 'rad', [(0, 1), (1, 0)]),)]
    pallas_call x1, Pallas kernels: 4.87 us -> 4.18 us  [local(): call(part(stages, n_ax, n_rad, ca, cz, slots), (struct((ndev, 1, 128)), s...]
    pallas_call x2 -> x1, Pallas kernels: 1.44 us -> 1.18 us  [local(): call(part(signals, slots), struct((obs_weight.shape[0], NB)), [VMEM] * 3,...]
  transfers between devices with their start and end apart: 8 -> 8, of which waited for: 5 -> 5; matrix products, arithmetic and copies ran while one was open for 0% -> 0% of each run, Pallas kernels for 7% -> 6%
where the time goes in v12:
time: 38.9 us; the launch traced here: 38.7 us
  starting transfers between devices  16.4 us (42%)
  waiting for transfers between devices  12.2 us (31%)
  Pallas kernels  9.41 us (24%)
  between operations  0.71 us (2%)
    ppermute x6, starting transfers between devices, swap(): return (lax.ppermute(first, axis, one), lax.ppermute(second, axis, two))  7.96 us
    all_to_all x1, starting transfers between devices, local(): lax.all_to_all(q, ('y', 'core', 'az', 'rad'), 0, 0, tiled=True)  6.88 us
    all_to_all x1, waiting for transfers between devices, local(): lax.all_to_all(q, ('y', 'core', 'az', 'rad'), 0, 0, tiled=True)  5.47 us
    pallas_call x1, Pallas kernels, local(): call(part(stages, n_ax, n_rad, ca, cz, slots), (struct((ndev, 1, 128)), s...  4.18 us
    ppermute x6, waiting for transfers between devices, swap(): return (lax.ppermute(first, axis, one), lax.ppermute(second, axis, two))  4.06 us
    ppermute x1, waiting for transfers between devices, local(): sides = (lax.ppermute(got[1], 'rad', [(0, 1), (1, 0)]),)  2.65 us
    pallas_call x1, Pallas kernels, local(): call(part(last_stage, ca, cz), struct((5, ca, cz, cr)), [VMEM] * 3, [pltp...  1.57 us
    ppermute x1, starting transfers between devices, local(): sides = (lax.ppermute(got[1], 'rad', [(0, 1), (1, 0)]),)  1.56 us
  transfers between devices with their start and end apart: 8, of which 5 were waited for; matrix products, arithmetic and copies ran while one was open for 0% of the time, Pallas kernels for 6%

profile of v12, /device:TPU:0, one launch (start us, length us, event | category | flops | bytes accessed | tf_op | source)
XLA Modules:
  0.0 38.7 jit_solution(7480219896658869774)
XLA Ops:
  0.6 1.1 %shard_map.77 = (f32[640,128]{1,0:T(8,128)S(1)}, bf16[480,128]{1,0:T(8,128)(2,1)S(1)}, bf16[480,128]{1,0:T(8,128)(2,1)S(1)}, bf16[240,128]{1,0:T(8,128)(2,1)S(1)}, bf16[240,128]{1,0:T(8,128)(2,1)S(1)}) custom-call(f32[128,128]{1,0:T(8,128)} %bitcast.8, f32[384,128]{1,0:T(8,128)} %bitcast.7, f32[128,128]{1,0:T(8,128)} %bitcast.9), custom_call_target="tpu_custom_call" | custom-call | tf_op jit(solution)/shard_map/pallas_call | solution.py:538
  1.7 0.5 %collective-permute-start = (bf16[480,128]{1,0:T(8,128)(2,1)S(1)}, bf16[480,128]{1,0:T(8,128)(2,1)S(1)}, u32[]{:S(2)}, u32[]{:S(2)}) collective-permute-start(bf16[480,128]{1,0:T(8,128)(2,1)S(1)} %get-tuple-element.20), channel_id=1, source_target_pairs={{0,8},{8,0},{16,24},{24,16},{1,9},{9,1},{17,25},{25,17},{2,10},{10... | collective-permute-start | bytes 368648 | tf_op jit(solution)/shard_map/ppermute | solution.py:524
  2.2 0.7 %collective-permute-start.1 = (bf16[480,128]{1,0:T(8,128)(2,1)S(1)}, bf16[480,128]{1,0:T(8,128)(2,1)S(1)}, u32[]{:S(2)}, u32[]{:S(2)}) collective-permute-start(bf16[480,128]{1,0:T(8,128)(2,1)S(1)} %get-tuple-element.21), channel_id=1, source_target_pairs={{0,0},{8,16},{16,8},{24,24},{1,1},{9,17},{17,9},{25,25},{2,2},{10,... | collective-permute-start | bytes 368648 | tf_op jit(solution)/shard_map/ppermute | solution.py:524
  2.9 2.7 %collective-permute-start.2 = (bf16[240,128]{1,0:T(8,128)(2,1)S(1)}, bf16[240,128]{1,0:T(8,128)(2,1)S(1)}, u32[]{:S(2)}, u32[]{:S(2)}) collective-permute-start(bf16[240,128]{1,0:T(8,128)(2,1)S(1)} %get-tuple-element.22), channel_id=1, source_target_pairs={{0,2},{2,0},{4,6},{6,4},{1,3},{3,1},{5,7},{7,5},{8,10},{10,8},{12,... | collective-permute-start | bytes 184328 | tf_op jit(solution)/shard_map/ppermute | solution.py:524
  5.6 2.5 %collective-permute-start.3 = (bf16[240,128]{1,0:T(8,128)(2,1)S(1)}, bf16[240,128]{1,0:T(8,128)(2,1)S(1)}, u32[]{:S(2)}, u32[]{:S(2)}) collective-permute-start(bf16[240,128]{1,0:T(8,128)(2,1)S(1)} %get-tuple-element.23), channel_id=1, source_target_pairs={{0,6},{2,4},{4,2},{6,0},{1,7},{3,5},{5,3},{7,1},{8,14},{10,12},{12... | collective-permute-start | bytes 184328 | tf_op jit(solution)/shard_map/ppermute | solution.py:524
  8.1 0.0 collective-permute-done.ax1.got1
  8.1 0.0 collective-permute-done.1.ax2.got2
  8.1 0.1 shard_map.80
  8.2 0.7 %collective-permute-start.4 = (bf16[160,128]{1,0:T(8,128)(2,1)S(1)}, bf16[160,128]{1,0:T(8,128)(2,1)S(1)}, u32[]{:S(2)}, u32[]{:S(2)}) collective-permute-start(bf16[160,128]{1,0:T(8,128)(2,1)S(1)} %get-tuple-element.24), channel_id=1, source_target_pairs={{0,2},{2,0},{4,6},{6,4},{1,3},{3,1},{5,7},{7,5},{8,10},{10,8},{12,... | collective-permute-start | bytes 122888 | tf_op jit(solution)/shard_map/ppermute | solution.py:524
  8.9 0.9 %collective-permute-start.5 = (bf16[160,128]{1,0:T(8,128)(2,1)S(1)}, bf16[160,128]{1,0:T(8,128)(2,1)S(1)}, u32[]{:S(2)}, u32[]{:S(2)}) collective-permute-start(bf16[160,128]{1,0:T(8,128)(2,1)S(1)} %get-tuple-element.25), channel_id=1, source_target_pairs={{0,6},{2,4},{4,2},{6,0},{1,7},{3,5},{5,3},{7,1},{8,14},{10,12},{12... | collective-permute-start | bytes 122888 | tf_op jit(solution)/shard_map/ppermute | solution.py:524
  9.8 0.5 %shard_map.78 = (f32[3200,128]{1,0:T(8,128)S(1)}, bf16[256,256]{1,0:T(8,128)(2,1)S(1)}, bf16[2048,128]{1,0:T(8,128)(2,1)S(1)}, bf16[128,512]{1,0:T(8,128)(2,1)S(1)}) custom-call(f32[640,128]{1,0:T(8,128)S(1)} %get-tuple-element.18.home), custom_call_target="tpu_custom_call" | custom-call | tf_op jit(solution)/shard_map/pallas_call | solution.py:550
  10.3 0.0 collective-permute-done.2.az1
  10.3 1.4 %collective-permute-done.3.az2 = bf16[240,128]{1,0:T(8,128)(2,1)S(1)} collective-permute-done((bf16[240,128]{1,0:T(8,128)(2,1)S(1)}, bf16[240,128]{1,0:T(8,128)(2,1)S(1)}, u32[]{:S(2)}, u32[]{:S(2)}) %collective-permute-start.3) | collective-permute-done | bytes 61472 | tf_op jit(solution)/shard_map/ppermute | solution.py:524
  11.8 0.3 shard_map.79.block_in
  12.1 0.1 collective-permute-done.4.corner1
  12.2 2.5 %collective-permute-done.5.corner2 = bf16[160,128]{1,0:T(8,128)(2,1)S(1)} collective-permute-done((bf16[160,128]{1,0:T(8,128)(2,1)S(1)}, bf16[160,128]{1,0:T(8,128)(2,1)S(1)}, u32[]{:S(2)}, u32[]{:S(2)}) %collective-permute-start.5) | collective-permute-done | bytes 40992 | tf_op jit(solution)/shard_map/ppermute | solution.py:524
  14.7 0.5 %shard_map.81 = (f32[3200,128]{1,0:T(8,128)S(1)}, bf16[160,128]{1,0:T(8,128)(2,1)S(1)}) custom-call(f32[3200,128]{1,0:T(8,128)S(1)} %shard_map.79.block_in, bf16[160,128]{1,0:T(8,128)(2,1)S(1)} %collective-permute-done.4.corner1, bf16[160,128]{1,0:T(8,128)(2,1)S(1)} %collective-permute-done.5.corner2, ...), custom_call_target="tpu_custom_call", output_to_operand_aliasing={{0}: (0, {})} | custom-call | tf_op jit(solution)/shard_map/pallas_call | solution.py:572
  15.2 1.6 %collective-permute-start.6 = (bf16[160,128]{1,0:T(8,128)(2,1)S(1)}, bf16[160,128]{1,0:T(8,128)(2,1)S(1)}, u32[]{:S(2)}, u32[]{:S(2)}) collective-permute-start(bf16[160,128]{1,0:T(8,128)(2,1)S(1)} %get-tuple-element.29), channel_id=1, source_target_pairs={{0,1},{1,0},{2,3},{3,2},{4,5},{5,4},{6,7},{7,6},{8,9},{9,8},{10,11... | collective-permute-start | bytes 122888 | tf_op jit(solution)/shard_map/ppermute | solution.py:582
  16.7 2.7 %collective-permute-done.6.refs_0_ = bf16[160,128]{1,0:T(8,128)(2,1)S(1)} collective-permute-done((bf16[160,128]{1,0:T(8,128)(2,1)S(1)}, bf16[160,128]{1,0:T(8,128)(2,1)S(1)}, u32[]{:S(2)}, u32[]{:S(2)}) %collective-permute-start.6) | collective-permute-done | bytes 40992 | tf_op jit(solution)/shard_map/ppermute | solution.py:582
  19.4 4.2 %shard_map.82 = (f32[32,1,128]{2,1,0:T(1,128)}, f32[5,12,40,128]{3,2,1,0:T(8,128)S(1)}, f32[5,8,32,128]{3,2,1,0:T(8,128)S(1)}) custom-call(f32[5,20,32,128]{3,2,1,0:T(8,128)S(1)} %bitcast.5, bf16[256,256]{1,0:T(8,128)(2,1)S(1)} %get-tuple-element.28.banded, s32[32]{0:T(128)} %cells_far.1, bf16[160,128]{1,0:T(8,128)(2,1)S(1)} %collective-permute-done.6.refs_0_, ...), custom_call_target="tpu_custom_call" | custom-call | tf_op jit(solution)/shard_map/pallas_call | solution.py:588
  23.6 0.0 copy-start
  23.6 0.0 copy-start.1
  23.6 6.9 %all-to-all-start = ((f32[32,1,128]{2,1,0:T(1,128)}), f32[32,1,128]{2,1,0:T(1,128)S(1)}, u32[]{:S(2)}, u32[]{:S(2)}) async-start(f32[32,1,128]{2,1,0:T(1,128)} %get-tuple-element.33), calls=%async_computation | async-start | bytes 32768 | tf_op jit(solution)/shard_map/all_to_all | solution.py:599
  30.5 1.6 %shard_map.83 = f32[5,8,16,128]{3,2,1,0:T(8,128)} custom-call(f32[5,12,40,128]{3,2,1,0:T(8,128)S(1)} %get-tuple-element.31.u2, f32[5,8,32,128]{3,2,1,0:T(8,128)S(1)} %get-tuple-element.32.u0, bf16[256,256]{1,0:T(8,128)(2,1)S(1)} %get-tuple-element.28.banded), custom_call_target="tpu_custom_call" | custom-call | flops 400000000 | bytes 8000000 | tf_op jit(solution)/shard_map/pallas_call | solution.py:602
  32.1 5.5 %all-to-all-done = f32[32,1,128]{2,1,0:T(1,128)S(1)} async-done(((f32[32,1,128]{2,1,0:T(1,128)}), f32[32,1,128]{2,1,0:T(1,128)S(1)}, u32[]{:S(2)}, u32[]{:S(2)}) %all-to-all-start) | async-done | bytes 16416 | tf_op jit(solution)/shard_map/all_to_all | solution.py:599
  37.5 0.0 copy-done
  37.5 0.0 copy-done.1
  37.5 1.2 %shard_map.84 = f32[256,128]{1,0:T(8,128)} custom-call(f32[32,128]{1,0:T(8,128)S(1)} %bitcast.6, s32[1,32]{1,0:T(1,128)S(1)} %copy-done.1, bf16[256,1024]{1,0:T(8,128)(2,1)S(1)} %copy-done), custom_call_target="tpu_custom_call" | custom-call | tf_op jit(solution)/shard_map/pallas_call | solution.py:610
Async XLA Ops:
  1.7 6.3 %collective-permute-start = (bf16[480,128]{1,0:T(8,128)(2,1)S(1)}, bf16[480,128]{1,0:T(8,128)(2,1)S(1)}, u32[]{:S(2)}, u32[]{:S(2)}) collective-permute-start(bf16[480,128]{1,0:T(8,128)(2,1)S(1)} %get-tuple-element.20), channel_id=1, source_target_pairs={{0,8},{8,0},{16,24},{24,16},{1,9},{9,1},{17,25},{25,17},{2,10},{10... | collective-permute-start | bytes 368648 | tf_op jit(solution)/shard_map/ppermute | solution.py:524
  2.2 5.8 %collective-permute-start.1 = (bf16[480,128]{1,0:T(8,128)(2,1)S(1)}, bf16[480,128]{1,0:T(8,128)(2,1)S(1)}, u32[]{:S(2)}, u32[]{:S(2)}) collective-permute-start(bf16[480,128]{1,0:T(8,128)(2,1)S(1)} %get-tuple-element.21), channel_id=1, source_target_pairs={{0,0},{8,16},{16,8},{24,24},{1,1},{9,17},{17,9},{25,25},{2,2},{10,... | collective-permute-start | bytes 368648 | tf_op jit(solution)/shard_map/ppermute | solution.py:524
  2.9 7.4 %collective-permute-start.2 = (bf16[240,128]{1,0:T(8,128)(2,1)S(1)}, bf16[240,128]{1,0:T(8,128)(2,1)S(1)}, u32[]{:S(2)}, u32[]{:S(2)}) collective-permute-start(bf16[240,128]{1,0:T(8,128)(2,1)S(1)} %get-tuple-element.22), channel_id=1, source_target_pairs={{0,2},{2,0},{4,6},{6,4},{1,3},{3,1},{5,7},{7,5},{8,10},{10,8},{12,... | collective-permute-start | bytes 184328 | tf_op jit(solution)/shard_map/ppermute | solution.py:524
  5.6 6.2 %collective-permute-start.3 = (bf16[240,128]{1,0:T(8,128)(2,1)S(1)}, bf16[240,128]{1,0:T(8,128)(2,1)S(1)}, u32[]{:S(2)}, u32[]{:S(2)}) collective-permute-start(bf16[240,128]{1,0:T(8,128)(2,1)S(1)} %get-tuple-element.23), channel_id=1, source_target_pairs={{0,6},{2,4},{4,2},{6,0},{1,7},{3,5},{5,3},{7,1},{8,14},{10,12},{12... | collective-permute-start | bytes 184328 | tf_op jit(solution)/shard_map/ppermute | solution.py:524
  8.2 4.1 %collective-permute-start.4 = (bf16[160,128]{1,0:T(8,128)(2,1)S(1)}, bf16[160,128]{1,0:T(8,128)(2,1)S(1)}, u32[]{:S(2)}, u32[]{:S(2)}) collective-permute-start(bf16[160,128]{1,0:T(8,128)(2,1)S(1)} %get-tuple-element.24), channel_id=1, source_target_pairs={{0,2},{2,0},{4,6},{6,4},{1,3},{3,1},{5,7},{7,5},{8,10},{10,8},{12,... | collective-permute-start | bytes 122888 | tf_op jit(solution)/shard_map/ppermute | solution.py:524
  8.9 5.8 %collective-permute-start.5 = (bf16[160,128]{1,0:T(8,128)(2,1)S(1)}, bf16[160,128]{1,0:T(8,128)(2,1)S(1)}, u32[]{:S(2)}, u32[]{:S(2)}) collective-permute-start(bf16[160,128]{1,0:T(8,128)(2,1)S(1)} %get-tuple-element.25), channel_id=1, source_target_pairs={{0,6},{2,4},{4,2},{6,0},{1,7},{3,5},{5,3},{7,1},{8,14},{10,12},{12... | collective-permute-start | bytes 122888 | tf_op jit(solution)/shard_map/ppermute | solution.py:524
  15.2 4.2 %collective-permute-start.6 = (bf16[160,128]{1,0:T(8,128)(2,1)S(1)}, bf16[160,128]{1,0:T(8,128)(2,1)S(1)}, u32[]{:S(2)}, u32[]{:S(2)}) collective-permute-start(bf16[160,128]{1,0:T(8,128)(2,1)S(1)} %get-tuple-element.29), channel_id=1, source_target_pairs={{0,1},{1,0},{2,3},{3,2},{4,5},{5,4},{6,7},{7,6},{8,9},{9,8},{10,11... | collective-permute-start | bytes 122888 | tf_op jit(solution)/shard_map/ppermute | solution.py:582
  23.6 14.0 %copy-start = (bf16[256,1024]{1,0:T(8,128)(2,1)S(1)}, bf16[256,1024]{1,0:T(8,128)(2,1)}, u32[]{:S(2)}) copy-start(bf16[256,1024]{1,0:T(8,128)(2,1)} %weight.1) | copy-start | bytes 1572868
  23.6 13.9 %copy-start.1 = (s32[1,32]{1,0:T(1,128)S(1)}, s32[1,32]{1,0:T(1,128)}, u32[]{:S(2)}) copy-start(s32[1,32]{1,0:T(1,128)} %offsets.1) | copy-start | bytes 388
  23.6 13.9 %all-to-all-start = ((f32[32,1,128]{2,1,0:T(1,128)}), f32[32,1,128]{2,1,0:T(1,128)S(1)}, u32[]{:S(2)}, u32[]{:S(2)}) async-start(f32[32,1,128]{2,1,0:T(1,128)} %get-tuple-element.33), calls=%async_computation | async-start | bytes 32768 | tf_op jit(solution)/shard_map/all_to_all | solution.py:599

commit v13 on v12

--- a/solution.py
+++ b/solution.py
@@ -18,7 +18,7 @@
 OFF = 8
 SPAN = 32
 TALL = ROWS + 8
-STEP = 4
+STEPS = 2
 SLOT = 8
 HBM = pltpu.MemorySpace.HBM
 VMEM = pltpu.MemorySpace.VMEM
@@ -358,9 +358,11 @@
     for j in (low - 6, low - 5, high + 4, high + 5):
         ax_only(start_state(j, False)[1], fax, j)
 
-    @pl.loop(0, (ca + 8) // STEP)
+    step = (ca + 2 * MID) // STEPS
+
+    @pl.loop(0, STEPS)
     def _(i):
-        js = [low - 4 + STEP * i + k for k in range(STEP)]
+        js = [low - 4 + step * i + k for k in range(step)]
         us = []
         for j in js:
             rho, u = start_state(j, True)
@@ -405,9 +407,11 @@
     for j in (low - 4, low - 3, high + 2, high + 3):
         ax_only(split_state([second[f, j, 0:ROWS] for f in range(5)]), fax, j)
 
-    @pl.loop(0, (ca + 4) // STEP)
+    step2 = (ca + MID) // STEPS
+
+    @pl.loop(0, STEPS)
     def _(i):
-        js = [low - 2 + STEP * i + k for k in range(STEP)]
+        js = [low - 2 + step2 * i + k for k in range(step2)]
         us = []
         for j in js:
             u = split_state([second[f, j] for f in range(5)])
@@ -458,9 +462,11 @@
     for j in (0, 1, ca + 2, ca + 3):
         ax_only(split_state([u2[f, j, 0:ROWS] for f in range(5)]), fax, j)
 
-    @pl.loop(0, ca // STEP)
+    step = ca // STEPS
+
+    @pl.loop(0, STEPS)
     def _(i):
-        js = [2 + STEP * i + k for k in range(STEP)]
+        js = [2 + step * i + k for k in range(step)]
         us = [split_state([u2[f, j] for f in range(5)]) for j in js]
         both_sides(us, js, fax, part, banded)
 

time: 38.9 us -> 38.7 us (level)
  no operation moved by 1% of the time
where the time goes in v13:
time: 38.7 us; the launch traced here: 38.5 us
  starting transfers between devices  16.4 us (42%)
  waiting for transfers between devices  12.2 us (32%)
  Pallas kernels  9.18 us (24%)
  between operations  0.71 us (2%)
    ppermute x6, starting transfers between devices, swap(): return (lax.ppermute(first, axis, one), lax.ppermute(second, axis, two))  7.96 us
    all_to_all x1, starting transfers between devices, local(): lax.all_to_all(q, ('y', 'core', 'az', 'rad'), 0, 0, tiled=True)  6.88 us
    all_to_all x1, waiting for transfers between devices, local(): lax.all_to_all(q, ('y', 'core', 'az', 'rad'), 0, 0, tiled=True)  5.47 us
    ppermute x6, waiting for transfers between devices, swap(): return (lax.ppermute(first, axis, one), lax.ppermute(second, axis, two))  4.06 us
    pallas_call x1, Pallas kernels, local(): call(part(stages, n_ax, n_rad, ca, cz, slots), (struct((ndev, 1, 128)), s...  3.96 us
    ppermute x1, waiting for transfers between devices, local(): sides = (lax.ppermute(got[1], 'rad', [(0, 1), (1, 0)]),)  2.65 us
    pallas_call x1, Pallas kernels, local(): call(part(last_stage, ca, cz), struct((5, ca, cz, cr)), [VMEM] * 3, [pltp...  1.57 us
    ppermute x1, starting transfers between devices, local(): sides = (lax.ppermute(got[1], 'rad', [(0, 1), (1, 0)]),)  1.56 us
  transfers between devices with their start and end apart: 8, of which 5 were waited for; matrix products, arithmetic and copies ran while one was open for 0% of the time, Pallas kernels for 6%

profile of v13, /device:TPU:0, one launch (start us, length us, event | category | flops | bytes accessed | tf_op | source)
XLA Modules:
  0.0 38.5 jit_solution(9710220761514965014)
XLA Ops:
  0.6 1.1 %shard_map.77 = (f32[640,128]{1,0:T(8,128)S(1)}, bf16[480,128]{1,0:T(8,128)(2,1)S(1)}, bf16[480,128]{1,0:T(8,128)(2,1)S(1)}, bf16[240,128]{1,0:T(8,128)(2,1)S(1)}, bf16[240,128]{1,0:T(8,128)(2,1)S(1)}) custom-call(f32[128,128]{1,0:T(8,128)} %bitcast.8, f32[384,128]{1,0:T(8,128)} %bitcast.7, f32[128,128]{1,0:T(8,128)} %bitcast.9), custom_call_target="tpu_custom_call" | custom-call | tf_op jit(solution)/shard_map/pallas_call | solution.py:544
  1.7 0.5 %collective-permute-start = (bf16[480,128]{1,0:T(8,128)(2,1)S(1)}, bf16[480,128]{1,0:T(8,128)(2,1)S(1)}, u32[]{:S(2)}, u32[]{:S(2)}) collective-permute-start(bf16[480,128]{1,0:T(8,128)(2,1)S(1)} %get-tuple-element.20), channel_id=1, source_target_pairs={{0,8},{8,0},{16,24},{24,16},{1,9},{9,1},{17,25},{25,17},{2,10},{10... | collective-permute-start | bytes 368648 | tf_op jit(solution)/shard_map/ppermute | solution.py:530
  2.2 0.7 %collective-permute-start.1 = (bf16[480,128]{1,0:T(8,128)(2,1)S(1)}, bf16[480,128]{1,0:T(8,128)(2,1)S(1)}, u32[]{:S(2)}, u32[]{:S(2)}) collective-permute-start(bf16[480,128]{1,0:T(8,128)(2,1)S(1)} %get-tuple-element.21), channel_id=1, source_target_pairs={{0,0},{8,16},{16,8},{24,24},{1,1},{9,17},{17,9},{25,25},{2,2},{10,... | collective-permute-start | bytes 368648 | tf_op jit(solution)/shard_map/ppermute | solution.py:530
  2.9 2.7 %collective-permute-start.2 = (bf16[240,128]{1,0:T(8,128)(2,1)S(1)}, bf16[240,128]{1,0:T(8,128)(2,1)S(1)}, u32[]{:S(2)}, u32[]{:S(2)}) collective-permute-start(bf16[240,128]{1,0:T(8,128)(2,1)S(1)} %get-tuple-element.22), channel_id=1, source_target_pairs={{0,2},{2,0},{4,6},{6,4},{1,3},{3,1},{5,7},{7,5},{8,10},{10,8},{12,... | collective-permute-start | bytes 184328 | tf_op jit(solution)/shard_map/ppermute | solution.py:530
  5.6 2.5 %collective-permute-start.3 = (bf16[240,128]{1,0:T(8,128)(2,1)S(1)}, bf16[240,128]{1,0:T(8,128)(2,1)S(1)}, u32[]{:S(2)}, u32[]{:S(2)}) collective-permute-start(bf16[240,128]{1,0:T(8,128)(2,1)S(1)} %get-tuple-element.23), channel_id=1, source_target_pairs={{0,6},{2,4},{4,2},{6,0},{1,7},{3,5},{5,3},{7,1},{8,14},{10,12},{12... | collective-permute-start | bytes 184328 | tf_op jit(solution)/shard_map/ppermute | solution.py:530
  8.1 0.0 collective-permute-done.ax1.got1
  8.1 0.0 collective-permute-done.1.ax2.got2
  8.1 0.1 shard_map.80
  8.2 0.7 %collective-permute-start.4 = (bf16[160,128]{1,0:T(8,128)(2,1)S(1)}, bf16[160,128]{1,0:T(8,128)(2,1)S(1)}, u32[]{:S(2)}, u32[]{:S(2)}) collective-permute-start(bf16[160,128]{1,0:T(8,128)(2,1)S(1)} %get-tuple-element.24), channel_id=1, source_target_pairs={{0,2},{2,0},{4,6},{6,4},{1,3},{3,1},{5,7},{7,5},{8,10},{10,8},{12,... | collective-permute-start | bytes 122888 | tf_op jit(solution)/shard_map/ppermute | solution.py:530
  8.9 0.9 %collective-permute-start.5 = (bf16[160,128]{1,0:T(8,128)(2,1)S(1)}, bf16[160,128]{1,0:T(8,128)(2,1)S(1)}, u32[]{:S(2)}, u32[]{:S(2)}) collective-permute-start(bf16[160,128]{1,0:T(8,128)(2,1)S(1)} %get-tuple-element.25), channel_id=1, source_target_pairs={{0,6},{2,4},{4,2},{6,0},{1,7},{3,5},{5,3},{7,1},{8,14},{10,12},{12... | collective-permute-start | bytes 122888 | tf_op jit(solution)/shard_map/ppermute | solution.py:530
  9.8 0.5 %shard_map.78 = (f32[3200,128]{1,0:T(8,128)S(1)}, bf16[256,256]{1,0:T(8,128)(2,1)S(1)}, bf16[2048,128]{1,0:T(8,128)(2,1)S(1)}, bf16[128,512]{1,0:T(8,128)(2,1)S(1)}) custom-call(f32[640,128]{1,0:T(8,128)S(1)} %get-tuple-element.18.home), custom_call_target="tpu_custom_call" | custom-call | tf_op jit(solution)/shard_map/pallas_call | solution.py:556
  10.3 0.0 collective-permute-done.2.az1
  10.3 1.4 %collective-permute-done.3.az2 = bf16[240,128]{1,0:T(8,128)(2,1)S(1)} collective-permute-done((bf16[240,128]{1,0:T(8,128)(2,1)S(1)}, bf16[240,128]{1,0:T(8,128)(2,1)S(1)}, u32[]{:S(2)}, u32[]{:S(2)}) %collective-permute-start.3) | collective-permute-done | bytes 61472 | tf_op jit(solution)/shard_map/ppermute | solution.py:530
  11.8 0.3 shard_map.79.block_in
  12.1 0.1 collective-permute-done.4.corner1
  12.2 2.5 %collective-permute-done.5.corner2 = bf16[160,128]{1,0:T(8,128)(2,1)S(1)} collective-permute-done((bf16[160,128]{1,0:T(8,128)(2,1)S(1)}, bf16[160,128]{1,0:T(8,128)(2,1)S(1)}, u32[]{:S(2)}, u32[]{:S(2)}) %collective-permute-start.5) | collective-permute-done | bytes 40992 | tf_op jit(solution)/shard_map/ppermute | solution.py:530
  14.7 0.5 %shard_map.81 = (f32[3200,128]{1,0:T(8,128)S(1)}, bf16[160,128]{1,0:T(8,128)(2,1)S(1)}) custom-call(f32[3200,128]{1,0:T(8,128)S(1)} %shard_map.79.block_in, bf16[160,128]{1,0:T(8,128)(2,1)S(1)} %collective-permute-done.4.corner1, bf16[160,128]{1,0:T(8,128)(2,1)S(1)} %collective-permute-done.5.corner2, ...), custom_call_target="tpu_custom_call", output_to_operand_aliasing={{0}: (0, {})} | custom-call | tf_op jit(solution)/shard_map/pallas_call | solution.py:578
  15.2 1.6 %collective-permute-start.6 = (bf16[160,128]{1,0:T(8,128)(2,1)S(1)}, bf16[160,128]{1,0:T(8,128)(2,1)S(1)}, u32[]{:S(2)}, u32[]{:S(2)}) collective-permute-start(bf16[160,128]{1,0:T(8,128)(2,1)S(1)} %get-tuple-element.29), channel_id=1, source_target_pairs={{0,1},{1,0},{2,3},{3,2},{4,5},{5,4},{6,7},{7,6},{8,9},{9,8},{10,11... | collective-permute-start | bytes 122888 | tf_op jit(solution)/shard_map/ppermute | solution.py:588
  16.7 2.7 %collective-permute-done.6.refs_0_ = bf16[160,128]{1,0:T(8,128)(2,1)S(1)} collective-permute-done((bf16[160,128]{1,0:T(8,128)(2,1)S(1)}, bf16[160,128]{1,0:T(8,128)(2,1)S(1)}, u32[]{:S(2)}, u32[]{:S(2)}) %collective-permute-start.6) | collective-permute-done | bytes 40992 | tf_op jit(solution)/shard_map/ppermute | solution.py:588
  19.4 4.0 %shard_map.82 = (f32[32,1,128]{2,1,0:T(1,128)}, f32[5,12,40,128]{3,2,1,0:T(8,128)S(1)}, f32[5,8,32,128]{3,2,1,0:T(8,128)S(1)}) custom-call(f32[5,20,32,128]{3,2,1,0:T(8,128)S(1)} %bitcast.5, bf16[256,256]{1,0:T(8,128)(2,1)S(1)} %get-tuple-element.28.banded, s32[32]{0:T(128)} %cells_far.1, bf16[160,128]{1,0:T(8,128)(2,1)S(1)} %collective-permute-done.6.refs_0_, ...), custom_call_target="tpu_custom_call" | custom-call | tf_op jit(solution)/shard_map/pallas_call | solution.py:594
  23.4 0.0 copy-start
  23.4 0.0 copy-start.1
  23.4 6.9 %all-to-all-start = ((f32[32,1,128]{2,1,0:T(1,128)}), f32[32,1,128]{2,1,0:T(1,128)S(1)}, u32[]{:S(2)}, u32[]{:S(2)}) async-start(f32[32,1,128]{2,1,0:T(1,128)} %get-tuple-element.33), calls=%async_computation | async-start | bytes 32768 | tf_op jit(solution)/shard_map/all_to_all | solution.py:605
  30.3 1.6 %shard_map.83 = f32[5,8,16,128]{3,2,1,0:T(8,128)} custom-call(f32[5,12,40,128]{3,2,1,0:T(8,128)S(1)} %get-tuple-element.31.u2, f32[5,8,32,128]{3,2,1,0:T(8,128)S(1)} %get-tuple-element.32.u0, bf16[256,256]{1,0:T(8,128)(2,1)S(1)} %get-tuple-element.28.banded), custom_call_target="tpu_custom_call" | custom-call | flops 400000000 | bytes 8000000 | tf_op jit(solution)/shard_map/pallas_call | solution.py:608
  31.8 5.5 %all-to-all-done = f32[32,1,128]{2,1,0:T(1,128)S(1)} async-done(((f32[32,1,128]{2,1,0:T(1,128)}), f32[32,1,128]{2,1,0:T(1,128)S(1)}, u32[]{:S(2)}, u32[]{:S(2)}) %all-to-all-start) | async-done | bytes 16416 | tf_op jit(solution)/shard_map/all_to_all | solution.py:605
  37.3 0.0 copy-done
  37.3 0.0 copy-done.1
  37.3 1.2 %shard_map.84 = f32[256,128]{1,0:T(8,128)} custom-call(f32[32,128]{1,0:T(8,128)S(1)} %bitcast.6, s32[1,32]{1,0:T(1,128)S(1)} %copy-done.1, bf16[256,1024]{1,0:T(8,128)(2,1)S(1)} %copy-done), custom_call_target="tpu_custom_call" | custom-call | tf_op jit(solution)/shard_map/pallas_call | solution.py:616
Async XLA Ops:
  1.7 6.3 %collective-permute-start = (bf16[480,128]{1,0:T(8,128)(2,1)S(1)}, bf16[480,128]{1,0:T(8,128)(2,1)S(1)}, u32[]{:S(2)}, u32[]{:S(2)}) collective-permute-start(bf16[480,128]{1,0:T(8,128)(2,1)S(1)} %get-tuple-element.20), channel_id=1, source_target_pairs={{0,8},{8,0},{16,24},{24,16},{1,9},{9,1},{17,25},{25,17},{2,10},{10... | collective-permute-start | bytes 368648 | tf_op jit(solution)/shard_map/ppermute | solution.py:530
  2.2 5.8 %collective-permute-start.1 = (bf16[480,128]{1,0:T(8,128)(2,1)S(1)}, bf16[480,128]{1,0:T(8,128)(2,1)S(1)}, u32[]{:S(2)}, u32[]{:S(2)}) collective-permute-start(bf16[480,128]{1,0:T(8,128)(2,1)S(1)} %get-tuple-element.21), channel_id=1, source_target_pairs={{0,0},{8,16},{16,8},{24,24},{1,1},{9,17},{17,9},{25,25},{2,2},{10,... | collective-permute-start | bytes 368648 | tf_op jit(solution)/shard_map/ppermute | solution.py:530
  2.9 7.4 %collective-permute-start.2 = (bf16[240,128]{1,0:T(8,128)(2,1)S(1)}, bf16[240,128]{1,0:T(8,128)(2,1)S(1)}, u32[]{:S(2)}, u32[]{:S(2)}) collective-permute-start(bf16[240,128]{1,0:T(8,128)(2,1)S(1)} %get-tuple-element.22), channel_id=1, source_target_pairs={{0,2},{2,0},{4,6},{6,4},{1,3},{3,1},{5,7},{7,5},{8,10},{10,8},{12,... | collective-permute-start | bytes 184328 | tf_op jit(solution)/shard_map/ppermute | solution.py:530
  5.6 6.2 %collective-permute-start.3 = (bf16[240,128]{1,0:T(8,128)(2,1)S(1)}, bf16[240,128]{1,0:T(8,128)(2,1)S(1)}, u32[]{:S(2)}, u32[]{:S(2)}) collective-permute-start(bf16[240,128]{1,0:T(8,128)(2,1)S(1)} %get-tuple-element.23), channel_id=1, source_target_pairs={{0,6},{2,4},{4,2},{6,0},{1,7},{3,5},{5,3},{7,1},{8,14},{10,12},{12... | collective-permute-start | bytes 184328 | tf_op jit(solution)/shard_map/ppermute | solution.py:530
  8.2 4.1 %collective-permute-start.4 = (bf16[160,128]{1,0:T(8,128)(2,1)S(1)}, bf16[160,128]{1,0:T(8,128)(2,1)S(1)}, u32[]{:S(2)}, u32[]{:S(2)}) collective-permute-start(bf16[160,128]{1,0:T(8,128)(2,1)S(1)} %get-tuple-element.24), channel_id=1, source_target_pairs={{0,2},{2,0},{4,6},{6,4},{1,3},{3,1},{5,7},{7,5},{8,10},{10,8},{12,... | collective-permute-start | bytes 122888 | tf_op jit(solution)/shard_map/ppermute | solution.py:530
  8.9 5.8 %collective-permute-start.5 = (bf16[160,128]{1,0:T(8,128)(2,1)S(1)}, bf16[160,128]{1,0:T(8,128)(2,1)S(1)}, u32[]{:S(2)}, u32[]{:S(2)}) collective-permute-start(bf16[160,128]{1,0:T(8,128)(2,1)S(1)} %get-tuple-element.25), channel_id=1, source_target_pairs={{0,6},{2,4},{4,2},{6,0},{1,7},{3,5},{5,3},{7,1},{8,14},{10,12},{12... | collective-permute-start | bytes 122888 | tf_op jit(solution)/shard_map/ppermute | solution.py:530
  15.2 4.2 %collective-permute-start.6 = (bf16[160,128]{1,0:T(8,128)(2,1)S(1)}, bf16[160,128]{1,0:T(8,128)(2,1)S(1)}, u32[]{:S(2)}, u32[]{:S(2)}) collective-permute-start(bf16[160,128]{1,0:T(8,128)(2,1)S(1)} %get-tuple-element.29), channel_id=1, source_target_pairs={{0,1},{1,0},{2,3},{3,2},{4,5},{5,4},{6,7},{7,6},{8,9},{9,8},{10,11... | collective-permute-start | bytes 122888 | tf_op jit(solution)/shard_map/ppermute | solution.py:588
  23.4 14.0 %copy-start = (bf16[256,1024]{1,0:T(8,128)(2,1)S(1)}, bf16[256,1024]{1,0:T(8,128)(2,1)}, u32[]{:S(2)}) copy-start(bf16[256,1024]{1,0:T(8,128)(2,1)} %weight.1) | copy-start | bytes 1572868
  23.4 13.9 %copy-start.1 = (s32[1,32]{1,0:T(1,128)S(1)}, s32[1,32]{1,0:T(1,128)}, u32[]{:S(2)}) copy-start(s32[1,32]{1,0:T(1,128)} %offsets.1) | copy-start | bytes 388
  23.4 13.9 %all-to-all-start = ((f32[32,1,128]{2,1,0:T(1,128)}), f32[32,1,128]{2,1,0:T(1,128)S(1)}, u32[]{:S(2)}, u32[]{:S(2)}) async-start(f32[32,1,128]{2,1,0:T(1,128)} %get-tuple-element.33), calls=%async_computation | async-start | bytes 32768 | tf_op jit(solution)/shard_map/all_to_all | solution.py:605

commit v14 on v13

--- a/solution.py
+++ b/solution.py
@@ -18,7 +18,7 @@
 OFF = 8
 SPAN = 32
 TALL = ROWS + 8
-STEPS = 2
+STEPS = 1
 SLOT = 8
 HBM = pltpu.MemorySpace.HBM
 VMEM = pltpu.MemorySpace.VMEM
@@ -57,7 +57,9 @@
 
 
 def first_is_up(axis):
-    return lax.axis_index("core" if axis == "ax" else axis) % 2 == 0
+    if axis == "ax":
+        return lax.axis_index("core") == 0
+    return lax.axis_index("az") % 2 == 1
 
 
 def load_and_pack(ca, cz, den, vel, pre, home, ax1, ax2, az1, az2, sems):
@@ -527,6 +529,8 @@
     for name in (axis,) if isinstance(axis, str) else axis:
         count = count * lax.axis_size(name)
     one, two = swap_pairs(count, periodic)
+    if periodic:
+        one, two = two, one
     return lax.ppermute(first, axis, one), lax.ppermute(second, axis, two)
 
 

time: 38.7 us -> 38.1 us (0.984)
  waiting for transfers between devices: 12.2 us -> 11.1 us
  starting transfers between devices: 16.4 us -> 17.1 us
    ppermute x6, waiting for transfers between devices: 4.06 us -> 3.06 us  [swap(): return (lax.ppermute(first, axis, one), lax.ppermute(second, axis, two))]
    all_to_all x1, starting transfers between devices: 6.88 us -> 7.55 us  [local(): lax.all_to_all(q, ('y', 'core', 'az', 'rad'), 0, 0, tiled=True)]
  transfers between devices with their start and end apart: 8 -> 8, of which waited for: 5 -> 4; matrix products, arithmetic and copies ran while one was open for 0% -> 0% of each run, Pallas kernels for 6% -> 6%
where the time goes in v14:
time: 38.1 us; the launch traced here: 37.9 us
  starting transfers between devices  17.1 us (45%)
  waiting for transfers between devices  11.1 us (29%)
  Pallas kernels  8.95 us (23%)
  between operations  0.71 us (2%)
    ppermute x6, starting transfers between devices, swap(): return (lax.ppermute(first, axis, one), lax.ppermute(second, axis, two))  8.02 us
    all_to_all x1, starting transfers between devices, local(): lax.all_to_all(q, ('y', 'core', 'az', 'rad'), 0, 0, tiled=True)  7.55 us
    all_to_all x1, waiting for transfers between devices, local(): lax.all_to_all(q, ('y', 'core', 'az', 'rad'), 0, 0, tiled=True)  5.56 us
    pallas_call x1, Pallas kernels, local(): call(part(stages, n_ax, n_rad, ca, cz, slots), (struct((ndev, 1, 128)), s...  3.85 us
    ppermute x6, waiting for transfers between devices, swap(): return (lax.ppermute(first, axis, one), lax.ppermute(second, axis, two))  3.06 us
    ppermute x1, waiting for transfers between devices, local(): sides = (lax.ppermute(got[1], 'rad', [(0, 1), (1, 0)]),)  2.51 us
    ppermute x1, starting transfers between devices, local(): sides = (lax.ppermute(got[1], 'rad', [(0, 1), (1, 0)]),)  1.56 us
    pallas_call x1, Pallas kernels, local(): call(part(last_stage, ca, cz), struct((5, ca, cz, cr)), [VMEM] * 3, [pltp...  1.48 us
  transfers between devices with their start and end apart: 8, of which 4 were waited for; matrix products, arithmetic and copies ran while one was open for 0% of the time, Pallas kernels for 6%

profile of v14, /device:TPU:0, one launch (start us, length us, event | category | flops | bytes accessed | tf_op | source)
XLA Modules:
  0.0 37.9 jit_solution(13428213272047735341)
XLA Ops:
  0.6 1.1 %shard_map.77 = (f32[640,128]{1,0:T(8,128)S(1)}, bf16[480,128]{1,0:T(8,128)(2,1)S(1)}, bf16[480,128]{1,0:T(8,128)(2,1)S(1)}, bf16[240,128]{1,0:T(8,128)(2,1)S(1)}, bf16[240,128]{1,0:T(8,128)(2,1)S(1)}) custom-call(f32[128,128]{1,0:T(8,128)} %bitcast.8, f32[384,128]{1,0:T(8,128)} %bitcast.7, f32[128,128]{1,0:T(8,128)} %bitcast.9), custom_call_target="tpu_custom_call" | custom-call | tf_op jit(solution)/shard_map/pallas_call | solution.py:548
  1.7 0.5 %collective-permute-start = (bf16[480,128]{1,0:T(8,128)(2,1)S(1)}, bf16[480,128]{1,0:T(8,128)(2,1)S(1)}, u32[]{:S(2)}, u32[]{:S(2)}) collective-permute-start(bf16[480,128]{1,0:T(8,128)(2,1)S(1)} %get-tuple-element.20), channel_id=1, source_target_pairs={{0,8},{8,0},{16,24},{24,16},{1,9},{9,1},{17,25},{25,17},{2,10},{10... | collective-permute-start | bytes 368648 | tf_op jit(solution)/shard_map/ppermute | solution.py:534
  2.2 0.7 %collective-permute-start.1 = (bf16[480,128]{1,0:T(8,128)(2,1)S(1)}, bf16[480,128]{1,0:T(8,128)(2,1)S(1)}, u32[]{:S(2)}, u32[]{:S(2)}) collective-permute-start(bf16[480,128]{1,0:T(8,128)(2,1)S(1)} %get-tuple-element.21), channel_id=1, source_target_pairs={{0,0},{8,16},{16,8},{24,24},{1,1},{9,17},{17,9},{25,25},{2,2},{10,... | collective-permute-start | bytes 368648 | tf_op jit(solution)/shard_map/ppermute | solution.py:534
  2.9 4.7 %collective-permute-start.2 = (bf16[240,128]{1,0:T(8,128)(2,1)S(1)}, bf16[240,128]{1,0:T(8,128)(2,1)S(1)}, u32[]{:S(2)}, u32[]{:S(2)}) collective-permute-start(bf16[240,128]{1,0:T(8,128)(2,1)S(1)} %get-tuple-element.22), channel_id=1, source_target_pairs={{0,6},{2,4},{4,2},{6,0},{1,7},{3,5},{5,3},{7,1},{8,14},{10,12},{12... | collective-permute-start | bytes 184328 | tf_op jit(solution)/shard_map/ppermute | solution.py:534
  7.6 0.0 collective-permute-start.3
  7.6 0.0 collective-permute-done.ax1.got1
  7.6 0.0 collective-permute-done.1.ax2.got2
  7.6 0.1 shard_map.80
  7.7 1.0 %collective-permute-start.4 = (bf16[160,128]{1,0:T(8,128)(2,1)S(1)}, bf16[160,128]{1,0:T(8,128)(2,1)S(1)}, u32[]{:S(2)}, u32[]{:S(2)}) collective-permute-start(bf16[160,128]{1,0:T(8,128)(2,1)S(1)} %get-tuple-element.24), channel_id=1, source_target_pairs={{0,6},{2,4},{4,2},{6,0},{1,7},{3,5},{5,3},{7,1},{8,14},{10,12},{12... | collective-permute-start | bytes 122888 | tf_op jit(solution)/shard_map/ppermute | solution.py:534
  8.7 1.2 %collective-permute-start.5 = (bf16[160,128]{1,0:T(8,128)(2,1)S(1)}, bf16[160,128]{1,0:T(8,128)(2,1)S(1)}, u32[]{:S(2)}, u32[]{:S(2)}) collective-permute-start(bf16[160,128]{1,0:T(8,128)(2,1)S(1)} %get-tuple-element.25), channel_id=1, source_target_pairs={{0,2},{2,0},{4,6},{6,4},{1,3},{3,1},{5,7},{7,5},{8,10},{10,8},{12,... | collective-permute-start | bytes 122888 | tf_op jit(solution)/shard_map/ppermute | solution.py:534
  9.9 0.5 %shard_map.78 = (f32[3200,128]{1,0:T(8,128)S(1)}, bf16[256,256]{1,0:T(8,128)(2,1)S(1)}, bf16[2048,128]{1,0:T(8,128)(2,1)S(1)}, bf16[128,512]{1,0:T(8,128)(2,1)S(1)}) custom-call(f32[640,128]{1,0:T(8,128)S(1)} %get-tuple-element.18.home), custom_call_target="tpu_custom_call" | custom-call | tf_op jit(solution)/shard_map/pallas_call | solution.py:560
  10.4 0.0 collective-permute-done.2.az1
  10.4 2.1 %collective-permute-done.3.az2 = bf16[240,128]{1,0:T(8,128)(2,1)S(1)} collective-permute-done((bf16[240,128]{1,0:T(8,128)(2,1)S(1)}, bf16[240,128]{1,0:T(8,128)(2,1)S(1)}, u32[]{:S(2)}, u32[]{:S(2)}) %collective-permute-start.3) | collective-permute-done | bytes 61472 | tf_op jit(solution)/shard_map/ppermute | solution.py:534
  12.5 0.3 shard_map.79.block_in
  12.8 1.0 %collective-permute-done.4.corner1 = bf16[160,128]{1,0:T(8,128)(2,1)S(1)} collective-permute-done((bf16[160,128]{1,0:T(8,128)(2,1)S(1)}, bf16[160,128]{1,0:T(8,128)(2,1)S(1)}, u32[]{:S(2)}, u32[]{:S(2)}) %collective-permute-start.4) | collective-permute-done | bytes 40992 | tf_op jit(solution)/shard_map/ppermute | solution.py:534
  13.7 0.0 collective-permute-done.5.corner2
  13.7 0.5 %shard_map.81 = (f32[3200,128]{1,0:T(8,128)S(1)}, bf16[160,128]{1,0:T(8,128)(2,1)S(1)}) custom-call(f32[3200,128]{1,0:T(8,128)S(1)} %shard_map.79.block_in, bf16[160,128]{1,0:T(8,128)(2,1)S(1)} %collective-permute-done.4.corner1, bf16[160,128]{1,0:T(8,128)(2,1)S(1)} %collective-permute-done.5.corner2, ...), custom_call_target="tpu_custom_call", output_to_operand_aliasing={{0}: (0, {})} | custom-call | tf_op jit(solution)/shard_map/pallas_call | solution.py:582
  14.2 1.6 %collective-permute-start.6 = (bf16[160,128]{1,0:T(8,128)(2,1)S(1)}, bf16[160,128]{1,0:T(8,128)(2,1)S(1)}, u32[]{:S(2)}, u32[]{:S(2)}) collective-permute-start(bf16[160,128]{1,0:T(8,128)(2,1)S(1)} %get-tuple-element.29), channel_id=1, source_target_pairs={{0,1},{1,0},{2,3},{3,2},{4,5},{5,4},{6,7},{7,6},{8,9},{9,8},{10,11... | collective-permute-start | bytes 122888 | tf_op jit(solution)/shard_map/ppermute | solution.py:592
  15.8 2.5 %collective-permute-done.6.refs_0_ = bf16[160,128]{1,0:T(8,128)(2,1)S(1)} collective-permute-done((bf16[160,128]{1,0:T(8,128)(2,1)S(1)}, bf16[160,128]{1,0:T(8,128)(2,1)S(1)}, u32[]{:S(2)}, u32[]{:S(2)}) %collective-permute-start.6) | collective-permute-done | bytes 40992 | tf_op jit(solution)/shard_map/ppermute | solution.py:592
  18.3 3.8 %shard_map.82 = (f32[32,1,128]{2,1,0:T(1,128)}, f32[5,12,40,128]{3,2,1,0:T(8,128)S(1)}, f32[5,8,32,128]{3,2,1,0:T(8,128)S(1)}) custom-call(f32[5,20,32,128]{3,2,1,0:T(8,128)S(1)} %bitcast.5, bf16[256,256]{1,0:T(8,128)(2,1)S(1)} %get-tuple-element.28.banded, s32[32]{0:T(128)} %cells_far.1, bf16[160,128]{1,0:T(8,128)(2,1)S(1)} %collective-permute-done.6.refs_0_, ...), custom_call_target="tpu_custom_call" | custom-call | tf_op jit(solution)/shard_map/pallas_call | solution.py:598
  22.1 0.0 copy-start
  22.1 0.0 copy-start.1
  22.2 7.5 %all-to-all-start = ((f32[32,1,128]{2,1,0:T(1,128)}), f32[32,1,128]{2,1,0:T(1,128)S(1)}, u32[]{:S(2)}, u32[]{:S(2)}) async-start(f32[32,1,128]{2,1,0:T(1,128)} %get-tuple-element.33), calls=%async_computation | async-start | bytes 32768 | tf_op jit(solution)/shard_map/all_to_all | solution.py:609
  29.7 1.5 %shard_map.83 = f32[5,8,16,128]{3,2,1,0:T(8,128)} custom-call(f32[5,12,40,128]{3,2,1,0:T(8,128)S(1)} %get-tuple-element.31.u2, f32[5,8,32,128]{3,2,1,0:T(8,128)S(1)} %get-tuple-element.32.u0, bf16[256,256]{1,0:T(8,128)(2,1)S(1)} %get-tuple-element.28.banded), custom_call_target="tpu_custom_call" | custom-call | flops 400000000 | bytes 8000000 | tf_op jit(solution)/shard_map/pallas_call | solution.py:612
  31.2 5.6 %all-to-all-done = f32[32,1,128]{2,1,0:T(1,128)S(1)} async-done(((f32[32,1,128]{2,1,0:T(1,128)}), f32[32,1,128]{2,1,0:T(1,128)S(1)}, u32[]{:S(2)}, u32[]{:S(2)}) %all-to-all-start) | async-done | bytes 16416 | tf_op jit(solution)/shard_map/all_to_all | solution.py:609
  36.8 0.0 copy-done
  36.8 0.0 copy-done.1
  36.8 1.2 %shard_map.84 = f32[256,128]{1,0:T(8,128)} custom-call(f32[32,128]{1,0:T(8,128)S(1)} %bitcast.6, s32[1,32]{1,0:T(1,128)S(1)} %copy-done.1, bf16[256,1024]{1,0:T(8,128)(2,1)S(1)} %copy-done), custom_call_target="tpu_custom_call" | custom-call | tf_op jit(solution)/shard_map/pallas_call | solution.py:620
Async XLA Ops:
  1.7 5.9 %collective-permute-start = (bf16[480,128]{1,0:T(8,128)(2,1)S(1)}, bf16[480,128]{1,0:T(8,128)(2,1)S(1)}, u32[]{:S(2)}, u32[]{:S(2)}) collective-permute-start(bf16[480,128]{1,0:T(8,128)(2,1)S(1)} %get-tuple-element.20), channel_id=1, source_target_pairs={{0,8},{8,0},{16,24},{24,16},{1,9},{9,1},{17,25},{25,17},{2,10},{10... | collective-permute-start | bytes 368648 | tf_op jit(solution)/shard_map/ppermute | solution.py:534
  2.2 5.4 %collective-permute-start.1 = (bf16[480,128]{1,0:T(8,128)(2,1)S(1)}, bf16[480,128]{1,0:T(8,128)(2,1)S(1)}, u32[]{:S(2)}, u32[]{:S(2)}) collective-permute-start(bf16[480,128]{1,0:T(8,128)(2,1)S(1)} %get-tuple-element.21), channel_id=1, source_target_pairs={{0,0},{8,16},{16,8},{24,24},{1,1},{9,17},{17,9},{25,25},{2,2},{10,... | collective-permute-start | bytes 368648 | tf_op jit(solution)/shard_map/ppermute | solution.py:534
  2.9 7.5 %collective-permute-start.2 = (bf16[240,128]{1,0:T(8,128)(2,1)S(1)}, bf16[240,128]{1,0:T(8,128)(2,1)S(1)}, u32[]{:S(2)}, u32[]{:S(2)}) collective-permute-start(bf16[240,128]{1,0:T(8,128)(2,1)S(1)} %get-tuple-element.22), channel_id=1, source_target_pairs={{0,6},{2,4},{4,2},{6,0},{1,7},{3,5},{5,3},{7,1},{8,14},{10,12},{12... | collective-permute-start | bytes 184328 | tf_op jit(solution)/shard_map/ppermute | solution.py:534
  7.6 4.9 %collective-permute-start.3 = (bf16[240,128]{1,0:T(8,128)(2,1)S(1)}, bf16[240,128]{1,0:T(8,128)(2,1)S(1)}, u32[]{:S(2)}, u32[]{:S(2)}) collective-permute-start(bf16[240,128]{1,0:T(8,128)(2,1)S(1)} %get-tuple-element.23), channel_id=1, source_target_pairs={{0,2},{2,0},{4,6},{6,4},{1,3},{3,1},{5,7},{7,5},{8,10},{10,8},{12,... | collective-permute-start | bytes 184328 | tf_op jit(solution)/shard_map/ppermute | solution.py:534
  7.7 6.0 %collective-permute-start.4 = (bf16[160,128]{1,0:T(8,128)(2,1)S(1)}, bf16[160,128]{1,0:T(8,128)(2,1)S(1)}, u32[]{:S(2)}, u32[]{:S(2)}) collective-permute-start(bf16[160,128]{1,0:T(8,128)(2,1)S(1)} %get-tuple-element.24), channel_id=1, source_target_pairs={{0,6},{2,4},{4,2},{6,0},{1,7},{3,5},{5,3},{7,1},{8,14},{10,12},{12... | collective-permute-start | bytes 122888 | tf_op jit(solution)/shard_map/ppermute | solution.py:534
  8.7 5.1 %collective-permute-start.5 = (bf16[160,128]{1,0:T(8,128)(2,1)S(1)}, bf16[160,128]{1,0:T(8,128)(2,1)S(1)}, u32[]{:S(2)}, u32[]{:S(2)}) collective-permute-start(bf16[160,128]{1,0:T(8,128)(2,1)S(1)} %get-tuple-element.25), channel_id=1, source_target_pairs={{0,2},{2,0},{4,6},{6,4},{1,3},{3,1},{5,7},{7,5},{8,10},{10,8},{12,... | collective-permute-start | bytes 122888 | tf_op jit(solution)/shard_map/ppermute | solution.py:534
  14.2 4.1 %collective-permute-start.6 = (bf16[160,128]{1,0:T(8,128)(2,1)S(1)}, bf16[160,128]{1,0:T(8,128)(2,1)S(1)}, u32[]{:S(2)}, u32[]{:S(2)}) collective-permute-start(bf16[160,128]{1,0:T(8,128)(2,1)S(1)} %get-tuple-element.29), channel_id=1, source_target_pairs={{0,1},{1,0},{2,3},{3,2},{4,5},{5,4},{6,7},{7,6},{8,9},{9,8},{10,11... | collective-permute-start | bytes 122888 | tf_op jit(solution)/shard_map/ppermute | solution.py:592
  22.1 14.6 %copy-start = (bf16[256,1024]{1,0:T(8,128)(2,1)S(1)}, bf16[256,1024]{1,0:T(8,128)(2,1)}, u32[]{:S(2)}) copy-start(bf16[256,1024]{1,0:T(8,128)(2,1)} %weight.1) | copy-start | bytes 1572868
  22.1 14.6 %copy-start.1 = (s32[1,32]{1,0:T(1,128)S(1)}, s32[1,32]{1,0:T(1,128)}, u32[]{:S(2)}) copy-start(s32[1,32]{1,0:T(1,128)} %offsets.1) | copy-start | bytes 388
  22.2 14.6 %all-to-all-start = ((f32[32,1,128]{2,1,0:T(1,128)}), f32[32,1,128]{2,1,0:T(1,128)S(1)}, u32[]{:S(2)}, u32[]{:S(2)}) async-start(f32[32,1,128]{2,1,0:T(1,128)} %get-tuple-element.33), calls=%async_computation | async-start | bytes 32768 | tf_op jit(solution)/shard_map/all_to_all | solution.py:609

commit v15 on v14

--- a/solution.py
+++ b/solution.py
@@ -74,7 +74,7 @@
     for copy in copies:
         copy.wait()
     up = first_is_up("ax")
-    edge = REACH * cz
+    edge = MID * cz
     for f in range(5):
         at = f * size
         low = home[at : at + edge, :]
@@ -104,12 +104,11 @@
 
 def pack_corners(n_ax, cz, got1, got2, first_out, second_out, near):
     up = first_is_up("az")
-    half = MID * cz
-    size = REACH * cz
+    size = MID * cz
     for f in range(5):
         lo, hi = ax_sides(n_ax, got1, got2, slice(f * size, (f + 1) * size))
-        near[f, 0:half, :] = lo[size - half :]
-        near[f, half : 2 * half, :] = hi[0:half]
+        near[f, 0:size, :] = lo
+        near[f, size : 2 * size, :] = hi
     low, high = [], []
     for f in range(5):
         for d in range(MID):
@@ -161,14 +160,14 @@
 
 def add_sides(n_ax, ca, cz, block_in, ax1, ax2, az1, az2, block, sides, strips):
     planes = ca + 2 * REACH
-    size = REACH * cz
+    size = MID * cz
     for f in range(5):
         lo, hi = ax_sides(n_ax, ax1, ax2, slice(f * size, (f + 1) * size))
         sides[f, 0:size, :] = lo
         sides[f, size : 2 * size, :] = hi
     for f in range(5):
-        for k in range(REACH):
-            spread_rows(planes, cz, f, k, sides.at[f], k * cz, block)
+        for k in range(MID):
+            spread_rows(planes, cz, f, REACH - MID + k, sides.at[f], k * cz, block)
             spread_rows(planes, cz, f, REACH + ca + k, sides.at[f], size + k * cz, block)
     up = first_is_up("az")
     a, b = az1[...].astype(F32), az2[...].astype(F32)
@@ -181,8 +180,9 @@
                 block[pl.ds(at, ca, stride=ROWS), :] = strips[side, pl.ds((f * REACH + d) * ca, ca), :]
 
 
-def add_corners(count, ca, cz, block_in, corner1, corner2, *rest):
-    edges, block, outs, corners = rest[:count], rest[count], rest[count + 1 : -1], rest[-1]
+def add_corners(count, ca, cz, block_in, home, corner1, corner2, *rest):
+    edges, block, outs, corners = rest[:count], rest[count], rest[count + 1 : -3], rest[-1]
+    far1, far2 = rest[-3:-1]
     cr = corner1.shape[1]
     planes = ca + 2 * REACH
     up = first_is_up("az")
@@ -198,6 +198,16 @@
                 block[pl.ds(at + (REACH - MID) * ROWS, MID, stride=ROWS), :] = got
                 got = corners[side, pl.ds(start + MID, MID), :]
                 block[pl.ds(at + (REACH + ca) * ROWS, MID, stride=ROWS), :] = got
+
+    up = first_is_up("ax")
+    size = (REACH - MID) * cz
+    for f in range(5):
+        at = f * ca * cz
+        low = home[at + MID * cz : at + REACH * cz, :]
+        high = home[at + (ca - REACH) * cz : at + (ca - MID) * cz, :]
+        rows = slice(f * size, (f + 1) * size)
+        far1[rows, :] = jnp.where(up, high, low).astype(BF16)
+        far2[rows, :] = jnp.where(up, low, high).astype(BF16)
 
     tiles = cr // SLOT
     step = tiles * 8
@@ -310,9 +320,10 @@
 
 
 def stages(n_ax, n_rad, ca, cz, slots, block, banded, cells_far, *refs):
-    sides, refs = refs[: len(refs) - 12], refs[len(refs) - 12 :]
+    sides, refs = refs[: len(refs) - 14], refs[len(refs) - 14 :]
+    sides, (far1, far2) = sides[:-2], sides[-2:]
     sides, places = sides[: len(sides) // 2], sides[len(sides) // 2 :]
-    q_out, u2_out, u0_out, ghost, first, second, fax, part, value, picked, cells, cells_sem = refs
+    q_out, u2_out, u0_out, ghost, first, second, fax, part, value, picked, cells, cells_sem, outer, layers = refs
     fetch = pltpu.make_async_copy(cells_far, cells, cells_sem)
     fetch.start()
     cr = block.shape[-1]
@@ -349,6 +360,9 @@
         for f in range(5):
             x = block[f, j]
             u.append(jnp.concatenate([x, ghost[f, j - (REACH - MID)]], axis=0) if both else x)
+        return conserved(u)
+
+    def conserved(u):
         rho, vel, pres = u[0], u[1:4], u[4]
         mom = [rho * x for x in vel]
         energy = pres * (1.0 / GAMMA_M) + 0.5 * (mom[0] * vel[0] + mom[1] * vel[1] + mom[2] * vel[2])
@@ -357,8 +371,12 @@
     def note(s, j, u):
         value[s, j] = (u[2] - P_REF + u[0][0])[0:ROWS]
 
-    for j in (low - 6, low - 5, high + 4, high + 5):
-        ax_only(start_state(j, False)[1], fax, j)
+    layers[0], layers[1] = ax_sides(n_ax, far1, far2, slice(0, far1.shape[0]))
+    for f in range(5):
+        for k in range(4):
+            spread_rows(4, cz, f, k, layers.at[k // 2], (f * 2 + k % 2) * cz, outer)
+    for k, j in enumerate((low - 6, low - 5, high + 4, high + 5)):
+        ax_only(conserved([outer[(f * 4 + k) * ROWS : (f * 4 + k + 1) * ROWS, :] for f in range(5)])[1], fax, j)
 
     step = (ca + 2 * MID) // STEPS
 
@@ -543,7 +561,7 @@
     part = functools.partial
     given = (density.reshape(ca * cz, cr), velocity.reshape(3 * ca * cz, cr), pressure.reshape(ca * cz, cr))
 
-    edge = struct((5 * REACH * cz, cr), BF16)
+    edge = struct((5 * MID * cz, cr), BF16)
     strip = struct((5 * REACH * ca, cr), BF16)
     home, ax1, ax2, az1, az2 = call(
         part(load_and_pack, ca, cz),
@@ -574,19 +592,20 @@
         part(add_sides, n_ax, ca, cz),
         grid,
         [VMEM] * 5,
-        [pltpu.VMEM((5, 2 * REACH * cz, cr), F32), pltpu.VMEM((2,) + strip.shape, F32)],
+        [pltpu.VMEM((5, 2 * MID * cz, cr), F32), pltpu.VMEM((2,) + strip.shape, F32)],
         mib=8,
         alias={0: 0},
         cost=pl.CostEstimate(flops=100_000_000, bytes_accessed=4_000_000, transcendentals=0),
     )(block, ax1, ax2, az1, az2)
+    far_edge = struct((5 * (REACH - MID) * cz, cr), BF16)
     got = call(
         part(add_corners, len(ends), ca, cz),
-        (grid,) + tuple(side for _ in ends),
-        [VMEM] * (3 + len(ends)),
+        (grid,) + tuple(side for _ in ends) + (far_edge,) * 2,
+        [VMEM] * (4 + len(ends)),
         [pltpu.VMEM((2,) + corner.shape, F32)],
         mib=8,
         alias={0: 0},
-    )(block, corner1, corner2, *edges)
+    )(block, home, corner1, corner2, *edges)
     block = got[0].reshape(5, planes, ROWS, cr)
     if n_rad == 2:
         sides = (lax.ppermute(got[1], "rad", [(0, 1), (1, 0)]),)
@@ -594,17 +613,20 @@
         up = [(i, i + 1) for i in range(n_rad - 1)]
         sides = (lax.ppermute(got[1], "rad", [(j, i) for i, j in up]), lax.ppermute(got[2], "rad", up))
 
+    far1, far2 = swap(got[-2], got[-1], ("y", "core"), False)
+
     grid = (5, planes, TALL, cr)
     q, u2, u0 = call(
         part(stages, n_ax, n_rad, ca, cz, slots),
         (struct((ndev, 1, 128)), struct((5, ca + 4, TALL, cr)), struct((5, ca, ROWS, cr))),
-        [VMEM, VMEM, HBM] + [VMEM] * (2 * len(sides)),
+        [VMEM, VMEM, HBM] + [VMEM] * (2 * len(sides) + 2),
         [pltpu.VMEM((5, ca + 2 * MID, 8, cr), F32)]
         + [pltpu.VMEM(grid, F32) for _ in range(4)]
         + [pltpu.VMEM((3, planes, ROWS, cr), F32), pltpu.VMEM((128, cr), F32)]
-        + [pltpu.SMEM((slots,), jnp.int32), pltpu.SemaphoreType.DMA],
+        + [pltpu.SMEM((slots,), jnp.int32), pltpu.SemaphoreType.DMA]
+        + [pltpu.VMEM((5 * 4 * ROWS, cr), F32), pltpu.VMEM((2,) + far_edge.shape, F32)],
         mib=28,
-    )(block, banded, far(panel_cell), *sides, *places)
+    )(block, banded, far(panel_cell), *sides, *places, far1, far2)
 
     rows = lax.all_to_all(q, ("y", "core", "az", "rad"), 0, 0, tiled=True).reshape(ndev, 128)
 

time: 38.1 us -> 39.6 us (1.039)
  starting transfers between devices: 17.1 us -> 20.8 us
  waiting for transfers between devices: 11.1 us -> 8.88 us
    ppermute x6 -> x8, starting transfers between devices: 8.02 us -> 10.8 us  [swap(): return (lax.ppermute(first, axis, one), lax.ppermute(second, axis, two))]
    ppermute x1, waiting for transfers between devices: 2.51 us -> 0.01 us  [local(): sides = (lax.ppermute(got[1], 'rad', [(0, 1), (1, 0)]),)]
    all_to_all x1, starting transfers between devices: 7.55 us -> 8.49 us  [local(): lax.all_to_all(q, ('y', 'core', 'az', 'rad'), 0, 0, tiled=True)]
    ppermute x6 -> x8, waiting for transfers between devices: 3.06 us -> 3.32 us  [swap(): return (lax.ppermute(first, axis, one), lax.ppermute(second, axis, two))]
  transfers between devices with their start and end apart: 8 -> 10, of which waited for: 4 -> 4; matrix products, arithmetic and copies ran while one was open for 0% -> 0% of each run, Pallas kernels for 6% -> 6%
where the time goes in v15:
time: 39.6 us; the launch traced here: 39.4 us
  starting transfers between devices  20.8 us (53%)
  Pallas kernels  8.93 us (23%)
  waiting for transfers between devices  8.88 us (22%)
  between operations  0.73 us (2%)
    ppermute x8, starting transfers between devices, swap(): return (lax.ppermute(first, axis, one), lax.ppermute(second, axis, two))  10.8 us
    all_to_all x1, starting transfers between devices, local(): lax.all_to_all(q, ('y', 'core', 'az', 'rad'), 0, 0, tiled=True)  8.49 us
    all_to_all x1, waiting for transfers between devices, local(): lax.all_to_all(q, ('y', 'core', 'az', 'rad'), 0, 0, tiled=True)  5.56 us
    pallas_call x1, Pallas kernels, local(): call(part(stages, n_ax, n_rad, ca, cz, slots), (struct((ndev, 1, 128)), s...  3.87 us
    ppermute x8, waiting for transfers between devices, swap(): return (lax.ppermute(first, axis, one), lax.ppermute(second, axis, two))  3.32 us
    ppermute x1, starting transfers between devices, local(): sides = (lax.ppermute(got[1], 'rad', [(0, 1), (1, 0)]),)  1.56 us
    pallas_call x1, Pallas kernels, local(): call(part(last_stage, ca, cz), struct((5, ca, cz, cr)), [VMEM] * 3, [pltp...  1.48 us
    pallas_call x1, Pallas kernels, local(): call(part(signals, slots), struct((obs_weight.shape[0], NB)), [VMEM] * 3,...  1.18 us
  transfers between devices with their start and end apart: 10, of which 4 were waited for; matrix products, arithmetic and copies ran while one was open for 0% of the time, Pallas kernels for 6%

profile of v15, /device:TPU:0, one launch (start us, length us, event | category | flops | bytes accessed | tf_op | source)
XLA Modules:
  0.0 39.4 jit_solution(11648584920771882372)
XLA Ops:
  0.6 1.1 %shard_map.77 = (f32[640,128]{1,0:T(8,128)S(1)}, bf16[320,128]{1,0:T(8,128)(2,1)S(1)}, bf16[320,128]{1,0:T(8,128)(2,1)S(1)}, bf16[240,128]{1,0:T(8,128)(2,1)S(1)}, bf16[240,128]{1,0:T(8,128)(2,1)S(1)}) custom-call(f32[128,128]{1,0:T(8,128)} %bitcast.8, f32[384,128]{1,0:T(8,128)} %bitcast.7, f32[128,128]{1,0:T(8,128)} %bitcast.9), custom_call_target="tpu_custom_call" | custom-call | tf_op jit(solution)/shard_map/pallas_call | solution.py:566
  1.7 0.5 %collective-permute-start = (bf16[320,128]{1,0:T(8,128)(2,1)S(1)}, bf16[320,128]{1,0:T(8,128)(2,1)S(1)}, u32[]{:S(2)}, u32[]{:S(2)}) collective-permute-start(bf16[320,128]{1,0:T(8,128)(2,1)S(1)} %get-tuple-element.22), channel_id=1, source_target_pairs={{0,8},{8,0},{16,24},{24,16},{1,9},{9,1},{17,25},{25,17},{2,10},{10... | collective-permute-start | bytes 245768 | tf_op jit(solution)/shard_map/ppermute | solution.py:552
  2.2 0.7 %collective-permute-start.1 = (bf16[320,128]{1,0:T(8,128)(2,1)S(1)}, bf16[320,128]{1,0:T(8,128)(2,1)S(1)}, u32[]{:S(2)}, u32[]{:S(2)}) collective-permute-start(bf16[320,128]{1,0:T(8,128)(2,1)S(1)} %get-tuple-element.23), channel_id=1, source_target_pairs={{0,0},{8,16},{16,8},{24,24},{1,1},{9,17},{17,9},{25,25},{2,2},{10,... | collective-permute-start | bytes 245768 | tf_op jit(solution)/shard_map/ppermute | solution.py:552
  2.9 4.7 %collective-permute-start.2 = (bf16[240,128]{1,0:T(8,128)(2,1)S(1)}, bf16[240,128]{1,0:T(8,128)(2,1)S(1)}, u32[]{:S(2)}, u32[]{:S(2)}) collective-permute-start(bf16[240,128]{1,0:T(8,128)(2,1)S(1)} %get-tuple-element.24), channel_id=1, source_target_pairs={{0,6},{2,4},{4,2},{6,0},{1,7},{3,5},{5,3},{7,1},{8,14},{10,12},{12... | collective-permute-start | bytes 184328 | tf_op jit(solution)/shard_map/ppermute | solution.py:552
  7.6 0.0 collective-permute-start.3
  7.6 0.0 collective-permute-done.ax1.got1
  7.6 0.0 collective-permute-done.1.ax2.got2
  7.6 0.1 shard_map.80
  7.7 1.0 %collective-permute-start.4 = (bf16[160,128]{1,0:T(8,128)(2,1)S(1)}, bf16[160,128]{1,0:T(8,128)(2,1)S(1)}, u32[]{:S(2)}, u32[]{:S(2)}) collective-permute-start(bf16[160,128]{1,0:T(8,128)(2,1)S(1)} %get-tuple-element.26), channel_id=1, source_target_pairs={{0,6},{2,4},{4,2},{6,0},{1,7},{3,5},{5,3},{7,1},{8,14},{10,12},{12... | collective-permute-start | bytes 122888 | tf_op jit(solution)/shard_map/ppermute | solution.py:552
  8.7 1.2 %collective-permute-start.5 = (bf16[160,128]{1,0:T(8,128)(2,1)S(1)}, bf16[160,128]{1,0:T(8,128)(2,1)S(1)}, u32[]{:S(2)}, u32[]{:S(2)}) collective-permute-start(bf16[160,128]{1,0:T(8,128)(2,1)S(1)} %get-tuple-element.27), channel_id=1, source_target_pairs={{0,2},{2,0},{4,6},{6,4},{1,3},{3,1},{5,7},{7,5},{8,10},{10,8},{12,... | collective-permute-start | bytes 122888 | tf_op jit(solution)/shard_map/ppermute | solution.py:552
  9.9 0.5 %shard_map.78 = (f32[3200,128]{1,0:T(8,128)S(1)}, bf16[256,256]{1,0:T(8,128)(2,1)S(1)}, bf16[2048,128]{1,0:T(8,128)(2,1)S(1)}, bf16[128,512]{1,0:T(8,128)(2,1)S(1)}) custom-call(f32[640,128]{1,0:T(8,128)S(1)} %get-tuple-element.20.home), custom_call_target="tpu_custom_call" | custom-call | tf_op jit(solution)/shard_map/pallas_call | solution.py:578
  10.4 0.0 collective-permute-done.2.az1
  10.4 2.1 %collective-permute-done.3.az2 = bf16[240,128]{1,0:T(8,128)(2,1)S(1)} collective-permute-done((bf16[240,128]{1,0:T(8,128)(2,1)S(1)}, bf16[240,128]{1,0:T(8,128)(2,1)S(1)}, u32[]{:S(2)}, u32[]{:S(2)}) %collective-permute-start.3) | collective-permute-done | bytes 61472 | tf_op jit(solution)/shard_map/ppermute | solution.py:552
  12.5 0.2 shard_map.79.block_in
  12.7 1.0 %collective-permute-done.4.corner1 = bf16[160,128]{1,0:T(8,128)(2,1)S(1)} collective-permute-done((bf16[160,128]{1,0:T(8,128)(2,1)S(1)}, bf16[160,128]{1,0:T(8,128)(2,1)S(1)}, u32[]{:S(2)}, u32[]{:S(2)}) %collective-permute-start.4) | collective-permute-done | bytes 40992 | tf_op jit(solution)/shard_map/ppermute | solution.py:552
  13.7 0.0 collective-permute-done.5.corner2
  13.7 0.5 %shard_map.81 = (f32[3200,128]{1,0:T(8,128)S(1)}, bf16[160,128]{1,0:T(8,128)(2,1)S(1)}, bf16[160,128]{1,0:T(8,128)(2,1)S(1)}, bf16[160,128]{1,0:T(8,128)(2,1)S(1)}) custom-call(f32[3200,128]{1,0:T(8,128)S(1)} %shard_map.79.block_in, f32[640,128]{1,0:T(8,128)S(1)} %get-tuple-element.20.home, ...), custom_call_target="tpu_custom_call", output_to_operand_aliasing={{0}: (0, {})} | custom-call | tf_op jit(solution)/shard_map/pallas_call | solution.py:601
  14.2 1.6 %collective-permute-start.6 = (bf16[160,128]{1,0:T(8,128)(2,1)S(1)}, bf16[160,128]{1,0:T(8,128)(2,1)S(1)}, u32[]{:S(2)}, u32[]{:S(2)}) collective-permute-start(bf16[160,128]{1,0:T(8,128)(2,1)S(1)} %get-tuple-element.31), channel_id=1, source_target_pairs={{0,1},{1,0},{2,3},{3,2},{4,5},{5,4},{6,7},{7,6},{8,9},{9,8},{10,11... | collective-permute-start | bytes 122888 | tf_op jit(solution)/shard_map/ppermute | solution.py:611
  15.8 2.1 %collective-permute-start.7 = (bf16[160,128]{1,0:T(8,128)(2,1)S(1)}, bf16[160,128]{1,0:T(8,128)(2,1)S(1)}, u32[]{:S(2)}, u32[]{:S(2)}) collective-permute-start(bf16[160,128]{1,0:T(8,128)(2,1)S(1)} %get-tuple-element.33), channel_id=1, source_target_pairs={{0,8},{8,0},{16,24},{24,16},{1,9},{9,1},{17,25},{25,17},{2,10},{10... | collective-permute-start | bytes 122888 | tf_op jit(solution)/shard_map/ppermute | solution.py:552
  17.9 0.7 %collective-permute-start.8 = (bf16[160,128]{1,0:T(8,128)(2,1)S(1)}, bf16[160,128]{1,0:T(8,128)(2,1)S(1)}, u32[]{:S(2)}, u32[]{:S(2)}) collective-permute-start(bf16[160,128]{1,0:T(8,128)(2,1)S(1)} %get-tuple-element.34), channel_id=1, source_target_pairs={{0,0},{8,16},{16,8},{24,24},{1,1},{9,17},{17,9},{25,25},{2,2},{10,... | collective-permute-start | bytes 122888 | tf_op jit(solution)/shard_map/ppermute | solution.py:552
  18.6 0.0 collective-permute-done.6.refs_0_
  18.6 0.2 collective-permute-done.7.refs_2_
  18.8 0.0 collective-permute-done.8.refs_3_
  18.8 3.9 %shard_map.82 = (f32[32,1,128]{2,1,0:T(1,128)}, f32[5,12,40,128]{3,2,1,0:T(8,128)S(1)}, f32[5,8,32,128]{3,2,1,0:T(8,128)S(1)}) custom-call(f32[5,20,32,128]{3,2,1,0:T(8,128)S(1)} %bitcast.5, bf16[256,256]{1,0:T(8,128)(2,1)S(1)} %get-tuple-element.30.banded, s32[32]{0:T(128)} %cells_far.1, bf16[160,128]{1,0:T(8,128)(2,1)S(1)} %collective-permute-done.6.refs_0_, ...), custom_call_target="tpu_custom_call" | custom-call | tf_op jit(solution)/shard_map/pallas_call | solution.py:619
  22.6 0.0 copy-start
  22.7 0.0 copy-start.1
  22.7 8.5 %all-to-all-start = ((f32[32,1,128]{2,1,0:T(1,128)}), f32[32,1,128]{2,1,0:T(1,128)S(1)}, u32[]{:S(2)}, u32[]{:S(2)}) async-start(f32[32,1,128]{2,1,0:T(1,128)} %get-tuple-element.37), calls=%async_computation | async-start | bytes 32768 | tf_op jit(solution)/shard_map/all_to_all | solution.py:631
  31.2 1.5 %shard_map.83 = f32[5,8,16,128]{3,2,1,0:T(8,128)} custom-call(f32[5,12,40,128]{3,2,1,0:T(8,128)S(1)} %get-tuple-element.35.u2, f32[5,8,32,128]{3,2,1,0:T(8,128)S(1)} %get-tuple-element.36.u0, bf16[256,256]{1,0:T(8,128)(2,1)S(1)} %get-tuple-element.30.banded), custom_call_target="tpu_custom_call" | custom-call | flops 400000000 | bytes 8000000 | tf_op jit(solution)/shard_map/pallas_call | solution.py:634
  32.7 5.6 %all-to-all-done = f32[32,1,128]{2,1,0:T(1,128)S(1)} async-done(((f32[32,1,128]{2,1,0:T(1,128)}), f32[32,1,128]{2,1,0:T(1,128)S(1)}, u32[]{:S(2)}, u32[]{:S(2)}) %all-to-all-start) | async-done | bytes 16416 | tf_op jit(solution)/shard_map/all_to_all | solution.py:631
  38.2 0.0 copy-done
  38.2 0.0 copy-done.1
  38.2 1.2 %shard_map.84 = f32[256,128]{1,0:T(8,128)} custom-call(f32[32,128]{1,0:T(8,128)S(1)} %bitcast.6, s32[1,32]{1,0:T(1,128)S(1)} %copy-done.1, bf16[256,1024]{1,0:T(8,128)(2,1)S(1)} %copy-done), custom_call_target="tpu_custom_call" | custom-call | tf_op jit(solution)/shard_map/pallas_call | solution.py:642
Async XLA Ops:
  1.7 5.9 %collective-permute-start = (bf16[320,128]{1,0:T(8,128)(2,1)S(1)}, bf16[320,128]{1,0:T(8,128)(2,1)S(1)}, u32[]{:S(2)}, u32[]{:S(2)}) collective-permute-start(bf16[320,128]{1,0:T(8,128)(2,1)S(1)} %get-tuple-element.22), channel_id=1, source_target_pairs={{0,8},{8,0},{16,24},{24,16},{1,9},{9,1},{17,25},{25,17},{2,10},{10... | collective-permute-start | bytes 245768 | tf_op jit(solution)/shard_map/ppermute | solution.py:552
  2.2 5.4 %collective-permute-start.1 = (bf16[320,128]{1,0:T(8,128)(2,1)S(1)}, bf16[320,128]{1,0:T(8,128)(2,1)S(1)}, u32[]{:S(2)}, u32[]{:S(2)}) collective-permute-start(bf16[320,128]{1,0:T(8,128)(2,1)S(1)} %get-tuple-element.23), channel_id=1, source_target_pairs={{0,0},{8,16},{16,8},{24,24},{1,1},{9,17},{17,9},{25,25},{2,2},{10,... | collective-permute-start | bytes 245768 | tf_op jit(solution)/shard_map/ppermute | solution.py:552
  2.9 7.5 %collective-permute-start.2 = (bf16[240,128]{1,0:T(8,128)(2,1)S(1)}, bf16[240,128]{1,0:T(8,128)(2,1)S(1)}, u32[]{:S(2)}, u32[]{:S(2)}) collective-permute-start(bf16[240,128]{1,0:T(8,128)(2,1)S(1)} %get-tuple-element.24), channel_id=1, source_target_pairs={{0,6},{2,4},{4,2},{6,0},{1,7},{3,5},{5,3},{7,1},{8,14},{10,12},{12... | collective-permute-start | bytes 184328 | tf_op jit(solution)/shard_map/ppermute | solution.py:552
  7.6 4.9 %collective-permute-start.3 = (bf16[240,128]{1,0:T(8,128)(2,1)S(1)}, bf16[240,128]{1,0:T(8,128)(2,1)S(1)}, u32[]{:S(2)}, u32[]{:S(2)}) collective-permute-start(bf16[240,128]{1,0:T(8,128)(2,1)S(1)} %get-tuple-element.25), channel_id=1, source_target_pairs={{0,2},{2,0},{4,6},{6,4},{1,3},{3,1},{5,7},{7,5},{8,10},{10,8},{12,... | collective-permute-start | bytes 184328 | tf_op jit(solution)/shard_map/ppermute | solution.py:552
  7.7 6.0 %collective-permute-start.4 = (bf16[160,128]{1,0:T(8,128)(2,1)S(1)}, bf16[160,128]{1,0:T(8,128)(2,1)S(1)}, u32[]{:S(2)}, u32[]{:S(2)}) collective-permute-start(bf16[160,128]{1,0:T(8,128)(2,1)S(1)} %get-tuple-element.26), channel_id=1, source_target_pairs={{0,6},{2,4},{4,2},{6,0},{1,7},{3,5},{5,3},{7,1},{8,14},{10,12},{12... | collective-permute-start | bytes 122888 | tf_op jit(solution)/shard_map/ppermute | solution.py:552
  8.7 5.1 %collective-permute-start.5 = (bf16[160,128]{1,0:T(8,128)(2,1)S(1)}, bf16[160,128]{1,0:T(8,128)(2,1)S(1)}, u32[]{:S(2)}, u32[]{:S(2)}) collective-permute-start(bf16[160,128]{1,0:T(8,128)(2,1)S(1)} %get-tuple-element.27), channel_id=1, source_target_pairs={{0,2},{2,0},{4,6},{6,4},{1,3},{3,1},{5,7},{7,5},{8,10},{10,8},{12,... | collective-permute-start | bytes 122888 | tf_op jit(solution)/shard_map/ppermute | solution.py:552
  14.2 4.3 %collective-permute-start.6 = (bf16[160,128]{1,0:T(8,128)(2,1)S(1)}, bf16[160,128]{1,0:T(8,128)(2,1)S(1)}, u32[]{:S(2)}, u32[]{:S(2)}) collective-permute-start(bf16[160,128]{1,0:T(8,128)(2,1)S(1)} %get-tuple-element.31), channel_id=1, source_target_pairs={{0,1},{1,0},{2,3},{3,2},{4,5},{5,4},{6,7},{7,6},{8,9},{9,8},{10,11... | collective-permute-start | bytes 122888 | tf_op jit(solution)/shard_map/ppermute | solution.py:611
  15.8 3.0 %collective-permute-start.7 = (bf16[160,128]{1,0:T(8,128)(2,1)S(1)}, bf16[160,128]{1,0:T(8,128)(2,1)S(1)}, u32[]{:S(2)}, u32[]{:S(2)}) collective-permute-start(bf16[160,128]{1,0:T(8,128)(2,1)S(1)} %get-tuple-element.33), channel_id=1, source_target_pairs={{0,8},{8,0},{16,24},{24,16},{1,9},{9,1},{17,25},{25,17},{2,10},{10... | collective-permute-start | bytes 122888 | tf_op jit(solution)/shard_map/ppermute | solution.py:552
  17.9 0.9 %collective-permute-start.8 = (bf16[160,128]{1,0:T(8,128)(2,1)S(1)}, bf16[160,128]{1,0:T(8,128)(2,1)S(1)}, u32[]{:S(2)}, u32[]{:S(2)}) collective-permute-start(bf16[160,128]{1,0:T(8,128)(2,1)S(1)} %get-tuple-element.34), channel_id=1, source_target_pairs={{0,0},{8,16},{16,8},{24,24},{1,1},{9,17},{17,9},{25,25},{2,2},{10,... | collective-permute-start | bytes 122888 | tf_op jit(solution)/shard_map/ppermute | solution.py:552
  22.6 15.6 %copy-start = (bf16[256,1024]{1,0:T(8,128)(2,1)S(1)}, bf16[256,1024]{1,0:T(8,128)(2,1)}, u32[]{:S(2)}) copy-start(bf16[256,1024]{1,0:T(8,128)(2,1)} %weight.1) | copy-start | bytes 1572868
  22.7 15.6 %copy-start.1 = (s32[1,32]{1,0:T(1,128)S(1)}, s32[1,32]{1,0:T(1,128)}, u32[]{:S(2)}) copy-start(s32[1,32]{1,0:T(1,128)} %offsets.1) | copy-start | bytes 388
  22.7 15.5 %all-to-all-start = ((f32[32,1,128]{2,1,0:T(1,128)}), f32[32,1,128]{2,1,0:T(1,128)S(1)}, u32[]{:S(2)}, u32[]{:S(2)}) async-start(f32[32,1,128]{2,1,0:T(1,128)} %get-tuple-element.37), calls=%async_computation | async-start | bytes 32768 | tf_op jit(solution)/shard_map/all_to_all | solution.py:631

commit v16 on v14

--- a/solution.py
+++ b/solution.py
@@ -62,7 +62,7 @@
     return lax.axis_index("az") % 2 == 1
 
 
-def load_and_pack(ca, cz, den, vel, pre, home, ax1, ax2, az1, az2, sems):
+def load_and_pack(ca, cz, den, vel, pre, home, ax1, ax2, sems):
     size = ca * cz
     copies = [
         pltpu.make_async_copy(den, home.at[pl.ds(0, size)], sems.at[0]),
@@ -82,6 +82,10 @@
         rows = slice(f * edge, (f + 1) * edge)
         ax1[rows, :] = jnp.where(up, high, low).astype(BF16)
         ax2[rows, :] = jnp.where(up, low, high).astype(BF16)
+
+
+def pack_az(ca, cz, home, az1, az2):
+    size = ca * cz
     up = first_is_up("az")
     low, high = [], []
     for f in range(5):
@@ -378,7 +382,7 @@
         a = max(low - j, j - (high - 1), 0)
         a = (a + 1) // 2
         lim = 2 - stage
-        base = jnp.where(f == 0, 1.0, 0.0)
+        base = 1.0 if f == 0 else 0.0
         size = ROWS if a == lim else TALL
         new = change(fa, part, f, j, size)
         u0 = first[f, j, 0:size]
@@ -397,8 +401,7 @@
             ok = ok & jnp.logical_not(beyond)
         return home, jnp.where(ok, new[ROWS:], base)
 
-    @pl.loop(0, 5)
-    def _(f):
+    for f in range(5):
         fa = window(fax, f)
         for j in range(low - 4, high + 4):
             home, side = update(f, j, fa, 0)
@@ -421,8 +424,7 @@
             us.append(u)
         both_sides(us, js, fax, part, banded)
 
-    @pl.loop(0, 5)
-    def _(f):
+    for f in range(5):
         fa = window(fax, f)
         for j in range(low - 2, high + 2):
             home, side = update(f, j, fa, 1)
@@ -545,12 +547,13 @@
 
     edge = struct((5 * REACH * cz, cr), BF16)
     strip = struct((5 * REACH * ca, cr), BF16)
-    home, ax1, ax2, az1, az2 = call(
+    home, ax1, ax2 = call(
         part(load_and_pack, ca, cz),
-        (struct((5 * ca * cz, cr)), edge, edge, strip, strip),
+        (struct((5 * ca * cz, cr)), edge, edge),
         [HBM] * 3,
         [pltpu.SemaphoreType.DMA((3,))],
     )(*[far(x) for x in given])
+    az1, az2 = call(part(pack_az, ca, cz), (strip, strip), [VMEM])(home)
     ax1, ax2 = swap(ax1, ax2, ("y", "core"), False)
     az1, az2 = swap(az1, az2, "az", True)
     grid = struct((5 * planes * ROWS, cr))

time: 38.1 us -> 37.8 us (level)
    pallas_call x1 -> x2, Pallas kernels: 1.09 us -> 1.1 us  [the longest x1 1.03 us: local(): call(part(load_and_pack, ca, cz), (struct((5 * ca * cz, cr)), edge, edge)...]
  transfers between devices with their start and end apart: 8 -> 8, of which waited for: 4 -> 4; matrix products, arithmetic and copies ran while one was open for 0% -> 0% of each run, Pallas kernels for 6% -> 7%
where the time goes in v16:
time: 37.8 us; the launch traced here: 37.6 us
  starting transfers between devices  17 us (45%)
  waiting for transfers between devices  11.1 us (29%)
  Pallas kernels  8.74 us (23%)
  between operations  0.72 us (2%)
    ppermute x6, starting transfers between devices, swap(): return (lax.ppermute(first, axis, one), lax.ppermute(second, axis, two))  8.02 us
    all_to_all x1, starting transfers between devices, local(): lax.all_to_all(q, ('y', 'core', 'az', 'rad'), 0, 0, tiled=True)  7.46 us
    all_to_all x1, waiting for transfers between devices, local(): lax.all_to_all(q, ('y', 'core', 'az', 'rad'), 0, 0, tiled=True)  5.56 us
    pallas_call x1, Pallas kernels, local(): call(part(stages, n_ax, n_rad, ca, cz, slots), (struct((ndev, 1, 128)), s...  3.62 us
    ppermute x6, waiting for transfers between devices, swap(): return (lax.ppermute(first, axis, one), lax.ppermute(second, axis, two))  3.06 us
    ppermute x1, waiting for transfers between devices, local(): sides = (lax.ppermute(got[1], 'rad', [(0, 1), (1, 0)]),)  2.51 us
    ppermute x1, starting transfers between devices, local(): sides = (lax.ppermute(got[1], 'rad', [(0, 1), (1, 0)]),)  1.55 us
    pallas_call x1, Pallas kernels, local(): call(part(last_stage, ca, cz), struct((5, ca, cz, cr)), [VMEM] * 3, [pltp...  1.48 us
  transfers between devices with their start and end apart: 8, of which 4 were waited for; matrix products, arithmetic and copies ran while one was open for 0% of the time, Pallas kernels for 7%

profile of v16, /device:TPU:0, one launch (start us, length us, event | category | flops | bytes accessed | tf_op | source)
XLA Modules:
  0.0 37.6 jit_solution(7204312573211399298)
XLA Ops:
  0.6 1.0 %shard_map.77 = (f32[640,128]{1,0:T(8,128)S(1)}, bf16[480,128]{1,0:T(8,128)(2,1)S(1)}, bf16[480,128]{1,0:T(8,128)(2,1)S(1)}) custom-call(f32[128,128]{1,0:T(8,128)} %bitcast.8, f32[384,128]{1,0:T(8,128)} %bitcast.7, f32[128,128]{1,0:T(8,128)} %bitcast.9), custom_call_target="tpu_custom_call" | custom-call | tf_op jit(solution)/shard_map/pallas_call | solution.py:550
  1.7 0.5 %collective-permute-start = (bf16[480,128]{1,0:T(8,128)(2,1)S(1)}, bf16[480,128]{1,0:T(8,128)(2,1)S(1)}, u32[]{:S(2)}, u32[]{:S(2)}) collective-permute-start(bf16[480,128]{1,0:T(8,128)(2,1)S(1)} %get-tuple-element.20), channel_id=1, source_target_pairs={{0,8},{8,0},{16,24},{24,16},{1,9},{9,1},{17,25},{25,17},{2,10},{10... | collective-permute-start | bytes 368648 | tf_op jit(solution)/shard_map/ppermute | solution.py:536
  2.2 0.7 %collective-permute-start.1 = (bf16[480,128]{1,0:T(8,128)(2,1)S(1)}, bf16[480,128]{1,0:T(8,128)(2,1)S(1)}, u32[]{:S(2)}, u32[]{:S(2)}) collective-permute-start(bf16[480,128]{1,0:T(8,128)(2,1)S(1)} %get-tuple-element.21), channel_id=1, source_target_pairs={{0,0},{8,16},{16,8},{24,24},{1,1},{9,17},{17,9},{25,25},{2,2},{10,... | collective-permute-start | bytes 368648 | tf_op jit(solution)/shard_map/ppermute | solution.py:536
  2.8 0.1 shard_map.79
  2.9 4.7 %collective-permute-start.2 = (bf16[240,128]{1,0:T(8,128)(2,1)S(1)}, bf16[240,128]{1,0:T(8,128)(2,1)S(1)}, u32[]{:S(2)}, u32[]{:S(2)}) collective-permute-start(bf16[240,128]{1,0:T(8,128)(2,1)S(1)} %get-tuple-element.22), channel_id=1, source_target_pairs={{0,6},{2,4},{4,2},{6,0},{1,7},{3,5},{5,3},{7,1},{8,14},{10,12},{12... | collective-permute-start | bytes 184328 | tf_op jit(solution)/shard_map/ppermute | solution.py:536
  7.6 0.0 collective-permute-start.3
  7.6 0.0 collective-permute-done.ax1.got1
  7.6 0.0 collective-permute-done.1.ax2.got2
  7.6 0.1 shard_map.81
  7.7 1.0 %collective-permute-start.4 = (bf16[160,128]{1,0:T(8,128)(2,1)S(1)}, bf16[160,128]{1,0:T(8,128)(2,1)S(1)}, u32[]{:S(2)}, u32[]{:S(2)}) collective-permute-start(bf16[160,128]{1,0:T(8,128)(2,1)S(1)} %get-tuple-element.24), channel_id=1, source_target_pairs={{0,6},{2,4},{4,2},{6,0},{1,7},{3,5},{5,3},{7,1},{8,14},{10,12},{12... | collective-permute-start | bytes 122888 | tf_op jit(solution)/shard_map/ppermute | solution.py:536
  8.7 1.2 %collective-permute-start.5 = (bf16[160,128]{1,0:T(8,128)(2,1)S(1)}, bf16[160,128]{1,0:T(8,128)(2,1)S(1)}, u32[]{:S(2)}, u32[]{:S(2)}) collective-permute-start(bf16[160,128]{1,0:T(8,128)(2,1)S(1)} %get-tuple-element.25), channel_id=1, source_target_pairs={{0,2},{2,0},{4,6},{6,4},{1,3},{3,1},{5,7},{7,5},{8,10},{10,8},{12,... | collective-permute-start | bytes 122888 | tf_op jit(solution)/shard_map/ppermute | solution.py:536
  9.9 0.5 %shard_map.78 = (f32[3200,128]{1,0:T(8,128)S(1)}, bf16[256,256]{1,0:T(8,128)(2,1)S(1)}, bf16[2048,128]{1,0:T(8,128)(2,1)S(1)}, bf16[128,512]{1,0:T(8,128)(2,1)S(1)}) custom-call(f32[640,128]{1,0:T(8,128)S(1)} %get-tuple-element.18.home), custom_call_target="tpu_custom_call" | custom-call | tf_op jit(solution)/shard_map/pallas_call | solution.py:563
  10.4 0.0 collective-permute-done.2.az1
  10.4 2.1 %collective-permute-done.3.az2 = bf16[240,128]{1,0:T(8,128)(2,1)S(1)} collective-permute-done((bf16[240,128]{1,0:T(8,128)(2,1)S(1)}, bf16[240,128]{1,0:T(8,128)(2,1)S(1)}, u32[]{:S(2)}, u32[]{:S(2)}) %collective-permute-start.3) | collective-permute-done | bytes 61472 | tf_op jit(solution)/shard_map/ppermute | solution.py:536
  12.5 0.3 shard_map.80.block_in
  12.8 1.0 %collective-permute-done.4.corner1 = bf16[160,128]{1,0:T(8,128)(2,1)S(1)} collective-permute-done((bf16[160,128]{1,0:T(8,128)(2,1)S(1)}, bf16[160,128]{1,0:T(8,128)(2,1)S(1)}, u32[]{:S(2)}, u32[]{:S(2)}) %collective-permute-start.4) | collective-permute-done | bytes 40992 | tf_op jit(solution)/shard_map/ppermute | solution.py:536
  13.8 0.0 collective-permute-done.5.corner2
  13.8 0.5 %shard_map.82 = (f32[3200,128]{1,0:T(8,128)S(1)}, bf16[160,128]{1,0:T(8,128)(2,1)S(1)}) custom-call(f32[3200,128]{1,0:T(8,128)S(1)} %shard_map.80.block_in, bf16[160,128]{1,0:T(8,128)(2,1)S(1)} %collective-permute-done.4.corner1, bf16[160,128]{1,0:T(8,128)(2,1)S(1)} %collective-permute-done.5.corner2, ...), custom_call_target="tpu_custom_call", output_to_operand_aliasing={{0}: (0, {})} | custom-call | tf_op jit(solution)/shard_map/pallas_call | solution.py:585
  14.2 1.6 %collective-permute-start.6 = (bf16[160,128]{1,0:T(8,128)(2,1)S(1)}, bf16[160,128]{1,0:T(8,128)(2,1)S(1)}, u32[]{:S(2)}, u32[]{:S(2)}) collective-permute-start(bf16[160,128]{1,0:T(8,128)(2,1)S(1)} %get-tuple-element.29), channel_id=1, source_target_pairs={{0,1},{1,0},{2,3},{3,2},{4,5},{5,4},{6,7},{7,6},{8,9},{9,8},{10,11... | collective-permute-start | bytes 122888 | tf_op jit(solution)/shard_map/ppermute | solution.py:595
  15.8 2.5 %collective-permute-done.6.refs_0_ = bf16[160,128]{1,0:T(8,128)(2,1)S(1)} collective-permute-done((bf16[160,128]{1,0:T(8,128)(2,1)S(1)}, bf16[160,128]{1,0:T(8,128)(2,1)S(1)}, u32[]{:S(2)}, u32[]{:S(2)}) %collective-permute-start.6) | collective-permute-done | bytes 40992 | tf_op jit(solution)/shard_map/ppermute | solution.py:595
  18.3 3.6 %shard_map.83 = (f32[32,1,128]{2,1,0:T(1,128)}, f32[5,12,40,128]{3,2,1,0:T(8,128)S(1)}, f32[5,8,32,128]{3,2,1,0:T(8,128)S(1)}) custom-call(f32[5,20,32,128]{3,2,1,0:T(8,128)S(1)} %bitcast.5, bf16[256,256]{1,0:T(8,128)(2,1)S(1)} %get-tuple-element.28.banded, s32[32]{0:T(128)} %cells_far.1, bf16[160,128]{1,0:T(8,128)(2,1)S(1)} %collective-permute-done.6.refs_0_, ...), custom_call_target="tpu_custom_call" | custom-call | tf_op jit(solution)/shard_map/pallas_call | solution.py:601
  21.9 0.0 copy-start
  21.9 0.0 copy-start.1
  21.9 7.5 %all-to-all-start = ((f32[32,1,128]{2,1,0:T(1,128)}), f32[32,1,128]{2,1,0:T(1,128)S(1)}, u32[]{:S(2)}, u32[]{:S(2)}) async-start(f32[32,1,128]{2,1,0:T(1,128)} %get-tuple-element.33), calls=%async_computation | async-start | bytes 32768 | tf_op jit(solution)/shard_map/all_to_all | solution.py:612
  29.4 1.5 %shard_map.84 = f32[5,8,16,128]{3,2,1,0:T(8,128)} custom-call(f32[5,12,40,128]{3,2,1,0:T(8,128)S(1)} %get-tuple-element.31.u2, f32[5,8,32,128]{3,2,1,0:T(8,128)S(1)} %get-tuple-element.32.u0, bf16[256,256]{1,0:T(8,128)(2,1)S(1)} %get-tuple-element.28.banded), custom_call_target="tpu_custom_call" | custom-call | flops 400000000 | bytes 8000000 | tf_op jit(solution)/shard_map/pallas_call | solution.py:615
  30.9 5.6 %all-to-all-done = f32[32,1,128]{2,1,0:T(1,128)S(1)} async-done(((f32[32,1,128]{2,1,0:T(1,128)}), f32[32,1,128]{2,1,0:T(1,128)S(1)}, u32[]{:S(2)}, u32[]{:S(2)}) %all-to-all-start) | async-done | bytes 16416 | tf_op jit(solution)/shard_map/all_to_all | solution.py:612
  36.5 0.0 copy-done
  36.5 0.0 copy-done.1
  36.5 1.2 %shard_map.85 = f32[256,128]{1,0:T(8,128)} custom-call(f32[32,128]{1,0:T(8,128)S(1)} %bitcast.6, s32[1,32]{1,0:T(1,128)S(1)} %copy-done.1, bf16[256,1024]{1,0:T(8,128)(2,1)S(1)} %copy-done), custom_call_target="tpu_custom_call" | custom-call | tf_op jit(solution)/shard_map/pallas_call | solution.py:623
Async XLA Ops:
  1.7 6.0 %collective-permute-start = (bf16[480,128]{1,0:T(8,128)(2,1)S(1)}, bf16[480,128]{1,0:T(8,128)(2,1)S(1)}, u32[]{:S(2)}, u32[]{:S(2)}) collective-permute-start(bf16[480,128]{1,0:T(8,128)(2,1)S(1)} %get-tuple-element.20), channel_id=1, source_target_pairs={{0,8},{8,0},{16,24},{24,16},{1,9},{9,1},{17,25},{25,17},{2,10},{10... | collective-permute-start | bytes 368648 | tf_op jit(solution)/shard_map/ppermute | solution.py:536
  2.2 5.4 %collective-permute-start.1 = (bf16[480,128]{1,0:T(8,128)(2,1)S(1)}, bf16[480,128]{1,0:T(8,128)(2,1)S(1)}, u32[]{:S(2)}, u32[]{:S(2)}) collective-permute-start(bf16[480,128]{1,0:T(8,128)(2,1)S(1)} %get-tuple-element.21), channel_id=1, source_target_pairs={{0,0},{8,16},{16,8},{24,24},{1,1},{9,17},{17,9},{25,25},{2,2},{10,... | collective-permute-start | bytes 368648 | tf_op jit(solution)/shard_map/ppermute | solution.py:536
  2.9 7.5 %collective-permute-start.2 = (bf16[240,128]{1,0:T(8,128)(2,1)S(1)}, bf16[240,128]{1,0:T(8,128)(2,1)S(1)}, u32[]{:S(2)}, u32[]{:S(2)}) collective-permute-start(bf16[240,128]{1,0:T(8,128)(2,1)S(1)} %get-tuple-element.22), channel_id=1, source_target_pairs={{0,6},{2,4},{4,2},{6,0},{1,7},{3,5},{5,3},{7,1},{8,14},{10,12},{12... | collective-permute-start | bytes 184328 | tf_op jit(solution)/shard_map/ppermute | solution.py:536
  7.6 4.9 %collective-permute-start.3 = (bf16[240,128]{1,0:T(8,128)(2,1)S(1)}, bf16[240,128]{1,0:T(8,128)(2,1)S(1)}, u32[]{:S(2)}, u32[]{:S(2)}) collective-permute-start(bf16[240,128]{1,0:T(8,128)(2,1)S(1)} %get-tuple-element.23), channel_id=1, source_target_pairs={{0,2},{2,0},{4,6},{6,4},{1,3},{3,1},{5,7},{7,5},{8,10},{10,8},{12,... | collective-permute-start | bytes 184328 | tf_op jit(solution)/shard_map/ppermute | solution.py:536
  7.7 6.0 %collective-permute-start.4 = (bf16[160,128]{1,0:T(8,128)(2,1)S(1)}, bf16[160,128]{1,0:T(8,128)(2,1)S(1)}, u32[]{:S(2)}, u32[]{:S(2)}) collective-permute-start(bf16[160,128]{1,0:T(8,128)(2,1)S(1)} %get-tuple-element.24), channel_id=1, source_target_pairs={{0,6},{2,4},{4,2},{6,0},{1,7},{3,5},{5,3},{7,1},{8,14},{10,12},{12... | collective-permute-start | bytes 122888 | tf_op jit(solution)/shard_map/ppermute | solution.py:536
  8.7 5.1 %collective-permute-start.5 = (bf16[160,128]{1,0:T(8,128)(2,1)S(1)}, bf16[160,128]{1,0:T(8,128)(2,1)S(1)}, u32[]{:S(2)}, u32[]{:S(2)}) collective-permute-start(bf16[160,128]{1,0:T(8,128)(2,1)S(1)} %get-tuple-element.25), channel_id=1, source_target_pairs={{0,2},{2,0},{4,6},{6,4},{1,3},{3,1},{5,7},{7,5},{8,10},{10,8},{12,... | collective-permute-start | bytes 122888 | tf_op jit(solution)/shard_map/ppermute | solution.py:536
  14.2 4.1 %collective-permute-start.6 = (bf16[160,128]{1,0:T(8,128)(2,1)S(1)}, bf16[160,128]{1,0:T(8,128)(2,1)S(1)}, u32[]{:S(2)}, u32[]{:S(2)}) collective-permute-start(bf16[160,128]{1,0:T(8,128)(2,1)S(1)} %get-tuple-element.29), channel_id=1, source_target_pairs={{0,1},{1,0},{2,3},{3,2},{4,5},{5,4},{6,7},{7,6},{8,9},{9,8},{10,11... | collective-permute-start | bytes 122888 | tf_op jit(solution)/shard_map/ppermute | solution.py:595
  21.9 14.5 %copy-start = (bf16[256,1024]{1,0:T(8,128)(2,1)S(1)}, bf16[256,1024]{1,0:T(8,128)(2,1)}, u32[]{:S(2)}) copy-start(bf16[256,1024]{1,0:T(8,128)(2,1)} %weight.1) | copy-start | bytes 1572868
  21.9 14.5 %copy-start.1 = (s32[1,32]{1,0:T(1,128)S(1)}, s32[1,32]{1,0:T(1,128)}, u32[]{:S(2)}) copy-start(s32[1,32]{1,0:T(1,128)} %offsets.1) | copy-start | bytes 388
  21.9 14.5 %all-to-all-start = ((f32[32,1,128]{2,1,0:T(1,128)}), f32[32,1,128]{2,1,0:T(1,128)S(1)}, u32[]{:S(2)}, u32[]{:S(2)}) async-start(f32[32,1,128]{2,1,0:T(1,128)} %get-tuple-element.33), calls=%async_computation | async-start | bytes 32768 | tf_op jit(solution)/shard_map/all_to_all | solution.py:612

commit v17 on v16

--- a/solution.py
+++ b/solution.py
@@ -366,8 +366,7 @@
 
     step = (ca + 2 * MID) // STEPS
 
-    @pl.loop(0, STEPS)
-    def _(i):
+    for i in range(STEPS):
         js = [low - 4 + step * i + k for k in range(step)]
         us = []
         for j in js:
@@ -414,8 +413,7 @@
 
     step2 = (ca + MID) // STEPS
 
-    @pl.loop(0, STEPS)
-    def _(i):
+    for i in range(STEPS):
         js = [low - 2 + step2 * i + k for k in range(step2)]
         us = []
         for j in js:
@@ -434,8 +432,7 @@
         for j in range(low, high):
             u0_out[f, j - low] = first[f, j, 0:ROWS]
 
-    @pl.loop(0, ca)
-    def _(i):
+    for i in range(ca):
         u = split_state([u2_out[f, i + 2, 0:ROWS] for f in range(5)])
         note(2, low + i, u)
 
@@ -468,8 +465,7 @@
 
     step = ca // STEPS
 
-    @pl.loop(0, STEPS)
-    def _(i):
+    for i in range(STEPS):
         js = [2 + step * i + k for k in range(step)]
         us = [split_state([u2[f, j] for f in range(5)]) for j in js]
         both_sides(us, js, fax, part, banded)

time: 37.8 us -> 37.7 us (level)
  no operation moved by 1% of the time
where the time goes in v17:
time: 37.7 us; the launch traced here: 37.6 us
  starting transfers between devices  17 us (45%)
  waiting for transfers between devices  11.1 us (29%)
  Pallas kernels  8.65 us (23%)
  between operations  0.72 us (2%)
    ppermute x6, starting transfers between devices, swap(): return (lax.ppermute(first, axis, one), lax.ppermute(second, axis, two))  8.02 us
    all_to_all x1, starting transfers between devices, local(): lax.all_to_all(q, ('y', 'core', 'az', 'rad'), 0, 0, tiled=True)  7.46 us
    all_to_all x1, waiting for transfers between devices, local(): lax.all_to_all(q, ('y', 'core', 'az', 'rad'), 0, 0, tiled=True)  5.56 us
    pallas_call x1, Pallas kernels, local(): call(part(stages, n_ax, n_rad, ca, cz, slots), (struct((ndev, 1, 128)), s...  3.53 us
    ppermute x6, waiting for transfers between devices, swap(): return (lax.ppermute(first, axis, one), lax.ppermute(second, axis, two))  3.06 us
    ppermute x1, waiting for transfers between devices, local(): sides = (lax.ppermute(got[1], 'rad', [(0, 1), (1, 0)]),)  2.51 us
    ppermute x1, starting transfers between devices, local(): sides = (lax.ppermute(got[1], 'rad', [(0, 1), (1, 0)]),)  1.55 us
    pallas_call x1, Pallas kernels, local(): call(part(last_stage, ca, cz), struct((5, ca, cz, cr)), [VMEM] * 3, [pltp...  1.48 us
  transfers between devices with their start and end apart: 8, of which 4 were waited for; matrix products, arithmetic and copies ran while one was open for 0% of the time, Pallas kernels for 7%

profile of v17, /device:TPU:0, one launch (start us, length us, event | category | flops | bytes accessed | tf_op | source)
XLA Modules:
  0.0 37.6 jit_solution(5274281135498355988)
XLA Ops:
  0.6 1.0 %shard_map.77 = (f32[640,128]{1,0:T(8,128)S(1)}, bf16[480,128]{1,0:T(8,128)(2,1)S(1)}, bf16[480,128]{1,0:T(8,128)(2,1)S(1)}) custom-call(f32[128,128]{1,0:T(8,128)} %bitcast.8, f32[384,128]{1,0:T(8,128)} %bitcast.7, f32[128,128]{1,0:T(8,128)} %bitcast.9), custom_call_target="tpu_custom_call" | custom-call | tf_op jit(solution)/shard_map/pallas_call | solution.py:546
  1.7 0.5 %collective-permute-start = (bf16[480,128]{1,0:T(8,128)(2,1)S(1)}, bf16[480,128]{1,0:T(8,128)(2,1)S(1)}, u32[]{:S(2)}, u32[]{:S(2)}) collective-permute-start(bf16[480,128]{1,0:T(8,128)(2,1)S(1)} %get-tuple-element.20), channel_id=1, source_target_pairs={{0,8},{8,0},{16,24},{24,16},{1,9},{9,1},{17,25},{25,17},{2,10},{10... | collective-permute-start | bytes 368648 | tf_op jit(solution)/shard_map/ppermute | solution.py:532
  2.2 0.7 %collective-permute-start.1 = (bf16[480,128]{1,0:T(8,128)(2,1)S(1)}, bf16[480,128]{1,0:T(8,128)(2,1)S(1)}, u32[]{:S(2)}, u32[]{:S(2)}) collective-permute-start(bf16[480,128]{1,0:T(8,128)(2,1)S(1)} %get-tuple-element.21), channel_id=1, source_target_pairs={{0,0},{8,16},{16,8},{24,24},{1,1},{9,17},{17,9},{25,25},{2,2},{10,... | collective-permute-start | bytes 368648 | tf_op jit(solution)/shard_map/ppermute | solution.py:532
  2.8 0.1 shard_map.79
  2.9 4.7 %collective-permute-start.2 = (bf16[240,128]{1,0:T(8,128)(2,1)S(1)}, bf16[240,128]{1,0:T(8,128)(2,1)S(1)}, u32[]{:S(2)}, u32[]{:S(2)}) collective-permute-start(bf16[240,128]{1,0:T(8,128)(2,1)S(1)} %get-tuple-element.22), channel_id=1, source_target_pairs={{0,6},{2,4},{4,2},{6,0},{1,7},{3,5},{5,3},{7,1},{8,14},{10,12},{12... | collective-permute-start | bytes 184328 | tf_op jit(solution)/shard_map/ppermute | solution.py:532
  7.6 0.0 collective-permute-start.3
  7.6 0.0 collective-permute-done.ax1.got1
  7.6 0.0 collective-permute-done.1.ax2.got2
  7.6 0.1 shard_map.81
  7.7 1.0 %collective-permute-start.4 = (bf16[160,128]{1,0:T(8,128)(2,1)S(1)}, bf16[160,128]{1,0:T(8,128)(2,1)S(1)}, u32[]{:S(2)}, u32[]{:S(2)}) collective-permute-start(bf16[160,128]{1,0:T(8,128)(2,1)S(1)} %get-tuple-element.24), channel_id=1, source_target_pairs={{0,6},{2,4},{4,2},{6,0},{1,7},{3,5},{5,3},{7,1},{8,14},{10,12},{12... | collective-permute-start | bytes 122888 | tf_op jit(solution)/shard_map/ppermute | solution.py:532
  8.7 1.2 %collective-permute-start.5 = (bf16[160,128]{1,0:T(8,128)(2,1)S(1)}, bf16[160,128]{1,0:T(8,128)(2,1)S(1)}, u32[]{:S(2)}, u32[]{:S(2)}) collective-permute-start(bf16[160,128]{1,0:T(8,128)(2,1)S(1)} %get-tuple-element.25), channel_id=1, source_target_pairs={{0,2},{2,0},{4,6},{6,4},{1,3},{3,1},{5,7},{7,5},{8,10},{10,8},{12,... | collective-permute-start | bytes 122888 | tf_op jit(solution)/shard_map/ppermute | solution.py:532
  9.9 0.5 %shard_map.78 = (f32[3200,128]{1,0:T(8,128)S(1)}, bf16[256,256]{1,0:T(8,128)(2,1)S(1)}, bf16[2048,128]{1,0:T(8,128)(2,1)S(1)}, bf16[128,512]{1,0:T(8,128)(2,1)S(1)}) custom-call(f32[640,128]{1,0:T(8,128)S(1)} %get-tuple-element.18.home), custom_call_target="tpu_custom_call" | custom-call | tf_op jit(solution)/shard_map/pallas_call | solution.py:559
  10.4 0.0 collective-permute-done.2.az1
  10.4 2.1 %collective-permute-done.3.az2 = bf16[240,128]{1,0:T(8,128)(2,1)S(1)} collective-permute-done((bf16[240,128]{1,0:T(8,128)(2,1)S(1)}, bf16[240,128]{1,0:T(8,128)(2,1)S(1)}, u32[]{:S(2)}, u32[]{:S(2)}) %collective-permute-start.3) | collective-permute-done | bytes 61472 | tf_op jit(solution)/shard_map/ppermute | solution.py:532
  12.5 0.3 shard_map.80.block_in
  12.8 1.0 %collective-permute-done.4.corner1 = bf16[160,128]{1,0:T(8,128)(2,1)S(1)} collective-permute-done((bf16[160,128]{1,0:T(8,128)(2,1)S(1)}, bf16[160,128]{1,0:T(8,128)(2,1)S(1)}, u32[]{:S(2)}, u32[]{:S(2)}) %collective-permute-start.4) | collective-permute-done | bytes 40992 | tf_op jit(solution)/shard_map/ppermute | solution.py:532
  13.8 0.0 collective-permute-done.5.corner2
  13.8 0.5 %shard_map.82 = (f32[3200,128]{1,0:T(8,128)S(1)}, bf16[160,128]{1,0:T(8,128)(2,1)S(1)}) custom-call(f32[3200,128]{1,0:T(8,128)S(1)} %shard_map.80.block_in, bf16[160,128]{1,0:T(8,128)(2,1)S(1)} %collective-permute-done.4.corner1, bf16[160,128]{1,0:T(8,128)(2,1)S(1)} %collective-permute-done.5.corner2, ...), custom_call_target="tpu_custom_call", output_to_operand_aliasing={{0}: (0, {})} | custom-call | tf_op jit(solution)/shard_map/pallas_call | solution.py:581
  14.2 1.6 %collective-permute-start.6 = (bf16[160,128]{1,0:T(8,128)(2,1)S(1)}, bf16[160,128]{1,0:T(8,128)(2,1)S(1)}, u32[]{:S(2)}, u32[]{:S(2)}) collective-permute-start(bf16[160,128]{1,0:T(8,128)(2,1)S(1)} %get-tuple-element.29), channel_id=1, source_target_pairs={{0,1},{1,0},{2,3},{3,2},{4,5},{5,4},{6,7},{7,6},{8,9},{9,8},{10,11... | collective-permute-start | bytes 122888 | tf_op jit(solution)/shard_map/ppermute | solution.py:591
  15.8 2.5 %collective-permute-done.6.refs_0_ = bf16[160,128]{1,0:T(8,128)(2,1)S(1)} collective-permute-done((bf16[160,128]{1,0:T(8,128)(2,1)S(1)}, bf16[160,128]{1,0:T(8,128)(2,1)S(1)}, u32[]{:S(2)}, u32[]{:S(2)}) %collective-permute-start.6) | collective-permute-done | bytes 40992 | tf_op jit(solution)/shard_map/ppermute | solution.py:591
  18.3 3.5 %shard_map.83 = (f32[32,1,128]{2,1,0:T(1,128)}, f32[5,12,40,128]{3,2,1,0:T(8,128)S(1)}, f32[5,8,32,128]{3,2,1,0:T(8,128)S(1)}) custom-call(f32[5,20,32,128]{3,2,1,0:T(8,128)S(1)} %bitcast.5, bf16[256,256]{1,0:T(8,128)(2,1)S(1)} %get-tuple-element.28.banded, s32[32]{0:T(128)} %cells_far.1, bf16[160,128]{1,0:T(8,128)(2,1)S(1)} %collective-permute-done.6.refs_0_, ...), custom_call_target="tpu_custom_call" | custom-call | tf_op jit(solution)/shard_map/pallas_call | solution.py:597
  21.8 0.0 copy-start
  21.8 0.0 copy-start.1
  21.9 7.5 %all-to-all-start = ((f32[32,1,128]{2,1,0:T(1,128)}), f32[32,1,128]{2,1,0:T(1,128)S(1)}, u32[]{:S(2)}, u32[]{:S(2)}) async-start(f32[32,1,128]{2,1,0:T(1,128)} %get-tuple-element.33), calls=%async_computation | async-start | bytes 32768 | tf_op jit(solution)/shard_map/all_to_all | solution.py:608
  29.3 1.5 %shard_map.84 = f32[5,8,16,128]{3,2,1,0:T(8,128)} custom-call(f32[5,12,40,128]{3,2,1,0:T(8,128)S(1)} %get-tuple-element.31.u2, f32[5,8,32,128]{3,2,1,0:T(8,128)S(1)} %get-tuple-element.32.u0, bf16[256,256]{1,0:T(8,128)(2,1)S(1)} %get-tuple-element.28.banded), custom_call_target="tpu_custom_call" | custom-call | flops 400000000 | bytes 8000000 | tf_op jit(solution)/shard_map/pallas_call | solution.py:611
  30.8 5.6 %all-to-all-done = f32[32,1,128]{2,1,0:T(1,128)S(1)} async-done(((f32[32,1,128]{2,1,0:T(1,128)}), f32[32,1,128]{2,1,0:T(1,128)S(1)}, u32[]{:S(2)}, u32[]{:S(2)}) %all-to-all-start) | async-done | bytes 16416 | tf_op jit(solution)/shard_map/all_to_all | solution.py:608
  36.4 0.0 copy-done
  36.4 0.0 copy-done.1
  36.4 1.2 %shard_map.85 = f32[256,128]{1,0:T(8,128)} custom-call(f32[32,128]{1,0:T(8,128)S(1)} %bitcast.6, s32[1,32]{1,0:T(1,128)S(1)} %copy-done.1, bf16[256,1024]{1,0:T(8,128)(2,1)S(1)} %copy-done), custom_call_target="tpu_custom_call" | custom-call | tf_op jit(solution)/shard_map/pallas_call | solution.py:619
Async XLA Ops:
  1.7 6.0 %collective-permute-start = (bf16[480,128]{1,0:T(8,128)(2,1)S(1)}, bf16[480,128]{1,0:T(8,128)(2,1)S(1)}, u32[]{:S(2)}, u32[]{:S(2)}) collective-permute-start(bf16[480,128]{1,0:T(8,128)(2,1)S(1)} %get-tuple-element.20), channel_id=1, source_target_pairs={{0,8},{8,0},{16,24},{24,16},{1,9},{9,1},{17,25},{25,17},{2,10},{10... | collective-permute-start | bytes 368648 | tf_op jit(solution)/shard_map/ppermute | solution.py:532
  2.2 5.4 %collective-permute-start.1 = (bf16[480,128]{1,0:T(8,128)(2,1)S(1)}, bf16[480,128]{1,0:T(8,128)(2,1)S(1)}, u32[]{:S(2)}, u32[]{:S(2)}) collective-permute-start(bf16[480,128]{1,0:T(8,128)(2,1)S(1)} %get-tuple-element.21), channel_id=1, source_target_pairs={{0,0},{8,16},{16,8},{24,24},{1,1},{9,17},{17,9},{25,25},{2,2},{10,... | collective-permute-start | bytes 368648 | tf_op jit(solution)/shard_map/ppermute | solution.py:532
  2.9 7.5 %collective-permute-start.2 = (bf16[240,128]{1,0:T(8,128)(2,1)S(1)}, bf16[240,128]{1,0:T(8,128)(2,1)S(1)}, u32[]{:S(2)}, u32[]{:S(2)}) collective-permute-start(bf16[240,128]{1,0:T(8,128)(2,1)S(1)} %get-tuple-element.22), channel_id=1, source_target_pairs={{0,6},{2,4},{4,2},{6,0},{1,7},{3,5},{5,3},{7,1},{8,14},{10,12},{12... | collective-permute-start | bytes 184328 | tf_op jit(solution)/shard_map/ppermute | solution.py:532
  7.6 4.9 %collective-permute-start.3 = (bf16[240,128]{1,0:T(8,128)(2,1)S(1)}, bf16[240,128]{1,0:T(8,128)(2,1)S(1)}, u32[]{:S(2)}, u32[]{:S(2)}) collective-permute-start(bf16[240,128]{1,0:T(8,128)(2,1)S(1)} %get-tuple-element.23), channel_id=1, source_target_pairs={{0,2},{2,0},{4,6},{6,4},{1,3},{3,1},{5,7},{7,5},{8,10},{10,8},{12,... | collective-permute-start | bytes 184328 | tf_op jit(solution)/shard_map/ppermute | solution.py:532
  7.7 6.0 %collective-permute-start.4 = (bf16[160,128]{1,0:T(8,128)(2,1)S(1)}, bf16[160,128]{1,0:T(8,128)(2,1)S(1)}, u32[]{:S(2)}, u32[]{:S(2)}) collective-permute-start(bf16[160,128]{1,0:T(8,128)(2,1)S(1)} %get-tuple-element.24), channel_id=1, source_target_pairs={{0,6},{2,4},{4,2},{6,0},{1,7},{3,5},{5,3},{7,1},{8,14},{10,12},{12... | collective-permute-start | bytes 122888 | tf_op jit(solution)/shard_map/ppermute | solution.py:532
  8.7 5.1 %collective-permute-start.5 = (bf16[160,128]{1,0:T(8,128)(2,1)S(1)}, bf16[160,128]{1,0:T(8,128)(2,1)S(1)}, u32[]{:S(2)}, u32[]{:S(2)}) collective-permute-start(bf16[160,128]{1,0:T(8,128)(2,1)S(1)} %get-tuple-element.25), channel_id=1, source_target_pairs={{0,2},{2,0},{4,6},{6,4},{1,3},{3,1},{5,7},{7,5},{8,10},{10,8},{12,... | collective-permute-start | bytes 122888 | tf_op jit(solution)/shard_map/ppermute | solution.py:532
  14.2 4.1 %collective-permute-start.6 = (bf16[160,128]{1,0:T(8,128)(2,1)S(1)}, bf16[160,128]{1,0:T(8,128)(2,1)S(1)}, u32[]{:S(2)}, u32[]{:S(2)}) collective-permute-start(bf16[160,128]{1,0:T(8,128)(2,1)S(1)} %get-tuple-element.29), channel_id=1, source_target_pairs={{0,1},{1,0},{2,3},{3,2},{4,5},{5,4},{6,7},{7,6},{8,9},{9,8},{10,11... | collective-permute-start | bytes 122888 | tf_op jit(solution)/shard_map/ppermute | solution.py:591
  21.8 14.5 %copy-start = (bf16[256,1024]{1,0:T(8,128)(2,1)S(1)}, bf16[256,1024]{1,0:T(8,128)(2,1)}, u32[]{:S(2)}) copy-start(bf16[256,1024]{1,0:T(8,128)(2,1)} %weight.1) | copy-start | bytes 1572868
  21.8 14.5 %copy-start.1 = (s32[1,32]{1,0:T(1,128)S(1)}, s32[1,32]{1,0:T(1,128)}, u32[]{:S(2)}) copy-start(s32[1,32]{1,0:T(1,128)} %offsets.1) | copy-start | bytes 388
  21.9 14.5 %all-to-all-start = ((f32[32,1,128]{2,1,0:T(1,128)}), f32[32,1,128]{2,1,0:T(1,128)S(1)}, u32[]{:S(2)}, u32[]{:S(2)}) async-start(f32[32,1,128]{2,1,0:T(1,128)} %get-tuple-element.33), calls=%async_computation | async-start | bytes 32768 | tf_op jit(solution)/shard_map/all_to_all | solution.py:608
